TPU v7x, 32 devices: a whole 2x2x4 slice. The times are simulated.
32 devices in a mesh: lvl: 2 (over x), patch: 16 (over z, y, core).
Axes of the slice: x: 2, y: 2, z: 4, core: 2. Of those that a mesh axis runs over, the one named last changes fastest.
Arguments:
- coarse_input: float32 [16, 64, 192], P('patch', 'lvl'), may hold values from -6 to 6
- coarse_weight: float32 [192, 320], replicated, may hold values from -0.4375 to 0.4375
- fine_input: float32 [256, 256, 768], P(('lvl', 'patch')), may hold values from -6 to 6
- fine_target: float32 [256, 256, 768], P(('lvl', 'patch')), may hold values from -6 to 6
- crops: int32 [256, 4], P(('lvl', 'patch')), may hold values from 0 to 15, as said below
- in_weight: float32 [768, 320], replicated, may hold values from -0.21875 to 0.21875
- context_weight: float32 [320, 320], replicated, may hold values from -0.3125 to 0.3125
- out_weight: float32 [320, 768], replicated, may hold values from -0.3125 to 0.3125
Outputs:
- coarse_grad: float32 [16, 64, 192], P('patch', 'lvl')
- fine_grad: float32 [256, 256, 768], P(('lvl', 'patch'))
Inputs may be any that keep to these rules, and one draw needn't show every extreme that they name: `crops`: Columns: frame 0 to 15, offsets y and x 0 to 8 - 2 s, scale s 1 or 2; frames are unevenly used. In one device's aligned block of 8 patches no frame is named twice, and at most min(8, 1) of them name frames of one index of patch (frames 1 i to 1 i + 1 - 1); this most is reached on every device.
All inputs are finite; a program needn't handle non-finite values.
Results may differ from a plain program's by a relative error of at most 0.0003.
Values sent between devices are 32-bit elements; how exact they have to be, the bound alone decides.
No kernel may reach another device: no remote copies, remote signals or barrier semaphores. Data moves between devices by JAX's collectives and lax.ppermute only.
A program may use at most 128 MiB of HBM per device.

v0:
```python
import functools

import jax
import jax.numpy as jnp
from jax import lax
from jax.experimental import pallas as pl
from jax.experimental.pallas import tpu as pltpu
from jax.sharding import PartitionSpec as P

F32 = jnp.float32
BF16 = jnp.bfloat16
NN = (((1,), (0,)), ((), ()))
NT = (((1,), (1,)), ((), ()))
TN = (((0,), (0,)), ((), ()))
ROWS = 512
SIDE = 8
TALL = 12
LIMIT = 40 * 1024 * 1024


def split(value):
    high = value.astype(BF16)
    low = (value - high.astype(F32)).astype(BF16)
    return high, low


def dot(left, right, dims=NN):
    return lax.dot_general(left, right, dims, preferred_element_type=F32)


def dot3(left, right, dims=NN):
    return (
        dot(left[0], right[1], dims) + dot(left[1], right[0], dims) + dot(left[0], right[0], dims)
    )


def call(kernel, name, flops, out_shape, **kwargs):
    shapes = jax.tree.leaves(out_shape)
    moved = 2 * sum(s.size * 4 for s in shapes)
    return pl.pallas_call(
        kernel,
        out_shape=out_shape,
        name=name,
        cost_estimate=pl.CostEstimate(flops=flops, bytes_accessed=moved, transcendentals=0),
        compiler_params=pltpu.CompilerParams(vmem_limit_bytes=LIMIT),
        **kwargs,
    )


SMEM = pl.BlockSpec(memory_space=pltpu.SMEM)
VMEM = pl.BlockSpec(memory_space=pltpu.VMEM)


def find_crops(place_ref, table_ref, found_ref, peers, patches):
    for d in range(peers):
        found_ref[d] = -1

        def one(j, _):
            @pl.when(table_ref[d * patches + j, 0] == place_ref[0])
            def _():
                found_ref[d] = table_ref[d * patches + j, 1] * SIDE + table_ref[d * patches + j, 2]

            return 0

        lax.fori_loop(0, patches, one, 0, unroll=True)


def grid_row(row):
    return pl.ds(pl.multiple_of(row * SIDE, SIDE), SIDE)


def crop_kernel(peers, patches, place_ref, table_ref, mine_ref, other_ref, send_ref, found_ref, pad):
    half = place_ref[1]
    pad[8 * SIDE :, :] = jnp.zeros((4 * SIDE, pad.shape[1]), F32)
    for row in range(4):
        pad[grid_row(half * 4 + row), :] = mine_ref[0, row * SIDE : (row + 1) * SIDE, :]
        pad[grid_row((1 - half) * 4 + row), :] = other_ref[0, row * SIDE : (row + 1) * SIDE, :]
    find_crops(place_ref, table_ref, found_ref, peers, patches)
    for d in range(peers):
        base = jnp.maximum(found_ref[d], 0)
        top, left = base // SIDE, base % SIDE
        for a in range(4):
            line = pltpu.roll(pad[grid_row(top + a), :], SIDE - left, 0)
            send_ref[d * 16 + a * 4 : d * 16 + a * 4 + 4, :] = line[:4, :]


def scatter_kernel(peers, place_ref, found_ref, recv_ref, mine_ref, other_ref, pad):
    pad[...] = jnp.zeros_like(pad)
    blank = jnp.zeros((4, pad.shape[1]), F32)
    for d in range(peers):

        @pl.when(found_ref[d] >= 0)
        def _():
            top, left = found_ref[d] // SIDE, found_ref[d] % SIDE
            for a in range(4):
                part = recv_ref[d * 16 + a * 4 : d * 16 + a * 4 + 4, :]
                line = pltpu.roll(jnp.concatenate([part, blank], axis=0), left, 0)
                pad[grid_row(top + a), :] += line

    half = place_ref[1]
    for row in range(4):
        mine_ref[0, row * SIDE : (row + 1) * SIDE, :] = pad[grid_row(half * 4 + row), :]
        other_ref[0, row * SIDE : (row + 1) * SIDE, :] = pad[grid_row((1 - half) * 4 + row), :]


def first_kernel(x_ref, t_ref, win_ref, wo_ref, xw_ref, tw_ref, gram_ref, win_hi, win_lo, wo_hi, wo_lo):
    @pl.when(pl.program_id(0) == 0)
    def _():
        win_hi[...], win_lo[...] = split(win_ref[...])
        high, low = split(wo_ref[...])
        wo_hi[...], wo_lo[...] = high, low
        gram_ref[...] = dot3((high, low), (high, low), NT) + dot(low, low, NT)

    xw_ref[...] = dot3(split(x_ref[...]), (win_hi[...], win_lo[...]))
    tw_ref[...] = dot3(split(t_ref[...]), (wo_hi[...], wo_lo[...]), NT)


def row_scale(crops_ref, patches, shape, axis, each):
    index = lax.broadcasted_iota(jnp.int32, shape, axis) // each
    scale = jnp.zeros(shape, jnp.int32)
    for j in range(patches):
        scale = jnp.where(index == j, crops_ref[j, 3], scale)
    return scale


def chosen(crops_ref, patches, rows_first):
    shape = (patches * 64, patches * 16) if rows_first else (patches * 16, patches * 64)
    token_axis = 0 if rows_first else 1
    token = lax.broadcasted_iota(jnp.int32, shape, token_axis)
    slot = lax.broadcasted_iota(jnp.int32, shape, 1 - token_axis)
    scale = row_scale(crops_ref, patches, shape, token_axis, 64)
    group, column = (token // 16) % 4, token % 16
    wanted = token // 64 * 16 + (group * scale // 2) * 4 + column * scale // 8
    return jnp.where(slot == wanted, 1.0, 0.0).astype(BF16)


def middle_kernel(
    patches,
    peers,
    crops_ref,
    recv_ref,
    xw_ref,
    tw_ref,
    gram_ref,
    cwgt_ref,
    xwgt_ref,
    de_ref,
    send_ref,
    rows,
    slope,
    context,
    sums,
    gram_hi,
    gram_lo,
):
    step = pl.program_id(0)
    per_step = ROWS // 4

    @pl.when(step == 0)
    def _():
        for j in range(patches):
            start = pl.multiple_of(crops_ref[j, 0] * 16, 16)
            rows[j * 16 : j * 16 + 16, :] = recv_ref[pl.ds(start, 16), :]
        pre = dot3(split(rows[...]), split(cwgt_ref[...]))
        gate = jax.nn.sigmoid(pre)
        slope[...] = gate * (1.0 + pre * (1.0 - gate))
        projected = split(dot3(split(pre * gate), split(xwgt_ref[...])))
        pick = chosen(crops_ref, patches, True)
        context[...] = dot(pick, projected[1]) + dot(pick, projected[0])
        gram_hi[...], gram_lo[...] = split(gram_ref[...])

    width = xw_ref.shape[1]
    here = pl.ds(pl.multiple_of(step * per_step, per_step), per_step)
    groups = per_step // 16
    spread = context[here, :].reshape(groups, 1, 16, width)
    pre = xw_ref[...].reshape(groups, 4, 16, width) + spread
    pre = pre.reshape(ROWS, width)
    gate = jax.nn.sigmoid(pre)
    hidden = pre * gate
    dhidden = dot3(split(hidden), (gram_hi[...], gram_lo[...])) - tw_ref[...]
    de = dhidden * (gate * (1.0 + pre * (1.0 - gate)))
    de_ref[...] = de
    sums[here, :] = de.reshape(groups, 4, 16, width).sum(axis=1).reshape(per_step, width)

    @pl.when(step == pl.num_programs(0) - 1)
    def _():
        pick = chosen(crops_ref, patches, False)
        high, low = split(sums[...])
        dslot = dot(pick, low) + dot(pick, high)
        dcontext = dot3(split(dslot), split(xwgt_ref[...]), NT)
        grad = dot3(split(dcontext * slope[...]), split(cwgt_ref[...]), NT)
        send_ref[...] = jnp.zeros_like(send_ref)
        for j in range(patches):
            start = pl.multiple_of(crops_ref[j, 0] * 16, 16)
            send_ref[pl.ds(start, 16), :] = grad[j * 16 : j * 16 + 16, :]


def last_kernel(de_ref, win_ref, out_ref, win_hi, win_lo):
    @pl.when(pl.program_id(0) == 0)
    def _():
        win_hi[...], win_lo[...] = split(win_ref[...])

    out_ref[...] = dot3(split(de_ref[...]), (win_hi[...], win_lo[...]), NT)


def whole(shape):
    return pl.BlockSpec(shape, lambda i: (0,) * len(shape))


def by_rows(width):
    return pl.BlockSpec((ROWS, width), lambda i: (i, 0))


def body(coarse_input, coarse_weight, fine_input, fine_target, crops, in_weight, context_weight, out_weight):
    peers = lax.axis_size("patch")
    patches, tokens, values = fine_input.shape
    width = in_weight.shape[1]
    pixels = coarse_weight.shape[0]
    half = coarse_input.shape[1]
    count = patches * tokens
    steps = count // ROWS
    place = jnp.stack([lax.axis_index("patch"), lax.axis_index("lvl")]).astype(jnp.int32)
    swap = [(0, 1), (1, 0)]

    table = lax.all_to_all(
        jnp.broadcast_to(crops[None], (peers,) + crops.shape), "patch", 0, 0
    ).reshape(peers * patches, 4)
    other = lax.ppermute(coarse_input, "lvl", swap)

    send, found = call(
        functools.partial(crop_kernel, peers, patches),
        "crop",
        10000,
        (
            jax.ShapeDtypeStruct((peers * 16, pixels), F32),
            jax.ShapeDtypeStruct((peers,), jnp.int32),
        ),
        in_specs=[SMEM, SMEM, VMEM, VMEM],
        out_specs=(VMEM, SMEM),
        scratch_shapes=[pltpu.VMEM((TALL * SIDE, pixels), F32)],
    )(place, table, coarse_input, other)
    recv = lax.all_to_all(send, "patch", 0, 0, tiled=True)

    xw, tw, gram = call(
        first_kernel,
        "first",
        12 * count * values * width,
        (
            jax.ShapeDtypeStruct((count, width), F32),
            jax.ShapeDtypeStruct((count, width), F32),
            jax.ShapeDtypeStruct((width, width), F32),
        ),
        grid=(steps,),
        in_specs=[by_rows(values), by_rows(values), whole((values, width)), whole((width, values))],
        out_specs=(by_rows(width), by_rows(width), whole((width, width))),
        scratch_shapes=[pltpu.VMEM((values, width), BF16)] * 2 + [pltpu.VMEM((width, values), BF16)] * 2,
    )(fine_input.reshape(count, values), fine_target.reshape(count, values), in_weight, out_weight)

    de, back = call(
        functools.partial(middle_kernel, patches, peers),
        "middle",
        6 * count * width * width,
        (
            jax.ShapeDtypeStruct((count, width), F32),
            jax.ShapeDtypeStruct((peers * 16, pixels), F32),
        ),
        grid=(steps,),
        in_specs=[
            SMEM,
            whole((peers * 16, pixels)),
            by_rows(width),
            by_rows(width),
            whole((width, width)),
            whole((pixels, width)),
            whole((width, width)),
        ],
        out_specs=(by_rows(width), whole((peers * 16, pixels))),
        scratch_shapes=[
            pltpu.VMEM((patches * 16, pixels), F32),
            pltpu.VMEM((patches * 16, width), F32),
            pltpu.VMEM((patches * 64, width), F32),
            pltpu.VMEM((patches * 64, width), F32),
            pltpu.VMEM((width, width), BF16),
            pltpu.VMEM((width, width), BF16),
        ],
    )(crops, recv, xw, tw, gram, coarse_weight, context_weight)
    returned = lax.all_to_all(back, "patch", 0, 0, tiled=True)

    fine_grad = call(
        last_kernel,
        "last",
        6 * count * values * width,
        jax.ShapeDtypeStruct((count, values), F32),
        grid=(steps,),
        in_specs=[by_rows(width), whole((values, width))],
        out_specs=by_rows(values),
        scratch_shapes=[pltpu.VMEM((values, width), BF16)] * 2,
    )(de, in_weight)

    mine, theirs = call(
        functools.partial(scatter_kernel, peers),
        "scatter",
        10000,
        (
            jax.ShapeDtypeStruct((1, half, pixels), F32),
            jax.ShapeDtypeStruct((1, half, pixels), F32),
        ),
        in_specs=[SMEM, SMEM, VMEM],
        out_specs=(VMEM, VMEM),
        scratch_shapes=[pltpu.VMEM((TALL * SIDE, pixels), F32)],
    )(place, found, returned)
    coarse_grad = mine + lax.ppermute(theirs, "lvl", swap)
    return (coarse_grad, fine_grad.reshape(fine_input.shape))


def solution(mesh):
    in_specs = (
        P("patch", "lvl", None),
        P(),
        P(("lvl", "patch"), None, None),
        P(("lvl", "patch"), None, None),
        P(("lvl", "patch"), None),
        P(),
        P(),
        P(),
    )
    out_specs = (P("patch", "lvl", None), P(("lvl", "patch"), None, None))
    return jax.shard_map(body, mesh=mesh, in_specs=in_specs, out_specs=out_specs, check_vma=False)
```

profile of v0, /device:TPU:0, one launch (start us, length us, event | category | flops | bytes accessed | tf_op | source)
XLA Modules:
  0.0 79.9 jit_solution(5112671676351143806)
XLA Ops:
  0.6 1.3 %broadcast_in_dim.2 = s32[16,8,4]{1,2,0:T(4,128)} broadcast(s32[8,4]{0,1:T(4,128)} %param.12), dimensions={1,2} | broadcast | bytes 2176 | tf_op jit(solution)/shard_map/broadcast_in_dim | solution.py:226
  1.9 7.4 %all-to-all-start = ((s32[16,8,4]{1,2,0:T(4,128)}), s32[16,8,4]{1,2,0:T(4,128)S(1)}, u32[]{:S(2)}, u32[]{:S(2)}) async-start(s32[16,8,4]{1,2,0:T(4,128)} %broadcast_in_dim.2), calls=%async_computation | async-start | bytes 65536 | tf_op jit(solution)/shard_map/all_to_all | solution.py:225
  9.3 1.6 %collective-permute-start = (f32[1,32,192]{2,1,0:T(8,128)}, f32[1,32,192]{2,1,0:T(8,128)S(1)}, u32[]{:S(2)}, u32[]{:S(2)}) collective-permute-start(f32[1,32,192]{2,1,0:T(8,128)} %mine_ref.1), channel_id=1, source_target_pairs={{0,16},{16,0},{1,17},{17,1},{2,18},{18,2},{3,19},{19,3},{4,20},{20... | collective-permute-start | bytes 73736 | tf_op jit(solution)/shard_map/ppermute | solution.py:228
  10.9 0.1 pad_add_fusion.place_ref
  11.0 0.8 copy.16.crops_ref
  11.7 2.6 %copy.15.win_ref = f32[768,320]{1,0:T(8,128)} copy(f32[768,320]{0,1:T(8,128)} %param.13) | data formatting | bytes 1966080 | tf_op args[5]
  14.3 1.6 %all-to-all-done = s32[16,8,4]{1,2,0:T(4,128)S(1)} async-done(((s32[16,8,4]{1,2,0:T(4,128)}), s32[16,8,4]{1,2,0:T(4,128)S(1)}, u32[]{:S(2)}, u32[]{:S(2)}) %all-to-all-start) | async-done | bytes 2080 | tf_op jit(solution)/shard_map/all_to_all | solution.py:225
  16.0 0.2 copy.14
  16.1 0.0 collective-permute-done.other_ref
  16.1 0.0 copy-start.8
  16.1 0.8 copy-done.8
  16.9 2.7 %crop.1 = (f32[256,192]{1,0:T(8,128)}, s32[16]{0:T(128)S(1)}) custom-call(s32[2]{0:T(128)S(1)} %pad_add_fusion.place_ref, s32[128,4]{1,0:T(8,128)S(1)} %bitcast.13, f32[1,32,192]{2,1,0:T(8,128)S(1)} %copy-done.8, f32[1,32,192]{2,1,0:T(8,128)S(1)} %collective-permute-done.other_ref), custom_call_target="tpu_custom_call" | custom-call | flops 10000 | bytes 393344 | tf_op jit(solution)/shard_map/crop/pallas_call | solution.py:230
  19.6 4.3 %all-to-all-start.1 = ((f32[16,16,192]{2,1,0:T(8,128)}), f32[16,16,192]{2,1,0:T(8,128)S(1)}, u32[]{:S(2)}, u32[]{:S(2)}) async-start(f32[16,16,192]{2,1,0:T(8,128)} %bitcast.3), calls=%async_computation.1 | async-start | bytes 524288 | tf_op jit(solution)/shard_map/all_to_all | solution.py:242
  24.0 0.0 copy-start.2
  24.0 1.3 %copy-done.2 = f32[768,320]{1,0:T(8,128)S(1)} copy-done((f32[768,320]{1,0:T(8,128)S(1)}, f32[768,320]{1,0:T(8,128)}, u32[]{:S(2)}) %copy-start.2) | copy-done | bytes 983064
  25.2 0.0 copy-start.9
  25.2 1.2 %copy-done.9 = f32[320,768]{1,0:T(8,128)S(1)} copy-done((f32[320,768]{1,0:T(8,128)S(1)}, f32[320,768]{1,0:T(8,128)}, u32[]{:S(2)}) %copy-start.9) | copy-done | bytes 983064
  26.4 13.9 %first.1 = (f32[2048,320]{1,0:T(8,128)S(1)}, f32[2048,320]{1,0:T(8,128)S(1)}, f32[320,320]{1,0:T(8,128)S(1)}) custom-call(f32[2048,768]{1,0:T(8,128)} %bitcast.14, f32[2048,768]{1,0:T(8,128)} %bitcast.15, f32[768,320]{1,0:T(8,128)S(1)} %copy-done.2, f32[320,768]{1,0:T(8,128)S(1)} %copy-done.9), custom_call_target="tpu_custom_call" | custom-call | flops 6039797760 | bytes 11304960 | tf_op jit(solution)/shard_map/first/pallas_call | solution.py:244
  40.3 0.0 copy-start
  40.3 1.7 %copy-done = f32[2048,320]{1,0:T(8,128)} copy-done((f32[2048,320]{1,0:T(8,128)}, f32[2048,320]{1,0:T(8,128)S(1)}, u32[]{:S(2)}) %copy-start) | copy-done | bytes 2621464
  42.0 0.0 copy-start.5
  42.0 0.8 copy-done.5
  42.8 0.0 all-to-all-done.1
  42.8 0.0 copy-start.1
  42.8 1.9 %copy-done.1 = f32[2048,320]{1,0:T(8,128)S(1)} copy-done((f32[2048,320]{1,0:T(8,128)S(1)}, f32[2048,320]{1,0:T(8,128)}, u32[]{:S(2)}) %copy-start.1) | copy-done | bytes 2621464
  44.7 0.0 copy-start.4
  44.7 1.0 %copy-done.4 = f32[320,320]{1,0:T(8,128)S(1)} copy-done((f32[320,320]{1,0:T(8,128)S(1)}, f32[320,320]{1,0:T(8,128)}, u32[]{:S(2)}) %copy-start.4) | copy-done | bytes 409624
  45.7 0.0 copy-start.6
  45.7 1.0 %copy-done.6 = f32[320,320]{1,0:T(8,128)S(1)} copy-done((f32[320,320]{1,0:T(8,128)S(1)}, f32[320,320]{1,0:T(8,128)}, u32[]{:S(2)}) %copy-start.6) | copy-done | bytes 409624
  46.7 0.0 copy-start.7
  46.7 1.0 %copy-done.7 = f32[192,320]{1,0:T(8,128)S(1)} copy-done((f32[192,320]{1,0:T(8,128)S(1)}, f32[192,320]{1,0:T(8,128)}, u32[]{:S(2)}) %copy-start.7) | copy-done | bytes 245784
  47.7 0.0 copy-start.3
  47.7 7.2 %middle.1 = (f32[2048,320]{1,0:T(8,128)S(1)}, f32[256,192]{1,0:T(8,128)S(1)}) custom-call(s32[8,4]{1,0:T(8,128)S(1)} %copy.16.crops_ref, f32[256,192]{1,0:T(8,128)S(1)} %bitcast.10, f32[2048,320]{1,0:T(8,128)S(1)} %get-tuple-element.13.xw_ref, f32[2048,320]{1,0:T(8,128)S(1)} %copy-done.1, f32[320,320]{1,0:T(8,128)S(1)} %copy-done.6, ...), custom_call_target="tpu_custom_call" | custom-call | flops 1258291200 | bytes 5636096 | tf_op jit(solution)/shard_map/middle/pallas_call | solution.py:259
  54.9 15.9 %all_to_all.27 = f32[16,16,192]{2,1,0:T(8,128)S(1)} all-to-all(f32[16,16,192]{2,1,0:T(8,128)S(1)} %bitcast.12), channel_id=1, replica_groups=mesh['lvl'=2,'patch'=16] {'patch'}, dimensions={0} | all-to-all | bytes 393216 | tf_op jit(solution)/shard_map/all_to_all | solution.py:287
  70.7 0.8 %scatter.1 = (f32[1,32,192]{2,1,0:T(8,128)S(1)}, f32[1,32,192]{2,1,0:T(8,128)S(1)}) custom-call(s32[2]{0:T(128)S(1)} %pad_add_fusion.place_ref, s32[16]{0:T(128)S(1)} %get-tuple-element.11.found_ref, f32[256,192]{1,0:T(8,128)S(1)} %bitcast.11), custom_call_target="tpu_custom_call" | custom-call | flops 10000 | bytes 98304 | tf_op jit(solution)/shard_map/scatter/pallas_call | solution.py:300
  71.5 0.7 collective-permute-start.1
  72.3 0.0 copy-done.3
  72.3 7.0 %last.1 = f32[2048,768]{1,0:T(8,128)} custom-call(f32[2048,320]{1,0:T(8,128)S(1)} %get-tuple-element.19.de_ref, f32[768,320]{1,0:T(8,128)S(1)} %copy-done.3), custom_call_target="tpu_custom_call" | custom-call | flops 3019898880 | bytes 12582912 | tf_op jit(solution)/shard_map/last/pallas_call | solution.py:289
  79.3 0.0 collective-permute-done.1
  79.3 0.6 add.3
Async XLA Ops:
  1.9 14.0 %all-to-all-start = ((s32[16,8,4]{1,2,0:T(4,128)}), s32[16,8,4]{1,2,0:T(4,128)S(1)}, u32[]{:S(2)}, u32[]{:S(2)}) async-start(s32[16,8,4]{1,2,0:T(4,128)} %broadcast_in_dim.2), calls=%async_computation | async-start | bytes 65536 | tf_op jit(solution)/shard_map/all_to_all | solution.py:225
  9.3 6.8 %collective-permute-start = (f32[1,32,192]{2,1,0:T(8,128)}, f32[1,32,192]{2,1,0:T(8,128)S(1)}, u32[]{:S(2)}, u32[]{:S(2)}) collective-permute-start(f32[1,32,192]{2,1,0:T(8,128)} %mine_ref.1), channel_id=1, source_target_pairs={{0,16},{16,0},{1,17},{17,1},{2,18},{18,2},{3,19},{19,3},{4,20},{20... | collective-permute-start | bytes 73736 | tf_op jit(solution)/shard_map/ppermute | solution.py:228
  16.1 0.8 copy-start.8
  19.6 23.2 %all-to-all-start.1 = ((f32[16,16,192]{2,1,0:T(8,128)}), f32[16,16,192]{2,1,0:T(8,128)S(1)}, u32[]{:S(2)}, u32[]{:S(2)}) async-start(f32[16,16,192]{2,1,0:T(8,128)} %bitcast.3), calls=%async_computation.1 | async-start | bytes 524288 | tf_op jit(solution)/shard_map/all_to_all | solution.py:242
  24.0 1.3 %copy-start.2 = (f32[768,320]{1,0:T(8,128)S(1)}, f32[768,320]{1,0:T(8,128)}, u32[]{:S(2)}) copy-start(f32[768,320]{1,0:T(8,128)} %copy.15.win_ref) | copy-start | bytes 2949124
  25.2 1.2 %copy-start.9 = (f32[320,768]{1,0:T(8,128)S(1)}, f32[320,768]{1,0:T(8,128)}, u32[]{:S(2)}) copy-start(f32[320,768]{1,0:T(8,128)} %wo_ref.1) | copy-start | bytes 2949124
  40.3 1.7 %copy-start = (f32[2048,320]{1,0:T(8,128)}, f32[2048,320]{1,0:T(8,128)S(1)}, u32[]{:S(2)}) copy-start(f32[2048,320]{1,0:T(8,128)S(1)} %get-tuple-element.14.tw_ref) | copy-start | bytes 7864324
  42.0 0.8 copy-start.5
  42.8 1.9 %copy-start.1 = (f32[2048,320]{1,0:T(8,128)S(1)}, f32[2048,320]{1,0:T(8,128)}, u32[]{:S(2)}) copy-start(f32[2048,320]{1,0:T(8,128)} %copy-done) | copy-start | bytes 7864324
  44.7 1.0 %copy-start.4 = (f32[320,320]{1,0:T(8,128)S(1)}, f32[320,320]{1,0:T(8,128)}, u32[]{:S(2)}) copy-start(f32[320,320]{1,0:T(8,128)} %xwgt_ref.1) | copy-start | bytes 1228804
  45.7 1.0 %copy-start.6 = (f32[320,320]{1,0:T(8,128)S(1)}, f32[320,320]{1,0:T(8,128)}, u32[]{:S(2)}) copy-start(f32[320,320]{1,0:T(8,128)} %copy-done.5) | copy-start | bytes 1228804
  46.7 1.0 %copy-start.7 = (f32[192,320]{1,0:T(8,128)S(1)}, f32[192,320]{1,0:T(8,128)}, u32[]{:S(2)}) copy-start(f32[192,320]{1,0:T(8,128)} %cwgt_ref.1) | copy-start | bytes 737284
  47.7 24.6 %copy-start.3 = (f32[768,320]{1,0:T(8,128)S(1)}, f32[768,320]{1,0:T(8,128)}, u32[]{:S(2)}) copy-start(f32[768,320]{1,0:T(8,128)} %copy.15.win_ref) | copy-start | bytes 2949124
  71.5 7.7 %collective-permute-start.1 = (f32[1,32,192]{2,1,0:T(8,128)S(1)}, f32[1,32,192]{2,1,0:T(8,128)S(1)}, u32[]{:S(2)}, u32[]{:S(2)}) collective-permute-start(f32[1,32,192]{2,1,0:T(8,128)S(1)} %get-tuple-element.18), channel_id=1, source_target_pairs={{0,16},{16,0},{1,17},{17,1},{2,18},{18,2},{3,19},{19,3},{4,20},{20... | collective-permute-start | bytes 73736 | tf_op jit(solution)/shard_map/ppermute | solution.py:312
where the time goes:
time: 80.6 us; the launch traced here: 79.9 us
  Pallas kernels  31.6 us (39%)
  blocking collectives  15.9 us (20%)
  local copies, waits for them, and re-layouts  15.4 us (19%)
  starting transfers between devices  14 us (17%)
  waiting for transfers between devices  1.63 us (2%)
    all_to_all x1, blocking collectives, body(): returned = lax.all_to_all(back, 'patch', 0, 0, tiled=True)  15.9 us
    unnamed x22, local copies, waits for them, and re-layouts  14 us
    pallas_call x1, Pallas kernels, body(): call(first_kernel, 'first', 12 * count * values * width, (jax.ShapeDtypeS...  13.9 us
    all_to_all x1, starting transfers between devices, body(): lax.all_to_all(jnp.broadcast_to(crops[None], (peers,) + crops.shape), 'pa...  7.39 us
    pallas_call x1, Pallas kernels, body(): call(functools.partial(middle_kernel, patches, peers), 'middle', 6 * coun...  7.16 us
    pallas_call x1, Pallas kernels, body(): call(last_kernel, 'last', 6 * count * values * width, jax.ShapeDtypeStruc...  6.99 us
    all_to_all x1, starting transfers between devices, body(): recv = lax.all_to_all(send, 'patch', 0, 0, tiled=True)  4.34 us
    pallas_call x1, Pallas kernels, body(): call(functools.partial(crop_kernel, peers, patches), 'crop', 10000, (jax....  2.72 us
  transfers between devices with their start and end apart: 4, of which 1 were waited for; matrix products, arithmetic and copies ran while one was open for 5% of the time, Pallas kernels for 26%

commit v1 on v0

v1 whole, which is shorter than its diff:
```python
import functools

import jax
import jax.numpy as jnp
from jax import lax
from jax.experimental import pallas as pl
from jax.experimental.pallas import tpu as pltpu
from jax.sharding import PartitionSpec as P

F32 = jnp.float32
BF16 = jnp.bfloat16
NN = (((1,), (0,)), ((), ()))
NT = (((1,), (1,)), ((), ()))
TN = (((0,), (0,)), ((), ()))
ROWS = 512
SIDE = 8
MAIN = 256
LANES = 256
LIMIT = 60 * 1024 * 1024
SMEM = pl.BlockSpec(memory_space=pltpu.SMEM)
VMEM = pl.BlockSpec(memory_space=pltpu.VMEM)


def split(value):
    high = value.astype(BF16)
    low = (value - high.astype(F32)).astype(BF16)
    return high, low


def dot(left, right, dims=NN):
    return lax.dot_general(left, right, dims, preferred_element_type=F32)


def dot3(left, right, dims=NN):
    return (
        dot(left[0], right[1], dims) + dot(left[1], right[0], dims) + dot(left[0], right[0], dims)
    )


def sigmoid(value):
    return 0.5 * jnp.tanh(0.5 * value) + 0.5


def deep_left(value):
    high, low = split(value)
    tails = [high[:, MAIN:], low[:, MAIN:], high[:, MAIN:]]
    return jnp.concatenate([high[:, :MAIN], low[:, :MAIN], high[:, :MAIN]] + tails, axis=1)


def fill_deep_right(ref, value):
    high, low = split(value)
    tail = value.shape[0] - MAIN
    for part, rows in enumerate((low, high, high)):
        ref[part * MAIN : (part + 1) * MAIN, :] = rows[:MAIN]
        start = 3 * MAIN + part * tail
        ref[start : start + tail, :] = rows[MAIN:]


def call(kernel, name, flops, out_shape, **kwargs):
    shapes = jax.tree.leaves(out_shape)
    moved = 2 * sum(s.size * 4 for s in shapes)
    return pl.pallas_call(
        kernel,
        out_shape=out_shape,
        name=name,
        cost_estimate=pl.CostEstimate(flops=flops, bytes_accessed=moved, transcendentals=0),
        compiler_params=pltpu.CompilerParams(vmem_limit_bytes=LIMIT),
        **kwargs,
    )


def fill_wide(weight_ref, main, tail):
    values = weight_ref.shape[1]
    high, low = split(weight_ref[...])
    for part, block in enumerate((low, high, high)):
        main[:, part * values : (part + 1) * values] = block[:MAIN]
    rest = high.shape[0] - MAIN
    tail[:rest, :values] = high[MAIN:]
    tail[:rest, values:] = high[MAIN:]
    tail[rest:, :values] = low[MAIN:]
    tail[rest:, values:] = jnp.zeros((rest, values), BF16)
    return high, low


def wide_product(value, main, tail, out_ref):
    high, low = split(value)
    rest = tail.shape[0] // 2
    out_ref[:, :MAIN] = dot(jnp.concatenate([high, low, high], axis=1), main[...], NT)
    both = dot(jnp.concatenate([high, low], axis=1), tail[...], NT)
    out_ref[:, MAIN:] = both[:, :rest] + both[:, rest:]


def input_kernel(x_ref, weight_ref, out_ref, main, tail):
    @pl.when(pl.program_id(0) == 0)
    def _():
        fill_wide(weight_ref, main, tail)

    wide_product(x_ref[...], main, tail, out_ref)


def target_kernel(t_ref, weight_ref, out_ref, gram_ref, main, tail):
    @pl.when(pl.program_id(0) == 0)
    def _():
        high, low = fill_wide(weight_ref, main, tail)
        gram_ref[...] = dot3((high, low), (high, low), NT) + dot(low, low, NT)

    wide_product(t_ref[...], main, tail, out_ref)


def row_value(crops_ref, column, patches, shape, axis, each):
    index = lax.broadcasted_iota(jnp.int32, shape, axis) // each
    found = jnp.zeros(shape, jnp.int32)
    for j in range(patches):
        found = jnp.where(index == j, crops_ref[column, j], found)
    return found


def chosen(crops_ref, patches, rows_first):
    shape = (patches * 64, patches * 16) if rows_first else (patches * 16, patches * 64)
    token_axis = 0 if rows_first else 1
    token = lax.broadcasted_iota(jnp.int32, shape, token_axis)
    slot = lax.broadcasted_iota(jnp.int32, shape, 1 - token_axis)
    scale = row_value(crops_ref, 3, patches, shape, token_axis, 64)
    group, column = (token // 16) % 4, token % 16
    wanted = token // 64 * 16 + (group * scale // 2) * 4 + column * scale // 8
    return jnp.where(slot == wanted, 1.0, 0.0).astype(BF16)


def middle_kernel(
    patches,
    peers,
    place_ref,
    crops_ref,
    *refs,
):
    shard_refs, refs = refs[:8], refs[8:]
    xw_ref, tw_ref, gram_ref, cwgt_ref, xwgt_ref, de_ref = refs[:6]
    send_refs, refs = refs[6 : 6 + peers], refs[6 + peers :]
    shards, rows, slope, context, sums, gram, grads = refs
    step = pl.program_id(0)
    per_step = ROWS // 4
    far = peers // 4
    half = shard_refs[0].shape[1]
    pixels = cwgt_ref.shape[0]

    @pl.when(step == 0)
    def _():
        for code, ref in enumerate(shard_refs):
            for k in range(far):
                start = (code * far + k) * half
                shards[start : start + half, :] = ref[k]
        me, side = place_ref[0], place_ref[1]
        for j in range(patches):
            frame, top, left = crops_ref[0, j], crops_ref[1, j], crops_ref[2, j]
            near = lax.bitwise_xor(frame % 4, me % 4)
            k = (me // 4 - frame // 4 + far) % far
            for a in range(4):
                row = jnp.minimum(top + a, SIDE - 1)
                code = lax.bitwise_xor(row // 4, side) * 4 + near
                start = pl.multiple_of(((code * far + k) * 4 + row % 4) * SIDE, SIDE)
                line = pltpu.roll(shards[pl.ds(start, SIDE), :], SIDE - left, 0)
                rows[j * 16 + a * 4 : j * 16 + a * 4 + 4, :] = line[:4, :]
        pre = dot3(split(rows[...]), split(cwgt_ref[...]))
        gate = sigmoid(pre)
        slope[...] = gate * (1.0 + pre * (1.0 - gate))
        projected = split(dot3(split(pre * gate), split(xwgt_ref[...])))
        pick = chosen(crops_ref, patches, True)
        context[...] = dot(pick, projected[1]) + dot(pick, projected[0])
        fill_deep_right(gram, gram_ref[...])

    width = xw_ref.shape[1]
    here = pl.ds(pl.multiple_of(step * per_step, per_step), per_step)
    groups = per_step // 16
    spread = context[here, :].reshape(groups, 1, 16, width)
    pre = xw_ref[...].reshape(groups, 4, 16, width) + spread
    pre = pre.reshape(ROWS, width)
    gate = sigmoid(pre)
    hidden = pre * gate
    dhidden = dot(deep_left(hidden), gram[...]) - tw_ref[...]
    de = dhidden * (gate + hidden * (1.0 - gate))
    de_ref[...] = de
    sums[here, :] = de.reshape(groups, 4, 16, width).sum(axis=1).reshape(per_step, width)

    @pl.when(step == pl.num_programs(0) - 1)
    def _():
        pick = chosen(crops_ref, patches, False)
        high, low = split(sums[...])
        dslot = dot(pick, low) + dot(pick, high)
        dcontext = dot3(split(dslot), split(xwgt_ref[...]), NT)
        grads[:, :pixels] = dot3(split(dcontext * slope[...]), split(cwgt_ref[...]), NT)
        shape = (patches * 16, LANES - pixels)
        slot = lax.broadcasted_iota(jnp.int32, shape, 0) % 16
        top = row_value(crops_ref, 1, patches, shape, 0, 16)
        left = row_value(crops_ref, 2, patches, shape, 0, 16)
        grads[:, pixels:] = ((top + slot // 4) * SIDE + left + slot % 4).astype(F32)
        for k, ref in enumerate(send_refs):
            target = (place_ref[0] + k) % peers
            found = jnp.int32(-1)
            for j in range(patches):
                found = jnp.where(crops_ref[0, j] == target, j, found)
            start = pl.multiple_of(jnp.maximum(found, 0) * 16, 16)
            ref[...] = jnp.where(found >= 0, grads[pl.ds(start, 16), :], 0.0)


def scatter_kernel(peers, place_ref, *refs):
    message_refs, (mine_ref, other_ref, total) = refs[:peers], refs[peers:]
    pixels = mine_ref.shape[2]
    message = jnp.concatenate([ref[...] for ref in message_refs], axis=0)
    number = lax.broadcasted_iota(jnp.int32, (peers * 16, SIDE * SIDE), 1).astype(F32)
    pick = jnp.where(message[:, pixels : pixels + 1] == number, 1.0, 0.0).astype(BF16)
    high, low = split(message[:, :pixels])
    total[...] = dot(pick, low, TN) + dot(pick, high, TN)
    half = mine_ref.shape[1]
    side = place_ref[1]
    mine_ref[0] = total[pl.ds(pl.multiple_of(side * half, half), half), :]
    other_ref[0] = total[pl.ds(pl.multiple_of((1 - side) * half, half), half), :]


def last_kernel(de_ref, weight_ref, out_ref, deep):
    @pl.when(pl.program_id(0) == 0)
    def _():
        fill_deep_right(deep, weight_ref[...])

    out_ref[...] = dot(deep_left(de_ref[...]), deep[...])


def whole(shape):
    return pl.BlockSpec(shape, lambda i: (0,) * len(shape))


def by_rows(width):
    return pl.BlockSpec((ROWS, width), lambda i: (i, 0))


def body(coarse_input, coarse_weight, fine_input, fine_target, crops, in_weight, context_weight, out_weight):
    peers = lax.axis_size("patch")
    far = peers // 4
    patches, tokens, values = fine_input.shape
    width = in_weight.shape[1]
    pixels = coarse_weight.shape[0]
    half = coarse_input.shape[1]
    count = patches * tokens
    steps = count // ROWS
    depth = 3 * width
    place = jnp.stack([lax.axis_index("patch"), lax.axis_index("lvl")]).astype(jnp.int32)

    def to_peer(value, shift):
        return lax.ppermute(value, "patch", [(p, (p + shift) % peers) for p in range(peers)])

    def to_near(value, side, flip):
        both = [(s * peers + p, (s ^ side) * peers + (p ^ flip)) for s in range(2) for p in range(peers)]
        return lax.ppermute(value, ("lvl", "patch"), both)

    column = [coarse_input] + [to_peer(coarse_input, 4 * k) for k in range(1, far)]
    column = jnp.concatenate(column, axis=0)
    shards = {0: column}
    for code in (4, 2, 6, 1):
        shards[code] = to_near(column, code // 4, code % 4)
    for code in (2, 4, 6):
        shards[code + 1] = to_near(shards[code], 0, 1)
    shards = [shards[code] for code in range(8)]

    weight = in_weight.T
    scratch = [pltpu.VMEM((MAIN, 3 * values), BF16), pltpu.VMEM((2 * (width - MAIN), 2 * values), BF16)]
    xw = call(
        input_kernel,
        "input",
        6 * count * values * width,
        jax.ShapeDtypeStruct((count, width), F32),
        grid=(steps,),
        in_specs=[by_rows(values), whole((width, values))],
        out_specs=by_rows(width),
        scratch_shapes=scratch,
    )(fine_input.reshape(count, values), weight)
    tw, gram = call(
        target_kernel,
        "target",
        6 * count * values * width,
        (jax.ShapeDtypeStruct((count, width), F32), jax.ShapeDtypeStruct((width, width), F32)),
        grid=(steps,),
        in_specs=[by_rows(values), whole((width, values))],
        out_specs=(by_rows(width), whole((width, width))),
        scratch_shapes=scratch,
    )(fine_target.reshape(count, values), out_weight)

    message = (16, LANES)
    de, *sends = call(
        functools.partial(middle_kernel, patches, peers),
        "middle",
        6 * count * width * width,
        [jax.ShapeDtypeStruct((count, width), F32)] + [jax.ShapeDtypeStruct(message, F32)] * peers,
        grid=(steps,),
        in_specs=[SMEM, SMEM]
        + [whole((far, half, pixels))] * 8
        + [
            by_rows(width),
            by_rows(width),
            whole((width, width)),
            whole((pixels, width)),
            whole((width, width)),
        ],
        out_specs=[by_rows(width)] + [whole(message)] * peers,
        scratch_shapes=[
            pltpu.VMEM((8 * far * half, pixels), F32),
            pltpu.VMEM((patches * 16, pixels), F32),
            pltpu.VMEM((patches * 16, width), F32),
            pltpu.VMEM((patches * 64, width), F32),
            pltpu.VMEM((patches * 64, width), F32),
            pltpu.VMEM((depth, width), BF16),
            pltpu.VMEM((patches * 16, LANES), F32),
        ],
    )(place, crops.T, *shards, xw, tw, gram, coarse_weight, context_weight)
    returned = [sends[0]] + [to_peer(sends[k], k) for k in range(1, peers)]

    fine_grad = call(
        last_kernel,
        "last",
        6 * count * values * width,
        jax.ShapeDtypeStruct((count, values), F32),
        grid=(steps,),
        in_specs=[by_rows(width), whole((width, values))],
        out_specs=by_rows(values),
        scratch_shapes=[pltpu.VMEM((depth, values), BF16)],
    )(de, weight)

    part = jax.ShapeDtypeStruct((1, half, pixels), F32)
    mine, theirs = call(
        functools.partial(scatter_kernel, peers),
        "scatter",
        10000,
        (part, part),
        in_specs=[SMEM] + [VMEM] * peers,
        out_specs=(VMEM, VMEM),
        scratch_shapes=[pltpu.VMEM((SIDE * SIDE, pixels), F32)],
    )(place, *returned)
    coarse_grad = mine + to_near(theirs, 1, 0)
    return (coarse_grad, fine_grad.reshape(fine_input.shape))


def solution(mesh):
    in_specs = (
        P("patch", "lvl", None),
        P(),
        P(("lvl", "patch"), None, None),
        P(("lvl", "patch"), None, None),
        P(("lvl", "patch"), None),
        P(),
        P(),
        P(),
    )
    out_specs = (P("patch", "lvl", None), P(("lvl", "patch"), None, None))
    return jax.shard_map(body, mesh=mesh, in_specs=in_specs, out_specs=out_specs, check_vma=False)
```

time: 80.6 us -> 79.1 us (0.981); the launches traced: 79.9 us -> 77.5 us
  starting transfers between devices: 14 us -> 31.2 us
  blocking collectives: 15.9 us -> 0 us
  local copies, waits for them, and re-layouts: 15.4 us -> 1.24 us
  Pallas kernels: 31.6 us -> 37.1 us
  waiting for transfers between devices: 1.63 us -> 5.88 us
    ppermute x2 -> x26, starting transfers between devices: 2.3 us -> 31.2 us  [the longest x18 25 us: to_peer(): lax.ppermute(value, 'patch', [(p, (p + shift) % peers) for p in range(pee...]
    all_to_all x1 -> x0, blocking collectives: 15.9 us -> none  [body(): returned = lax.all_to_all(back, 'patch', 0, 0, tiled=True)]
    unnamed x22 -> x53, local copies, waits for them, and re-layouts: 14 us -> 1.23 us
    all_to_all x2 -> x0, starting transfers between devices: 11.7 us -> none  [the longest x1 7.39 us: body(): lax.all_to_all(jnp.broadcast_to(crops[None], (peers,) + crops.shape), 'pa...]
    ppermute x2 -> x26, waiting for transfers between devices: 0.01 us -> 5.88 us  [the longest x18 5.48 us: to_peer(): lax.ppermute(value, 'patch', [(p, (p + shift) % peers) for p in range(pee...]
    pallas_call x1, Pallas kernels: 7.16 us -> 9.99 us  [body(): call(functools.partial(middle_kernel, patches, peers), 'middle', 6 * coun...]
    pallas_call x3, Pallas kernels: 17.4 us -> 19.6 us  [the longest x1 9.45 us: body(): call(target_kernel, 'target', 6 * count * values * width, (jax.ShapeDtype...]
    all_to_all x2 -> x0, waiting for transfers between devices: 1.63 us -> none  [the longest x1 1.62 us: body(): lax.all_to_all(jnp.broadcast_to(crops[None], (peers,) + crops.shape), 'pa...]
  transfers between devices with their start and end apart: 4 -> 26, of which waited for: 1 -> 7; matrix products, arithmetic and copies ran while one was open for 5% -> 1% of each run, Pallas kernels for 26% -> 33%
where the time goes in v1:
time: 79.1 us; the launch traced here: 77.5 us
  Pallas kernels  37.1 us (47%)
  starting transfers between devices  31.2 us (39%)
  waiting for transfers between devices  5.88 us (7%)
  local copies, waits for them, and re-layouts  1.24 us (2%)
  other arithmetic  1.23 us (2%)
  between operations  0.91 us (1%)
    ppermute x18, starting transfers between devices, to_peer(): lax.ppermute(value, 'patch', [(p, (p + shift) % peers) for p in range(pee...  25 us
    pallas_call x1, Pallas kernels, body(): call(functools.partial(middle_kernel, patches, peers), 'middle', 6 * coun...  9.99 us
    pallas_call x1, Pallas kernels, body(): call(target_kernel, 'target', 6 * count * values * width, (jax.ShapeDtype...  9.45 us
    pallas_call x1, Pallas kernels, body(): call(input_kernel, 'input', 6 * count * values * width, jax.ShapeDtypeStr...  8.4 us
    pallas_call x1, Pallas kernels, body(): call(last_kernel, 'last', 6 * count * values * width, jax.ShapeDtypeStruc...  7.48 us
    ppermute x8, starting transfers between devices, to_near(): return lax.ppermute(value, ('lvl', 'patch'), both)  6.12 us
    ppermute x18, waiting for transfers between devices, to_peer(): lax.ppermute(value, 'patch', [(p, (p + shift) % peers) for p in range(pee...  5.48 us
    pallas_call x1, Pallas kernels, body(): call(functools.partial(scatter_kernel, peers), 'scatter', 10000, (part, p...  1.8 us
  transfers between devices with their start and end apart: 26, of which 7 were waited for; matrix products, arithmetic and copies ran while one was open for 1% of the time, Pallas kernels for 33%

profile of v1, /device:TPU:0, one launch (start us, length us, event | category | flops | bytes accessed | tf_op | source)
XLA Modules:
  0.0 77.5 jit_solution(8601787431135599599)
XLA Ops:
  0.6 4.1 %collective-permute-start.1 = (f32[1,32,192]{2,1,0:T(8,128)}, f32[1,32,192]{2,1,0:T(8,128)S(1)}, u32[]{:S(2)}, u32[]{:S(2)}) collective-permute-start(f32[1,32,192]{2,1,0:T(8,128)} %param.8), channel_id=1, source_target_pairs={{0,8},{1,9},{2,10},{3,11},{4,12},{5,13},{6,14},{7,15},{8,0},{9,1},... | collective-permute-start | bytes 73736 | tf_op jit(solution)/shard_map/ppermute | solution.py:248
  4.7 1.6 %collective-permute-start = (f32[1,32,192]{2,1,0:T(8,128)}, f32[1,32,192]{2,1,0:T(8,128)S(1)}, u32[]{:S(2)}, u32[]{:S(2)}) collective-permute-start(f32[1,32,192]{2,1,0:T(8,128)} %param.8), channel_id=1, source_target_pairs={{0,4},{1,5},{2,6},{3,7},{4,8},{5,9},{6,10},{7,11},{8,12},{9,13},{1... | collective-permute-start | bytes 73736 | tf_op jit(solution)/shard_map/ppermute | solution.py:248
  6.3 2.2 %collective-permute-start.2 = (f32[1,32,192]{2,1,0:T(8,128)}, f32[1,32,192]{2,1,0:T(8,128)S(1)}, u32[]{:S(2)}, u32[]{:S(2)}) collective-permute-start(f32[1,32,192]{2,1,0:T(8,128)} %param.8), channel_id=1, source_target_pairs={{0,12},{1,13},{2,14},{3,15},{4,0},{5,1},{6,2},{7,3},{8,4},{9,5},{1... | collective-permute-start | bytes 73736 | tf_op jit(solution)/shard_map/ppermute | solution.py:248
  8.6 8.4 %input.1.refs_8_ = f32[2048,320]{1,0:T(8,128)} custom-call(f32[2048,768]{1,0:T(8,128)} %bitcast.8, f32[320,768]{1,0:T(8,128)} %bitcast.10), custom_call_target="tpu_custom_call" | custom-call | flops 3019898880 | bytes 5242880 | tf_op jit(solution)/shard_map/input/pallas_call | solution.py:265
  17.0 0.0 collective-permute-done
  17.0 0.0 collective-permute-done.1
  17.1 2.5 %collective-permute-start.8 = (f32[4,32,192]{2,1,0:T(8,128)S(1)}, f32[4,32,192]{2,1,0:T(8,128)S(1)}, u32[]{:S(2)}, u32[]{:S(2)}) collective-permute-start(f32[4,32,192]{2,1,0:T(8,128)S(1)} %constant_dynamic-update-slice_fusion.refs_0_), channel_id=1, source_target_pairs={{0,18},{1,19},{2,16},{3,17},{4,22},{5,23},{6,20},{7,21},{8,26},{9,... | collective-permute-start | bytes 294920 | tf_op jit(solution)/shard_map/ppermute | solution.py:252
  19.6 0.5 collective-permute-start.6
  20.1 0.5 collective-permute-start.4
  20.6 9.4 %target.1 = (f32[2048,320]{1,0:T(8,128)}, f32[320,320]{1,0:T(8,128)}) custom-call(f32[2048,768]{1,0:T(8,128)} %bitcast.9, f32[320,768]{1,0:T(8,128)} %weight_ref.1), custom_call_target="tpu_custom_call" | custom-call | flops 3019898880 | bytes 6062080 | tf_op jit(solution)/shard_map/target/pallas_call | solution.py:275
  30.1 0.0 collective-permute-start.3
  30.1 0.0 collective-permute-done.8.refs_6_
  30.1 0.5 collective-permute-start.9
  30.6 0.0 collective-permute-done.6.refs_4_
  30.6 0.1 collective-permute-start.7
  30.7 0.0 collective-permute-done.4.refs_2_
  30.7 0.4 collective-permute-start.5
  31.1 0.6 pad_add_fusion.place_ref
  31.7 0.2 collective-permute-done.7.refs_5_
  31.9 0.2 collective-permute-done.5.refs_3_
  32.1 0.2 copy-done.4
  32.4 0.1 copy-done.5
  32.4 0.2 copy-done.6
  32.6 0.2 copy-done.7
  32.8 10.0 %middle.1 = (f32[2048,320]{1,0:T(8,128)}, f32[16,256]{1,0:T(8,128)}, f32[16,256]{1,0:T(8,128)}, f32[16,256]{1,0:T(8,128)}, f32[16,256]{1,0:T(8,128)}, /*index=5*...) custom-call(s32[2]{0:T(128)} %pad_add_fusion.place_ref, ...), custom_call_target="tpu_custom_call" | custom-call | flops 1258291200 | bytes 5767168 | tf_op jit(solution)/shard_map/middle/pallas_call | solution.py:287
  42.8 0.4 collective-permute-start.10
  43.2 1.5 %collective-permute-start.11 = (f32[16,256]{1,0:T(8,128)}, f32[16,256]{1,0:T(8,128)S(1)}, u32[]{:S(2)}, u32[]{:S(2)}) collective-permute-start(f32[16,256]{1,0:T(8,128)} %get-tuple-element.27), channel_id=1, source_target_pairs={{0,2},{1,3},{2,4},{3,5},{4,6},{5,7},{6,8},{7,9},{8,10},{9,11},{10,... | collective-permute-start | bytes 49160 | tf_op jit(solution)/shard_map/ppermute | solution.py:248
  44.7 0.4 collective-permute-start.12
  45.1 0.2 collective-permute-start.14
  45.3 3.7 %collective-permute-done.10.refs_1_ = f32[16,256]{1,0:T(8,128)S(1)} collective-permute-done((f32[16,256]{1,0:T(8,128)}, f32[16,256]{1,0:T(8,128)S(1)}, u32[]{:S(2)}, u32[]{:S(2)}) %collective-permute-start.10) | collective-permute-done | bytes 16416 | tf_op jit(solution)/shard_map/ppermute | solution.py:248
  48.9 0.7 collective-permute-start.15
  49.7 0.2 collective-permute-done.11.refs_2_
  49.8 0.7 collective-permute-start.16
  50.5 0.0 collective-permute-done.12.refs_3_
  50.5 2.8 %collective-permute-start.17 = (f32[16,256]{1,0:T(8,128)}, f32[16,256]{1,0:T(8,128)S(1)}, u32[]{:S(2)}, u32[]{:S(2)}) collective-permute-start(f32[16,256]{1,0:T(8,128)} %get-tuple-element.33), channel_id=1, source_target_pairs={{0,8},{1,9},{2,10},{3,11},{4,12},{5,13},{6,14},{7,15},{8,0},{9,1},... | collective-permute-start | bytes 49160 | tf_op jit(solution)/shard_map/ppermute | solution.py:248
  53.3 2.6 %collective-permute-start.19 = (f32[16,256]{1,0:T(8,128)}, f32[16,256]{1,0:T(8,128)S(1)}, u32[]{:S(2)}, u32[]{:S(2)}) collective-permute-start(f32[16,256]{1,0:T(8,128)} %get-tuple-element.35), channel_id=1, source_target_pairs={{0,10},{1,11},{2,12},{3,13},{4,14},{5,15},{6,0},{7,1},{8,2},{9,3},... | collective-permute-start | bytes 49160 | tf_op jit(solution)/shard_map/ppermute | solution.py:248
  56.0 4.1 %collective-permute-start.20 = (f32[16,256]{1,0:T(8,128)}, f32[16,256]{1,0:T(8,128)S(1)}, u32[]{:S(2)}, u32[]{:S(2)}) collective-permute-start(f32[16,256]{1,0:T(8,128)} %get-tuple-element.36), channel_id=1, source_target_pairs={{0,11},{1,12},{2,13},{3,14},{4,15},{5,0},{6,1},{7,2},{8,3},{9,4},{... | collective-permute-start | bytes 49160 | tf_op jit(solution)/shard_map/ppermute | solution.py:248
  60.1 0.6 collective-permute-start.22
  60.8 2.2 %collective-permute-start.23 = (f32[16,256]{1,0:T(8,128)}, f32[16,256]{1,0:T(8,128)S(1)}, u32[]{:S(2)}, u32[]{:S(2)}) collective-permute-start(f32[16,256]{1,0:T(8,128)} %get-tuple-element.39), channel_id=1, source_target_pairs={{0,14},{1,15},{2,0},{3,1},{4,2},{5,3},{6,4},{7,5},{8,6},{9,7},{10,... | collective-permute-start | bytes 49160 | tf_op jit(solution)/shard_map/ppermute | solution.py:248
  62.9 0.9 %collective-permute-start.24 = (f32[16,256]{1,0:T(8,128)}, f32[16,256]{1,0:T(8,128)S(1)}, u32[]{:S(2)}, u32[]{:S(2)}) collective-permute-start(f32[16,256]{1,0:T(8,128)} %get-tuple-element.40), channel_id=1, source_target_pairs={{0,15},{1,0},{2,1},{3,2},{4,3},{5,4},{6,5},{7,6},{8,7},{9,8},{10,9... | collective-permute-start | bytes 49160 | tf_op jit(solution)/shard_map/ppermute | solution.py:248
  63.8 0.2 collective-permute-done.21.refs_12_
  64.1 0.6 collective-permute-done.23.refs_14_
  64.7 0.8 collective-permute-done.24.refs_15_
  65.6 0.5 copy-done.24
  66.1 1.8 %scatter.1 = (f32[1,32,192]{2,1,0:T(8,128)}, f32[1,32,192]{2,1,0:T(8,128)}) custom-call(s32[2]{0:T(128)} %pad_add_fusion.place_ref, f32[16,256]{1,0:T(8,128)} %get-tuple-element.25.refs_0_, f32[16,256]{1,0:T(8,128)} %copy-done.10, f32[16,256]{1,0:T(8,128)} %copy-done.11, f32[16,256]{1,0:T(8,128)} %copy-done.12, f32[16,256]{1,0:T(8,128)} %copy-done.13, ...), custom_call_target="tpu_custom_call" | custom-call | flops 10000 | bytes 98304 | tf_op jit(solution)/shard_map/scatter/pallas_call | solution.py:327
  67.9 1.6 %collective-permute-start.25 = (f32[1,32,192]{2,1,0:T(8,128)}, f32[1,32,192]{2,1,0:T(8,128)S(1)}, u32[]{:S(2)}, u32[]{:S(2)}) collective-permute-start(f32[1,32,192]{2,1,0:T(8,128)} %get-tuple-element.42), channel_id=1, source_target_pairs={{0,16},{1,17},{2,18},{3,19},{4,20},{5,21},{6,22},{7,23},{8,24},{9,... | collective-permute-start | bytes 73736 | tf_op jit(solution)/shard_map/ppermute | solution.py:252
  69.4 7.5 %last.1 = f32[2048,768]{1,0:T(8,128)} custom-call(f32[2048,320]{1,0:T(8,128)} %get-tuple-element.43.de_ref, f32[320,768]{1,0:T(8,128)} %bitcast.11), custom_call_target="tpu_custom_call" | custom-call | flops 3019898880 | bytes 12582912 | tf_op jit(solution)/shard_map/last/pallas_call | solution.py:315
  76.9 0.6 add.3
  (65 shorter events, 0.1 us)
Async XLA Ops:
  0.6 16.3 %copy-start.9 = (f32[1,32,192]{2,1,0:T(8,128)S(1)}, f32[1,32,192]{2,1,0:T(8,128)}, u32[]{:S(2)}) copy-start(f32[1,32,192]{2,1,0:T(8,128)} %param.8) | copy-start | bytes 73732
  0.6 16.4 %collective-permute-start.1 = (f32[1,32,192]{2,1,0:T(8,128)}, f32[1,32,192]{2,1,0:T(8,128)S(1)}, u32[]{:S(2)}, u32[]{:S(2)}) collective-permute-start(f32[1,32,192]{2,1,0:T(8,128)} %param.8), channel_id=1, source_target_pairs={{0,8},{1,9},{2,10},{3,11},{4,12},{5,13},{6,14},{7,15},{8,0},{9,1},... | collective-permute-start | bytes 73736 | tf_op jit(solution)/shard_map/ppermute | solution.py:248
  4.7 12.2 %collective-permute-start = (f32[1,32,192]{2,1,0:T(8,128)}, f32[1,32,192]{2,1,0:T(8,128)S(1)}, u32[]{:S(2)}, u32[]{:S(2)}) collective-permute-start(f32[1,32,192]{2,1,0:T(8,128)} %param.8), channel_id=1, source_target_pairs={{0,4},{1,5},{2,6},{3,7},{4,8},{5,9},{6,10},{7,11},{8,12},{9,13},{1... | collective-permute-start | bytes 73736 | tf_op jit(solution)/shard_map/ppermute | solution.py:248
  6.3 10.7 %collective-permute-start.2 = (f32[1,32,192]{2,1,0:T(8,128)}, f32[1,32,192]{2,1,0:T(8,128)S(1)}, u32[]{:S(2)}, u32[]{:S(2)}) collective-permute-start(f32[1,32,192]{2,1,0:T(8,128)} %param.8), channel_id=1, source_target_pairs={{0,12},{1,13},{2,14},{3,15},{4,0},{5,1},{6,2},{7,3},{8,4},{9,5},{1... | collective-permute-start | bytes 73736 | tf_op jit(solution)/shard_map/ppermute | solution.py:248
  17.0 15.1 %copy-start = (f32[4,32,192]{2,1,0:T(8,128)}, f32[4,32,192]{2,1,0:T(8,128)S(1)}, u32[]{:S(2)}) copy-start(f32[4,32,192]{2,1,0:T(8,128)S(1)} %constant_dynamic-update-slice_fusion.refs_0_) | copy-start | bytes 294916
  17.1 13.0 %collective-permute-start.8 = (f32[4,32,192]{2,1,0:T(8,128)S(1)}, f32[4,32,192]{2,1,0:T(8,128)S(1)}, u32[]{:S(2)}, u32[]{:S(2)}) collective-permute-start(f32[4,32,192]{2,1,0:T(8,128)S(1)} %constant_dynamic-update-slice_fusion.refs_0_), channel_id=1, source_target_pairs={{0,18},{1,19},{2,16},{3,17},{4,22},{5,23},{6,20},{7,21},{8,26},{9,... | collective-permute-start | bytes 294920 | tf_op jit(solution)/shard_map/ppermute | solution.py:252
  19.6 11.0 %collective-permute-start.6 = (f32[4,32,192]{2,1,0:T(8,128)S(1)}, f32[4,32,192]{2,1,0:T(8,128)S(1)}, u32[]{:S(2)}, u32[]{:S(2)}) collective-permute-start(f32[4,32,192]{2,1,0:T(8,128)S(1)} %constant_dynamic-update-slice_fusion.refs_0_), channel_id=1, source_target_pairs={{0,16},{1,17},{2,18},{3,19},{4,20},{5,21},{6,22},{7,23},{8,24},{9,... | collective-permute-start | bytes 294920 | tf_op jit(solution)/shard_map/ppermute | solution.py:252
  20.1 10.6 %collective-permute-start.4 = (f32[4,32,192]{2,1,0:T(8,128)S(1)}, f32[4,32,192]{2,1,0:T(8,128)S(1)}, u32[]{:S(2)}, u32[]{:S(2)}) collective-permute-start(f32[4,32,192]{2,1,0:T(8,128)S(1)} %constant_dynamic-update-slice_fusion.refs_0_), channel_id=1, source_target_pairs={{0,2},{1,3},{2,0},{3,1},{4,6},{5,7},{6,4},{7,5},{8,10},{9,11},{10,... | collective-permute-start | bytes 294920 | tf_op jit(solution)/shard_map/ppermute | solution.py:252
  30.1 1.7 %collective-permute-start.3 = (f32[4,32,192]{2,1,0:T(8,128)S(1)}, f32[4,32,192]{2,1,0:T(8,128)S(1)}, u32[]{:S(2)}, u32[]{:S(2)}) collective-permute-start(f32[4,32,192]{2,1,0:T(8,128)S(1)} %constant_dynamic-update-slice_fusion.refs_0_), channel_id=1, source_target_pairs={{0,1},{1,0},{2,3},{3,2},{4,5},{5,4},{6,7},{7,6},{8,9},{9,8},{10,11... | collective-permute-start | bytes 294920 | tf_op jit(solution)/shard_map/ppermute | solution.py:252
  30.1 2.1 %copy-start.1 = (f32[4,32,192]{2,1,0:T(8,128)}, f32[4,32,192]{2,1,0:T(8,128)S(1)}, u32[]{:S(2)}) copy-start(f32[4,32,192]{2,1,0:T(8,128)S(1)} %collective-permute-done.8.refs_6_) | copy-start | bytes 294916
  30.1 1.6 %collective-permute-start.9 = (f32[4,32,192]{2,1,0:T(8,128)S(1)}, f32[4,32,192]{2,1,0:T(8,128)S(1)}, u32[]{:S(2)}, u32[]{:S(2)}) collective-permute-start(f32[4,32,192]{2,1,0:T(8,128)S(1)} %collective-permute-done.8.refs_6_), channel_id=1, source_target_pairs={{0,1},{1,0},{2,3},{3,2},{4,5},{5,4},{6,7},{7,6},{8,9},{9,8},{10,11... | collective-permute-start | bytes 294920 | tf_op jit(solution)/shard_map/ppermute | solution.py:252
  30.6 1.5 %copy-start.2 = (f32[4,32,192]{2,1,0:T(8,128)}, f32[4,32,192]{2,1,0:T(8,128)S(1)}, u32[]{:S(2)}) copy-start(f32[4,32,192]{2,1,0:T(8,128)S(1)} %collective-permute-done.6.refs_4_) | copy-start | bytes 294916
  30.6 1.3 %collective-permute-start.7 = (f32[4,32,192]{2,1,0:T(8,128)S(1)}, f32[4,32,192]{2,1,0:T(8,128)S(1)}, u32[]{:S(2)}, u32[]{:S(2)}) collective-permute-start(f32[4,32,192]{2,1,0:T(8,128)S(1)} %collective-permute-done.6.refs_4_), channel_id=1, source_target_pairs={{0,1},{1,0},{2,3},{3,2},{4,5},{5,4},{6,7},{7,6},{8,9},{9,8},{10,11... | collective-permute-start | bytes 294920 | tf_op jit(solution)/shard_map/ppermute | solution.py:252
  30.7 1.5 %copy-start.3 = (f32[4,32,192]{2,1,0:T(8,128)}, f32[4,32,192]{2,1,0:T(8,128)S(1)}, u32[]{:S(2)}) copy-start(f32[4,32,192]{2,1,0:T(8,128)S(1)} %collective-permute-done.4.refs_2_) | copy-start | bytes 294916
  30.7 1.4 %collective-permute-start.5 = (f32[4,32,192]{2,1,0:T(8,128)S(1)}, f32[4,32,192]{2,1,0:T(8,128)S(1)}, u32[]{:S(2)}, u32[]{:S(2)}) collective-permute-start(f32[4,32,192]{2,1,0:T(8,128)S(1)} %collective-permute-done.4.refs_2_), channel_id=1, source_target_pairs={{0,1},{1,0},{2,3},{3,2},{4,5},{5,4},{6,7},{7,6},{8,9},{9,8},{10,11... | collective-permute-start | bytes 294920 | tf_op jit(solution)/shard_map/ppermute | solution.py:252
  31.7 0.7 copy-start.5
  32.1 0.7 copy-start.7
  42.8 6.1 %collective-permute-start.10 = (f32[16,256]{1,0:T(8,128)}, f32[16,256]{1,0:T(8,128)S(1)}, u32[]{:S(2)}, u32[]{:S(2)}) collective-permute-start(f32[16,256]{1,0:T(8,128)} %get-tuple-element.26), channel_id=1, source_target_pairs={{0,1},{1,2},{2,3},{3,4},{4,5},{5,6},{6,7},{7,8},{8,9},{9,10},{10,1... | collective-permute-start | bytes 49160 | tf_op jit(solution)/shard_map/ppermute | solution.py:248
  43.2 6.6 %collective-permute-start.11 = (f32[16,256]{1,0:T(8,128)}, f32[16,256]{1,0:T(8,128)S(1)}, u32[]{:S(2)}, u32[]{:S(2)}) collective-permute-start(f32[16,256]{1,0:T(8,128)} %get-tuple-element.27), channel_id=1, source_target_pairs={{0,2},{1,3},{2,4},{3,5},{4,6},{5,7},{6,8},{7,9},{8,10},{9,11},{10,... | collective-permute-start | bytes 49160 | tf_op jit(solution)/shard_map/ppermute | solution.py:248
  44.7 5.8 %collective-permute-start.12 = (f32[16,256]{1,0:T(8,128)}, f32[16,256]{1,0:T(8,128)S(1)}, u32[]{:S(2)}, u32[]{:S(2)}) collective-permute-start(f32[16,256]{1,0:T(8,128)} %get-tuple-element.28), channel_id=1, source_target_pairs={{0,3},{1,4},{2,5},{3,6},{4,7},{5,8},{6,9},{7,10},{8,11},{9,12},{10... | collective-permute-start | bytes 49160 | tf_op jit(solution)/shard_map/ppermute | solution.py:248
  45.1 8.2 %collective-permute-start.13 = (f32[16,256]{1,0:T(8,128)}, f32[16,256]{1,0:T(8,128)S(1)}, u32[]{:S(2)}, u32[]{:S(2)}) collective-permute-start(f32[16,256]{1,0:T(8,128)} %get-tuple-element.29), channel_id=1, source_target_pairs={{0,4},{1,5},{2,6},{3,7},{4,8},{5,9},{6,10},{7,11},{8,12},{9,13},{1... | collective-permute-start | bytes 49160 | tf_op jit(solution)/shard_map/ppermute | solution.py:248
  45.1 8.2 %collective-permute-start.14 = (f32[16,256]{1,0:T(8,128)}, f32[16,256]{1,0:T(8,128)S(1)}, u32[]{:S(2)}, u32[]{:S(2)}) collective-permute-start(f32[16,256]{1,0:T(8,128)} %get-tuple-element.30), channel_id=1, source_target_pairs={{0,5},{1,6},{2,7},{3,8},{4,9},{5,10},{6,11},{7,12},{8,13},{9,14},{... | collective-permute-start | bytes 49160 | tf_op jit(solution)/shard_map/ppermute | solution.py:248
  48.9 16.6 %copy-start.10 = (f32[16,256]{1,0:T(8,128)}, f32[16,256]{1,0:T(8,128)S(1)}, u32[]{:S(2)}) copy-start(f32[16,256]{1,0:T(8,128)S(1)} %collective-permute-done.10.refs_1_) | copy-start | bytes 49156
  48.9 7.0 %collective-permute-start.15 = (f32[16,256]{1,0:T(8,128)}, f32[16,256]{1,0:T(8,128)S(1)}, u32[]{:S(2)}, u32[]{:S(2)}) collective-permute-start(f32[16,256]{1,0:T(8,128)} %get-tuple-element.31), channel_id=1, source_target_pairs={{0,6},{1,7},{2,8},{3,9},{4,10},{5,11},{6,12},{7,13},{8,14},{9,15},... | collective-permute-start | bytes 49160 | tf_op jit(solution)/shard_map/ppermute | solution.py:248
  49.8 15.7 %copy-start.11 = (f32[16,256]{1,0:T(8,128)}, f32[16,256]{1,0:T(8,128)S(1)}, u32[]{:S(2)}) copy-start(f32[16,256]{1,0:T(8,128)S(1)} %collective-permute-done.11.refs_2_) | copy-start | bytes 49156
  49.8 10.3 %collective-permute-start.16 = (f32[16,256]{1,0:T(8,128)}, f32[16,256]{1,0:T(8,128)S(1)}, u32[]{:S(2)}, u32[]{:S(2)}) collective-permute-start(f32[16,256]{1,0:T(8,128)} %get-tuple-element.32), channel_id=1, source_target_pairs={{0,7},{1,8},{2,9},{3,10},{4,11},{5,12},{6,13},{7,14},{8,15},{9,0},... | collective-permute-start | bytes 49160 | tf_op jit(solution)/shard_map/ppermute | solution.py:248
  50.5 15.0 %copy-start.12 = (f32[16,256]{1,0:T(8,128)}, f32[16,256]{1,0:T(8,128)S(1)}, u32[]{:S(2)}) copy-start(f32[16,256]{1,0:T(8,128)S(1)} %collective-permute-done.12.refs_3_) | copy-start | bytes 49156
  50.5 9.6 %collective-permute-start.17 = (f32[16,256]{1,0:T(8,128)}, f32[16,256]{1,0:T(8,128)S(1)}, u32[]{:S(2)}, u32[]{:S(2)}) collective-permute-start(f32[16,256]{1,0:T(8,128)} %get-tuple-element.33), channel_id=1, source_target_pairs={{0,8},{1,9},{2,10},{3,11},{4,12},{5,13},{6,14},{7,15},{8,0},{9,1},... | collective-permute-start | bytes 49160 | tf_op jit(solution)/shard_map/ppermute | solution.py:248
  53.3 12.2 %copy-start.13 = (f32[16,256]{1,0:T(8,128)}, f32[16,256]{1,0:T(8,128)S(1)}, u32[]{:S(2)}) copy-start(f32[16,256]{1,0:T(8,128)S(1)} %collective-permute-done.13.refs_4_) | copy-start | bytes 49156
  53.3 7.5 %collective-permute-start.18 = (f32[16,256]{1,0:T(8,128)}, f32[16,256]{1,0:T(8,128)S(1)}, u32[]{:S(2)}, u32[]{:S(2)}) collective-permute-start(f32[16,256]{1,0:T(8,128)} %get-tuple-element.34), channel_id=1, source_target_pairs={{0,9},{1,10},{2,11},{3,12},{4,13},{5,14},{6,15},{7,0},{8,1},{9,2},... | collective-permute-start | bytes 49160 | tf_op jit(solution)/shard_map/ppermute | solution.py:248
  53.3 12.2 %copy-start.14 = (f32[16,256]{1,0:T(8,128)}, f32[16,256]{1,0:T(8,128)S(1)}, u32[]{:S(2)}) copy-start(f32[16,256]{1,0:T(8,128)S(1)} %collective-permute-done.14.refs_5_) | copy-start | bytes 49156
  53.3 9.6 %collective-permute-start.19 = (f32[16,256]{1,0:T(8,128)}, f32[16,256]{1,0:T(8,128)S(1)}, u32[]{:S(2)}, u32[]{:S(2)}) collective-permute-start(f32[16,256]{1,0:T(8,128)} %get-tuple-element.35), channel_id=1, source_target_pairs={{0,10},{1,11},{2,12},{3,13},{4,14},{5,15},{6,0},{7,1},{8,2},{9,3},... | collective-permute-start | bytes 49160 | tf_op jit(solution)/shard_map/ppermute | solution.py:248
  56.0 9.5 %copy-start.15 = (f32[16,256]{1,0:T(8,128)}, f32[16,256]{1,0:T(8,128)S(1)}, u32[]{:S(2)}) copy-start(f32[16,256]{1,0:T(8,128)S(1)} %collective-permute-done.15.refs_6_) | copy-start | bytes 49156
  56.0 7.8 %collective-permute-start.20 = (f32[16,256]{1,0:T(8,128)}, f32[16,256]{1,0:T(8,128)S(1)}, u32[]{:S(2)}, u32[]{:S(2)}) collective-permute-start(f32[16,256]{1,0:T(8,128)} %get-tuple-element.36), channel_id=1, source_target_pairs={{0,11},{1,12},{2,13},{3,14},{4,15},{5,0},{6,1},{7,2},{8,3},{9,4},{... | collective-permute-start | bytes 49160 | tf_op jit(solution)/shard_map/ppermute | solution.py:248
  60.1 5.4 %copy-start.16 = (f32[16,256]{1,0:T(8,128)}, f32[16,256]{1,0:T(8,128)S(1)}, u32[]{:S(2)}) copy-start(f32[16,256]{1,0:T(8,128)S(1)} %collective-permute-done.16.refs_7_) | copy-start | bytes 49156
  60.1 4.0 %collective-permute-start.21 = (f32[16,256]{1,0:T(8,128)}, f32[16,256]{1,0:T(8,128)S(1)}, u32[]{:S(2)}, u32[]{:S(2)}) collective-permute-start(f32[16,256]{1,0:T(8,128)} %get-tuple-element.37), channel_id=1, source_target_pairs={{0,12},{1,13},{2,14},{3,15},{4,0},{5,1},{6,2},{7,3},{8,4},{9,5},{1... | collective-permute-start | bytes 49160 | tf_op jit(solution)/shard_map/ppermute | solution.py:248
  60.1 5.4 %copy-start.17 = (f32[16,256]{1,0:T(8,128)}, f32[16,256]{1,0:T(8,128)S(1)}, u32[]{:S(2)}) copy-start(f32[16,256]{1,0:T(8,128)S(1)} %collective-permute-done.17.refs_8_) | copy-start | bytes 49156
  60.1 3.9 %collective-permute-start.22 = (f32[16,256]{1,0:T(8,128)}, f32[16,256]{1,0:T(8,128)S(1)}, u32[]{:S(2)}, u32[]{:S(2)}) collective-permute-start(f32[16,256]{1,0:T(8,128)} %get-tuple-element.38), channel_id=1, source_target_pairs={{0,13},{1,14},{2,15},{3,0},{4,1},{5,2},{6,3},{7,4},{8,5},{9,6},{10... | collective-permute-start | bytes 49160 | tf_op jit(solution)/shard_map/ppermute | solution.py:248
  60.8 4.8 %copy-start.18 = (f32[16,256]{1,0:T(8,128)}, f32[16,256]{1,0:T(8,128)S(1)}, u32[]{:S(2)}) copy-start(f32[16,256]{1,0:T(8,128)S(1)} %collective-permute-done.18.refs_9_) | copy-start | bytes 49156
  60.8 4.0 %collective-permute-start.23 = (f32[16,256]{1,0:T(8,128)}, f32[16,256]{1,0:T(8,128)S(1)}, u32[]{:S(2)}, u32[]{:S(2)}) collective-permute-start(f32[16,256]{1,0:T(8,128)} %get-tuple-element.39), channel_id=1, source_target_pairs={{0,14},{1,15},{2,0},{3,1},{4,2},{5,3},{6,4},{7,5},{8,6},{9,7},{10,... | collective-permute-start | bytes 49160 | tf_op jit(solution)/shard_map/ppermute | solution.py:248
  62.9 2.6 %copy-start.19 = (f32[16,256]{1,0:T(8,128)}, f32[16,256]{1,0:T(8,128)S(1)}, u32[]{:S(2)}) copy-start(f32[16,256]{1,0:T(8,128)S(1)} %collective-permute-done.19.refs_10_) | copy-start | bytes 49156
  62.9 2.6 %collective-permute-start.24 = (f32[16,256]{1,0:T(8,128)}, f32[16,256]{1,0:T(8,128)S(1)}, u32[]{:S(2)}, u32[]{:S(2)}) collective-permute-start(f32[16,256]{1,0:T(8,128)} %get-tuple-element.40), channel_id=1, source_target_pairs={{0,15},{1,0},{2,1},{3,2},{4,3},{5,4},{6,5},{7,6},{8,7},{9,8},{10,9... | collective-permute-start | bytes 49160 | tf_op jit(solution)/shard_map/ppermute | solution.py:248
  63.8 1.7 %copy-start.20 = (f32[16,256]{1,0:T(8,128)}, f32[16,256]{1,0:T(8,128)S(1)}, u32[]{:S(2)}) copy-start(f32[16,256]{1,0:T(8,128)S(1)} %collective-permute-done.20.refs_11_) | copy-start | bytes 49156
  64.1 1.5 %copy-start.21 = (f32[16,256]{1,0:T(8,128)}, f32[16,256]{1,0:T(8,128)S(1)}, u32[]{:S(2)}) copy-start(f32[16,256]{1,0:T(8,128)S(1)} %collective-permute-done.21.refs_12_) | copy-start | bytes 49156
  64.1 1.5 %copy-start.22 = (f32[16,256]{1,0:T(8,128)}, f32[16,256]{1,0:T(8,128)S(1)}, u32[]{:S(2)}) copy-start(f32[16,256]{1,0:T(8,128)S(1)} %collective-permute-done.22.refs_13_) | copy-start | bytes 49156
  64.7 0.9 %copy-start.23 = (f32[16,256]{1,0:T(8,128)}, f32[16,256]{1,0:T(8,128)S(1)}, u32[]{:S(2)}) copy-start(f32[16,256]{1,0:T(8,128)S(1)} %collective-permute-done.23.refs_14_) | copy-start | bytes 49156
  67.9 9.0 %copy-start.8 = (f32[1,32,192]{2,1,0:T(8,128)S(1)}, f32[1,32,192]{2,1,0:T(8,128)}, u32[]{:S(2)}) copy-start(f32[1,32,192]{2,1,0:T(8,128)} %get-tuple-element.41) | copy-start | bytes 73732
  67.9 9.0 %collective-permute-start.25 = (f32[1,32,192]{2,1,0:T(8,128)}, f32[1,32,192]{2,1,0:T(8,128)S(1)}, u32[]{:S(2)}, u32[]{:S(2)}) collective-permute-start(f32[1,32,192]{2,1,0:T(8,128)} %get-tuple-element.42), channel_id=1, source_target_pairs={{0,16},{1,17},{2,18},{3,19},{4,20},{5,21},{6,22},{7,23},{8,24},{9,... | collective-permute-start | bytes 73736 | tf_op jit(solution)/shard_map/ppermute | solution.py:252
  (3 other events, 1.9 us)

commit v2 on v1

v2 whole, which is shorter than its diff:
```python
import functools

import jax
import jax.numpy as jnp
from jax import lax
from jax.experimental import pallas as pl
from jax.experimental.pallas import tpu as pltpu
from jax.sharding import PartitionSpec as P

F32 = jnp.float32
BF16 = jnp.bfloat16
NN = (((1,), (0,)), ((), ()))
NT = (((1,), (1,)), ((), ()))
TN = (((0,), (0,)), ((), ()))
ROWS = 512
SIDE = 8
MAIN = 256
LANES = 256
LIMIT = 60 * 1024 * 1024
SMEM = pl.BlockSpec(memory_space=pltpu.SMEM)
VMEM = pl.BlockSpec(memory_space=pltpu.VMEM)


def split(value):
    high = value.astype(BF16)
    low = (value - high.astype(F32)).astype(BF16)
    return high, low


def dot(left, right, dims=NN):
    return lax.dot_general(left, right, dims, preferred_element_type=F32)


def dot3(left, right, dims=NN):
    return (
        dot(left[0], right[1], dims) + dot(left[1], right[0], dims) + dot(left[0], right[0], dims)
    )


def sigmoid(value):
    return 0.5 * jnp.tanh(0.5 * value) + 0.5


def call(kernel, name, flops, out_shape, **kwargs):
    shapes = jax.tree.leaves(out_shape)
    moved = 2 * sum(s.size * 4 for s in shapes)
    return pl.pallas_call(
        kernel,
        out_shape=out_shape,
        name=name,
        cost_estimate=pl.CostEstimate(flops=flops, bytes_accessed=moved, transcendentals=0),
        compiler_params=pltpu.CompilerParams(vmem_limit_bytes=LIMIT),
        **kwargs,
    )


def row_value(crops_ref, column, patches, shape, axis, each):
    index = lax.broadcasted_iota(jnp.int32, shape, axis) // each
    found = jnp.zeros(shape, jnp.int32)
    for j in range(patches):
        found = jnp.where(index == j, crops_ref[column, j], found)
    return found


def chosen(crops_ref, patches, rows_first):
    shape = (patches * 64, patches * 16) if rows_first else (patches * 16, patches * 64)
    token_axis = 0 if rows_first else 1
    token = lax.broadcasted_iota(jnp.int32, shape, token_axis)
    slot = lax.broadcasted_iota(jnp.int32, shape, 1 - token_axis)
    scale = row_value(crops_ref, 3, patches, shape, token_axis, 64)
    group, column = (token // 16) % 4, token % 16
    wanted = token // 64 * 16 + (group * scale // 2) * 4 + column * scale // 8
    return jnp.where(slot == wanted, 1.0, 0.0).astype(BF16)


def middle_kernel(
    patches,
    peers,
    place_ref,
    crops_ref,
    own_ref,
    other_ref,
    xw_ref,
    tw_ref,
    gram_ref,
    cwgt_ref,
    xwgt_ref,
    de_ref,
    send_ref,
    rows,
    slope,
    context,
    sums,
    gram_hi,
    gram_lo,
):
    step = pl.program_id(0)
    per_step = ROWS // 4
    far = peers // 4
    pixels = cwgt_ref.shape[0]

    @pl.when(step == 0)
    def _():
        core = place_ref[0] % 2
        for j in range(patches):
            frame, top, left = crops_ref[0, j], crops_ref[1, j], crops_ref[2, j]
            here = frame % 2 == core
            for a in range(4):
                row = jnp.minimum(top + a, SIDE - 1)
                shard = (row // 4 * 2 + frame // 2 % 2) * far + frame // 4
                start = pl.ds(pl.multiple_of((shard * 4 + row % 4) * SIDE, SIDE), SIDE)
                line = jnp.where(here, own_ref[start, :], other_ref[start, :])
                rows[j * 16 + a * 4 : j * 16 + a * 4 + 4, :] = pltpu.roll(line, SIDE - left, 0)[:4, :]
        pre = dot3(split(rows[...]), split(cwgt_ref[...]))
        gate = sigmoid(pre)
        slope[...] = gate * (1.0 + pre * (1.0 - gate))
        projected = split(dot3(split(pre * gate), split(xwgt_ref[...])))
        pick = chosen(crops_ref, patches, True)
        context[...] = dot(pick, projected[1]) + dot(pick, projected[0])
        gram_hi[...], gram_lo[...] = split(gram_ref[...])

    width = xw_ref.shape[1]
    here = pl.ds(pl.multiple_of(step * per_step, per_step), per_step)
    groups = per_step // 16
    spread = context[here, :].reshape(groups, 1, 16, width)
    pre = xw_ref[...].reshape(groups, 4, 16, width) + spread
    pre = pre.reshape(ROWS, width)
    gate = sigmoid(pre)
    hidden = pre * gate
    dhidden = dot3(split(hidden), (gram_hi[...], gram_lo[...])) - tw_ref[...]
    de = dhidden * (gate + hidden * (1.0 - gate))
    de_ref[...] = de
    sums[here, :] = de.reshape(groups, 4, 16, width).sum(axis=1).reshape(per_step, width)

    @pl.when(step == pl.num_programs(0) - 1)
    def _():
        pick = chosen(crops_ref, patches, False)
        high, low = split(sums[...])
        dslot = dot(pick, low) + dot(pick, high)
        dcontext = dot3(split(dslot), split(xwgt_ref[...]), NT)
        grad = dot3(split(dcontext * slope[...]), split(cwgt_ref[...]), NT)
        shape = (patches * 16, LANES - pixels)
        slot = lax.broadcasted_iota(jnp.int32, shape, 0) % 16
        top = row_value(crops_ref, 1, patches, shape, 0, 16)
        left = row_value(crops_ref, 2, patches, shape, 0, 16)
        number = ((top + slot // 4) * SIDE + left + slot % 4).astype(F32)
        send_ref[...] = jnp.zeros_like(send_ref)
        for j in range(patches):
            start = pl.ds(pl.multiple_of(crops_ref[0, j] * 16, 16), 16)
            send_ref[start, :pixels] = grad[j * 16 : j * 16 + 16, :]
            send_ref[start, pixels:] = number[j * 16 : j * 16 + 16, :]


def scatter_kernel(place_ref, message_ref, done_ref, mine_ref, other_ref, total):
    del done_ref
    pixels = mine_ref.shape[2]
    message = message_ref[...]
    number = lax.broadcasted_iota(jnp.int32, (message.shape[0], SIDE * SIDE), 1).astype(F32)
    pick = jnp.where(message[:, pixels : pixels + 1] == number, 1.0, 0.0).astype(BF16)
    high, low = split(message[:, :pixels])
    total[...] = dot(pick, low, TN) + dot(pick, high, TN)
    half = mine_ref.shape[1]
    side = place_ref[1]
    mine_ref[0] = total[pl.ds(pl.multiple_of(side * half, half), half), :]
    other_ref[0] = total[pl.ds(pl.multiple_of((1 - side) * half, half), half), :]


def whole(shape):
    return pl.BlockSpec(shape, lambda i: (0,) * len(shape))


def by_rows(width):
    return pl.BlockSpec((ROWS, width), lambda i: (i, 0))


def body(coarse_input, coarse_weight, fine_input, fine_target, crops, in_weight, context_weight, out_weight):
    high = lax.Precision.HIGH
    patch = ("far", "y", "core")
    peers = lax.axis_size(patch)
    far = peers // 4
    patches, tokens, values = fine_input.shape
    width = in_weight.shape[1]
    pixels = coarse_weight.shape[0]
    half = coarse_input.shape[1]
    count = patches * tokens
    place = jnp.stack([lax.axis_index(patch), lax.axis_index("lvl")]).astype(jnp.int32)
    swap = [(0, 1), (1, 0)]

    def gather(value, axes):
        copies = jnp.broadcast_to(value[None], (lax.axis_size(axes),) + value.shape)
        return lax.all_to_all(copies, axes, 0, 0)

    column = gather(coarse_input[0], "far")
    own = gather(column, ("lvl", "y")).reshape(-1, pixels)
    other = lax.ppermute(own, "core", swap)

    xw = jnp.dot(fine_input.reshape(count, values), in_weight, precision=high)
    tw = jnp.dot(fine_target.reshape(count, values), out_weight.T, precision=high)
    gram = jnp.dot(out_weight, out_weight.T, precision=lax.Precision.HIGHEST)

    shape = (peers * 16, LANES)
    de, back = call(
        functools.partial(middle_kernel, patches, peers),
        "middle",
        6 * count * width * width,
        (jax.ShapeDtypeStruct((count, width), F32), jax.ShapeDtypeStruct(shape, F32)),
        grid=(count // ROWS,),
        in_specs=[
            SMEM,
            SMEM,
            whole(own.shape),
            whole(own.shape),
            by_rows(width),
            by_rows(width),
            whole((width, width)),
            whole((pixels, width)),
            whole((width, width)),
        ],
        out_specs=(by_rows(width), whole(shape)),
        scratch_shapes=[
            pltpu.VMEM((patches * 16, pixels), F32),
            pltpu.VMEM((patches * 16, width), F32),
            pltpu.VMEM((patches * 64, width), F32),
            pltpu.VMEM((patches * 64, width), F32),
            pltpu.VMEM((width, width), BF16),
            pltpu.VMEM((width, width), BF16),
        ],
    )(place, crops.T, own, other, xw, tw, gram, coarse_weight, context_weight)
    returned = lax.all_to_all(back, patch, 0, 0, tiled=True)
    fine_grad = jnp.dot(de, in_weight.T, precision=high)

    part = jax.ShapeDtypeStruct((1, half, pixels), F32)
    mine, theirs = call(
        scatter_kernel,
        "scatter",
        10000,
        (part, part),
        in_specs=[SMEM, VMEM, pl.BlockSpec(memory_space=pl.ANY)],
        out_specs=(VMEM, VMEM),
        scratch_shapes=[pltpu.VMEM((SIDE * SIDE, pixels), F32)],
    )(place, returned, fine_grad)
    coarse_grad = mine + lax.ppermute(theirs, "lvl", swap)
    return (coarse_grad, fine_grad.reshape(fine_input.shape))


def solution(mesh):
    sides, peers = mesh.shape["lvl"], mesh.shape["patch"]
    fine = jax.sharding.Mesh(mesh.devices.reshape(sides, peers // 4, 2, 2), ("lvl", "far", "y", "core"))
    patch = ("far", "y", "core")
    both = ("lvl",) + patch
    in_specs = (
        P(patch, "lvl", None),
        P(),
        P(both, None, None),
        P(both, None, None),
        P(both, None),
        P(),
        P(),
        P(),
    )
    out_specs = (P(patch, "lvl", None), P(both, None, None))
    return jax.shard_map(body, mesh=fine, in_specs=in_specs, out_specs=out_specs, check_vma=False)
```

time: 79.1 us -> 74.4 us (0.941); the launches traced: 77.5 us -> 73.8 us
  matrix products: 0 us -> 28.1 us
  Pallas kernels: 37.1 us -> 12.5 us
  starting transfers between devices: 31.2 us -> 17 us
  waiting for transfers between devices: 5.88 us -> 9.7 us
  local copies, waits for them, and re-layouts: 1.24 us -> 3.86 us
    ppermute x26 -> x2, starting transfers between devices: 31.2 us -> 0.52 us  [the longest x1 0.51 us: body(): coarse_grad = mine + lax.ppermute(theirs, 'lvl', swap)]
    dot_general x0 -> x4, matrix products: none -> 28.1 us  [the longest x1 8.58 us: body(): fine_grad = jnp.dot(de, in_weight.T, precision=high)]
    pallas_call x4 -> x1, Pallas kernels: 27.1 us -> 1.86 us  [body(): call(scatter_kernel, 'scatter', 10000, (part, part), in_specs=[SMEM, VMEM...]
    all_to_all x0 -> x3, starting transfers between devices: none -> 16.5 us  [the longest x2 10 us: gather(): return lax.all_to_all(copies, axes, 0, 0)]
    all_to_all x0 -> x3, waiting for transfers between devices: none -> 6.09 us  [the longest x2 4.62 us: gather(): return lax.all_to_all(copies, axes, 0, 0)]
    broadcast_in_dim x0 -> x2, local copies, waits for them, and re-layouts: none -> 2.35 us  [gather(): copies = jnp.broadcast_to(value[None], (lax.axis_size(axes),) + value.shape)]
    ppermute x26 -> x2, waiting for transfers between devices: 5.88 us -> 3.61 us  [the longest x1 3.61 us: body(): coarse_grad = mine + lax.ppermute(theirs, 'lvl', swap)]
  transfers between devices with their start and end apart: 26 -> 5, of which waited for: 7 -> 3; matrix products, arithmetic and copies ran while one was open for 1% -> 39% of each run, Pallas kernels for 33% -> 0%
where the time goes in v2:
time: 74.4 us; the launch traced here: 73.8 us
  matrix products  28.1 us (38%)
  starting transfers between devices  17 us (23%)
  Pallas kernels  12.5 us (17%)
  waiting for transfers between devices  9.7 us (13%)
  local copies, waits for them, and re-layouts  3.86 us (5%)
  other arithmetic  1.99 us (3%)
    pallas_call x1, Pallas kernels, body(): call(functools.partial(middle_kernel, patches, peers), 'middle', 6 * coun...  10.6 us
    all_to_all x2, starting transfers between devices, gather(): return lax.all_to_all(copies, axes, 0, 0)  10 us
    dot_general x1, matrix products, body(): fine_grad = jnp.dot(de, in_weight.T, precision=high)  8.58 us
    dot_general x1, matrix products, body(): jnp.dot(fine_target.reshape(count, values), out_weight.T, precision=high)  8.57 us
    dot_general x1, matrix products, body(): xw = jnp.dot(fine_input.reshape(count, values), in_weight, precision=high)  8.43 us
    all_to_all x1, starting transfers between devices, body(): returned = lax.all_to_all(back, patch, 0, 0, tiled=True)  6.44 us
    all_to_all x2, waiting for transfers between devices, gather(): return lax.all_to_all(copies, axes, 0, 0)  4.62 us
    ppermute x1, waiting for transfers between devices, body(): coarse_grad = mine + lax.ppermute(theirs, 'lvl', swap)  3.61 us
  transfers between devices with their start and end apart: 5, of which 3 were waited for; matrix products, arithmetic and copies ran while one was open for 39% of the time, Pallas kernels for 0%

profile of v2, /device:TPU:0, one launch (start us, length us, event | category | flops | bytes accessed | tf_op | source)
XLA Modules:
  0.0 73.8 jit_solution(1647420417560030950)
XLA Ops:
  0.6 0.0 copy-start
  0.6 1.5 %broadcast_in_dim.14 = f32[4,32,192]{2,1,0:T(8,128)} broadcast(f32[32,192]{1,0:T(8,128)} %bitcast.25), dimensions={1,2} | broadcast | bytes 122880 | tf_op jit(solution)/shard_map/broadcast_in_dim | solution.py:190
  2.1 6.3 %all-to-all-start = ((f32[4,32,192]{2,1,0:T(8,128)}), f32[4,32,192]{2,1,0:T(8,128)S(1)}, u32[]{:S(2)}, u32[]{:S(2)}) async-start(f32[4,32,192]{2,1,0:T(8,128)} %broadcast_in_dim.14), calls=%async_computation | async-start | bytes 262144 | tf_op jit(solution)/shard_map/all_to_all | solution.py:191
  8.5 0.0 copy-start.1
  8.5 8.6 %fusion.1.tw_ref = f32[2048,320]{1,0:T(8,128)} fusion(f32[2048,768]{1,0:T(8,128)} %bitcast.19, f32[320,768]{1,0:T(8,128)} %param.15), kind=kOutput, calls=%fused_computation.2 | convolution fusion | flops 3019898880 | bytes 9895936 | tf_op jit(solution)/shard_map/dot_general | solution.py:198
  17.0 0.0 all-to-all-done
  17.0 0.8 %broadcast_in_dim.15 = f32[4,4,32,192]{3,2,1,0:T(8,128)} broadcast(f32[4,32,192]{2,1,0:T(8,128)S(1)} %all-to-all-done), dimensions={1,2,3} | broadcast | bytes 491520 | tf_op jit(solution)/shard_map/broadcast_in_dim | solution.py:190
  17.9 3.7 %all-to-all-start.1 = ((f32[4,4,32,192]{3,2,1,0:T(8,128)}), f32[4,4,32,192]{3,2,1,0:T(8,128)S(1)}, u32[]{:S(2)}, u32[]{:S(2)}) async-start(f32[4,4,32,192]{3,2,1,0:T(8,128)} %broadcast_in_dim.15), calls=%async_computation.1 | async-start | bytes 1048576 | tf_op jit(solution)/shard_map/all_to_all | solution.py:191
  21.6 0.6 pad_add_fusion.place_ref
  22.2 0.0 copy-done.1
  22.2 2.5 %fusion.2.gram_ref = f32[320,320]{1,0:T(8,128)} fusion(f32[320,768]{1,0:T(8,128)S(1)} %copy-done.1), kind=kOutput, calls=%fused_computation.3 | convolution fusion | flops 943718400 | bytes 1392640 | tf_op jit(solution)/shard_map/dot_general | solution.py:199
  24.7 4.6 %all-to-all-done.1 = f32[4,4,32,192]{3,2,1,0:T(8,128)S(1)} async-done(((f32[4,4,32,192]{3,2,1,0:T(8,128)}), f32[4,4,32,192]{3,2,1,0:T(8,128)S(1)}, u32[]{:S(2)}, u32[]{:S(2)}) %all-to-all-start.1) | async-done | bytes 393248 | tf_op jit(solution)/shard_map/all_to_all | solution.py:191
  29.4 0.0 copy-start.2
  29.4 0.0 collective-permute-start
  29.4 0.0 copy-done
  29.4 8.4 %fusion.xw_ref = f32[2048,320]{1,0:T(8,128)} fusion(f32[2048,768]{1,0:T(8,128)} %bitcast.20, f32[768,320]{0,1:T(8,128)S(1)} %copy-done), kind=kOutput, calls=%fused_computation.1 | convolution fusion | flops 3019898880 | bytes 9895936 | tf_op jit(solution)/shard_map/dot_general | solution.py:197
  37.8 0.0 copy-done.2
  37.8 0.0 collective-permute-done.other_ref
  37.8 0.0 copy-start.4
  37.8 0.8 %copy-done.4 = f32[512,192]{1,0:T(8,128)} copy-done((f32[512,192]{1,0:T(8,128)}, f32[512,192]{1,0:T(8,128)S(1)}, u32[]{:S(2)}) %copy-start.4) | copy-done | bytes 393240
  38.6 10.6 %middle.1 = (f32[2048,320]{1,0:T(8,128)}, f32[256,256]{1,0:T(8,128)}) custom-call(s32[2]{0:T(128)} %pad_add_fusion.place_ref, s32[4,8]{1,0:T(4,128)} %bitcast.26, f32[512,192]{1,0:T(8,128)} %bitcast.22, f32[512,192]{1,0:T(8,128)} %copy-done.4, f32[2048,320]{1,0:T(8,128)} %fusion.xw_ref, f32[2048,320]{1,0:T(8,128)} %fusion.1.tw_ref, ...), custom_call_target="tpu_custom_call" | custom-call | flops 1258291200 | bytes 5767168 | tf_op jit(solution)/shard_map/middle/pallas_call | solution.py:202
  49.2 6.4 %all-to-all-start.2 = ((f32[16,16,256]{2,1,0:T(8,128)}), f32[16,16,256]{2,1,0:T(8,128)S(1)}, u32[]{:S(2)}, u32[]{:S(2)}) async-start(f32[16,16,256]{2,1,0:T(8,128)} %bitcast.24), calls=%async_computation.2 | async-start | bytes 524288 | tf_op jit(solution)/shard_map/all_to_all | solution.py:229
  55.7 8.6 %fusion.3.done_ref = f32[2048,768]{1,0:T(8,128)} fusion(f32[2048,320]{1,0:T(8,128)} %get-tuple-element.7, f32[768,320]{0,1:T(8,128)S(1)} %copy-done), kind=kOutput, calls=%fused_computation.4 | convolution fusion | flops 3019898880 | bytes 9895936 | tf_op jit(solution)/shard_map/dot_general | solution.py:230
  64.3 1.5 %all-to-all-done.2 = f32[16,16,256]{2,1,0:T(8,128)S(1)} async-done(((f32[16,16,256]{2,1,0:T(8,128)}), f32[16,16,256]{2,1,0:T(8,128)S(1)}, u32[]{:S(2)}, u32[]{:S(2)}) %all-to-all-start.2) | async-done | bytes 262176 | tf_op jit(solution)/shard_map/all_to_all | solution.py:229
  65.7 0.0 copy-start.3
  65.7 0.7 copy-done.3
  66.4 1.9 %scatter.1 = (f32[1,32,192]{2,1,0:T(8,128)}, f32[1,32,192]{2,1,0:T(8,128)}) custom-call(s32[2]{0:T(128)} %pad_add_fusion.place_ref, f32[256,256]{1,0:T(8,128)} %bitcast.23, f32[2048,768]{1,0:T(8,128)} %fusion.3.done_ref), custom_call_target="tpu_custom_call" | custom-call | flops 10000 | bytes 98304 | tf_op jit(solution)/shard_map/scatter/pallas_call | solution.py:233
  68.3 0.5 collective-permute-start.1
  68.8 3.6 %collective-permute-done.1 = f32[1,32,192]{2,1,0:T(8,128)S(1)} collective-permute-done((f32[1,32,192]{2,1,0:T(8,128)}, f32[1,32,192]{2,1,0:T(8,128)S(1)}, u32[]{:S(2)}, u32[]{:S(2)}) %collective-permute-start.1) | collective-permute-done | bytes 24608 | tf_op jit(solution)/shard_map/ppermute | solution.py:242
  72.4 1.4 %add.11 = f32[1,32,192]{2,1,0:T(8,128)} add(f32[1,32,192]{2,1,0:T(8,128)} %get-tuple-element.8, f32[1,32,192]{2,1,0:T(8,128)S(1)} %collective-permute-done.1) | non-fusion elementwise | flops 6144 | bytes 73728 | tf_op jit(solution)/shard_map/add | solution.py:242
Async XLA Ops:
  0.6 28.7 %copy-start = (f32[768,320]{0,1:T(8,128)S(1)}, f32[768,320]{0,1:T(8,128)}, u32[]{:S(2)}) copy-start(f32[768,320]{0,1:T(8,128)} %param.13) | copy-start | bytes 2949124
  2.1 14.9 %all-to-all-start = ((f32[4,32,192]{2,1,0:T(8,128)}), f32[4,32,192]{2,1,0:T(8,128)S(1)}, u32[]{:S(2)}, u32[]{:S(2)}) async-start(f32[4,32,192]{2,1,0:T(8,128)} %broadcast_in_dim.14), calls=%async_computation | async-start | bytes 262144 | tf_op jit(solution)/shard_map/all_to_all | solution.py:191
  8.5 13.8 %copy-start.1 = (f32[320,768]{1,0:T(8,128)S(1)}, f32[320,768]{1,0:T(8,128)}, u32[]{:S(2)}) copy-start(f32[320,768]{1,0:T(8,128)} %param.15) | copy-start | bytes 2949124
  17.9 11.5 %all-to-all-start.1 = ((f32[4,4,32,192]{3,2,1,0:T(8,128)}), f32[4,4,32,192]{3,2,1,0:T(8,128)S(1)}, u32[]{:S(2)}, u32[]{:S(2)}) async-start(f32[4,4,32,192]{3,2,1,0:T(8,128)} %broadcast_in_dim.15), calls=%async_computation.1 | async-start | bytes 1048576 | tf_op jit(solution)/shard_map/all_to_all | solution.py:191
  29.4 8.4 %copy-start.2 = (f32[4,4,32,192]{3,2,1,0:T(8,128)}, f32[4,4,32,192]{3,2,1,0:T(8,128)S(1)}, u32[]{:S(2)}) copy-start(f32[4,4,32,192]{3,2,1,0:T(8,128)S(1)} %all-to-all-done.1) | copy-start | bytes 1179652
  29.4 8.4 %collective-permute-start = (f32[512,192]{1,0:T(8,128)S(1)}, f32[512,192]{1,0:T(8,128)S(1)}, u32[]{:S(2)}, u32[]{:S(2)}) collective-permute-start(f32[512,192]{1,0:T(8,128)S(1)} %bitcast.21), channel_id=1, source_target_pairs={{0,1},{1,0},{2,3},{3,2},{4,5},{5,4},{6,7},{7,6},{8,9},{9,8},{10,11... | collective-permute-start | bytes 1179656 | tf_op jit(solution)/shard_map/ppermute | solution.py:195
  37.8 0.8 %copy-start.4 = (f32[512,192]{1,0:T(8,128)}, f32[512,192]{1,0:T(8,128)S(1)}, u32[]{:S(2)}) copy-start(f32[512,192]{1,0:T(8,128)S(1)} %collective-permute-done.other_ref) | copy-start | bytes 1179652
  49.2 16.5 %all-to-all-start.2 = ((f32[16,16,256]{2,1,0:T(8,128)}), f32[16,16,256]{2,1,0:T(8,128)S(1)}, u32[]{:S(2)}, u32[]{:S(2)}) async-start(f32[16,16,256]{2,1,0:T(8,128)} %bitcast.24), calls=%async_computation.2 | async-start | bytes 524288 | tf_op jit(solution)/shard_map/all_to_all | solution.py:229
  65.7 0.7 copy-start.3
  68.3 4.1 %collective-permute-start.1 = (f32[1,32,192]{2,1,0:T(8,128)}, f32[1,32,192]{2,1,0:T(8,128)S(1)}, u32[]{:S(2)}, u32[]{:S(2)}) collective-permute-start(f32[1,32,192]{2,1,0:T(8,128)} %get-tuple-element.9), channel_id=1, source_target_pairs={{0,16},{16,0},{1,17},{17,1},{2,18},{18,2},{3,19},{19,3},{4,20},{20... | collective-permute-start | bytes 73736 | tf_op jit(solution)/shard_map/ppermute | solution.py:242

commit v3 on v2

v3 whole, which is shorter than its diff:
```python
import functools
import math

import jax
import jax.numpy as jnp
from jax import lax
from jax.experimental import pallas as pl
from jax.experimental.pallas import tpu as pltpu
from jax.sharding import PartitionSpec as P

F32 = jnp.float32
BF16 = jnp.bfloat16
NN = (((1,), (0,)), ((), ()))
NT = (((1,), (1,)), ((), ()))
TN = (((0,), (0,)), ((), ()))
ROWS = 512
SIDE = 8
MAIN = 256
LANES = 256
LIMIT = 60 * 1024 * 1024
ROOM = 40 * 1024 * 1024
SMEM = pl.BlockSpec(memory_space=pltpu.SMEM)
VMEM = pl.BlockSpec(memory_space=pltpu.VMEM)
HBM = pl.BlockSpec(memory_space=pltpu.HBM)


def split(value):
    high = value.astype(BF16)
    low = (value - high.astype(F32)).astype(BF16)
    return high, low


def dot(left, right, dims=NN):
    return lax.dot_general(left, right, dims, preferred_element_type=F32)


def dot3(left, right, dims=NN):
    return (
        dot(left[0], right[1], dims) + dot(left[1], right[0], dims) + dot(left[0], right[0], dims)
    )


def sigmoid(value):
    return 0.5 * jnp.tanh(0.5 * value) + 0.5


def call(kernel, name, flops, out_shape, limit=LIMIT, **kwargs):
    moved = 8 * sum(math.prod(s.shape) for s in jax.tree.leaves(out_shape))
    return pl.pallas_call(
        kernel,
        out_shape=out_shape,
        name=name,
        cost_estimate=pl.CostEstimate(flops=flops, bytes_accessed=moved, transcendentals=0),
        compiler_params=pltpu.CompilerParams(vmem_limit_bytes=limit),
        **kwargs,
    )


def wide_product(value, main_hi, main_lo, tail, out_ref, dims):
    high, low = split(value)
    rest = out_ref.shape[1] - MAIN
    out_ref[:, :MAIN] = dot3((high, low), (main_hi[...], main_lo[...]), dims)
    both = dot(high, tail[...], dims)
    tail_hi = tail[:rest] if dims == NT else tail[:, :rest]
    out_ref[:, MAIN:] = both[:, :rest] + (both[:, rest:] + dot(low, tail_hi, dims))


def input_kernel(x_ref, weight_ref, out_ref, high_ref, low_ref, tail):
    @pl.when(pl.program_id(0) == 0)
    def _():
        high, low = split(weight_ref[...])
        high_ref[...], low_ref[...] = high, low
        rest = high.shape[0] - MAIN
        tail[:rest], tail[rest:] = high[MAIN:], low[MAIN:]

    wide_product(x_ref[...], high_ref.at[:MAIN], low_ref.at[:MAIN], tail, out_ref, NT)


def gram_kernel(weight_ref, before_ref, gram_ref):
    del before_ref
    high, low = split(weight_ref[...])
    gram_ref[...] = dot3((high, low), (high, low), NT) + dot(low, low, NT)


def stack_kernel(*refs):
    *block_refs, _, out_ref = refs
    size = block_refs[0].shape[0]
    for k, ref in enumerate(block_refs):
        out_ref[k * size : (k + 1) * size] = ref[...]


def target_kernel(t_ref, weight_ref, out_ref, main_hi, main_lo, tail):
    @pl.when(pl.program_id(0) == 0)
    def _():
        high, low = split(weight_ref[...].T)
        main_hi[...], main_lo[...] = high[:, :MAIN], low[:, :MAIN]
        tail[...] = jnp.concatenate([high[:, MAIN:], low[:, MAIN:]], axis=1)

    wide_product(t_ref[...], main_hi, main_lo, tail, out_ref, NN)


def row_value(crops_ref, column, patches, shape, axis, each):
    index = lax.broadcasted_iota(jnp.int32, shape, axis) // each
    found = jnp.zeros(shape, jnp.int32)
    for j in range(patches):
        found = jnp.where(index == j, crops_ref[column, j], found)
    return found


def chosen(crops_ref, patches, rows_first):
    shape = (patches * 64, patches * 16) if rows_first else (patches * 16, patches * 64)
    token_axis = 0 if rows_first else 1
    token = lax.broadcasted_iota(jnp.int32, shape, token_axis)
    slot = lax.broadcasted_iota(jnp.int32, shape, 1 - token_axis)
    scale = row_value(crops_ref, 3, patches, shape, token_axis, 64)
    group, column = (token // 16) % 4, token % 16
    wanted = token // 64 * 16 + (group * scale // 2) * 4 + column * scale // 8
    return jnp.where(slot == wanted, 1.0, 0.0).astype(BF16)


def middle_kernel(
    patches,
    peers,
    crops_ref,
    own_ref,
    other_ref,
    xw_hbm,
    tw_hbm,
    gram_hbm,
    cwgt_hbm,
    xwgt_hbm,
    de_hbm,
    send_ref,
    xw,
    tw,
    gram,
    cwgt,
    xwgt,
    rows,
    context,
    sums,
    small_sems,
    in_sems,
    out_sems,
):
    pixels = cwgt.shape[0]
    count, width = xw.shape
    far = peers // 4
    steps = count // ROWS
    small = [
        pltpu.make_async_copy(source, target, small_sems.at[i])
        for i, (source, target) in enumerate(((cwgt_hbm, cwgt), (xwgt_hbm, xwgt), (gram_hbm, gram)))
    ]
    large = []
    for i in range(steps):
        here = slice(i * ROWS, (i + 1) * ROWS)
        large.append(
            (
                pltpu.make_async_copy(xw_hbm.at[here], xw.at[here], in_sems.at[0, i]),
                pltpu.make_async_copy(tw_hbm.at[here], tw.at[here], in_sems.at[1, i]),
            )
        )
    for copy in small:
        copy.start()
    for pair in large:
        for copy in pair:
            copy.start()

    me, side = lax.axis_index(("far", "y", "core")), lax.axis_index("lvl")
    for j in range(patches):
        frame, top, left = crops_ref[0, j], crops_ref[1, j], crops_ref[2, j]
        near = lax.bitwise_xor(frame % 4, me % 4)
        k = (me // 4 - frame // 4 + far) % far
        for a in range(4):
            row = jnp.minimum(top + a, SIDE - 1)
            shard = (lax.bitwise_xor(row // 4, side) * 2 + near // 2) * far + k
            start = pl.ds(pl.multiple_of((shard * 4 + row % 4) * SIDE, SIDE), SIDE)
            line = jnp.where(near % 2 == 0, own_ref[start, :], other_ref[start, :])
            rows[j * 16 + a * 4 : j * 16 + a * 4 + 4, :] = pltpu.roll(line, SIDE - left, 0)[:4, :]
    small[0].wait()
    coarse = split(cwgt[...])
    pre = dot3(split(rows[...]), coarse)
    gate = sigmoid(pre)
    slope = gate * (1.0 + pre * (1.0 - gate))
    small[1].wait()
    project = split(xwgt[...])
    projected = split(dot3(split(pre * gate), project))
    pick = chosen(crops_ref, patches, True)
    context[...] = dot(pick, projected[1]) + dot(pick, projected[0])
    small[2].wait()
    grams = split(gram[...])

    groups, part = ROWS // 64, ROWS // 4
    stores = []
    for i in range(steps):
        here = slice(i * ROWS, (i + 1) * ROWS)
        for copy in large[i]:
            copy.wait()
        spread = context[i * part : (i + 1) * part, :].reshape(groups, 1, 16, width)
        pre = (xw[here, :].reshape(groups, 4, 16, width) + spread).reshape(ROWS, width)
        gate = sigmoid(pre)
        hidden = pre * gate
        dhidden = dot3(split(hidden), grams) - tw[here, :]
        de = dhidden * (gate + hidden * (1.0 - gate))
        xw[here, :] = de
        stores.append(pltpu.make_async_copy(xw.at[here], de_hbm.at[here], out_sems.at[i]))
        stores[i].start()
        sums[i * part : (i + 1) * part, :] = de.reshape(groups, 4, 16, width).sum(axis=1).reshape(part, width)

    pick = chosen(crops_ref, patches, False)
    high, low = split(sums[...])
    dslot = dot(pick, low) + dot(pick, high)
    dcontext = dot3(split(dslot), project, NT)
    grad = dot3(split(dcontext * slope), coarse, NT)
    shape = (patches * 16, LANES - pixels)
    slot = lax.broadcasted_iota(jnp.int32, shape, 0) % 16
    top = row_value(crops_ref, 1, patches, shape, 0, 16)
    left = row_value(crops_ref, 2, patches, shape, 0, 16)
    number = ((top + slot // 4) * SIDE + left + slot % 4).astype(F32)
    send_ref[...] = jnp.zeros_like(send_ref)
    for j in range(patches):
        start = pl.ds(pl.multiple_of(crops_ref[0, j] * 16, 16), 16)
        send_ref[start, :pixels] = grad[j * 16 : j * 16 + 16, :]
        send_ref[start, pixels:] = number[j * 16 : j * 16 + 16, :]
    for copy in stores:
        copy.wait()


def scatter_kernel(message_ref, done_ref, mine_ref, other_ref, total):
    del done_ref
    pixels = mine_ref.shape[2]
    message = message_ref[...]
    number = lax.broadcasted_iota(jnp.int32, (message.shape[0], SIDE * SIDE), 1).astype(F32)
    pick = jnp.where(message[:, pixels : pixels + 1] == number, 1.0, 0.0).astype(BF16)
    high, low = split(message[:, :pixels])
    total[...] = dot(pick, low, TN) + dot(pick, high, TN)
    half = mine_ref.shape[1]
    side = lax.axis_index("lvl")
    mine_ref[0] = total[pl.ds(pl.multiple_of(side * half, half), half), :]
    other_ref[0] = total[pl.ds(pl.multiple_of((1 - side) * half, half), half), :]


def last_kernel(de_ref, high_ref, low_ref, *refs):
    out_ref, tail = refs[-2:]
    depth = high_ref.shape[0]
    rest = depth - MAIN

    @pl.when(pl.program_id(0) == 0)
    def _():
        tail[:rest], tail[rest : 2 * rest], tail[2 * rest :] = low_ref[MAIN:], high_ref[MAIN:], high_ref[MAIN:]

    high, low = split(de_ref[...])
    tails = jnp.concatenate([high[:, MAIN:], low[:, MAIN:], high[:, MAIN:]], axis=1)
    main = dot3((high[:, :MAIN], low[:, :MAIN]), (high_ref[:MAIN], low_ref[:MAIN]))
    out_ref[...] = main + dot(tails, tail[...])


def fixed(*values):
    return [pltpu.with_memory_space_constraint(value, pltpu.HBM) for value in values]


def stack(blocks, before):
    shape = (len(blocks) * blocks[0].shape[0],) + blocks[0].shape[1:]
    return call(
        stack_kernel,
        "stack",
        1000,
        jax.ShapeDtypeStruct(shape, F32),
        limit=ROOM,
        in_specs=[VMEM] * len(blocks) + [HBM],
        out_specs=VMEM,
    )(*blocks, *fixed(before))


def whole(shape):
    return pl.BlockSpec(shape, lambda i: (0,) * len(shape))


def by_rows(width, first=0):
    return pl.BlockSpec((ROWS, width), lambda i: (i + first, 0))


def body(coarse_input, coarse_weight, fine_input, fine_target, crops, in_weight, context_weight, out_weight):
    patch = ("far", "y", "core")
    peers = lax.axis_size(patch)
    far = peers // 4
    patches, tokens, values = fine_input.shape
    width = in_weight.shape[1]
    pixels = coarse_weight.shape[0]
    half = coarse_input.shape[1]
    count = patches * tokens
    steps = count // ROWS
    rest = width - MAIN
    swap = [(0, 1), (1, 0)]

    column = [coarse_input]
    for k in range(1, far):
        column.append(lax.ppermute(coarse_input, "far", [(p, (p + k) % far) for p in range(far)]))
    weight = in_weight.T
    weight_shape = jax.ShapeDtypeStruct((width, values), BF16)
    xw, win_hi, win_lo = call(
        input_kernel,
        "input",
        6 * count * values * width,
        (jax.ShapeDtypeStruct((count, width), F32), weight_shape, weight_shape),
        grid=(steps,),
        in_specs=[by_rows(values), whole((width, values))],
        out_specs=(by_rows(width), whole((width, values)), whole((width, values))),
        scratch_shapes=[pltpu.VMEM((2 * rest, values), BF16)],
    )(fine_input.reshape(count, values), weight)
    column = stack(column, xw)
    own = [column]
    for flip in range(1, 4):
        own.append(lax.ppermute(column, ("lvl", "y"), [(p, p ^ flip) for p in range(4)]))
    tw = call(
        target_kernel,
        "target",
        6 * count * values * width,
        jax.ShapeDtypeStruct((count, width), F32),
        grid=(steps,),
        in_specs=[by_rows(values), whole((width, values))],
        out_specs=by_rows(width),
        scratch_shapes=[
            pltpu.VMEM((values, MAIN), BF16),
            pltpu.VMEM((values, MAIN), BF16),
            pltpu.VMEM((values, 2 * rest), BF16),
        ],
    )(fine_target.reshape(count, values), out_weight)
    own = stack(own, tw).reshape(-1, pixels)
    other = lax.ppermute(own, "core", swap)
    gram = call(
        gram_kernel,
        "gram",
        8 * values * width * width,
        pltpu.HBM((width, width), F32),
        limit=ROOM,
        in_specs=[VMEM, HBM],
        out_specs=VMEM,
    )(out_weight, own)

    shape = (peers * 16, LANES)
    de, back = call(
        functools.partial(middle_kernel, patches, peers),
        "middle",
        6 * count * width * width,
        (pltpu.HBM((count, width), F32), jax.ShapeDtypeStruct(shape, F32)),
        limit=ROOM,
        in_specs=[SMEM, VMEM, VMEM] + [HBM] * 5,
        out_specs=(HBM, VMEM),
        scratch_shapes=[
            pltpu.VMEM((count, width), F32),
            pltpu.VMEM((count, width), F32),
            pltpu.VMEM((width, width), F32),
            pltpu.VMEM((pixels, width), F32),
            pltpu.VMEM((width, width), F32),
            pltpu.VMEM((patches * 16, pixels), F32),
            pltpu.VMEM((patches * 64, width), F32),
            pltpu.VMEM((patches * 64, width), F32),
            pltpu.SemaphoreType.DMA((3,)),
            pltpu.SemaphoreType.DMA((2, steps)),
            pltpu.SemaphoreType.DMA((steps,)),
        ],
    )(crops.T, own, other, *fixed(xw, tw, gram, coarse_weight, context_weight))
    returned = lax.all_to_all(back, patch, 0, 0, tiled=True)

    def last(first, number, *extra):
        return call(
            last_kernel,
            "last",
            6 * number * ROWS * values * width,
            jax.ShapeDtypeStruct((count, values), F32),
            grid=(number,),
            in_specs=[by_rows(width, first), whole((width, values)), whole((width, values))]
            + [HBM] * len(extra),
            out_specs=by_rows(values, first),
            scratch_shapes=[pltpu.VMEM((3 * rest, values), BF16)],
            input_output_aliases={3: 0} if extra else {},
        )(de, win_hi, win_lo, *fixed(*extra))

    early = steps - 1
    fine_grad = last(0, early)
    part = (1, half, pixels)
    mine, theirs = call(
        scatter_kernel,
        "scatter",
        10000,
        (pltpu.HBM(part, F32), jax.ShapeDtypeStruct(part, F32)),
        limit=ROOM,
        in_specs=[VMEM, HBM],
        out_specs=(VMEM, VMEM),
        scratch_shapes=[pltpu.VMEM((SIDE * SIDE, pixels), F32)],
    )(returned, *fixed(fine_grad))
    fine_grad = last(early, steps - early, fine_grad, mine)
    coarse_grad = mine + lax.ppermute(theirs, "lvl", swap)
    return (coarse_grad, fine_grad.reshape(fine_input.shape))


def solution(mesh):
    sides, peers = mesh.shape["lvl"], mesh.shape["patch"]
    fine = jax.sharding.Mesh(mesh.devices.reshape(sides, peers // 4, 2, 2), ("lvl", "far", "y", "core"))
    patch = ("far", "y", "core")
    both = ("lvl",) + patch
    in_specs = (
        P(patch, "lvl", None),
        P(),
        P(both, None, None),
        P(both, None, None),
        P(both, None),
        P(),
        P(),
        P(),
    )
    out_specs = (P(patch, "lvl", None), P(both, None, None))
    return jax.shard_map(body, mesh=fine, in_specs=in_specs, out_specs=out_specs, check_vma=False)
```

time: 74.4 us -> 61.8 us (0.83)
  matrix products: 28.1 us -> 0 us
  Pallas kernels: 12.5 us -> 40.6 us
  waiting for transfers between devices: 9.7 us -> 3.75 us
  local copies, waits for them, and re-layouts: 3.86 us -> 0.02 us
  other arithmetic: 1.99 us -> 0.62 us
  starting transfers between devices: 17 us -> 15.7 us
    pallas_call x1 -> x8, Pallas kernels: 1.86 us -> 30.4 us  [the longest x2 9.82 us: last(): call(last_kernel, 'last', 6 * number * ROWS * values * width, jax.ShapeDt...]
    dot_general x4 -> x0, matrix products: 28.1 us -> none  [the longest x1 8.58 us: body(): fine_grad = jnp.dot(de, in_weight.T, precision=high)]
    ppermute x0 -> x6, starting transfers between devices: none -> 10.6 us  [the longest x3 7.01 us: body(): lax.ppermute(coarse_input, 'far', [(p, (p + k) % far) for p in range(far)])]
    all_to_all x2 -> x0, starting transfers between devices: 10 us -> none  [gather(): return lax.all_to_all(copies, axes, 0, 0)]
    all_to_all x2 -> x0, waiting for transfers between devices: 4.62 us -> none  [gather(): return lax.all_to_all(copies, axes, 0, 0)]
    ppermute x1, waiting for transfers between devices: 3.61 us -> 0.01 us  [body(): coarse_grad = mine + lax.ppermute(theirs, 'lvl', swap)]
    all_to_all x1, starting transfers between devices: 6.44 us -> 3.54 us  [body(): returned = lax.all_to_all(back, patch, 0, 0, tiled=True)]
    broadcast_in_dim x2 -> x0, local copies, waits for them, and re-layouts: 2.35 us -> none  [gather(): copies = jnp.broadcast_to(value[None], (lax.axis_size(axes),) + value.shape)]
  transfers between devices with their start and end apart: 5 -> 9, of which waited for: 3 -> 1; matrix products, arithmetic and copies ran while one was open for 39% -> 0% of each run, Pallas kernels for 0% -> 48%
where the time goes in v3:
time: 61.8 us; the launch traced here: 61.4 us
  Pallas kernels  40.6 us (66%)
  starting transfers between devices  15.7 us (25%)
  waiting for transfers between devices  3.75 us (6%)
  between operations  0.73 us (1%)
  other arithmetic  0.62 us (1%)
    pallas_call x1, Pallas kernels, body(): call(functools.partial(middle_kernel, patches, peers), 'middle', 6 * coun...  10.2 us
    pallas_call x2, Pallas kernels, last(): call(last_kernel, 'last', 6 * number * ROWS * values * width, jax.ShapeDt...  9.82 us
    pallas_call x1, Pallas kernels, body(): call(target_kernel, 'target', 6 * count * values * width, jax.ShapeDtypeS...  9.1 us
    pallas_call x1, Pallas kernels, body(): call(input_kernel, 'input', 6 * count * values * width, (jax.ShapeDtypeSt...  8.58 us
    ppermute x3, starting transfers between devices, body(): lax.ppermute(coarse_input, 'far', [(p, (p + k) % far) for p in range(far)])  7.01 us
    all_to_all x1, waiting for transfers between devices, body(): returned = lax.all_to_all(back, patch, 0, 0, tiled=True)  3.73 us
    ppermute x3, starting transfers between devices, body(): lax.ppermute(column, ('lvl', 'y'), [(p, p ^ flip) for p in range(4)])  3.55 us
    all_to_all x1, starting transfers between devices, body(): returned = lax.all_to_all(back, patch, 0, 0, tiled=True)  3.54 us
  transfers between devices with their start and end apart: 9, of which 1 were waited for; matrix products, arithmetic and copies ran while one was open for 0% of the time, Pallas kernels for 48%

profile of v3, /device:TPU:0, one launch (start us, length us, event | category | flops | bytes accessed | tf_op | source)
XLA Modules:
  0.0 61.4 jit_solution(14997355490276144806)
XLA Ops:
  0.6 0.0 copy-start
  0.6 3.1 %collective-permute-start = (f32[1,32,192]{2,1,0:T(8,128)}, f32[1,32,192]{2,1,0:T(8,128)S(1)}, u32[]{:S(2)}, u32[]{:S(2)}) collective-permute-start(f32[1,32,192]{2,1,0:T(8,128)} %refs_0_.1), channel_id=1, source_target_pairs={{0,4},{4,8},{8,12},{12,0},{1,5},{5,9},{9,13},{13,1},{2,6},{6,10},{... | collective-permute-start | bytes 73736 | tf_op jit(solution)/shard_map/ppermute | solution.py:298
  3.7 2.6 %collective-permute-start.1 = (f32[1,32,192]{2,1,0:T(8,128)}, f32[1,32,192]{2,1,0:T(8,128)S(1)}, u32[]{:S(2)}, u32[]{:S(2)}) collective-permute-start(f32[1,32,192]{2,1,0:T(8,128)} %refs_0_.1), channel_id=1, source_target_pairs={{0,8},{4,12},{8,0},{12,4},{1,9},{5,13},{9,1},{13,5},{2,10},{6,14},... | collective-permute-start | bytes 73736 | tf_op jit(solution)/shard_map/ppermute | solution.py:298
  6.3 1.3 %collective-permute-start.2 = (f32[1,32,192]{2,1,0:T(8,128)}, f32[1,32,192]{2,1,0:T(8,128)S(1)}, u32[]{:S(2)}, u32[]{:S(2)}) collective-permute-start(f32[1,32,192]{2,1,0:T(8,128)} %refs_0_.1), channel_id=1, source_target_pairs={{0,12},{4,0},{8,4},{12,8},{1,13},{5,1},{9,5},{13,9},{2,14},{6,2},{... | collective-permute-start | bytes 73736 | tf_op jit(solution)/shard_map/ppermute | solution.py:298
  7.7 8.6 %input.1 = (f32[2048,320]{1,0:T(8,128)}, bf16[320,768]{1,0:T(8,128)(2,1)}, bf16[320,768]{1,0:T(8,128)(2,1)}) custom-call(f32[2048,768]{1,0:T(8,128)} %bitcast.14, f32[320,768]{1,0:T(8,128)} %bitcast.16), custom_call_target="tpu_custom_call" | custom-call | flops 3019898880 | bytes 9175040 | tf_op jit(solution)/shard_map/input/pallas_call | solution.py:301
  16.2 0.0 collective-permute-done.refs_1_
  16.2 0.0 collective-permute-done.1.refs_2_
  16.2 0.0 collective-permute-done.2.refs_3_
  16.2 0.0 copy-done
  16.3 1.6 %collective-permute-start.3 = (f32[4,32,192]{2,1,0:T(8,128)S(1)}, f32[4,32,192]{2,1,0:T(8,128)S(1)}, u32[]{:S(2)}, u32[]{:S(2)}) collective-permute-start(f32[4,32,192]{2,1,0:T(8,128)S(1)} %stack.2.refs_0_), channel_id=1, source_target_pairs={{0,2},{2,0},{16,18},{18,16},{1,3},{3,1},{17,19},{19,17},{4,6},{6,4... | collective-permute-start | bytes 294920 | tf_op jit(solution)/shard_map/ppermute | solution.py:314
  17.9 1.5 %collective-permute-start.4 = (f32[4,32,192]{2,1,0:T(8,128)S(1)}, f32[4,32,192]{2,1,0:T(8,128)S(1)}, u32[]{:S(2)}, u32[]{:S(2)}) collective-permute-start(f32[4,32,192]{2,1,0:T(8,128)S(1)} %stack.2.refs_0_), channel_id=1, source_target_pairs={{0,16},{2,18},{16,0},{18,2},{1,17},{3,19},{17,1},{19,3},{4,20},{6,... | collective-permute-start | bytes 294920 | tf_op jit(solution)/shard_map/ppermute | solution.py:314
  19.4 0.5 collective-permute-start.5
  19.8 0.0 copy-start.2
  19.8 0.0 copy-start.1
  19.8 9.1 %target.1.refs_4_.tw_hbm = f32[2048,320]{1,0:T(8,128)} custom-call(f32[2048,768]{1,0:T(8,128)} %bitcast.15, f32[320,768]{1,0:T(8,128)} %weight_ref.3), custom_call_target="tpu_custom_call" | custom-call | flops 3019898880 | bytes 5242880 | tf_op jit(solution)/shard_map/target/pallas_call | solution.py:315
  28.9 0.0 collective-permute-done.3.refs_1_
  28.9 0.0 collective-permute-done.4.refs_2_
  28.9 0.0 collective-permute-done.5.refs_3_
  29.0 0.1 collective-permute-start.6
  29.1 0.0 copy-done.2
  29.1 2.0 %gram.1.gram_hbm = f32[320,320]{1,0:T(8,128)} custom-call(f32[320,768]{1,0:T(8,128)S(1)} %copy-done.2, f32[512,192]{1,0:T(8,128)S(1)} %bitcast.9), custom_call_target="tpu_custom_call" | custom-call | flops 629145600 | bytes 819200 | tf_op jit(solution)/shard_map/gram/pallas_call | solution.py:331
  31.1 0.0 collective-permute-done.6.other_ref
  31.1 0.0 copy-done.1
  31.1 10.2 %middle.1 = (f32[2048,320]{1,0:T(8,128)}, f32[256,256]{1,0:T(8,128)}) custom-call(s32[4,8]{1,0:T(4,128)S(1)} %bitcast.12, f32[512,192]{1,0:T(8,128)S(1)} %bitcast.10, f32[512,192]{1,0:T(8,128)S(1)} %collective-permute-done.6.other_ref, f32[2048,320]{1,0:T(8,128)} %get-tuple-element.9.refs_4_.xw_hbm, f32[2048,320]{1,0:T(8,128)} %target.1.refs_4_.tw_hbm, ...), custom_call_target="tpu_custom_call" | custom-call | flops 1258291200 | bytes 5767168 | tf_op jit(solution)/shard_map/middle/pallas_call | solution.py:342
  41.3 3.5 %all-to-all-start = ((f32[16,16,256]{2,1,0:T(8,128)}), f32[16,16,256]{2,1,0:T(8,128)S(1)}, u32[]{:S(2)}, u32[]{:S(2)}) async-start(f32[16,16,256]{2,1,0:T(8,128)} %bitcast.5), calls=%async_computation | async-start | bytes 524288 | tf_op jit(solution)/shard_map/all_to_all | solution.py:364
  44.8 6.3 %last.2.done_ref.refs_0_ = f32[2048,768]{1,0:T(8,128)} custom-call(f32[2048,320]{1,0:T(8,128)} %get-tuple-element.11.de_ref, bf16[320,768]{1,0:T(8,128)(2,1)} %get-tuple-element.12.high_ref, bf16[320,768]{1,0:T(8,128)(2,1)} %get-tuple-element.13.low_ref), custom_call_target="tpu_custom_call" | custom-call | flops 2264924160 | bytes 12582912 | tf_op jit(solution)/shard_map/last/pallas_call | solution.py:367
  51.1 3.7 %all-to-all-done = f32[16,16,256]{2,1,0:T(8,128)S(1)} async-done(((f32[16,16,256]{2,1,0:T(8,128)}), f32[16,16,256]{2,1,0:T(8,128)S(1)}, u32[]{:S(2)}, u32[]{:S(2)}) %all-to-all-start) | async-done | bytes 262176 | tf_op jit(solution)/shard_map/all_to_all | solution.py:364
  54.8 0.9 %scatter.1 = (f32[1,32,192]{2,1,0:T(8,128)}, f32[1,32,192]{2,1,0:T(8,128)S(1)}) custom-call(f32[256,256]{1,0:T(8,128)S(1)} %bitcast.11, f32[2048,768]{1,0:T(8,128)} %last.2.done_ref.refs_0_), custom_call_target="tpu_custom_call" | custom-call | flops 10000 | bytes 98304 | tf_op jit(solution)/shard_map/scatter/pallas_call | solution.py:383
  55.7 1.5 %collective-permute-start.7 = (f32[1,32,192]{2,1,0:T(8,128)S(1)}, f32[1,32,192]{2,1,0:T(8,128)S(1)}, u32[]{:S(2)}, u32[]{:S(2)}) collective-permute-start(f32[1,32,192]{2,1,0:T(8,128)S(1)} %get-tuple-element.15), channel_id=1, source_target_pairs={{0,16},{16,0},{1,17},{17,1},{2,18},{18,2},{3,19},{19,3},{4,20},{20... | collective-permute-start | bytes 73736 | tf_op jit(solution)/shard_map/ppermute | solution.py:394
  57.2 0.0 copy-start.3
  57.2 3.5 %last.3 = f32[2048,768]{1,0:T(8,128)} custom-call(f32[2048,320]{1,0:T(8,128)} %get-tuple-element.11.de_ref, bf16[320,768]{1,0:T(8,128)(2,1)} %get-tuple-element.12.high_ref, bf16[320,768]{1,0:T(8,128)(2,1)} %get-tuple-element.13.low_ref, f32[2048,768]{1,0:T(8,128)} %last.2.done_ref.refs_0_, ...), custom_call_target="tpu_custom_call", output_to_operand_aliasing={{}: (3, {})} | custom-call | flops 754974720 | bytes 12582912 | tf_op jit(solution)/shard_map/last/pallas_call | solution.py:367
  60.8 0.0 collective-permute-done.7
  60.8 0.0 copy-done.3
  60.8 0.6 %add.3 = f32[1,32,192]{2,1,0:T(8,128)} add(f32[1,32,192]{2,1,0:T(8,128)S(1)} %copy-done.3, f32[1,32,192]{2,1,0:T(8,128)S(1)} %collective-permute-done.7) | non-fusion elementwise | flops 6144 | bytes 73728 | tf_op jit(solution)/shard_map/add | solution.py:394
  (2 shorter events, 0.0 us)
Async XLA Ops:
  0.6 15.6 %copy-start = (f32[1,32,192]{2,1,0:T(8,128)S(1)}, f32[1,32,192]{2,1,0:T(8,128)}, u32[]{:S(2)}) copy-start(f32[1,32,192]{2,1,0:T(8,128)} %refs_0_.1) | copy-start | bytes 73732
  0.6 15.6 %collective-permute-start = (f32[1,32,192]{2,1,0:T(8,128)}, f32[1,32,192]{2,1,0:T(8,128)S(1)}, u32[]{:S(2)}, u32[]{:S(2)}) collective-permute-start(f32[1,32,192]{2,1,0:T(8,128)} %refs_0_.1), channel_id=1, source_target_pairs={{0,4},{4,8},{8,12},{12,0},{1,5},{5,9},{9,13},{13,1},{2,6},{6,10},{... | collective-permute-start | bytes 73736 | tf_op jit(solution)/shard_map/ppermute | solution.py:298
  3.7 12.5 %collective-permute-start.1 = (f32[1,32,192]{2,1,0:T(8,128)}, f32[1,32,192]{2,1,0:T(8,128)S(1)}, u32[]{:S(2)}, u32[]{:S(2)}) collective-permute-start(f32[1,32,192]{2,1,0:T(8,128)} %refs_0_.1), channel_id=1, source_target_pairs={{0,8},{4,12},{8,0},{12,4},{1,9},{5,13},{9,1},{13,5},{2,10},{6,14},... | collective-permute-start | bytes 73736 | tf_op jit(solution)/shard_map/ppermute | solution.py:298
  6.3 9.9 %collective-permute-start.2 = (f32[1,32,192]{2,1,0:T(8,128)}, f32[1,32,192]{2,1,0:T(8,128)S(1)}, u32[]{:S(2)}, u32[]{:S(2)}) collective-permute-start(f32[1,32,192]{2,1,0:T(8,128)} %refs_0_.1), channel_id=1, source_target_pairs={{0,12},{4,0},{8,4},{12,8},{1,13},{5,1},{9,5},{13,9},{2,14},{6,2},{... | collective-permute-start | bytes 73736 | tf_op jit(solution)/shard_map/ppermute | solution.py:298
  16.3 12.7 %collective-permute-start.3 = (f32[4,32,192]{2,1,0:T(8,128)S(1)}, f32[4,32,192]{2,1,0:T(8,128)S(1)}, u32[]{:S(2)}, u32[]{:S(2)}) collective-permute-start(f32[4,32,192]{2,1,0:T(8,128)S(1)} %stack.2.refs_0_), channel_id=1, source_target_pairs={{0,2},{2,0},{16,18},{18,16},{1,3},{3,1},{17,19},{19,17},{4,6},{6,4... | collective-permute-start | bytes 294920 | tf_op jit(solution)/shard_map/ppermute | solution.py:314
  17.9 11.1 %collective-permute-start.4 = (f32[4,32,192]{2,1,0:T(8,128)S(1)}, f32[4,32,192]{2,1,0:T(8,128)S(1)}, u32[]{:S(2)}, u32[]{:S(2)}) collective-permute-start(f32[4,32,192]{2,1,0:T(8,128)S(1)} %stack.2.refs_0_), channel_id=1, source_target_pairs={{0,16},{2,18},{16,0},{18,2},{1,17},{3,19},{17,1},{19,3},{4,20},{6,... | collective-permute-start | bytes 294920 | tf_op jit(solution)/shard_map/ppermute | solution.py:314
  19.4 9.6 %collective-permute-start.5 = (f32[4,32,192]{2,1,0:T(8,128)S(1)}, f32[4,32,192]{2,1,0:T(8,128)S(1)}, u32[]{:S(2)}, u32[]{:S(2)}) collective-permute-start(f32[4,32,192]{2,1,0:T(8,128)S(1)} %stack.2.refs_0_), channel_id=1, source_target_pairs={{0,18},{2,16},{16,2},{18,0},{1,19},{3,17},{17,3},{19,1},{4,22},{6,... | collective-permute-start | bytes 294920 | tf_op jit(solution)/shard_map/ppermute | solution.py:314
  19.8 9.2 %copy-start.2 = (f32[320,768]{1,0:T(8,128)S(1)}, f32[320,768]{1,0:T(8,128)}, u32[]{:S(2)}) copy-start(f32[320,768]{1,0:T(8,128)} %weight_ref.3) | copy-start | bytes 2949124
  19.8 11.2 %copy-start.1 = (s32[8,4]{0,1:T(4,128)S(1)}, s32[8,4]{0,1:T(4,128)}, u32[]{:S(2)}) copy-start(s32[8,4]{0,1:T(4,128)} %param.12) | copy-start | bytes 388
  29.0 2.1 %collective-permute-start.6 = (f32[512,192]{1,0:T(8,128)S(1)}, f32[512,192]{1,0:T(8,128)S(1)}, u32[]{:S(2)}, u32[]{:S(2)}) collective-permute-start(f32[512,192]{1,0:T(8,128)S(1)} %bitcast.8), channel_id=1, source_target_pairs={{0,1},{1,0},{2,3},{3,2},{4,5},{5,4},{6,7},{7,6},{8,9},{9,8},{10,11... | collective-permute-start | bytes 1179656 | tf_op jit(solution)/shard_map/ppermute | solution.py:330
  41.3 13.6 %all-to-all-start = ((f32[16,16,256]{2,1,0:T(8,128)}), f32[16,16,256]{2,1,0:T(8,128)S(1)}, u32[]{:S(2)}, u32[]{:S(2)}) async-start(f32[16,16,256]{2,1,0:T(8,128)} %bitcast.5), calls=%async_computation | async-start | bytes 524288 | tf_op jit(solution)/shard_map/all_to_all | solution.py:364
  55.7 5.1 %collective-permute-start.7 = (f32[1,32,192]{2,1,0:T(8,128)S(1)}, f32[1,32,192]{2,1,0:T(8,128)S(1)}, u32[]{:S(2)}, u32[]{:S(2)}) collective-permute-start(f32[1,32,192]{2,1,0:T(8,128)S(1)} %get-tuple-element.15), channel_id=1, source_target_pairs={{0,16},{16,0},{1,17},{17,1},{2,18},{18,2},{3,19},{19,3},{4,20},{20... | collective-permute-start | bytes 73736 | tf_op jit(solution)/shard_map/ppermute | solution.py:394
  57.2 3.6 %copy-start.3 = (f32[1,32,192]{2,1,0:T(8,128)S(1)}, f32[1,32,192]{2,1,0:T(8,128)}, u32[]{:S(2)}) copy-start(f32[1,32,192]{2,1,0:T(8,128)} %get-tuple-element.14.refs_1_) | copy-start | bytes 73732

commit v4 on v3

--- a/solution.py
+++ b/solution.py
@@ -15,7 +15,7 @@
 TN = (((0,), (0,)), ((), ()))
 ROWS = 512
 SIDE = 8
-MAIN = 256
+AHEAD = 2
 LANES = 256
 LIMIT = 60 * 1024 * 1024
 ROOM = 40 * 1024 * 1024
@@ -56,24 +56,50 @@
     )
 
 
-def wide_product(value, main_hi, main_lo, tail, out_ref, dims):
-    high, low = split(value)
-    rest = out_ref.shape[1] - MAIN
-    out_ref[:, :MAIN] = dot3((high, low), (main_hi[...], main_lo[...]), dims)
-    both = dot(high, tail[...], dims)
-    tail_hi = tail[:rest] if dims == NT else tail[:, :rest]
-    out_ref[:, MAIN:] = both[:, :rest] + (both[:, rest:] + dot(low, tail_hi, dims))
-
-
-def input_kernel(x_ref, weight_ref, out_ref, high_ref, low_ref, tail):
-    @pl.when(pl.program_id(0) == 0)
-    def _():
-        high, low = split(weight_ref[...])
-        high_ref[...], low_ref[...] = high, low
-        rest = high.shape[0] - MAIN
-        tail[:rest], tail[rest:] = high[MAIN:], low[MAIN:]
-
-    wide_product(x_ref[...], high_ref.at[:MAIN], low_ref.at[:MAIN], tail, out_ref, NT)
+def stream(chunks, source, held, result, target, in_sems, out_sems, product, prepare=None):
+    loads, stores = [], []
+    for i, (start, size) in enumerate(chunks):
+        here = pl.ds(start, size)
+        loads.append(pltpu.make_async_copy(source.at[here], held.at[here], in_sems.at[i]))
+        stores.append(pltpu.make_async_copy(result.at[here], target.at[here], out_sems.at[i]))
+    for copy in loads[:AHEAD]:
+        copy.start()
+    if prepare is not None:
+        prepare()
+    for i, (start, size) in enumerate(chunks):
+        loads[i].wait()
+        if i + AHEAD < len(chunks):
+            loads[i + AHEAD].start()
+        result[start : start + size, :] = product(held[start : start + size, :])
+        stores[i].start()
+    for copy in stores:
+        copy.wait()
+
+
+def chunk_rows(first, last):
+    cuts = [first] + list(range(first + ROWS // 2, last - ROWS // 2 + 1, ROWS)) + [last]
+    return [(low, high - low) for low, high in zip(cuts, cuts[1:])]
+
+
+def wide_kernel(chunks, x_hbm, weight_hbm, *refs):
+    out_hbm, *split_hbm, x, out, weight, high_ref, low_ref, in_sems, out_sems, sems = refs
+    fetch = pltpu.make_async_copy(weight_hbm, weight, sems.at[0])
+    fetch.start()
+    keep = []
+
+    def prepare():
+        fetch.wait()
+        high_ref[...], low_ref[...] = split(weight[...])
+        for i, (ref, hbm) in enumerate(zip((high_ref, low_ref), split_hbm)):
+            keep.append(pltpu.make_async_copy(ref, hbm, sems.at[1 + i]))
+            keep[i].start()
+
+    def product(value):
+        return dot3(split(value), (high_ref[...], low_ref[...]), NT)
+
+    stream(chunks, x_hbm, x, out, out_hbm, in_sems, out_sems, product, prepare)
+    for copy in keep:
+        copy.wait()
 
 
 def gram_kernel(weight_ref, before_ref, gram_ref):
@@ -87,16 +113,6 @@
     size = block_refs[0].shape[0]
     for k, ref in enumerate(block_refs):
         out_ref[k * size : (k + 1) * size] = ref[...]
-
-
-def target_kernel(t_ref, weight_ref, out_ref, main_hi, main_lo, tail):
-    @pl.when(pl.program_id(0) == 0)
-    def _():
-        high, low = split(weight_ref[...].T)
-        main_hi[...], main_lo[...] = high[:, :MAIN], low[:, :MAIN]
-        tail[...] = jnp.concatenate([high[:, MAIN:], low[:, MAIN:]], axis=1)
-
-    wide_product(t_ref[...], main_hi, main_lo, tail, out_ref, NN)
 
 
 def row_value(crops_ref, column, patches, shape, axis, each):
@@ -192,10 +208,11 @@
 
     groups, part = ROWS // 64, ROWS // 4
     stores = []
+    for pair in large:
+        for copy in pair:
+            copy.wait()
     for i in range(steps):
         here = slice(i * ROWS, (i + 1) * ROWS)
-        for copy in large[i]:
-            copy.wait()
         spread = context[i * part : (i + 1) * part, :].reshape(groups, 1, 16, width)
         pre = (xw[here, :].reshape(groups, 4, 16, width) + spread).reshape(ROWS, width)
         gate = sigmoid(pre)
@@ -240,19 +257,23 @@
     other_ref[0] = total[pl.ds(pl.multiple_of((1 - side) * half, half), half), :]
 
 
-def last_kernel(de_ref, high_ref, low_ref, *refs):
-    out_ref, tail = refs[-2:]
-    depth = high_ref.shape[0]
-    rest = depth - MAIN
-
-    @pl.when(pl.program_id(0) == 0)
-    def _():
-        tail[:rest], tail[rest : 2 * rest], tail[2 * rest :] = low_ref[MAIN:], high_ref[MAIN:], high_ref[MAIN:]
-
-    high, low = split(de_ref[...])
-    tails = jnp.concatenate([high[:, MAIN:], low[:, MAIN:], high[:, MAIN:]], axis=1)
-    main = dot3((high[:, :MAIN], low[:, :MAIN]), (high_ref[:MAIN], low_ref[:MAIN]))
-    out_ref[...] = main + dot(tails, tail[...])
+def last_kernel(chunks, de_hbm, high_hbm, low_hbm, *refs):
+    out_hbm, de, out, high_ref, low_ref, in_sems, out_sems, sems = refs[-8:]
+    fetches = [
+        pltpu.make_async_copy(high_hbm, high_ref, sems.at[0]),
+        pltpu.make_async_copy(low_hbm, low_ref, sems.at[1]),
+    ]
+    for copy in fetches:
+        copy.start()
+
+    def prepare():
+        for copy in fetches:
+            copy.wait()
+
+    def product(value):
+        return dot3(split(value), (high_ref[...], low_ref[...]))
+
+    stream(chunks, de_hbm, de, out, out_hbm, in_sems, out_sems, product, prepare)
 
 
 def fixed(*values):
@@ -272,14 +293,6 @@
     )(*blocks, *fixed(before))
 
 
-def whole(shape):
-    return pl.BlockSpec(shape, lambda i: (0,) * len(shape))
-
-
-def by_rows(width, first=0):
-    return pl.BlockSpec((ROWS, width), lambda i: (i + first, 0))
-
-
 def body(coarse_input, coarse_weight, fine_input, fine_target, crops, in_weight, context_weight, out_weight):
     patch = ("far", "y", "core")
     peers = lax.axis_size(patch)
@@ -290,42 +303,41 @@
     half = coarse_input.shape[1]
     count = patches * tokens
     steps = count // ROWS
-    rest = width - MAIN
     swap = [(0, 1), (1, 0)]
 
     column = [coarse_input]
     for k in range(1, far):
         column.append(lax.ppermute(coarse_input, "far", [(p, (p + k) % far) for p in range(far)]))
-    weight = in_weight.T
-    weight_shape = jax.ShapeDtypeStruct((width, values), BF16)
-    xw, win_hi, win_lo = call(
-        input_kernel,
-        "input",
-        6 * count * values * width,
-        (jax.ShapeDtypeStruct((count, width), F32), weight_shape, weight_shape),
-        grid=(steps,),
-        in_specs=[by_rows(values), whole((width, values))],
-        out_specs=(by_rows(width), whole((width, values)), whole((width, values))),
-        scratch_shapes=[pltpu.VMEM((2 * rest, values), BF16)],
-    )(fine_input.reshape(count, values), weight)
+    chunks = chunk_rows(0, count)
+
+    def wide(name, value, weight, keep):
+        split_shape = (width, values)
+        out_shape = [pltpu.HBM((count, width), F32)] + [pltpu.HBM(split_shape, BF16)] * (2 * keep)
+        return call(
+            functools.partial(wide_kernel, chunks),
+            name,
+            6 * count * values * width,
+            out_shape,
+            in_specs=[HBM, HBM],
+            out_specs=[HBM] * len(out_shape),
+            scratch_shapes=[
+                pltpu.VMEM((count, values), F32),
+                pltpu.VMEM((count, width), F32),
+                pltpu.VMEM(split_shape, F32),
+                pltpu.VMEM(split_shape, BF16),
+                pltpu.VMEM(split_shape, BF16),
+                pltpu.SemaphoreType.DMA((len(chunks),)),
+                pltpu.SemaphoreType.DMA((len(chunks),)),
+                pltpu.SemaphoreType.DMA((3,)),
+            ],
+        )(*fixed(value.reshape(count, values), weight))
+
+    xw, win_hi, win_lo = wide("input", fine_input, in_weight.T, True)
     column = stack(column, xw)
     own = [column]
     for flip in range(1, 4):
         own.append(lax.ppermute(column, ("lvl", "y"), [(p, p ^ flip) for p in range(4)]))
-    tw = call(
-        target_kernel,
-        "target",
-        6 * count * values * width,
-        jax.ShapeDtypeStruct((count, width), F32),
-        grid=(steps,),
-        in_specs=[by_rows(values), whole((width, values))],
-        out_specs=by_rows(width),
-        scratch_shapes=[
-            pltpu.VMEM((values, MAIN), BF16),
-            pltpu.VMEM((values, MAIN), BF16),
-            pltpu.VMEM((values, 2 * rest), BF16),
-        ],
-    )(fine_target.reshape(count, values), out_weight)
+    (tw,) = wide("target", fine_target, out_weight, False)
     own = stack(own, tw).reshape(-1, pixels)
     other = lax.ppermute(own, "core", swap)
     gram = call(
@@ -363,21 +375,28 @@
     )(crops.T, own, other, *fixed(xw, tw, gram, coarse_weight, context_weight))
     returned = lax.all_to_all(back, patch, 0, 0, tiled=True)
 
-    def last(first, number, *extra):
+    def last(first, end, *extra):
+        mine = chunk_rows(first, end)
         return call(
-            last_kernel,
+            functools.partial(last_kernel, mine),
             "last",
-            6 * number * ROWS * values * width,
-            jax.ShapeDtypeStruct((count, values), F32),
-            grid=(number,),
-            in_specs=[by_rows(width, first), whole((width, values)), whole((width, values))]
-            + [HBM] * len(extra),
-            out_specs=by_rows(values, first),
-            scratch_shapes=[pltpu.VMEM((3 * rest, values), BF16)],
+            6 * (end - first) * values * width,
+            pltpu.HBM((count, values), F32),
+            in_specs=[HBM] * (3 + len(extra)),
+            out_specs=HBM,
+            scratch_shapes=[
+                pltpu.VMEM((count, width), F32),
+                pltpu.VMEM((count, values), F32),
+                pltpu.VMEM((width, values), BF16),
+                pltpu.VMEM((width, values), BF16),
+                pltpu.SemaphoreType.DMA((len(mine),)),
+                pltpu.SemaphoreType.DMA((len(mine),)),
+                pltpu.SemaphoreType.DMA((2,)),
+            ],
             input_output_aliases={3: 0} if extra else {},
-        )(de, win_hi, win_lo, *fixed(*extra))
-
-    early = steps - 1
+        )(*fixed(de, win_hi, win_lo, *extra))
+
+    early = count - ROWS
     fine_grad = last(0, early)
     part = (1, half, pixels)
     mine, theirs = call(
@@ -390,7 +409,7 @@
         out_specs=(VMEM, VMEM),
         scratch_shapes=[pltpu.VMEM((SIDE * SIDE, pixels), F32)],
     )(returned, *fixed(fine_grad))
-    fine_grad = last(early, steps - early, fine_grad, mine)
+    fine_grad = last(early, count, fine_grad, mine)
     coarse_grad = mine + lax.ppermute(theirs, "lvl", swap)
     return (coarse_grad, fine_grad.reshape(fine_input.shape))
 

time: 61.8 us -> 61.7 us (level)
  waiting for transfers between devices: 3.75 us -> 2.25 us
  Pallas kernels: 40.6 us -> 42 us
    pallas_call x4, Pallas kernels: 27.5 us -> 29.4 us  [the longest x2 16.8 us: wide(): call(functools.partial(wide_kernel, chunks), name, 6 * count * values * w...]
    all_to_all x1, waiting for transfers between devices: 3.73 us -> 2.23 us  [body(): returned = lax.all_to_all(back, patch, 0, 0, tiled=True)]
  transfers between devices with their start and end apart: 9 -> 9, of which waited for: 1 -> 1; matrix products, arithmetic and copies ran while one was open for 0% -> 0% of each run, Pallas kernels for 48% -> 51%
where the time goes in v4:
time: 61.7 us; the launch traced here: 61.4 us
  Pallas kernels  42 us (68%)
  starting transfers between devices  15.7 us (25%)
  waiting for transfers between devices  2.25 us (4%)
  between operations  0.8 us (1%)
  other arithmetic  0.62 us (1%)
    pallas_call x2, Pallas kernels, wide(): call(functools.partial(wide_kernel, chunks), name, 6 * count * values * w...  16.8 us
    pallas_call x2, Pallas kernels, last(): call(functools.partial(last_kernel, mine), 'last', 6 * (end - first) * va...  12.6 us
    pallas_call x1, Pallas kernels, body(): call(functools.partial(middle_kernel, patches, peers), 'middle', 6 * coun...  9.72 us
    ppermute x3, starting transfers between devices, body(): lax.ppermute(coarse_input, 'far', [(p, (p + k) % far) for p in range(far)])  7.01 us
    ppermute x3, starting transfers between devices, body(): lax.ppermute(column, ('lvl', 'y'), [(p, p ^ flip) for p in range(4)])  3.55 us
    all_to_all x1, starting transfers between devices, body(): returned = lax.all_to_all(back, patch, 0, 0, tiled=True)  3.54 us
    all_to_all x1, waiting for transfers between devices, body(): returned = lax.all_to_all(back, patch, 0, 0, tiled=True)  2.23 us
    pallas_call x1, Pallas kernels, body(): call(gram_kernel, 'gram', 8 * values * width * width, pltpu.HBM((width, w...  1.97 us
  transfers between devices with their start and end apart: 9, of which 1 were waited for; matrix products, arithmetic and copies ran while one was open for 0% of the time, Pallas kernels for 51%

profile of v4, /device:TPU:0, one launch (start us, length us, event | category | flops | bytes accessed | tf_op | source)
XLA Modules:
  0.0 61.4 jit_solution(2598859257761555224)
XLA Ops:
  0.6 0.0 copy-start
  0.6 3.1 %collective-permute-start = (f32[1,32,192]{2,1,0:T(8,128)}, f32[1,32,192]{2,1,0:T(8,128)S(1)}, u32[]{:S(2)}, u32[]{:S(2)}) collective-permute-start(f32[1,32,192]{2,1,0:T(8,128)} %refs_0_.1), channel_id=1, source_target_pairs={{0,4},{4,8},{8,12},{12,0},{1,5},{5,9},{9,13},{13,1},{2,6},{6,10},{... | collective-permute-start | bytes 73736 | tf_op jit(solution)/shard_map/ppermute | solution.py:310
  3.7 2.6 %collective-permute-start.1 = (f32[1,32,192]{2,1,0:T(8,128)}, f32[1,32,192]{2,1,0:T(8,128)S(1)}, u32[]{:S(2)}, u32[]{:S(2)}) collective-permute-start(f32[1,32,192]{2,1,0:T(8,128)} %refs_0_.1), channel_id=1, source_target_pairs={{0,8},{4,12},{8,0},{12,4},{1,9},{5,13},{9,1},{13,5},{2,10},{6,14},... | collective-permute-start | bytes 73736 | tf_op jit(solution)/shard_map/ppermute | solution.py:310
  6.3 1.3 %collective-permute-start.2 = (f32[1,32,192]{2,1,0:T(8,128)}, f32[1,32,192]{2,1,0:T(8,128)S(1)}, u32[]{:S(2)}, u32[]{:S(2)}) collective-permute-start(f32[1,32,192]{2,1,0:T(8,128)} %refs_0_.1), channel_id=1, source_target_pairs={{0,12},{4,0},{8,4},{12,8},{1,13},{5,1},{9,5},{13,9},{2,14},{6,2},{... | collective-permute-start | bytes 73736 | tf_op jit(solution)/shard_map/ppermute | solution.py:310
  7.7 8.2 %input.1 = (f32[2048,320]{1,0:T(8,128)}, bf16[320,768]{1,0:T(8,128)(2,1)}, bf16[320,768]{1,0:T(8,128)(2,1)}) custom-call(f32[2048,768]{1,0:T(8,128)} %bitcast.14, f32[320,768]{1,0:T(8,128)} %bitcast.16), custom_call_target="tpu_custom_call" | custom-call | flops 3019898880 | bytes 9175040 | tf_op jit(solution)/shard_map/input/pallas_call | solution.py:316
  15.9 0.0 collective-permute-done.refs_1_
  15.9 0.0 collective-permute-done.1.refs_2_
  15.9 0.0 collective-permute-done.2.refs_3_
  15.9 0.0 copy-done
  15.9 1.6 %collective-permute-start.3 = (f32[4,32,192]{2,1,0:T(8,128)S(1)}, f32[4,32,192]{2,1,0:T(8,128)S(1)}, u32[]{:S(2)}, u32[]{:S(2)}) collective-permute-start(f32[4,32,192]{2,1,0:T(8,128)S(1)} %stack.2.refs_0_), channel_id=1, source_target_pairs={{0,2},{2,0},{16,18},{18,16},{1,3},{3,1},{17,19},{19,17},{4,6},{6,4... | collective-permute-start | bytes 294920 | tf_op jit(solution)/shard_map/ppermute | solution.py:339
  17.5 1.5 %collective-permute-start.4 = (f32[4,32,192]{2,1,0:T(8,128)S(1)}, f32[4,32,192]{2,1,0:T(8,128)S(1)}, u32[]{:S(2)}, u32[]{:S(2)}) collective-permute-start(f32[4,32,192]{2,1,0:T(8,128)S(1)} %stack.2.refs_0_), channel_id=1, source_target_pairs={{0,16},{2,18},{16,0},{18,2},{1,17},{3,19},{17,1},{19,3},{4,20},{6,... | collective-permute-start | bytes 294920 | tf_op jit(solution)/shard_map/ppermute | solution.py:339
  19.0 0.5 collective-permute-start.5
  19.5 0.0 copy-start.2
  19.5 0.0 copy-start.1
  19.5 8.6 %target.1.refs_4_.tw_hbm = f32[2048,320]{1,0:T(8,128)} custom-call(f32[2048,768]{1,0:T(8,128)} %bitcast.15, f32[320,768]{1,0:T(8,128)} %weight_ref.1), custom_call_target="tpu_custom_call" | custom-call | flops 3019898880 | bytes 5242880 | tf_op jit(solution)/shard_map/target/pallas_call | solution.py:316
  28.0 0.0 collective-permute-done.3.refs_1_
  28.1 0.0 collective-permute-done.4.refs_2_
  28.1 0.0 collective-permute-done.5.refs_3_
  28.1 0.1 collective-permute-start.6
  28.2 0.0 copy-done.2
  28.2 2.0 %gram.1.gram_hbm = f32[320,320]{1,0:T(8,128)} custom-call(f32[320,768]{1,0:T(8,128)S(1)} %copy-done.2, f32[512,192]{1,0:T(8,128)S(1)} %bitcast.9), custom_call_target="tpu_custom_call" | custom-call | flops 629145600 | bytes 819200 | tf_op jit(solution)/shard_map/gram/pallas_call | solution.py:343
  30.2 0.0 collective-permute-done.6.other_ref
  30.2 0.0 copy-done.1
  30.2 9.7 %middle.1 = (f32[2048,320]{1,0:T(8,128)}, f32[256,256]{1,0:T(8,128)}) custom-call(s32[4,8]{1,0:T(4,128)S(1)} %bitcast.12, f32[512,192]{1,0:T(8,128)S(1)} %bitcast.10, f32[512,192]{1,0:T(8,128)S(1)} %collective-permute-done.6.other_ref, f32[2048,320]{1,0:T(8,128)} %get-tuple-element.9.refs_4_.xw_hbm, f32[2048,320]{1,0:T(8,128)} %target.1.refs_4_.tw_hbm, ...), custom_call_target="tpu_custom_call" | custom-call | flops 1258291200 | bytes 5767168 | tf_op jit(solution)/shard_map/middle/pallas_call | solution.py:354
  39.9 3.5 %all-to-all-start = ((f32[16,16,256]{2,1,0:T(8,128)}), f32[16,16,256]{2,1,0:T(8,128)S(1)}, u32[]{:S(2)}, u32[]{:S(2)}) async-start(f32[16,16,256]{2,1,0:T(8,128)} %bitcast.5), calls=%async_computation | async-start | bytes 524288 | tf_op jit(solution)/shard_map/all_to_all | solution.py:376
  43.5 7.8 %last.2.done_ref.refs_0_ = f32[2048,768]{1,0:T(8,128)} custom-call(f32[2048,320]{1,0:T(8,128)} %get-tuple-element.11.de_hbm, bf16[320,768]{1,0:T(8,128)(2,1)} %get-tuple-element.12.high_hbm, bf16[320,768]{1,0:T(8,128)(2,1)} %get-tuple-element.13.low_hbm), custom_call_target="tpu_custom_call" | custom-call | flops 2264924160 | bytes 12582912 | tf_op jit(solution)/shard_map/last/pallas_call | solution.py:380
  51.2 2.2 %all-to-all-done = f32[16,16,256]{2,1,0:T(8,128)S(1)} async-done(((f32[16,16,256]{2,1,0:T(8,128)}), f32[16,16,256]{2,1,0:T(8,128)S(1)}, u32[]{:S(2)}, u32[]{:S(2)}) %all-to-all-start) | async-done | bytes 262176 | tf_op jit(solution)/shard_map/all_to_all | solution.py:376
  53.5 0.9 %scatter.1 = (f32[1,32,192]{2,1,0:T(8,128)}, f32[1,32,192]{2,1,0:T(8,128)S(1)}) custom-call(f32[256,256]{1,0:T(8,128)S(1)} %bitcast.11, f32[2048,768]{1,0:T(8,128)} %last.2.done_ref.refs_0_), custom_call_target="tpu_custom_call" | custom-call | flops 10000 | bytes 98304 | tf_op jit(solution)/shard_map/scatter/pallas_call | solution.py:402
  54.4 1.5 %collective-permute-start.7 = (f32[1,32,192]{2,1,0:T(8,128)S(1)}, f32[1,32,192]{2,1,0:T(8,128)S(1)}, u32[]{:S(2)}, u32[]{:S(2)}) collective-permute-start(f32[1,32,192]{2,1,0:T(8,128)S(1)} %get-tuple-element.15), channel_id=1, source_target_pairs={{0,16},{16,0},{1,17},{17,1},{2,18},{18,2},{3,19},{19,3},{4,20},{20... | collective-permute-start | bytes 73736 | tf_op jit(solution)/shard_map/ppermute | solution.py:413
  55.9 0.0 copy-start.3
  55.9 4.9 %last.3 = f32[2048,768]{1,0:T(8,128)} custom-call(f32[2048,320]{1,0:T(8,128)} %get-tuple-element.11.de_hbm, bf16[320,768]{1,0:T(8,128)(2,1)} %get-tuple-element.12.high_hbm, bf16[320,768]{1,0:T(8,128)(2,1)} %get-tuple-element.13.low_hbm, f32[2048,768]{1,0:T(8,128)} %last.2.done_ref.refs_0_, ...), custom_call_target="tpu_custom_call", output_to_operand_aliasing={{}: (3, {})} | custom-call | flops 754974720 | bytes 12582912 | tf_op jit(solution)/shard_map/last/pallas_call | solution.py:380
  60.7 0.0 collective-permute-done.7
  60.8 0.0 copy-done.3
  60.8 0.6 %add.3 = f32[1,32,192]{2,1,0:T(8,128)} add(f32[1,32,192]{2,1,0:T(8,128)S(1)} %copy-done.3, f32[1,32,192]{2,1,0:T(8,128)S(1)} %collective-permute-done.7) | non-fusion elementwise | flops 6144 | bytes 73728 | tf_op jit(solution)/shard_map/add | solution.py:413
  (2 shorter events, 0.0 us)
Async XLA Ops:
  0.6 15.3 %copy-start = (f32[1,32,192]{2,1,0:T(8,128)S(1)}, f32[1,32,192]{2,1,0:T(8,128)}, u32[]{:S(2)}) copy-start(f32[1,32,192]{2,1,0:T(8,128)} %refs_0_.1) | copy-start | bytes 73732
  0.6 15.2 %collective-permute-start = (f32[1,32,192]{2,1,0:T(8,128)}, f32[1,32,192]{2,1,0:T(8,128)S(1)}, u32[]{:S(2)}, u32[]{:S(2)}) collective-permute-start(f32[1,32,192]{2,1,0:T(8,128)} %refs_0_.1), channel_id=1, source_target_pairs={{0,4},{4,8},{8,12},{12,0},{1,5},{5,9},{9,13},{13,1},{2,6},{6,10},{... | collective-permute-start | bytes 73736 | tf_op jit(solution)/shard_map/ppermute | solution.py:310
  3.7 12.2 %collective-permute-start.1 = (f32[1,32,192]{2,1,0:T(8,128)}, f32[1,32,192]{2,1,0:T(8,128)S(1)}, u32[]{:S(2)}, u32[]{:S(2)}) collective-permute-start(f32[1,32,192]{2,1,0:T(8,128)} %refs_0_.1), channel_id=1, source_target_pairs={{0,8},{4,12},{8,0},{12,4},{1,9},{5,13},{9,1},{13,5},{2,10},{6,14},... | collective-permute-start | bytes 73736 | tf_op jit(solution)/shard_map/ppermute | solution.py:310
  6.3 9.6 %collective-permute-start.2 = (f32[1,32,192]{2,1,0:T(8,128)}, f32[1,32,192]{2,1,0:T(8,128)S(1)}, u32[]{:S(2)}, u32[]{:S(2)}) collective-permute-start(f32[1,32,192]{2,1,0:T(8,128)} %refs_0_.1), channel_id=1, source_target_pairs={{0,12},{4,0},{8,4},{12,8},{1,13},{5,1},{9,5},{13,9},{2,14},{6,2},{... | collective-permute-start | bytes 73736 | tf_op jit(solution)/shard_map/ppermute | solution.py:310
  15.9 12.1 %collective-permute-start.3 = (f32[4,32,192]{2,1,0:T(8,128)S(1)}, f32[4,32,192]{2,1,0:T(8,128)S(1)}, u32[]{:S(2)}, u32[]{:S(2)}) collective-permute-start(f32[4,32,192]{2,1,0:T(8,128)S(1)} %stack.2.refs_0_), channel_id=1, source_target_pairs={{0,2},{2,0},{16,18},{18,16},{1,3},{3,1},{17,19},{19,17},{4,6},{6,4... | collective-permute-start | bytes 294920 | tf_op jit(solution)/shard_map/ppermute | solution.py:339
  17.5 10.5 %collective-permute-start.4 = (f32[4,32,192]{2,1,0:T(8,128)S(1)}, f32[4,32,192]{2,1,0:T(8,128)S(1)}, u32[]{:S(2)}, u32[]{:S(2)}) collective-permute-start(f32[4,32,192]{2,1,0:T(8,128)S(1)} %stack.2.refs_0_), channel_id=1, source_target_pairs={{0,16},{2,18},{16,0},{18,2},{1,17},{3,19},{17,1},{19,3},{4,20},{6,... | collective-permute-start | bytes 294920 | tf_op jit(solution)/shard_map/ppermute | solution.py:339
  19.0 9.1 %collective-permute-start.5 = (f32[4,32,192]{2,1,0:T(8,128)S(1)}, f32[4,32,192]{2,1,0:T(8,128)S(1)}, u32[]{:S(2)}, u32[]{:S(2)}) collective-permute-start(f32[4,32,192]{2,1,0:T(8,128)S(1)} %stack.2.refs_0_), channel_id=1, source_target_pairs={{0,18},{2,16},{16,2},{18,0},{1,19},{3,17},{17,3},{19,1},{4,22},{6,... | collective-permute-start | bytes 294920 | tf_op jit(solution)/shard_map/ppermute | solution.py:339
  19.5 8.7 %copy-start.2 = (f32[320,768]{1,0:T(8,128)S(1)}, f32[320,768]{1,0:T(8,128)}, u32[]{:S(2)}) copy-start(f32[320,768]{1,0:T(8,128)} %weight_ref.1) | copy-start | bytes 2949124
  19.5 10.7 %copy-start.1 = (s32[8,4]{0,1:T(4,128)S(1)}, s32[8,4]{0,1:T(4,128)}, u32[]{:S(2)}) copy-start(s32[8,4]{0,1:T(4,128)} %param.12) | copy-start | bytes 388
  28.1 2.1 %collective-permute-start.6 = (f32[512,192]{1,0:T(8,128)S(1)}, f32[512,192]{1,0:T(8,128)S(1)}, u32[]{:S(2)}, u32[]{:S(2)}) collective-permute-start(f32[512,192]{1,0:T(8,128)S(1)} %bitcast.8), channel_id=1, source_target_pairs={{0,1},{1,0},{2,3},{3,2},{4,5},{5,4},{6,7},{7,6},{8,9},{9,8},{10,11... | collective-permute-start | bytes 1179656 | tf_op jit(solution)/shard_map/ppermute | solution.py:342
  39.9 13.6 %all-to-all-start = ((f32[16,16,256]{2,1,0:T(8,128)}), f32[16,16,256]{2,1,0:T(8,128)S(1)}, u32[]{:S(2)}, u32[]{:S(2)}) async-start(f32[16,16,256]{2,1,0:T(8,128)} %bitcast.5), calls=%async_computation | async-start | bytes 524288 | tf_op jit(solution)/shard_map/all_to_all | solution.py:376
  54.4 6.4 %collective-permute-start.7 = (f32[1,32,192]{2,1,0:T(8,128)S(1)}, f32[1,32,192]{2,1,0:T(8,128)S(1)}, u32[]{:S(2)}, u32[]{:S(2)}) collective-permute-start(f32[1,32,192]{2,1,0:T(8,128)S(1)} %get-tuple-element.15), channel_id=1, source_target_pairs={{0,16},{16,0},{1,17},{17,1},{2,18},{18,2},{3,19},{19,3},{4,20},{20... | collective-permute-start | bytes 73736 | tf_op jit(solution)/shard_map/ppermute | solution.py:413
  55.9 4.9 %copy-start.3 = (f32[1,32,192]{2,1,0:T(8,128)S(1)}, f32[1,32,192]{2,1,0:T(8,128)}, u32[]{:S(2)}) copy-start(f32[1,32,192]{2,1,0:T(8,128)} %get-tuple-element.14.refs_1_) | copy-start | bytes 73732

commit v5 on v4

--- a/solution.py
+++ b/solution.py
@@ -13,7 +13,7 @@
 NN = (((1,), (0,)), ((), ()))
 NT = (((1,), (1,)), ((), ()))
 TN = (((0,), (0,)), ((), ()))
-ROWS = 512
+ROWS = 1024
 SIDE = 8
 AHEAD = 2
 LANES = 256
@@ -76,9 +76,8 @@
         copy.wait()
 
 
-def chunk_rows(first, last):
-    cuts = [first] + list(range(first + ROWS // 2, last - ROWS // 2 + 1, ROWS)) + [last]
-    return [(low, high - low) for low, high in zip(cuts, cuts[1:])]
+def chunk_rows(first, last, size):
+    return [(start, size) for start in range(first, last, size)]
 
 
 def wide_kernel(chunks, x_hbm, weight_hbm, *refs):
@@ -308,9 +307,9 @@
     column = [coarse_input]
     for k in range(1, far):
         column.append(lax.ppermute(coarse_input, "far", [(p, (p + k) % far) for p in range(far)]))
-    chunks = chunk_rows(0, count)
-
-    def wide(name, value, weight, keep):
+
+    def wide(name, value, weight, keep, rows):
+        chunks = chunk_rows(0, count, rows)
         split_shape = (width, values)
         out_shape = [pltpu.HBM((count, width), F32)] + [pltpu.HBM(split_shape, BF16)] * (2 * keep)
         return call(
@@ -332,12 +331,12 @@
             ],
         )(*fixed(value.reshape(count, values), weight))
 
-    xw, win_hi, win_lo = wide("input", fine_input, in_weight.T, True)
+    xw, win_hi, win_lo = wide("input", fine_input, in_weight.T, True, count // 2)
     column = stack(column, xw)
     own = [column]
     for flip in range(1, 4):
         own.append(lax.ppermute(column, ("lvl", "y"), [(p, p ^ flip) for p in range(4)]))
-    (tw,) = wide("target", fine_target, out_weight, False)
+    (tw,) = wide("target", fine_target, out_weight, False, count // 4)
     own = stack(own, tw).reshape(-1, pixels)
     other = lax.ppermute(own, "core", swap)
     gram = call(
@@ -375,8 +374,8 @@
     )(crops.T, own, other, *fixed(xw, tw, gram, coarse_weight, context_weight))
     returned = lax.all_to_all(back, patch, 0, 0, tiled=True)
 
-    def last(first, end, *extra):
-        mine = chunk_rows(first, end)
+    def last(first, end, rows, *extra):
+        mine = chunk_rows(first, end, rows)
         return call(
             functools.partial(last_kernel, mine),
             "last",
@@ -396,8 +395,8 @@
             input_output_aliases={3: 0} if extra else {},
         )(*fixed(de, win_hi, win_lo, *extra))
 
-    early = count - ROWS
-    fine_grad = last(0, early)
+    early = count * 3 // 4
+    fine_grad = last(0, early, early // 2)
     part = (1, half, pixels)
     mine, theirs = call(
         scatter_kernel,
@@ -409,7 +408,7 @@
         out_specs=(VMEM, VMEM),
         scratch_shapes=[pltpu.VMEM((SIDE * SIDE, pixels), F32)],
     )(returned, *fixed(fine_grad))
-    fine_grad = last(early, count, fine_grad, mine)
+    fine_grad = last(early, count, count - early, fine_grad, mine)
     coarse_grad = mine + lax.ppermute(theirs, "lvl", swap)
     return (coarse_grad, fine_grad.reshape(fine_input.shape))
 

time: 61.7 us -> 61.4 us (level)
  waiting for transfers between devices: 2.25 us -> 0.02 us
  Pallas kernels: 42 us -> 44 us
    all_to_all x1, waiting for transfers between devices: 2.23 us -> 0.01 us  [body(): returned = lax.all_to_all(back, patch, 0, 0, tiled=True)]
    pallas_call x2, Pallas kernels: 12.6 us -> 14.3 us  [last(): call(functools.partial(last_kernel, mine), 'last', 6 * (end - first) * va...]
  transfers between devices with their start and end apart: 9 -> 9, of which waited for: 1 -> 0; matrix products, arithmetic and copies ran while one was open for 0% -> 0% of each run, Pallas kernels for 51% -> 55%
where the time goes in v5:
time: 61.4 us; the launch traced here: 61.1 us
  Pallas kernels  44 us (72%)
  starting transfers between devices  15.7 us (26%)
  between operations  0.8 us (1%)
  other arithmetic  0.62 us (1%)
    pallas_call x2, Pallas kernels, wide(): call(functools.partial(wide_kernel, chunks), name, 6 * count * values * w...  17.4 us
    pallas_call x2, Pallas kernels, last(): call(functools.partial(last_kernel, mine), 'last', 6 * (end - first) * va...  14.3 us
    pallas_call x1, Pallas kernels, body(): call(functools.partial(middle_kernel, patches, peers), 'middle', 6 * coun...  9.41 us
    ppermute x3, starting transfers between devices, body(): lax.ppermute(coarse_input, 'far', [(p, (p + k) % far) for p in range(far)])  7.01 us
    ppermute x3, starting transfers between devices, body(): lax.ppermute(column, ('lvl', 'y'), [(p, p ^ flip) for p in range(4)])  3.55 us
    all_to_all x1, starting transfers between devices, body(): returned = lax.all_to_all(back, patch, 0, 0, tiled=True)  3.54 us
    pallas_call x1, Pallas kernels, body(): call(gram_kernel, 'gram', 8 * values * width * width, pltpu.HBM((width, w...  1.97 us
    ppermute x1, starting transfers between devices, body(): coarse_grad = mine + lax.ppermute(theirs, 'lvl', swap)  1.53 us
  transfers between devices with their start and end apart: 9, of which 0 were waited for; matrix products, arithmetic and copies ran while one was open for 0% of the time, Pallas kernels for 55%

profile of v5, /device:TPU:0, one launch (start us, length us, event | category | flops | bytes accessed | tf_op | source)
XLA Modules:
  0.0 61.1 jit_solution(6773524021185888315)
XLA Ops:
  0.6 0.0 copy-start
  0.6 3.1 %collective-permute-start = (f32[1,32,192]{2,1,0:T(8,128)}, f32[1,32,192]{2,1,0:T(8,128)S(1)}, u32[]{:S(2)}, u32[]{:S(2)}) collective-permute-start(f32[1,32,192]{2,1,0:T(8,128)} %refs_0_.1), channel_id=1, source_target_pairs={{0,4},{4,8},{8,12},{12,0},{1,5},{5,9},{9,13},{13,1},{2,6},{6,10},{... | collective-permute-start | bytes 73736 | tf_op jit(solution)/shard_map/ppermute | solution.py:309
  3.7 2.6 %collective-permute-start.1 = (f32[1,32,192]{2,1,0:T(8,128)}, f32[1,32,192]{2,1,0:T(8,128)S(1)}, u32[]{:S(2)}, u32[]{:S(2)}) collective-permute-start(f32[1,32,192]{2,1,0:T(8,128)} %refs_0_.1), channel_id=1, source_target_pairs={{0,8},{4,12},{8,0},{12,4},{1,9},{5,13},{9,1},{13,5},{2,10},{6,14},... | collective-permute-start | bytes 73736 | tf_op jit(solution)/shard_map/ppermute | solution.py:309
  6.3 1.3 %collective-permute-start.2 = (f32[1,32,192]{2,1,0:T(8,128)}, f32[1,32,192]{2,1,0:T(8,128)S(1)}, u32[]{:S(2)}, u32[]{:S(2)}) collective-permute-start(f32[1,32,192]{2,1,0:T(8,128)} %refs_0_.1), channel_id=1, source_target_pairs={{0,12},{4,0},{8,4},{12,8},{1,13},{5,1},{9,5},{13,9},{2,14},{6,2},{... | collective-permute-start | bytes 73736 | tf_op jit(solution)/shard_map/ppermute | solution.py:309
  7.7 8.7 %input.1 = (f32[2048,320]{1,0:T(8,128)}, bf16[320,768]{1,0:T(8,128)(2,1)}, bf16[320,768]{1,0:T(8,128)(2,1)}) custom-call(f32[2048,768]{1,0:T(8,128)} %bitcast.14, f32[320,768]{1,0:T(8,128)} %bitcast.16), custom_call_target="tpu_custom_call" | custom-call | flops 3019898880 | bytes 9175040 | tf_op jit(solution)/shard_map/input/pallas_call | solution.py:315
  16.4 0.0 collective-permute-done.refs_1_
  16.4 0.0 collective-permute-done.1.refs_2_
  16.4 0.0 collective-permute-done.2.refs_3_
  16.4 0.0 copy-done
  16.4 1.6 %collective-permute-start.3 = (f32[4,32,192]{2,1,0:T(8,128)S(1)}, f32[4,32,192]{2,1,0:T(8,128)S(1)}, u32[]{:S(2)}, u32[]{:S(2)}) collective-permute-start(f32[4,32,192]{2,1,0:T(8,128)S(1)} %stack.2.refs_0_), channel_id=1, source_target_pairs={{0,2},{2,0},{16,18},{18,16},{1,3},{3,1},{17,19},{19,17},{4,6},{6,4... | collective-permute-start | bytes 294920 | tf_op jit(solution)/shard_map/ppermute | solution.py:338
  18.0 1.5 %collective-permute-start.4 = (f32[4,32,192]{2,1,0:T(8,128)S(1)}, f32[4,32,192]{2,1,0:T(8,128)S(1)}, u32[]{:S(2)}, u32[]{:S(2)}) collective-permute-start(f32[4,32,192]{2,1,0:T(8,128)S(1)} %stack.2.refs_0_), channel_id=1, source_target_pairs={{0,16},{2,18},{16,0},{18,2},{1,17},{3,19},{17,1},{19,3},{4,20},{6,... | collective-permute-start | bytes 294920 | tf_op jit(solution)/shard_map/ppermute | solution.py:338
  19.5 0.5 collective-permute-start.5
  20.0 0.0 copy-start.2
  20.0 0.0 copy-start.1
  20.0 8.7 %target.1.refs_4_.tw_hbm = f32[2048,320]{1,0:T(8,128)} custom-call(f32[2048,768]{1,0:T(8,128)} %bitcast.15, f32[320,768]{1,0:T(8,128)} %weight_ref.1), custom_call_target="tpu_custom_call" | custom-call | flops 3019898880 | bytes 5242880 | tf_op jit(solution)/shard_map/target/pallas_call | solution.py:315
  28.7 0.0 collective-permute-done.3.refs_1_
  28.7 0.0 collective-permute-done.4.refs_2_
  28.7 0.0 collective-permute-done.5.refs_3_
  28.7 0.1 collective-permute-start.6
  28.8 0.0 copy-done.2
  28.8 2.0 %gram.1.gram_hbm = f32[320,320]{1,0:T(8,128)} custom-call(f32[320,768]{1,0:T(8,128)S(1)} %copy-done.2, f32[512,192]{1,0:T(8,128)S(1)} %bitcast.9), custom_call_target="tpu_custom_call" | custom-call | flops 629145600 | bytes 819200 | tf_op jit(solution)/shard_map/gram/pallas_call | solution.py:342
  30.8 0.0 collective-permute-done.6.other_ref
  30.8 0.0 copy-done.1
  30.8 9.4 %middle.1 = (f32[2048,320]{1,0:T(8,128)}, f32[256,256]{1,0:T(8,128)}) custom-call(s32[4,8]{1,0:T(4,128)S(1)} %bitcast.12, f32[512,192]{1,0:T(8,128)S(1)} %bitcast.10, f32[512,192]{1,0:T(8,128)S(1)} %collective-permute-done.6.other_ref, f32[2048,320]{1,0:T(8,128)} %get-tuple-element.9.refs_4_.xw_hbm, f32[2048,320]{1,0:T(8,128)} %target.1.refs_4_.tw_hbm, ...), custom_call_target="tpu_custom_call" | custom-call | flops 1258291200 | bytes 5767168 | tf_op jit(solution)/shard_map/middle/pallas_call | solution.py:353
  40.2 3.5 %all-to-all-start = ((f32[16,16,256]{2,1,0:T(8,128)}), f32[16,16,256]{2,1,0:T(8,128)S(1)}, u32[]{:S(2)}, u32[]{:S(2)}) async-start(f32[16,16,256]{2,1,0:T(8,128)} %bitcast.5), calls=%async_computation | async-start | bytes 524288 | tf_op jit(solution)/shard_map/all_to_all | solution.py:375
  43.8 10.3 %last.2.done_ref.refs_0_ = f32[2048,768]{1,0:T(8,128)} custom-call(f32[2048,320]{1,0:T(8,128)} %get-tuple-element.11.de_hbm, bf16[320,768]{1,0:T(8,128)(2,1)} %get-tuple-element.12.high_hbm, bf16[320,768]{1,0:T(8,128)(2,1)} %get-tuple-element.13.low_hbm), custom_call_target="tpu_custom_call" | custom-call | flops 2264924160 | bytes 12582912 | tf_op jit(solution)/shard_map/last/pallas_call | solution.py:379
  54.1 0.0 all-to-all-done
  54.1 0.9 %scatter.1 = (f32[1,32,192]{2,1,0:T(8,128)}, f32[1,32,192]{2,1,0:T(8,128)S(1)}) custom-call(f32[256,256]{1,0:T(8,128)S(1)} %bitcast.11, f32[2048,768]{1,0:T(8,128)} %last.2.done_ref.refs_0_), custom_call_target="tpu_custom_call" | custom-call | flops 10000 | bytes 98304 | tf_op jit(solution)/shard_map/scatter/pallas_call | solution.py:401
  55.0 1.5 %collective-permute-start.7 = (f32[1,32,192]{2,1,0:T(8,128)S(1)}, f32[1,32,192]{2,1,0:T(8,128)S(1)}, u32[]{:S(2)}, u32[]{:S(2)}) collective-permute-start(f32[1,32,192]{2,1,0:T(8,128)S(1)} %get-tuple-element.15), channel_id=1, source_target_pairs={{0,16},{16,0},{1,17},{17,1},{2,18},{18,2},{3,19},{19,3},{4,20},{20... | collective-permute-start | bytes 73736 | tf_op jit(solution)/shard_map/ppermute | solution.py:412
  56.5 0.0 copy-start.3
  56.5 4.0 %last.3 = f32[2048,768]{1,0:T(8,128)} custom-call(f32[2048,320]{1,0:T(8,128)} %get-tuple-element.11.de_hbm, bf16[320,768]{1,0:T(8,128)(2,1)} %get-tuple-element.12.high_hbm, bf16[320,768]{1,0:T(8,128)(2,1)} %get-tuple-element.13.low_hbm, f32[2048,768]{1,0:T(8,128)} %last.2.done_ref.refs_0_, ...), custom_call_target="tpu_custom_call", output_to_operand_aliasing={{}: (3, {})} | custom-call | flops 754974720 | bytes 12582912 | tf_op jit(solution)/shard_map/last/pallas_call | solution.py:379
  60.5 0.0 collective-permute-done.7
  60.5 0.0 copy-done.3
  60.5 0.6 %add.3 = f32[1,32,192]{2,1,0:T(8,128)} add(f32[1,32,192]{2,1,0:T(8,128)S(1)} %copy-done.3, f32[1,32,192]{2,1,0:T(8,128)S(1)} %collective-permute-done.7) | non-fusion elementwise | flops 6144 | bytes 73728 | tf_op jit(solution)/shard_map/add | solution.py:412
  (2 shorter events, 0.0 us)
Async XLA Ops:
  0.6 15.8 %copy-start = (f32[1,32,192]{2,1,0:T(8,128)S(1)}, f32[1,32,192]{2,1,0:T(8,128)}, u32[]{:S(2)}) copy-start(f32[1,32,192]{2,1,0:T(8,128)} %refs_0_.1) | copy-start | bytes 73732
  0.6 15.7 %collective-permute-start = (f32[1,32,192]{2,1,0:T(8,128)}, f32[1,32,192]{2,1,0:T(8,128)S(1)}, u32[]{:S(2)}, u32[]{:S(2)}) collective-permute-start(f32[1,32,192]{2,1,0:T(8,128)} %refs_0_.1), channel_id=1, source_target_pairs={{0,4},{4,8},{8,12},{12,0},{1,5},{5,9},{9,13},{13,1},{2,6},{6,10},{... | collective-permute-start | bytes 73736 | tf_op jit(solution)/shard_map/ppermute | solution.py:309
  3.7 12.7 %collective-permute-start.1 = (f32[1,32,192]{2,1,0:T(8,128)}, f32[1,32,192]{2,1,0:T(8,128)S(1)}, u32[]{:S(2)}, u32[]{:S(2)}) collective-permute-start(f32[1,32,192]{2,1,0:T(8,128)} %refs_0_.1), channel_id=1, source_target_pairs={{0,8},{4,12},{8,0},{12,4},{1,9},{5,13},{9,1},{13,5},{2,10},{6,14},... | collective-permute-start | bytes 73736 | tf_op jit(solution)/shard_map/ppermute | solution.py:309
  6.3 10.1 %collective-permute-start.2 = (f32[1,32,192]{2,1,0:T(8,128)}, f32[1,32,192]{2,1,0:T(8,128)S(1)}, u32[]{:S(2)}, u32[]{:S(2)}) collective-permute-start(f32[1,32,192]{2,1,0:T(8,128)} %refs_0_.1), channel_id=1, source_target_pairs={{0,12},{4,0},{8,4},{12,8},{1,13},{5,1},{9,5},{13,9},{2,14},{6,2},{... | collective-permute-start | bytes 73736 | tf_op jit(solution)/shard_map/ppermute | solution.py:309
  16.4 12.2 %collective-permute-start.3 = (f32[4,32,192]{2,1,0:T(8,128)S(1)}, f32[4,32,192]{2,1,0:T(8,128)S(1)}, u32[]{:S(2)}, u32[]{:S(2)}) collective-permute-start(f32[4,32,192]{2,1,0:T(8,128)S(1)} %stack.2.refs_0_), channel_id=1, source_target_pairs={{0,2},{2,0},{16,18},{18,16},{1,3},{3,1},{17,19},{19,17},{4,6},{6,4... | collective-permute-start | bytes 294920 | tf_op jit(solution)/shard_map/ppermute | solution.py:338
  18.0 10.7 %collective-permute-start.4 = (f32[4,32,192]{2,1,0:T(8,128)S(1)}, f32[4,32,192]{2,1,0:T(8,128)S(1)}, u32[]{:S(2)}, u32[]{:S(2)}) collective-permute-start(f32[4,32,192]{2,1,0:T(8,128)S(1)} %stack.2.refs_0_), channel_id=1, source_target_pairs={{0,16},{2,18},{16,0},{18,2},{1,17},{3,19},{17,1},{19,3},{4,20},{6,... | collective-permute-start | bytes 294920 | tf_op jit(solution)/shard_map/ppermute | solution.py:338
  19.5 9.2 %collective-permute-start.5 = (f32[4,32,192]{2,1,0:T(8,128)S(1)}, f32[4,32,192]{2,1,0:T(8,128)S(1)}, u32[]{:S(2)}, u32[]{:S(2)}) collective-permute-start(f32[4,32,192]{2,1,0:T(8,128)S(1)} %stack.2.refs_0_), channel_id=1, source_target_pairs={{0,18},{2,16},{16,2},{18,0},{1,19},{3,17},{17,3},{19,1},{4,22},{6,... | collective-permute-start | bytes 294920 | tf_op jit(solution)/shard_map/ppermute | solution.py:338
  20.0 8.8 %copy-start.2 = (f32[320,768]{1,0:T(8,128)S(1)}, f32[320,768]{1,0:T(8,128)}, u32[]{:S(2)}) copy-start(f32[320,768]{1,0:T(8,128)} %weight_ref.1) | copy-start | bytes 2949124
  20.0 10.8 %copy-start.1 = (s32[8,4]{0,1:T(4,128)S(1)}, s32[8,4]{0,1:T(4,128)}, u32[]{:S(2)}) copy-start(s32[8,4]{0,1:T(4,128)} %param.12) | copy-start | bytes 388
  28.7 2.1 %collective-permute-start.6 = (f32[512,192]{1,0:T(8,128)S(1)}, f32[512,192]{1,0:T(8,128)S(1)}, u32[]{:S(2)}, u32[]{:S(2)}) collective-permute-start(f32[512,192]{1,0:T(8,128)S(1)} %bitcast.8), channel_id=1, source_target_pairs={{0,1},{1,0},{2,3},{3,2},{4,5},{5,4},{6,7},{7,6},{8,9},{9,8},{10,11... | collective-permute-start | bytes 1179656 | tf_op jit(solution)/shard_map/ppermute | solution.py:341
  40.2 13.8 %all-to-all-start = ((f32[16,16,256]{2,1,0:T(8,128)}), f32[16,16,256]{2,1,0:T(8,128)S(1)}, u32[]{:S(2)}, u32[]{:S(2)}) async-start(f32[16,16,256]{2,1,0:T(8,128)} %bitcast.5), calls=%async_computation | async-start | bytes 524288 | tf_op jit(solution)/shard_map/all_to_all | solution.py:375
  55.0 5.5 %collective-permute-start.7 = (f32[1,32,192]{2,1,0:T(8,128)S(1)}, f32[1,32,192]{2,1,0:T(8,128)S(1)}, u32[]{:S(2)}, u32[]{:S(2)}) collective-permute-start(f32[1,32,192]{2,1,0:T(8,128)S(1)} %get-tuple-element.15), channel_id=1, source_target_pairs={{0,16},{16,0},{1,17},{17,1},{2,18},{18,2},{3,19},{19,3},{4,20},{20... | collective-permute-start | bytes 73736 | tf_op jit(solution)/shard_map/ppermute | solution.py:412
  56.5 4.0 %copy-start.3 = (f32[1,32,192]{2,1,0:T(8,128)S(1)}, f32[1,32,192]{2,1,0:T(8,128)}, u32[]{:S(2)}) copy-start(f32[1,32,192]{2,1,0:T(8,128)} %get-tuple-element.14.refs_1_) | copy-start | bytes 73732

commit v6 on v4

--- a/solution.py
+++ b/solution.py
@@ -56,48 +56,44 @@
     )
 
 
-def stream(chunks, source, held, result, target, in_sems, out_sems, product, prepare=None):
-    loads, stores = [], []
-    for i, (start, size) in enumerate(chunks):
-        here = pl.ds(start, size)
-        loads.append(pltpu.make_async_copy(source.at[here], held.at[here], in_sems.at[i]))
-        stores.append(pltpu.make_async_copy(result.at[here], target.at[here], out_sems.at[i]))
+def stream(loads, stores, product):
     for copy in loads[:AHEAD]:
         copy.start()
-    if prepare is not None:
-        prepare()
-    for i, (start, size) in enumerate(chunks):
-        loads[i].wait()
-        if i + AHEAD < len(chunks):
+    for i, (load, store) in enumerate(zip(loads, stores)):
+        load.wait()
+        if i + AHEAD < len(loads):
             loads[i + AHEAD].start()
-        result[start : start + size, :] = product(held[start : start + size, :])
-        stores[i].start()
+        product(i)
+        store.start()
     for copy in stores:
         copy.wait()
 
 
-def chunk_rows(first, last):
-    cuts = [first] + list(range(first + ROWS // 2, last - ROWS // 2 + 1, ROWS)) + [last]
-    return [(low, high - low) for low, high in zip(cuts, cuts[1:])]
-
-
 def wide_kernel(chunks, x_hbm, weight_hbm, *refs):
-    out_hbm, *split_hbm, x, out, weight, high_ref, low_ref, in_sems, out_sems, sems = refs
+    out_hbm, *split_hbm, x, out, weight, pair, in_sems, out_sems, sems = refs
+    width = weight.shape[0]
     fetch = pltpu.make_async_copy(weight_hbm, weight, sems.at[0])
     fetch.start()
-    keep = []
-
-    def prepare():
-        fetch.wait()
-        high_ref[...], low_ref[...] = split(weight[...])
-        for i, (ref, hbm) in enumerate(zip((high_ref, low_ref), split_hbm)):
-            keep.append(pltpu.make_async_copy(ref, hbm, sems.at[1 + i]))
-            keep[i].start()
-
-    def product(value):
-        return dot3(split(value), (high_ref[...], low_ref[...]), NT)
-
-    stream(chunks, x_hbm, x, out, out_hbm, in_sems, out_sems, product, prepare)
+    loads = [
+        pltpu.make_async_copy(x_hbm.at[here], x.at[here], in_sems.at[i]) for i, here in enumerate(chunks)
+    ]
+    stores = [
+        pltpu.make_async_copy(out.at[:, here], out_hbm.at[:, here], out_sems.at[i])
+        for i, here in enumerate(chunks)
+    ]
+    keep = [pltpu.make_async_copy(pair, hbm, sems.at[1]) for hbm in split_hbm]
+
+    def product(i):
+        if i == 0:
+            fetch.wait()
+            pair[:width], pair[width:] = split(weight[...])
+            for copy in keep:
+                copy.start()
+        high, low = split(x[chunks[i], :])
+        both = dot(pair[...], high, NT)
+        out[:, chunks[i]] = both[:width] + (both[width:] + dot(pair[:width], low, NT))
+
+    stream(loads, stores, product)
     for copy in keep:
         copy.wait()
 
@@ -123,14 +119,12 @@
     return found
 
 
-def chosen(crops_ref, patches, rows_first):
-    shape = (patches * 64, patches * 16) if rows_first else (patches * 16, patches * 64)
-    token_axis = 0 if rows_first else 1
-    token = lax.broadcasted_iota(jnp.int32, shape, token_axis)
-    slot = lax.broadcasted_iota(jnp.int32, shape, 1 - token_axis)
-    scale = row_value(crops_ref, 3, patches, shape, token_axis, 64)
-    group, column = (token // 16) % 4, token % 16
-    wanted = token // 64 * 16 + (group * scale // 2) * 4 + column * scale // 8
+def chosen(crops_ref, patches, tokens):
+    scale = row_value(crops_ref, 3, patches, (1, patches * tokens), 1, tokens)
+    token = lax.broadcasted_iota(jnp.int32, (1, patches * tokens), 1)
+    row, column = (token % tokens) // 16, token % 16
+    wanted = token // tokens * 16 + (row * scale // 8) * 4 + column * scale // 8
+    slot = lax.broadcasted_iota(jnp.int32, (patches * 16, patches * tokens), 0)
     return jnp.where(slot == wanted, 1.0, 0.0).astype(BF16)
 
 
@@ -153,34 +147,28 @@
     cwgt,
     xwgt,
     rows,
-    context,
-    sums,
+    pick,
     small_sems,
     in_sems,
     out_sems,
 ):
     pixels = cwgt.shape[0]
-    count, width = xw.shape
+    width, count = xw.shape
+    slots = patches * 16
     far = peers // 4
-    steps = count // ROWS
+    chunks = chunk_rows(0, count)
     small = [
         pltpu.make_async_copy(source, target, small_sems.at[i])
         for i, (source, target) in enumerate(((cwgt_hbm, cwgt), (xwgt_hbm, xwgt), (gram_hbm, gram)))
     ]
-    large = []
-    for i in range(steps):
-        here = slice(i * ROWS, (i + 1) * ROWS)
-        large.append(
-            (
-                pltpu.make_async_copy(xw_hbm.at[here], xw.at[here], in_sems.at[0, i]),
-                pltpu.make_async_copy(tw_hbm.at[here], tw.at[here], in_sems.at[1, i]),
-            )
-        )
-    for copy in small:
+    large = [pltpu.make_async_copy(xw_hbm, xw, in_sems.at[0]), pltpu.make_async_copy(tw_hbm, tw, in_sems.at[1])]
+    stores = [
+        pltpu.make_async_copy(xw.at[:, here], de_hbm.at[:, here], out_sems.at[i])
+        for i, here in enumerate(chunks)
+    ]
+    for copy in small + large:
         copy.start()
-    for pair in large:
-        for copy in pair:
-            copy.start()
+    pick[...] = chosen(crops_ref, patches, count // patches)
 
     me, side = lax.axis_index(("far", "y", "core")), lax.axis_index("lvl")
     for j in range(patches):
@@ -200,33 +188,28 @@
     slope = gate * (1.0 + pre * (1.0 - gate))
     small[1].wait()
     project = split(xwgt[...])
-    projected = split(dot3(split(pre * gate), project))
-    pick = chosen(crops_ref, patches, True)
-    context[...] = dot(pick, projected[1]) + dot(pick, projected[0])
+    high, low = split(dot3(split(pre * gate), project).T)
+    projected = jnp.concatenate([high, low], axis=1)
     small[2].wait()
-    grams = split(gram[...])
-
-    groups, part = ROWS // 64, ROWS // 4
-    stores = []
-    for pair in large:
-        for copy in pair:
-            copy.wait()
-    for i in range(steps):
-        here = slice(i * ROWS, (i + 1) * ROWS)
-        spread = context[i * part : (i + 1) * part, :].reshape(groups, 1, 16, width)
-        pre = (xw[here, :].reshape(groups, 4, 16, width) + spread).reshape(ROWS, width)
+    high, low = split(gram[...])
+    grams = jnp.concatenate([high, low, high], axis=1)
+    for copy in large:
+        copy.wait()
+
+    dslot = jnp.zeros((2 * width, slots), F32)
+    for i, here in enumerate(chunks):
+        taken = pick[:, here]
+        pre = xw[:, here] + dot(projected, jnp.concatenate([taken, taken], axis=0))
         gate = sigmoid(pre)
         hidden = pre * gate
-        dhidden = dot3(split(hidden), grams) - tw[here, :]
+        high, low = split(hidden)
+        dhidden = dot(grams, jnp.concatenate([high, high, low], axis=0)) - tw[:, here]
         de = dhidden * (gate + hidden * (1.0 - gate))
-        xw[here, :] = de
-        stores.append(pltpu.make_async_copy(xw.at[here], de_hbm.at[here], out_sems.at[i]))
+        xw[:, here] = de
         stores[i].start()
-        sums[i * part : (i + 1) * part, :] = de.reshape(groups, 4, 16, width).sum(axis=1).reshape(part, width)
-
-    pick = chosen(crops_ref, patches, False)
-    high, low = split(sums[...])
-    dslot = dot(pick, low) + dot(pick, high)
+        dslot = dslot + dot(jnp.concatenate(split(de), axis=0), taken, NT)
+
+    dslot = (dslot[:width] + dslot[width:]).T
     dcontext = dot3(split(dslot), project, NT)
     grad = dot3(split(dcontext * slope), coarse, NT)
     shape = (patches * 16, LANES - pixels)
@@ -257,23 +240,36 @@
     other_ref[0] = total[pl.ds(pl.multiple_of((1 - side) * half, half), half), :]
 
 
-def last_kernel(chunks, de_hbm, high_hbm, low_hbm, *refs):
-    out_hbm, de, out, high_ref, low_ref, in_sems, out_sems, sems = refs[-8:]
+def last_kernel(chunks, de_hbm, pair_hbm, *refs):
+    out_hbm, de, out, deep, in_sems, out_sems, sems = refs[-7:]
+    width = de.shape[0]
     fetches = [
-        pltpu.make_async_copy(high_hbm, high_ref, sems.at[0]),
-        pltpu.make_async_copy(low_hbm, low_ref, sems.at[1]),
+        pltpu.make_async_copy(pair_hbm, deep.at[: 2 * width], sems.at[0]),
+        pltpu.make_async_copy(pair_hbm.at[:width], deep.at[2 * width :], sems.at[1]),
     ]
     for copy in fetches:
         copy.start()
-
-    def prepare():
-        for copy in fetches:
-            copy.wait()
-
-    def product(value):
-        return dot3(split(value), (high_ref[...], low_ref[...]))
-
-    stream(chunks, de_hbm, de, out, out_hbm, in_sems, out_sems, product, prepare)
+    loads = [
+        pltpu.make_async_copy(de_hbm.at[:, here], de.at[:, here], in_sems.at[i])
+        for i, here in enumerate(chunks)
+    ]
+    stores = [
+        pltpu.make_async_copy(out.at[here], out_hbm.at[here], out_sems.at[i])
+        for i, here in enumerate(chunks)
+    ]
+
+    def product(i):
+        if i == 0:
+            for copy in fetches:
+                copy.wait()
+        high, low = split(de[:, chunks[i]])
+        out[chunks[i], :] = dot(jnp.concatenate([high, high, low], axis=0), deep[...], TN)
+
+    stream(loads, stores, product)
+
+
+def chunk_rows(first, last):
+    return [slice(start, start + ROWS) for start in range(first, last, ROWS)]
 
 
 def fixed(*values):
@@ -302,17 +298,17 @@
     pixels = coarse_weight.shape[0]
     half = coarse_input.shape[1]
     count = patches * tokens
-    steps = count // ROWS
     swap = [(0, 1), (1, 0)]
 
     column = [coarse_input]
     for k in range(1, far):
         column.append(lax.ppermute(coarse_input, "far", [(p, (p + k) % far) for p in range(far)]))
+
     chunks = chunk_rows(0, count)
+    pair_shape = (2 * width, values)
 
     def wide(name, value, weight, keep):
-        split_shape = (width, values)
-        out_shape = [pltpu.HBM((count, width), F32)] + [pltpu.HBM(split_shape, BF16)] * (2 * keep)
+        out_shape = [pltpu.HBM((width, count), F32)] + [pltpu.HBM(pair_shape, BF16)] * keep
         return call(
             functools.partial(wide_kernel, chunks),
             name,
@@ -322,17 +318,16 @@
             out_specs=[HBM] * len(out_shape),
             scratch_shapes=[
                 pltpu.VMEM((count, values), F32),
-                pltpu.VMEM((count, width), F32),
-                pltpu.VMEM(split_shape, F32),
-                pltpu.VMEM(split_shape, BF16),
-                pltpu.VMEM(split_shape, BF16),
+                pltpu.VMEM((width, count), F32),
+                pltpu.VMEM((width, values), F32),
+                pltpu.VMEM(pair_shape, BF16),
                 pltpu.SemaphoreType.DMA((len(chunks),)),
                 pltpu.SemaphoreType.DMA((len(chunks),)),
-                pltpu.SemaphoreType.DMA((3,)),
+                pltpu.SemaphoreType.DMA((2,)),
             ],
         )(*fixed(value.reshape(count, values), weight))
 
-    xw, win_hi, win_lo = wide("input", fine_input, in_weight.T, True)
+    xw, pair = wide("input", fine_input, in_weight.T, True)
     column = stack(column, xw)
     own = [column]
     for flip in range(1, 4):
@@ -355,22 +350,21 @@
         functools.partial(middle_kernel, patches, peers),
         "middle",
         6 * count * width * width,
-        (pltpu.HBM((count, width), F32), jax.ShapeDtypeStruct(shape, F32)),
+        (pltpu.HBM((width, count), F32), jax.ShapeDtypeStruct(shape, F32)),
         limit=ROOM,
         in_specs=[SMEM, VMEM, VMEM] + [HBM] * 5,
         out_specs=(HBM, VMEM),
         scratch_shapes=[
-            pltpu.VMEM((count, width), F32),
-            pltpu.VMEM((count, width), F32),
+            pltpu.VMEM((width, count), F32),
+            pltpu.VMEM((width, count), F32),
             pltpu.VMEM((width, width), F32),
             pltpu.VMEM((pixels, width), F32),
             pltpu.VMEM((width, width), F32),
             pltpu.VMEM((patches * 16, pixels), F32),
-            pltpu.VMEM((patches * 64, width), F32),
-            pltpu.VMEM((patches * 64, width), F32),
+            pltpu.VMEM((patches * 16, count), BF16),
             pltpu.SemaphoreType.DMA((3,)),
-            pltpu.SemaphoreType.DMA((2, steps)),
-            pltpu.SemaphoreType.DMA((steps,)),
+            pltpu.SemaphoreType.DMA((2,)),
+            pltpu.SemaphoreType.DMA((len(chunks),)),
         ],
     )(crops.T, own, other, *fixed(xw, tw, gram, coarse_weight, context_weight))
     returned = lax.all_to_all(back, patch, 0, 0, tiled=True)
@@ -382,19 +376,18 @@
             "last",
             6 * (end - first) * values * width,
             pltpu.HBM((count, values), F32),
-            in_specs=[HBM] * (3 + len(extra)),
+            in_specs=[HBM] * (2 + len(extra)),
             out_specs=HBM,
             scratch_shapes=[
-                pltpu.VMEM((count, width), F32),
+                pltpu.VMEM((width, count), F32),
                 pltpu.VMEM((count, values), F32),
-                pltpu.VMEM((width, values), BF16),
-                pltpu.VMEM((width, values), BF16),
+                pltpu.VMEM((3 * width, values), BF16),
                 pltpu.SemaphoreType.DMA((len(mine),)),
                 pltpu.SemaphoreType.DMA((len(mine),)),
                 pltpu.SemaphoreType.DMA((2,)),
             ],
-            input_output_aliases={3: 0} if extra else {},
-        )(*fixed(de, win_hi, win_lo, *extra))
+            input_output_aliases={2: 0} if extra else {},
+        )(*fixed(de, pair, *extra))
 
     early = count - ROWS
     fine_grad = last(0, early)

time: 61.7 us -> 56 us (0.908)
  Pallas kernels: 42 us -> 35.1 us
  waiting for transfers between devices: 2.25 us -> 3.31 us
    pallas_call x2, Pallas kernels: 16.8 us -> 13.3 us  [wide(): call(functools.partial(wide_kernel, chunks), name, 6 * count * values * w...]
    pallas_call x2, Pallas kernels: 12.6 us -> 10.3 us  [last(): call(functools.partial(last_kernel, mine), 'last', 6 * (end - first) * va...]
    pallas_call x1, Pallas kernels: 9.72 us -> 8.66 us  [body(): call(functools.partial(middle_kernel, patches, peers), 'middle', 6 * coun...]
    all_to_all x1, waiting for transfers between devices: 2.23 us -> 3.29 us  [body(): returned = lax.all_to_all(back, patch, 0, 0, tiled=True)]
  transfers between devices with their start and end apart: 9 -> 9, of which waited for: 1 -> 1; matrix products, arithmetic and copies ran while one was open for 0% -> 0% of each run, Pallas kernels for 51% -> 46%
where the time goes in v6:
time: 56 us; the launch traced here: 55.7 us
  Pallas kernels  35.1 us (63%)
  starting transfers between devices  15.8 us (28%)
  waiting for transfers between devices  3.31 us (6%)
  between operations  0.8 us (1%)
  other arithmetic  0.62 us (1%)
    pallas_call x2, Pallas kernels, wide(): call(functools.partial(wide_kernel, chunks), name, 6 * count * values * w...  13.3 us
    pallas_call x2, Pallas kernels, last(): call(functools.partial(last_kernel, mine), 'last', 6 * (end - first) * va...  10.3 us
    pallas_call x1, Pallas kernels, body(): call(functools.partial(middle_kernel, patches, peers), 'middle', 6 * coun...  8.66 us
    ppermute x3, starting transfers between devices, body(): lax.ppermute(coarse_input, 'far', [(p, (p + k) % far) for p in range(far)])  7.01 us
    all_to_all x1, starting transfers between devices, body(): returned = lax.all_to_all(back, patch, 0, 0, tiled=True)  3.72 us
    ppermute x3, starting transfers between devices, body(): lax.ppermute(column, ('lvl', 'y'), [(p, p ^ flip) for p in range(4)])  3.55 us
    all_to_all x1, waiting for transfers between devices, body(): returned = lax.all_to_all(back, patch, 0, 0, tiled=True)  3.29 us
    pallas_call x1, Pallas kernels, body(): call(gram_kernel, 'gram', 8 * values * width * width, pltpu.HBM((width, w...  1.98 us
  transfers between devices with their start and end apart: 9, of which 1 were waited for; matrix products, arithmetic and copies ran while one was open for 0% of the time, Pallas kernels for 46%

profile of v6, /device:TPU:0, one launch (start us, length us, event | category | flops | bytes accessed | tf_op | source)
XLA Modules:
  0.0 55.7 jit_solution(17310028292792441173)
XLA Ops:
  0.6 0.0 copy-start
  0.6 3.1 %collective-permute-start = (f32[1,32,192]{2,1,0:T(8,128)}, f32[1,32,192]{2,1,0:T(8,128)S(1)}, u32[]{:S(2)}, u32[]{:S(2)}) collective-permute-start(f32[1,32,192]{2,1,0:T(8,128)} %refs_0_.1), channel_id=1, source_target_pairs={{0,4},{4,8},{8,12},{12,0},{1,5},{5,9},{9,13},{13,1},{2,6},{6,10},{... | collective-permute-start | bytes 73736 | tf_op jit(solution)/shard_map/ppermute | solution.py:305
  3.7 2.6 %collective-permute-start.1 = (f32[1,32,192]{2,1,0:T(8,128)}, f32[1,32,192]{2,1,0:T(8,128)S(1)}, u32[]{:S(2)}, u32[]{:S(2)}) collective-permute-start(f32[1,32,192]{2,1,0:T(8,128)} %refs_0_.1), channel_id=1, source_target_pairs={{0,8},{4,12},{8,0},{12,4},{1,9},{5,13},{9,1},{13,5},{2,10},{6,14},... | collective-permute-start | bytes 73736 | tf_op jit(solution)/shard_map/ppermute | solution.py:305
  6.3 1.3 %collective-permute-start.2 = (f32[1,32,192]{2,1,0:T(8,128)}, f32[1,32,192]{2,1,0:T(8,128)S(1)}, u32[]{:S(2)}, u32[]{:S(2)}) collective-permute-start(f32[1,32,192]{2,1,0:T(8,128)} %refs_0_.1), channel_id=1, source_target_pairs={{0,12},{4,0},{8,4},{12,8},{1,13},{5,1},{9,5},{13,9},{2,14},{6,2},{... | collective-permute-start | bytes 73736 | tf_op jit(solution)/shard_map/ppermute | solution.py:305
  7.7 6.5 %input.1 = (f32[320,2048]{1,0:T(8,128)}, bf16[640,768]{1,0:T(8,128)(2,1)}) custom-call(f32[2048,768]{1,0:T(8,128)} %bitcast.14, f32[320,768]{1,0:T(8,128)} %bitcast.16), custom_call_target="tpu_custom_call" | custom-call | flops 3019898880 | bytes 9175040 | tf_op jit(solution)/shard_map/input/pallas_call | solution.py:312
  14.1 0.0 collective-permute-done.refs_1_
  14.1 0.0 collective-permute-done.1.refs_2_
  14.2 0.0 collective-permute-done.2.refs_3_
  14.2 0.0 copy-done
  14.2 1.6 %collective-permute-start.3 = (f32[4,32,192]{2,1,0:T(8,128)S(1)}, f32[4,32,192]{2,1,0:T(8,128)S(1)}, u32[]{:S(2)}, u32[]{:S(2)}) collective-permute-start(f32[4,32,192]{2,1,0:T(8,128)S(1)} %stack.2.refs_0_), channel_id=1, source_target_pairs={{0,2},{2,0},{16,18},{18,16},{1,3},{3,1},{17,19},{19,17},{4,6},{6,4... | collective-permute-start | bytes 294920 | tf_op jit(solution)/shard_map/ppermute | solution.py:334
  15.8 1.5 %collective-permute-start.4 = (f32[4,32,192]{2,1,0:T(8,128)S(1)}, f32[4,32,192]{2,1,0:T(8,128)S(1)}, u32[]{:S(2)}, u32[]{:S(2)}) collective-permute-start(f32[4,32,192]{2,1,0:T(8,128)S(1)} %stack.2.refs_0_), channel_id=1, source_target_pairs={{0,16},{2,18},{16,0},{18,2},{1,17},{3,19},{17,1},{19,3},{4,20},{6,... | collective-permute-start | bytes 294920 | tf_op jit(solution)/shard_map/ppermute | solution.py:334
  17.3 0.5 collective-permute-start.5
  17.7 0.0 copy-start.2
  17.7 0.0 copy-start.1
  17.8 6.8 %target.1.refs_4_.tw_hbm = f32[320,2048]{1,0:T(8,128)} custom-call(f32[2048,768]{1,0:T(8,128)} %bitcast.15, f32[320,768]{1,0:T(8,128)} %weight_ref.1), custom_call_target="tpu_custom_call" | custom-call | flops 3019898880 | bytes 5242880 | tf_op jit(solution)/shard_map/target/pallas_call | solution.py:312
  24.6 0.0 collective-permute-done.3.refs_1_
  24.6 0.0 collective-permute-done.4.refs_2_
  24.6 0.0 collective-permute-done.5.refs_3_
  24.6 0.1 collective-permute-start.6
  24.7 0.0 copy-done.2
  24.7 2.0 %gram.1.gram_hbm = f32[320,320]{1,0:T(8,128)} custom-call(f32[320,768]{1,0:T(8,128)S(1)} %copy-done.2, f32[512,192]{1,0:T(8,128)S(1)} %bitcast.9), custom_call_target="tpu_custom_call" | custom-call | flops 629145600 | bytes 819200 | tf_op jit(solution)/shard_map/gram/pallas_call | solution.py:338
  26.7 0.0 collective-permute-done.6.other_ref
  26.7 0.0 copy-done.1
  26.7 8.7 %middle.1 = (f32[320,2048]{1,0:T(8,128)}, f32[256,256]{1,0:T(8,128)}) custom-call(s32[4,8]{1,0:T(4,128)S(1)} %bitcast.12, f32[512,192]{1,0:T(8,128)S(1)} %bitcast.10, f32[512,192]{1,0:T(8,128)S(1)} %collective-permute-done.6.other_ref, f32[320,2048]{1,0:T(8,128)} %get-tuple-element.8.refs_4_.xw_hbm, f32[320,2048]{1,0:T(8,128)} %target.1.refs_4_.tw_hbm, ...), custom_call_target="tpu_custom_call" | custom-call | flops 1258291200 | bytes 5767168 | tf_op jit(solution)/shard_map/middle/pallas_call | solution.py:349
  35.4 3.7 %all-to-all-start = ((f32[16,16,256]{2,1,0:T(8,128)}), f32[16,16,256]{2,1,0:T(8,128)S(1)}, u32[]{:S(2)}, u32[]{:S(2)}) async-start(f32[16,16,256]{2,1,0:T(8,128)} %bitcast.5), calls=%async_computation | async-start | bytes 524288 | tf_op jit(solution)/shard_map/all_to_all | solution.py:370
  39.1 6.5 %last.2.done_ref.refs_0_ = f32[2048,768]{1,0:T(8,128)} custom-call(f32[320,2048]{1,0:T(8,128)} %get-tuple-element.10.de_hbm, bf16[640,768]{1,0:T(8,128)(2,1)} %get-tuple-element.11.pair_hbm), custom_call_target="tpu_custom_call" | custom-call | flops 2264924160 | bytes 12582912 | tf_op jit(solution)/shard_map/last/pallas_call | solution.py:374
  45.7 3.3 %all-to-all-done = f32[16,16,256]{2,1,0:T(8,128)S(1)} async-done(((f32[16,16,256]{2,1,0:T(8,128)}), f32[16,16,256]{2,1,0:T(8,128)S(1)}, u32[]{:S(2)}, u32[]{:S(2)}) %all-to-all-start) | async-done | bytes 262176 | tf_op jit(solution)/shard_map/all_to_all | solution.py:370
  48.9 0.9 %scatter.1 = (f32[1,32,192]{2,1,0:T(8,128)}, f32[1,32,192]{2,1,0:T(8,128)S(1)}) custom-call(f32[256,256]{1,0:T(8,128)S(1)} %bitcast.11, f32[2048,768]{1,0:T(8,128)} %last.2.done_ref.refs_0_), custom_call_target="tpu_custom_call" | custom-call | flops 10000 | bytes 98304 | tf_op jit(solution)/shard_map/scatter/pallas_call | solution.py:395
  49.8 1.5 %collective-permute-start.7 = (f32[1,32,192]{2,1,0:T(8,128)S(1)}, f32[1,32,192]{2,1,0:T(8,128)S(1)}, u32[]{:S(2)}, u32[]{:S(2)}) collective-permute-start(f32[1,32,192]{2,1,0:T(8,128)S(1)} %get-tuple-element.13), channel_id=1, source_target_pairs={{0,16},{16,0},{1,17},{17,1},{2,18},{18,2},{3,19},{19,3},{4,20},{20... | collective-permute-start | bytes 73736 | tf_op jit(solution)/shard_map/ppermute | solution.py:406
  51.3 0.0 copy-start.3
  51.3 3.8 %last.3 = f32[2048,768]{1,0:T(8,128)} custom-call(f32[320,2048]{1,0:T(8,128)} %get-tuple-element.10.de_hbm, bf16[640,768]{1,0:T(8,128)(2,1)} %get-tuple-element.11.pair_hbm, f32[2048,768]{1,0:T(8,128)} %last.2.done_ref.refs_0_, f32[1,32,192]{2,1,0:T(8,128)} %get-tuple-element.12.refs_1_), custom_call_target="tpu_custom_call", output_to_operand_aliasing={{}: (2, {})} | custom-call | flops 754974720 | bytes 12582912 | tf_op jit(solution)/shard_map/last/pallas_call | solution.py:374
  55.1 0.0 collective-permute-done.7
  55.1 0.0 copy-done.3
  55.1 0.6 %add.3 = f32[1,32,192]{2,1,0:T(8,128)} add(f32[1,32,192]{2,1,0:T(8,128)S(1)} %copy-done.3, f32[1,32,192]{2,1,0:T(8,128)S(1)} %collective-permute-done.7) | non-fusion elementwise | flops 6144 | bytes 73728 | tf_op jit(solution)/shard_map/add | solution.py:406
  (2 shorter events, 0.0 us)
Async XLA Ops:
  0.6 13.5 %copy-start = (f32[1,32,192]{2,1,0:T(8,128)S(1)}, f32[1,32,192]{2,1,0:T(8,128)}, u32[]{:S(2)}) copy-start(f32[1,32,192]{2,1,0:T(8,128)} %refs_0_.1) | copy-start | bytes 73732
  0.6 13.5 %collective-permute-start = (f32[1,32,192]{2,1,0:T(8,128)}, f32[1,32,192]{2,1,0:T(8,128)S(1)}, u32[]{:S(2)}, u32[]{:S(2)}) collective-permute-start(f32[1,32,192]{2,1,0:T(8,128)} %refs_0_.1), channel_id=1, source_target_pairs={{0,4},{4,8},{8,12},{12,0},{1,5},{5,9},{9,13},{13,1},{2,6},{6,10},{... | collective-permute-start | bytes 73736 | tf_op jit(solution)/shard_map/ppermute | solution.py:305
  3.7 10.4 %collective-permute-start.1 = (f32[1,32,192]{2,1,0:T(8,128)}, f32[1,32,192]{2,1,0:T(8,128)S(1)}, u32[]{:S(2)}, u32[]{:S(2)}) collective-permute-start(f32[1,32,192]{2,1,0:T(8,128)} %refs_0_.1), channel_id=1, source_target_pairs={{0,8},{4,12},{8,0},{12,4},{1,9},{5,13},{9,1},{13,5},{2,10},{6,14},... | collective-permute-start | bytes 73736 | tf_op jit(solution)/shard_map/ppermute | solution.py:305
  6.3 7.8 %collective-permute-start.2 = (f32[1,32,192]{2,1,0:T(8,128)}, f32[1,32,192]{2,1,0:T(8,128)S(1)}, u32[]{:S(2)}, u32[]{:S(2)}) collective-permute-start(f32[1,32,192]{2,1,0:T(8,128)} %refs_0_.1), channel_id=1, source_target_pairs={{0,12},{4,0},{8,4},{12,8},{1,13},{5,1},{9,5},{13,9},{2,14},{6,2},{... | collective-permute-start | bytes 73736 | tf_op jit(solution)/shard_map/ppermute | solution.py:305
  14.2 10.4 %collective-permute-start.3 = (f32[4,32,192]{2,1,0:T(8,128)S(1)}, f32[4,32,192]{2,1,0:T(8,128)S(1)}, u32[]{:S(2)}, u32[]{:S(2)}) collective-permute-start(f32[4,32,192]{2,1,0:T(8,128)S(1)} %stack.2.refs_0_), channel_id=1, source_target_pairs={{0,2},{2,0},{16,18},{18,16},{1,3},{3,1},{17,19},{19,17},{4,6},{6,4... | collective-permute-start | bytes 294920 | tf_op jit(solution)/shard_map/ppermute | solution.py:334
  15.8 8.8 %collective-permute-start.4 = (f32[4,32,192]{2,1,0:T(8,128)S(1)}, f32[4,32,192]{2,1,0:T(8,128)S(1)}, u32[]{:S(2)}, u32[]{:S(2)}) collective-permute-start(f32[4,32,192]{2,1,0:T(8,128)S(1)} %stack.2.refs_0_), channel_id=1, source_target_pairs={{0,16},{2,18},{16,0},{18,2},{1,17},{3,19},{17,1},{19,3},{4,20},{6,... | collective-permute-start | bytes 294920 | tf_op jit(solution)/shard_map/ppermute | solution.py:334
  17.3 7.3 %collective-permute-start.5 = (f32[4,32,192]{2,1,0:T(8,128)S(1)}, f32[4,32,192]{2,1,0:T(8,128)S(1)}, u32[]{:S(2)}, u32[]{:S(2)}) collective-permute-start(f32[4,32,192]{2,1,0:T(8,128)S(1)} %stack.2.refs_0_), channel_id=1, source_target_pairs={{0,18},{2,16},{16,2},{18,0},{1,19},{3,17},{17,3},{19,1},{4,22},{6,... | collective-permute-start | bytes 294920 | tf_op jit(solution)/shard_map/ppermute | solution.py:334
  17.7 7.0 %copy-start.2 = (f32[320,768]{1,0:T(8,128)S(1)}, f32[320,768]{1,0:T(8,128)}, u32[]{:S(2)}) copy-start(f32[320,768]{1,0:T(8,128)} %weight_ref.1) | copy-start | bytes 2949124
  17.7 9.0 %copy-start.1 = (s32[8,4]{0,1:T(4,128)S(1)}, s32[8,4]{0,1:T(4,128)}, u32[]{:S(2)}) copy-start(s32[8,4]{0,1:T(4,128)} %param.12) | copy-start | bytes 388
  24.6 2.1 %collective-permute-start.6 = (f32[512,192]{1,0:T(8,128)S(1)}, f32[512,192]{1,0:T(8,128)S(1)}, u32[]{:S(2)}, u32[]{:S(2)}) collective-permute-start(f32[512,192]{1,0:T(8,128)S(1)} %bitcast.8), channel_id=1, source_target_pairs={{0,1},{1,0},{2,3},{3,2},{4,5},{5,4},{6,7},{7,6},{8,9},{9,8},{10,11... | collective-permute-start | bytes 1179656 | tf_op jit(solution)/shard_map/ppermute | solution.py:337
  35.4 13.6 %all-to-all-start = ((f32[16,16,256]{2,1,0:T(8,128)}), f32[16,16,256]{2,1,0:T(8,128)S(1)}, u32[]{:S(2)}, u32[]{:S(2)}) async-start(f32[16,16,256]{2,1,0:T(8,128)} %bitcast.5), calls=%async_computation | async-start | bytes 524288 | tf_op jit(solution)/shard_map/all_to_all | solution.py:370
  49.8 5.2 %collective-permute-start.7 = (f32[1,32,192]{2,1,0:T(8,128)S(1)}, f32[1,32,192]{2,1,0:T(8,128)S(1)}, u32[]{:S(2)}, u32[]{:S(2)}) collective-permute-start(f32[1,32,192]{2,1,0:T(8,128)S(1)} %get-tuple-element.13), channel_id=1, source_target_pairs={{0,16},{16,0},{1,17},{17,1},{2,18},{18,2},{3,19},{19,3},{4,20},{20... | collective-permute-start | bytes 73736 | tf_op jit(solution)/shard_map/ppermute | solution.py:406
  51.3 3.8 %copy-start.3 = (f32[1,32,192]{2,1,0:T(8,128)S(1)}, f32[1,32,192]{2,1,0:T(8,128)}, u32[]{:S(2)}) copy-start(f32[1,32,192]{2,1,0:T(8,128)} %get-tuple-element.12.refs_1_) | copy-start | bytes 73732

commit v7 on v6

--- a/solution.py
+++ b/solution.py
@@ -40,6 +40,16 @@
     )
 
 
+def stacked(value):
+    high, low = split(value)
+    return jnp.concatenate([high, high, low], axis=0)
+
+
+def side_by_side(value):
+    high, low = split(value)
+    return jnp.concatenate([high, low, high], axis=1)
+
+
 def sigmoid(value):
     return 0.5 * jnp.tanh(0.5 * value) + 0.5
 
@@ -56,21 +66,26 @@
     )
 
 
-def stream(loads, stores, product):
+def stream(loads, stores, prepare, product):
     for copy in loads[:AHEAD]:
         copy.start()
-    for i, (load, store) in enumerate(zip(loads, stores)):
-        load.wait()
+    loads[0].wait()
+    prepare(0)
+    for i, store in enumerate(stores):
         if i + AHEAD < len(loads):
             loads[i + AHEAD].start()
+        if i + 1 < len(loads):
+            loads[i + 1].wait()
         product(i)
+        if i + 1 < len(loads):
+            prepare(i + 1)
         store.start()
     for copy in stores:
         copy.wait()
 
 
 def wide_kernel(chunks, x_hbm, weight_hbm, *refs):
-    out_hbm, *split_hbm, x, out, weight, pair, in_sems, out_sems, sems = refs
+    out_hbm, *split_hbm, x, out, weight, pair, high, low, in_sems, out_sems, sems = refs
     width = weight.shape[0]
     fetch = pltpu.make_async_copy(weight_hbm, weight, sems.at[0])
     fetch.start()
@@ -83,17 +98,19 @@
     ]
     keep = [pltpu.make_async_copy(pair, hbm, sems.at[1]) for hbm in split_hbm]
 
-    def product(i):
+    def prepare(i):
+        high[i % 2], low[i % 2] = split(x[chunks[i], :])
         if i == 0:
             fetch.wait()
             pair[:width], pair[width:] = split(weight[...])
             for copy in keep:
                 copy.start()
-        high, low = split(x[chunks[i], :])
-        both = dot(pair[...], high, NT)
-        out[:, chunks[i]] = both[:width] + (both[width:] + dot(pair[:width], low, NT))
-
-    stream(loads, stores, product)
+
+    def product(i):
+        both = dot(pair[...], high[i % 2], NT)
+        out[:, chunks[i]] = both[:width] + (both[width:] + dot(pair[:width], low[i % 2], NT))
+
+    stream(loads, stores, prepare, product)
     for copy in keep:
         copy.wait()
 
@@ -191,27 +208,33 @@
     high, low = split(dot3(split(pre * gate), project).T)
     projected = jnp.concatenate([high, low], axis=1)
     small[2].wait()
-    high, low = split(gram[...])
-    grams = jnp.concatenate([high, low, high], axis=1)
+    grams, projects, coarses = side_by_side(gram[...]), side_by_side(xwgt[...]), side_by_side(cwgt[...])
+    slope = slope.T
     for copy in large:
         copy.wait()
 
-    dslot = jnp.zeros((2 * width, slots), F32)
-    for i, here in enumerate(chunks):
-        taken = pick[:, here]
-        pre = xw[:, here] + dot(projected, jnp.concatenate([taken, taken], axis=0))
+    def first(i):
+        taken = pick[:, chunks[i]]
+        pre = xw[:, chunks[i]] + dot(projected, jnp.concatenate([taken, taken], axis=0))
         gate = sigmoid(pre)
         hidden = pre * gate
-        high, low = split(hidden)
-        dhidden = dot(grams, jnp.concatenate([high, high, low], axis=0)) - tw[:, here]
-        de = dhidden * (gate + hidden * (1.0 - gate))
+        return gate + hidden * (1.0 - gate), stacked(hidden)
+
+    dslot = jnp.zeros((2 * width, slots), F32)
+    ready = first(0)
+    for i, here in enumerate(chunks):
+        factor, stack = ready
+        product = dot(grams, stack)
+        if i + 1 < len(chunks):
+            ready = first(i + 1)
+        de = (product - tw[:, here]) * factor
         xw[:, here] = de
-        stores[i].start()
-        dslot = dslot + dot(jnp.concatenate(split(de), axis=0), taken, NT)
-
-    dslot = (dslot[:width] + dslot[width:]).T
-    dcontext = dot3(split(dslot), project, NT)
-    grad = dot3(split(dcontext * slope), coarse, NT)
+        dslot = dslot + dot(jnp.concatenate(split(de), axis=0), pick[:, here], NT)
+    for copy in stores:
+        copy.start()
+
+    dcontext = dot(projects, stacked(dslot[:width] + dslot[width:]))
+    grad = dot(coarses, stacked(dcontext * slope)).T
     shape = (patches * 16, LANES - pixels)
     slot = lax.broadcasted_iota(jnp.int32, shape, 0) % 16
     top = row_value(crops_ref, 1, patches, shape, 0, 16)
@@ -241,7 +264,7 @@
 
 
 def last_kernel(chunks, de_hbm, pair_hbm, *refs):
-    out_hbm, de, out, deep, in_sems, out_sems, sems = refs[-7:]
+    out_hbm, de, out, deep, cat, in_sems, out_sems, sems = refs
     width = de.shape[0]
     fetches = [
         pltpu.make_async_copy(pair_hbm, deep.at[: 2 * width], sems.at[0]),
@@ -258,14 +281,17 @@
         for i, here in enumerate(chunks)
     ]
 
-    def product(i):
+    def prepare(i):
+        high, low = split(de[:, chunks[i]])
+        cat[i % 2, :width], cat[i % 2, width : 2 * width], cat[i % 2, 2 * width :] = high, high, low
         if i == 0:
             for copy in fetches:
                 copy.wait()
-        high, low = split(de[:, chunks[i]])
-        out[chunks[i], :] = dot(jnp.concatenate([high, high, low], axis=0), deep[...], TN)
-
-    stream(loads, stores, product)
+
+    def product(i):
+        out[chunks[i], :] = dot(cat[i % 2], deep[...], TN)
+
+    stream(loads, stores, prepare, product)
 
 
 def chunk_rows(first, last):
@@ -321,6 +347,8 @@
                 pltpu.VMEM((width, count), F32),
                 pltpu.VMEM((width, values), F32),
                 pltpu.VMEM(pair_shape, BF16),
+                pltpu.VMEM((2, ROWS, values), BF16),
+                pltpu.VMEM((2, ROWS, values), BF16),
                 pltpu.SemaphoreType.DMA((len(chunks),)),
                 pltpu.SemaphoreType.DMA((len(chunks),)),
                 pltpu.SemaphoreType.DMA((2,)),
@@ -369,28 +397,23 @@
     )(crops.T, own, other, *fixed(xw, tw, gram, coarse_weight, context_weight))
     returned = lax.all_to_all(back, patch, 0, 0, tiled=True)
 
-    def last(first, end, *extra):
-        mine = chunk_rows(first, end)
-        return call(
-            functools.partial(last_kernel, mine),
-            "last",
-            6 * (end - first) * values * width,
-            pltpu.HBM((count, values), F32),
-            in_specs=[HBM] * (2 + len(extra)),
-            out_specs=HBM,
-            scratch_shapes=[
-                pltpu.VMEM((width, count), F32),
-                pltpu.VMEM((count, values), F32),
-                pltpu.VMEM((3 * width, values), BF16),
-                pltpu.SemaphoreType.DMA((len(mine),)),
-                pltpu.SemaphoreType.DMA((len(mine),)),
-                pltpu.SemaphoreType.DMA((2,)),
-            ],
-            input_output_aliases={2: 0} if extra else {},
-        )(*fixed(de, pair, *extra))
-
-    early = count - ROWS
-    fine_grad = last(0, early)
+    fine_grad = call(
+        functools.partial(last_kernel, chunks),
+        "last",
+        6 * count * values * width,
+        pltpu.HBM((count, values), F32),
+        in_specs=[HBM, HBM],
+        out_specs=HBM,
+        scratch_shapes=[
+            pltpu.VMEM((width, count), F32),
+            pltpu.VMEM((count, values), F32),
+            pltpu.VMEM((3 * width, values), BF16),
+            pltpu.VMEM((2, 3 * width, ROWS), BF16),
+            pltpu.SemaphoreType.DMA((len(chunks),)),
+            pltpu.SemaphoreType.DMA((len(chunks),)),
+            pltpu.SemaphoreType.DMA((2,)),
+        ],
+    )(*fixed(de, pair))
     part = (1, half, pixels)
     mine, theirs = call(
         scatter_kernel,
@@ -402,7 +425,6 @@
         out_specs=(VMEM, VMEM),
         scratch_shapes=[pltpu.VMEM((SIDE * SIDE, pixels), F32)],
     )(returned, *fixed(fine_grad))
-    fine_grad = last(early, count, fine_grad, mine)
     coarse_grad = mine + lax.ppermute(theirs, "lvl", swap)
     return (coarse_grad, fine_grad.reshape(fine_input.shape))
 

time: 56 us -> 58.7 us (1.048)
  waiting for transfers between devices: 3.31 us -> 4.98 us
  starting transfers between devices: 15.8 us -> 16.7 us
  other arithmetic: 0.62 us -> 1.38 us
  Pallas kernels: 35.1 us -> 34.4 us
    pallas_call x2 -> x1, Pallas kernels: 10.3 us -> 7.48 us  [body(): call(functools.partial(last_kernel, chunks), 'last', 6 * count * values *...]
    ppermute x1, waiting for transfers between devices: 0.01 us -> 2.45 us  [body(): coarse_grad = mine + lax.ppermute(theirs, 'lvl', swap)]
    pallas_call x2, Pallas kernels: 13.3 us -> 15.2 us  [wide(): call(functools.partial(wide_kernel, chunks), name, 6 * count * values * w...]
    ppermute x3, starting transfers between devices: 7.01 us -> 7.93 us  [body(): lax.ppermute(coarse_input, 'far', [(p, (p + k) % far) for p in range(far)])]
    all_to_all x1, waiting for transfers between devices: 3.29 us -> 2.51 us  [body(): returned = lax.all_to_all(back, patch, 0, 0, tiled=True)]
    add x1, other arithmetic: 0.62 us -> 1.38 us  [body(): coarse_grad = mine + lax.ppermute(theirs, 'lvl', swap)]
  transfers between devices with their start and end apart: 9 -> 9, of which waited for: 1 -> 2; matrix products, arithmetic and copies ran while one was open for 0% -> 0% of each run, Pallas kernels for 46% -> 42%
where the time goes in v7:
time: 58.7 us; the launch traced here: 58.3 us
  Pallas kernels  34.4 us (59%)
  starting transfers between devices  16.7 us (28%)
  waiting for transfers between devices  4.98 us (8%)
  other arithmetic  1.38 us (2%)
  between operations  0.77 us (1%)
    pallas_call x2, Pallas kernels, wide(): call(functools.partial(wide_kernel, chunks), name, 6 * count * values * w...  15.2 us
    pallas_call x1, Pallas kernels, body(): call(functools.partial(middle_kernel, patches, peers), 'middle', 6 * coun...  8.73 us
    ppermute x3, starting transfers between devices, body(): lax.ppermute(coarse_input, 'far', [(p, (p + k) % far) for p in range(far)])  7.93 us
    pallas_call x1, Pallas kernels, body(): call(functools.partial(last_kernel, chunks), 'last', 6 * count * values *...  7.48 us
    all_to_all x1, starting transfers between devices, body(): returned = lax.all_to_all(back, patch, 0, 0, tiled=True)  3.72 us
    ppermute x3, starting transfers between devices, body(): lax.ppermute(column, ('lvl', 'y'), [(p, p ^ flip) for p in range(4)])  3.55 us
    all_to_all x1, waiting for transfers between devices, body(): returned = lax.all_to_all(back, patch, 0, 0, tiled=True)  2.51 us
    ppermute x1, waiting for transfers between devices, body(): coarse_grad = mine + lax.ppermute(theirs, 'lvl', swap)  2.45 us
  transfers between devices with their start and end apart: 9, of which 2 were waited for; matrix products, arithmetic and copies ran while one was open for 0% of the time, Pallas kernels for 42%

profile of v7, /device:TPU:0, one launch (start us, length us, event | category | flops | bytes accessed | tf_op | source)
XLA Modules:
  0.0 58.3 jit_solution(10036785525265935164)
XLA Ops:
  0.6 0.0 copy-start
  0.6 4.1 %collective-permute-start.1 = (f32[1,32,192]{2,1,0:T(8,128)}, f32[1,32,192]{2,1,0:T(8,128)S(1)}, u32[]{:S(2)}, u32[]{:S(2)}) collective-permute-start(f32[1,32,192]{2,1,0:T(8,128)} %refs_0_.1), channel_id=1, source_target_pairs={{0,8},{4,12},{8,0},{12,4},{1,9},{5,13},{9,1},{13,5},{2,10},{6,14},... | collective-permute-start | bytes 73736 | tf_op jit(solution)/shard_map/ppermute | solution.py:331
  4.7 1.6 %collective-permute-start = (f32[1,32,192]{2,1,0:T(8,128)}, f32[1,32,192]{2,1,0:T(8,128)S(1)}, u32[]{:S(2)}, u32[]{:S(2)}) collective-permute-start(f32[1,32,192]{2,1,0:T(8,128)} %refs_0_.1), channel_id=1, source_target_pairs={{0,4},{4,8},{8,12},{12,0},{1,5},{5,9},{9,13},{13,1},{2,6},{6,10},{... | collective-permute-start | bytes 73736 | tf_op jit(solution)/shard_map/ppermute | solution.py:331
  6.3 2.2 %collective-permute-start.2 = (f32[1,32,192]{2,1,0:T(8,128)}, f32[1,32,192]{2,1,0:T(8,128)S(1)}, u32[]{:S(2)}, u32[]{:S(2)}) collective-permute-start(f32[1,32,192]{2,1,0:T(8,128)} %refs_0_.1), channel_id=1, source_target_pairs={{0,12},{4,0},{8,4},{12,8},{1,13},{5,1},{9,5},{13,9},{2,14},{6,2},{... | collective-permute-start | bytes 73736 | tf_op jit(solution)/shard_map/ppermute | solution.py:331
  8.6 7.6 %input.1 = (f32[320,2048]{1,0:T(8,128)}, bf16[640,768]{1,0:T(8,128)(2,1)}) custom-call(f32[2048,768]{1,0:T(8,128)} %bitcast.14, f32[320,768]{1,0:T(8,128)} %bitcast.16), custom_call_target="tpu_custom_call" | custom-call | flops 3019898880 | bytes 9175040 | tf_op jit(solution)/shard_map/input/pallas_call | solution.py:338
  16.2 0.0 collective-permute-done.1.refs_2_
  16.2 0.0 collective-permute-done.refs_1_
  16.2 0.0 collective-permute-done.2.refs_3_
  16.2 0.0 copy-done
  16.2 2.5 %collective-permute-start.5 = (f32[4,32,192]{2,1,0:T(8,128)S(1)}, f32[4,32,192]{2,1,0:T(8,128)S(1)}, u32[]{:S(2)}, u32[]{:S(2)}) collective-permute-start(f32[4,32,192]{2,1,0:T(8,128)S(1)} %stack.2.refs_0_), channel_id=1, source_target_pairs={{0,18},{2,16},{16,2},{18,0},{1,19},{3,17},{17,3},{19,1},{4,22},{6,... | collective-permute-start | bytes 294920 | tf_op jit(solution)/shard_map/ppermute | solution.py:362
  18.7 0.5 collective-permute-start.4
  19.3 0.5 collective-permute-start.3
  19.8 0.0 copy-start.2
  19.8 0.0 copy-start.1
  19.8 7.7 %target.1.refs_4_.tw_hbm = f32[320,2048]{1,0:T(8,128)} custom-call(f32[2048,768]{1,0:T(8,128)} %bitcast.15, f32[320,768]{1,0:T(8,128)} %weight_ref.1), custom_call_target="tpu_custom_call" | custom-call | flops 3019898880 | bytes 5242880 | tf_op jit(solution)/shard_map/target/pallas_call | solution.py:338
  27.4 0.0 collective-permute-done.5.refs_3_
  27.5 0.0 collective-permute-done.4.refs_2_
  27.5 0.0 collective-permute-done.3.refs_1_
  27.5 0.1 collective-permute-start.6
  27.6 0.0 copy-done.2
  27.6 2.0 %gram.1.gram_hbm = f32[320,320]{1,0:T(8,128)} custom-call(f32[320,768]{1,0:T(8,128)S(1)} %copy-done.2, f32[512,192]{1,0:T(8,128)S(1)} %bitcast.9), custom_call_target="tpu_custom_call" | custom-call | flops 629145600 | bytes 819200 | tf_op jit(solution)/shard_map/gram/pallas_call | solution.py:366
  29.6 0.0 collective-permute-done.6.other_ref
  29.6 0.0 copy-done.1
  29.6 8.7 %middle.1 = (f32[320,2048]{1,0:T(8,128)}, f32[256,256]{1,0:T(8,128)}) custom-call(s32[4,8]{1,0:T(4,128)S(1)} %bitcast.12, f32[512,192]{1,0:T(8,128)S(1)} %bitcast.10, f32[512,192]{1,0:T(8,128)S(1)} %collective-permute-done.6.other_ref, f32[320,2048]{1,0:T(8,128)} %get-tuple-element.8.refs_4_.xw_hbm, f32[320,2048]{1,0:T(8,128)} %target.1.refs_4_.tw_hbm, ...), custom_call_target="tpu_custom_call" | custom-call | flops 1258291200 | bytes 5767168 | tf_op jit(solution)/shard_map/middle/pallas_call | solution.py:377
  38.4 3.7 %all-to-all-start = ((f32[16,16,256]{2,1,0:T(8,128)}), f32[16,16,256]{2,1,0:T(8,128)S(1)}, u32[]{:S(2)}, u32[]{:S(2)}) async-start(f32[16,16,256]{2,1,0:T(8,128)} %bitcast.5), calls=%async_computation | async-start | bytes 524288 | tf_op jit(solution)/shard_map/all_to_all | solution.py:398
  42.1 7.5 %last.1.done_ref = f32[2048,768]{1,0:T(8,128)} custom-call(f32[320,2048]{1,0:T(8,128)} %get-tuple-element.10.de_hbm, bf16[640,768]{1,0:T(8,128)(2,1)} %get-tuple-element.11.pair_hbm), custom_call_target="tpu_custom_call" | custom-call | flops 3019898880 | bytes 12582912 | tf_op jit(solution)/shard_map/last/pallas_call | solution.py:400
  49.6 2.5 %all-to-all-done = f32[16,16,256]{2,1,0:T(8,128)S(1)} async-done(((f32[16,16,256]{2,1,0:T(8,128)}), f32[16,16,256]{2,1,0:T(8,128)S(1)}, u32[]{:S(2)}, u32[]{:S(2)}) %all-to-all-start) | async-done | bytes 262176 | tf_op jit(solution)/shard_map/all_to_all | solution.py:398
  52.1 0.9 %scatter.1 = (f32[1,32,192]{2,1,0:T(8,128)}, f32[1,32,192]{2,1,0:T(8,128)S(1)}) custom-call(f32[256,256]{1,0:T(8,128)S(1)} %bitcast.11, f32[2048,768]{1,0:T(8,128)} %last.1.done_ref), custom_call_target="tpu_custom_call" | custom-call | flops 10000 | bytes 98304 | tf_op jit(solution)/shard_map/scatter/pallas_call | solution.py:418
  53.0 1.5 %collective-permute-start.7 = (f32[1,32,192]{2,1,0:T(8,128)S(1)}, f32[1,32,192]{2,1,0:T(8,128)S(1)}, u32[]{:S(2)}, u32[]{:S(2)}) collective-permute-start(f32[1,32,192]{2,1,0:T(8,128)S(1)} %get-tuple-element.13), channel_id=1, source_target_pairs={{0,16},{16,0},{1,17},{17,1},{2,18},{18,2},{3,19},{19,3},{4,20},{20... | collective-permute-start | bytes 73736 | tf_op jit(solution)/shard_map/ppermute | solution.py:428
  54.5 2.4 %collective-permute-done.7 = f32[1,32,192]{2,1,0:T(8,128)S(1)} collective-permute-done((f32[1,32,192]{2,1,0:T(8,128)S(1)}, f32[1,32,192]{2,1,0:T(8,128)S(1)}, u32[]{:S(2)}, u32[]{:S(2)}) %collective-permute-start.7) | collective-permute-done | bytes 24608 | tf_op jit(solution)/shard_map/ppermute | solution.py:428
  56.9 1.4 %add.3 = f32[1,32,192]{2,1,0:T(8,128)} add(f32[1,32,192]{2,1,0:T(8,128)} %get-tuple-element.12, f32[1,32,192]{2,1,0:T(8,128)S(1)} %collective-permute-done.7) | non-fusion elementwise | flops 6144 | bytes 73728 | tf_op jit(solution)/shard_map/add | solution.py:428
  (2 shorter events, 0.0 us)
Async XLA Ops:
  0.6 15.6 %copy-start = (f32[1,32,192]{2,1,0:T(8,128)S(1)}, f32[1,32,192]{2,1,0:T(8,128)}, u32[]{:S(2)}) copy-start(f32[1,32,192]{2,1,0:T(8,128)} %refs_0_.1) | copy-start | bytes 73732
  0.6 15.5 %collective-permute-start.1 = (f32[1,32,192]{2,1,0:T(8,128)}, f32[1,32,192]{2,1,0:T(8,128)S(1)}, u32[]{:S(2)}, u32[]{:S(2)}) collective-permute-start(f32[1,32,192]{2,1,0:T(8,128)} %refs_0_.1), channel_id=1, source_target_pairs={{0,8},{4,12},{8,0},{12,4},{1,9},{5,13},{9,1},{13,5},{2,10},{6,14},... | collective-permute-start | bytes 73736 | tf_op jit(solution)/shard_map/ppermute | solution.py:331
  4.7 11.4 %collective-permute-start = (f32[1,32,192]{2,1,0:T(8,128)}, f32[1,32,192]{2,1,0:T(8,128)S(1)}, u32[]{:S(2)}, u32[]{:S(2)}) collective-permute-start(f32[1,32,192]{2,1,0:T(8,128)} %refs_0_.1), channel_id=1, source_target_pairs={{0,4},{4,8},{8,12},{12,0},{1,5},{5,9},{9,13},{13,1},{2,6},{6,10},{... | collective-permute-start | bytes 73736 | tf_op jit(solution)/shard_map/ppermute | solution.py:331
  6.3 9.9 %collective-permute-start.2 = (f32[1,32,192]{2,1,0:T(8,128)}, f32[1,32,192]{2,1,0:T(8,128)S(1)}, u32[]{:S(2)}, u32[]{:S(2)}) collective-permute-start(f32[1,32,192]{2,1,0:T(8,128)} %refs_0_.1), channel_id=1, source_target_pairs={{0,12},{4,0},{8,4},{12,8},{1,13},{5,1},{9,5},{13,9},{2,14},{6,2},{... | collective-permute-start | bytes 73736 | tf_op jit(solution)/shard_map/ppermute | solution.py:331
  16.2 11.2 %collective-permute-start.5 = (f32[4,32,192]{2,1,0:T(8,128)S(1)}, f32[4,32,192]{2,1,0:T(8,128)S(1)}, u32[]{:S(2)}, u32[]{:S(2)}) collective-permute-start(f32[4,32,192]{2,1,0:T(8,128)S(1)} %stack.2.refs_0_), channel_id=1, source_target_pairs={{0,18},{2,16},{16,2},{18,0},{1,19},{3,17},{17,3},{19,1},{4,22},{6,... | collective-permute-start | bytes 294920 | tf_op jit(solution)/shard_map/ppermute | solution.py:362
  18.7 8.7 %collective-permute-start.4 = (f32[4,32,192]{2,1,0:T(8,128)S(1)}, f32[4,32,192]{2,1,0:T(8,128)S(1)}, u32[]{:S(2)}, u32[]{:S(2)}) collective-permute-start(f32[4,32,192]{2,1,0:T(8,128)S(1)} %stack.2.refs_0_), channel_id=1, source_target_pairs={{0,16},{2,18},{16,0},{18,2},{1,17},{3,19},{17,1},{19,3},{4,20},{6,... | collective-permute-start | bytes 294920 | tf_op jit(solution)/shard_map/ppermute | solution.py:362
  19.3 8.2 %collective-permute-start.3 = (f32[4,32,192]{2,1,0:T(8,128)S(1)}, f32[4,32,192]{2,1,0:T(8,128)S(1)}, u32[]{:S(2)}, u32[]{:S(2)}) collective-permute-start(f32[4,32,192]{2,1,0:T(8,128)S(1)} %stack.2.refs_0_), channel_id=1, source_target_pairs={{0,2},{2,0},{16,18},{18,16},{1,3},{3,1},{17,19},{19,17},{4,6},{6,4... | collective-permute-start | bytes 294920 | tf_op jit(solution)/shard_map/ppermute | solution.py:362
  19.8 7.8 %copy-start.2 = (f32[320,768]{1,0:T(8,128)S(1)}, f32[320,768]{1,0:T(8,128)}, u32[]{:S(2)}) copy-start(f32[320,768]{1,0:T(8,128)} %weight_ref.1) | copy-start | bytes 2949124
  19.8 9.8 %copy-start.1 = (s32[8,4]{0,1:T(4,128)S(1)}, s32[8,4]{0,1:T(4,128)}, u32[]{:S(2)}) copy-start(s32[8,4]{0,1:T(4,128)} %param.12) | copy-start | bytes 388
  27.5 2.1 %collective-permute-start.6 = (f32[512,192]{1,0:T(8,128)S(1)}, f32[512,192]{1,0:T(8,128)S(1)}, u32[]{:S(2)}, u32[]{:S(2)}) collective-permute-start(f32[512,192]{1,0:T(8,128)S(1)} %bitcast.8), channel_id=1, source_target_pairs={{0,1},{1,0},{2,3},{3,2},{4,5},{5,4},{6,7},{7,6},{8,9},{9,8},{10,11... | collective-permute-start | bytes 1179656 | tf_op jit(solution)/shard_map/ppermute | solution.py:365
  38.4 13.7 %all-to-all-start = ((f32[16,16,256]{2,1,0:T(8,128)}), f32[16,16,256]{2,1,0:T(8,128)S(1)}, u32[]{:S(2)}, u32[]{:S(2)}) async-start(f32[16,16,256]{2,1,0:T(8,128)} %bitcast.5), calls=%async_computation | async-start | bytes 524288 | tf_op jit(solution)/shard_map/all_to_all | solution.py:398
  53.0 3.9 %collective-permute-start.7 = (f32[1,32,192]{2,1,0:T(8,128)S(1)}, f32[1,32,192]{2,1,0:T(8,128)S(1)}, u32[]{:S(2)}, u32[]{:S(2)}) collective-permute-start(f32[1,32,192]{2,1,0:T(8,128)S(1)} %get-tuple-element.13), channel_id=1, source_target_pairs={{0,16},{16,0},{1,17},{17,1},{2,18},{18,2},{3,19},{19,3},{4,20},{20... | collective-permute-start | bytes 73736 | tf_op jit(solution)/shard_map/ppermute | solution.py:428

commit v8 on v7

--- a/solution.py
+++ b/solution.py
@@ -66,28 +66,50 @@
     )
 
 
-def stream(loads, stores, prepare, product):
+def stream(loads, stores, product):
     for copy in loads[:AHEAD]:
         copy.start()
-    loads[0].wait()
-    prepare(0)
     for i, store in enumerate(stores):
+        loads[i].wait()
         if i + AHEAD < len(loads):
             loads[i + AHEAD].start()
-        if i + 1 < len(loads):
-            loads[i + 1].wait()
         product(i)
-        if i + 1 < len(loads):
-            prepare(i + 1)
         store.start()
     for copy in stores:
         copy.wait()
 
 
-def wide_kernel(chunks, x_hbm, weight_hbm, *refs):
-    out_hbm, *split_hbm, x, out, weight, pair, high, low, in_sems, out_sems, sems = refs
+def wide_product(pair, value):
+    width = pair.shape[0] // 2
+    high, low = split(value)
+    both = dot(pair[...], high, NT)
+    return both[:width] + (both[width:] + dot(pair[:width], low, NT))
+
+
+def input_kernel(
+    chunks,
+    x_hbm,
+    weight_hbm,
+    t_hbm,
+    next_weight_hbm,
+    out_hbm,
+    pair_hbm,
+    next_rows,
+    next_pair,
+    x,
+    out,
+    weight,
+    next_weight,
+    pair,
+    in_sems,
+    out_sems,
+    sems,
+):
     width = weight.shape[0]
     fetch = pltpu.make_async_copy(weight_hbm, weight, sems.at[0])
+    keep = pltpu.make_async_copy(pair, pair_hbm, sems.at[1])
+    fetch_next = pltpu.make_async_copy(next_weight_hbm, next_weight, sems.at[2])
+    fetch_rows = pltpu.make_async_copy(t_hbm.at[: next_rows.shape[0]], next_rows, sems.at[3])
     fetch.start()
     loads = [
         pltpu.make_async_copy(x_hbm.at[here], x.at[here], in_sems.at[i]) for i, here in enumerate(chunks)
@@ -96,29 +118,57 @@
         pltpu.make_async_copy(out.at[:, here], out_hbm.at[:, here], out_sems.at[i])
         for i, here in enumerate(chunks)
     ]
-    keep = [pltpu.make_async_copy(pair, hbm, sems.at[1]) for hbm in split_hbm]
-
-    def prepare(i):
-        high[i % 2], low[i % 2] = split(x[chunks[i], :])
+
+    def product(i):
         if i == 0:
             fetch.wait()
             pair[:width], pair[width:] = split(weight[...])
-            for copy in keep:
-                copy.start()
-
-    def product(i):
-        both = dot(pair[...], high[i % 2], NT)
-        out[:, chunks[i]] = both[:width] + (both[width:] + dot(pair[:width], low[i % 2], NT))
-
-    stream(loads, stores, prepare, product)
-    for copy in keep:
+            keep.start()
+            fetch_next.start()
+        if i == 1:
+            fetch_rows.start()
+        if i == len(chunks) - 1:
+            fetch_next.wait()
+            next_pair[:width], next_pair[width:] = split(next_weight[...])
+        out[:, chunks[i]] = wide_product(pair, x[chunks[i], :])
+
+    stream(loads, stores, product)
+    keep.wait()
+    fetch_rows.wait()
+
+
+def target_kernel(chunks, t_hbm, rows, pair, out_hbm, t, out, in_sems, out_sems):
+    loads = [
+        pltpu.make_async_copy(t_hbm.at[here], t.at[here], in_sems.at[i])
+        for i, here in enumerate(chunks[1:])
+    ]
+    stores = [
+        pltpu.make_async_copy(out.at[:, here], out_hbm.at[:, here], out_sems.at[i])
+        for i, here in enumerate(chunks)
+    ]
+    for copy in loads[:AHEAD]:
+        copy.start()
+    out[:, chunks[0]] = wide_product(pair, rows[...])
+    stores[0].start()
+    for i, copy in enumerate(loads):
         copy.wait()
-
-
-def gram_kernel(weight_ref, before_ref, gram_ref):
+        if i + AHEAD < len(loads):
+            loads[i + AHEAD].start()
+        here = chunks[i + 1]
+        out[:, here] = wide_product(pair, t[here, :])
+        stores[i + 1].start()
+    for copy in stores:
+        copy.wait()
+
+
+def prepare_kernel(patches, pair, cwgt, xwgt, crops_ref, before_ref, grams, projects, coarses, pick):
     del before_ref
-    high, low = split(weight_ref[...])
-    gram_ref[...] = dot3((high, low), (high, low), NT) + dot(low, low, NT)
+    width = xwgt.shape[0]
+    high, low = pair[:width], pair[width:]
+    grams[...] = side_by_side(dot3((high, low), (high, low), NT) + dot(low, low, NT))
+    projects[...] = side_by_side(xwgt[...])
+    coarses[...] = side_by_side(cwgt[...])
+    pick[...] = chosen(crops_ref, patches, pick.shape[1] // patches)
 
 
 def stack_kernel(*refs):
@@ -151,41 +201,32 @@
     crops_ref,
     own_ref,
     other_ref,
+    grams,
+    projects,
+    coarses,
+    pick,
     xw_hbm,
     tw_hbm,
-    gram_hbm,
-    cwgt_hbm,
-    xwgt_hbm,
     de_hbm,
     send_ref,
     xw,
     tw,
-    gram,
-    cwgt,
-    xwgt,
     rows,
-    pick,
-    small_sems,
     in_sems,
     out_sems,
 ):
-    pixels = cwgt.shape[0]
+    pixels = coarses.shape[0]
     width, count = xw.shape
     slots = patches * 16
     far = peers // 4
     chunks = chunk_rows(0, count)
-    small = [
-        pltpu.make_async_copy(source, target, small_sems.at[i])
-        for i, (source, target) in enumerate(((cwgt_hbm, cwgt), (xwgt_hbm, xwgt), (gram_hbm, gram)))
-    ]
     large = [pltpu.make_async_copy(xw_hbm, xw, in_sems.at[0]), pltpu.make_async_copy(tw_hbm, tw, in_sems.at[1])]
     stores = [
         pltpu.make_async_copy(xw.at[:, here], de_hbm.at[:, here], out_sems.at[i])
         for i, here in enumerate(chunks)
     ]
-    for copy in small + large:
+    for copy in large:
         copy.start()
-    pick[...] = chosen(crops_ref, patches, count // patches)
 
     me, side = lax.axis_index(("far", "y", "core")), lax.axis_index("lvl")
     for j in range(patches):
@@ -198,18 +239,11 @@
             start = pl.ds(pl.multiple_of((shard * 4 + row % 4) * SIDE, SIDE), SIDE)
             line = jnp.where(near % 2 == 0, own_ref[start, :], other_ref[start, :])
             rows[j * 16 + a * 4 : j * 16 + a * 4 + 4, :] = pltpu.roll(line, SIDE - left, 0)[:4, :]
-    small[0].wait()
-    coarse = split(cwgt[...])
-    pre = dot3(split(rows[...]), coarse)
+    pre = dot3(split(rows[...]), (coarses[:, :width], coarses[:, width : 2 * width]))
     gate = sigmoid(pre)
-    slope = gate * (1.0 + pre * (1.0 - gate))
-    small[1].wait()
-    project = split(xwgt[...])
-    high, low = split(dot3(split(pre * gate), project).T)
-    projected = jnp.concatenate([high, low], axis=1)
-    small[2].wait()
-    grams, projects, coarses = side_by_side(gram[...]), side_by_side(xwgt[...]), side_by_side(cwgt[...])
-    slope = slope.T
+    slope = (gate * (1.0 + pre * (1.0 - gate))).T
+    projected = dot3(split(pre * gate), (projects[:, :width], projects[:, width : 2 * width])).T
+    projected = jnp.concatenate(split(projected), axis=1)
     for copy in large:
         copy.wait()
 
@@ -224,7 +258,7 @@
     ready = first(0)
     for i, here in enumerate(chunks):
         factor, stack = ready
-        product = dot(grams, stack)
+        product = dot(grams[...], stack)
         if i + 1 < len(chunks):
             ready = first(i + 1)
         de = (product - tw[:, here]) * factor
@@ -233,8 +267,8 @@
     for copy in stores:
         copy.start()
 
-    dcontext = dot(projects, stacked(dslot[:width] + dslot[width:]))
-    grad = dot(coarses, stacked(dcontext * slope)).T
+    dcontext = dot(projects[...], stacked(dslot[:width] + dslot[width:]))
+    grad = dot(coarses[...], stacked(dcontext * slope)).T
     shape = (patches * 16, LANES - pixels)
     slot = lax.broadcasted_iota(jnp.int32, shape, 0) % 16
     top = row_value(crops_ref, 1, patches, shape, 0, 16)
@@ -264,7 +298,7 @@
 
 
 def last_kernel(chunks, de_hbm, pair_hbm, *refs):
-    out_hbm, de, out, deep, cat, in_sems, out_sems, sems = refs
+    out_hbm, de, out, deep, in_sems, out_sems, sems = refs
     width = de.shape[0]
     fetches = [
         pltpu.make_async_copy(pair_hbm, deep.at[: 2 * width], sems.at[0]),
@@ -281,25 +315,28 @@
         for i, here in enumerate(chunks)
     ]
 
-    def prepare(i):
-        high, low = split(de[:, chunks[i]])
-        cat[i % 2, :width], cat[i % 2, width : 2 * width], cat[i % 2, 2 * width :] = high, high, low
+    def product(i):
         if i == 0:
             for copy in fetches:
                 copy.wait()
-
-    def product(i):
-        out[chunks[i], :] = dot(cat[i % 2], deep[...], TN)
-
-    stream(loads, stores, prepare, product)
-
-
-def chunk_rows(first, last):
-    return [slice(start, start + ROWS) for start in range(first, last, ROWS)]
+        out[chunks[i], :] = dot(stacked(de[:, chunks[i]]), deep[...], TN)
+
+    stream(loads, stores, product)
+
+
+def chunk_rows(first, last, edge=ROWS):
+    cuts = [first] + list(range(first + edge, last, ROWS))
+    if cuts[-1] != last - edge:
+        cuts.append(last - edge)
+    return [slice(low, high) for low, high in zip(cuts, cuts[1:] + [last])]
 
 
 def fixed(*values):
     return [pltpu.with_memory_space_constraint(value, pltpu.HBM) for value in values]
+
+
+def near(*values):
+    return [pltpu.with_memory_space_constraint(value, pltpu.VMEM) for value in values]
 
 
 def stack(blocks, before):
@@ -331,47 +368,68 @@
         column.append(lax.ppermute(coarse_input, "far", [(p, (p + k) % far) for p in range(far)]))
 
     chunks = chunk_rows(0, count)
+    edges = chunk_rows(0, count, ROWS // 2)
     pair_shape = (2 * width, values)
-
-    def wide(name, value, weight, keep):
-        out_shape = [pltpu.HBM((width, count), F32)] + [pltpu.HBM(pair_shape, BF16)] * keep
-        return call(
-            functools.partial(wide_kernel, chunks),
-            name,
-            6 * count * values * width,
-            out_shape,
-            in_specs=[HBM, HBM],
-            out_specs=[HBM] * len(out_shape),
-            scratch_shapes=[
-                pltpu.VMEM((count, values), F32),
-                pltpu.VMEM((width, count), F32),
-                pltpu.VMEM((width, values), F32),
-                pltpu.VMEM(pair_shape, BF16),
-                pltpu.VMEM((2, ROWS, values), BF16),
-                pltpu.VMEM((2, ROWS, values), BF16),
-                pltpu.SemaphoreType.DMA((len(chunks),)),
-                pltpu.SemaphoreType.DMA((len(chunks),)),
-                pltpu.SemaphoreType.DMA((2,)),
-            ],
-        )(*fixed(value.reshape(count, values), weight))
-
-    xw, pair = wide("input", fine_input, in_weight.T, True)
+    x, t = fine_input.reshape(count, values), fine_target.reshape(count, values)
+    xw, pair, rows, next_pair = call(
+        functools.partial(input_kernel, edges),
+        "input",
+        6 * count * values * width,
+        (
+            pltpu.HBM((width, count), F32),
+            pltpu.HBM(pair_shape, BF16),
+            pltpu.VMEM((ROWS // 2, values), F32),
+            pltpu.VMEM(pair_shape, BF16),
+        ),
+        in_specs=[HBM] * 4,
+        out_specs=(HBM, HBM, VMEM, VMEM),
+        scratch_shapes=[
+            pltpu.VMEM((count, values), F32),
+            pltpu.VMEM((width, count), F32),
+            pltpu.VMEM((width, values), F32),
+            pltpu.VMEM((width, values), F32),
+            pltpu.VMEM(pair_shape, BF16),
+            pltpu.SemaphoreType.DMA((len(edges),)),
+            pltpu.SemaphoreType.DMA((len(edges),)),
+            pltpu.SemaphoreType.DMA((4,)),
+        ],
+    )(*fixed(x, in_weight.T, t, out_weight))
     column = stack(column, xw)
     own = [column]
     for flip in range(1, 4):
         own.append(lax.ppermute(column, ("lvl", "y"), [(p, p ^ flip) for p in range(4)]))
-    (tw,) = wide("target", fine_target, out_weight, False)
+    tw = call(
+        functools.partial(target_kernel, edges),
+        "target",
+        6 * count * values * width,
+        pltpu.HBM((width, count), F32),
+        limit=ROOM,
+        in_specs=[HBM, VMEM, VMEM],
+        out_specs=HBM,
+        scratch_shapes=[
+            pltpu.VMEM((count, values), F32),
+            pltpu.VMEM((width, count), F32),
+            pltpu.SemaphoreType.DMA((len(edges),)),
+            pltpu.SemaphoreType.DMA((len(edges),)),
+        ],
+    )(*fixed(t), *near(rows, next_pair))
     own = stack(own, tw).reshape(-1, pixels)
     other = lax.ppermute(own, "core", swap)
-    gram = call(
-        gram_kernel,
-        "gram",
+    crops = crops.T
+    prepared = call(
+        functools.partial(prepare_kernel, patches),
+        "prepare",
         8 * values * width * width,
-        pltpu.HBM((width, width), F32),
+        (
+            pltpu.VMEM((width, 3 * width), BF16),
+            pltpu.VMEM((width, 3 * width), BF16),
+            pltpu.VMEM((pixels, 3 * width), BF16),
+            pltpu.VMEM((patches * 16, count), BF16),
+        ),
         limit=ROOM,
-        in_specs=[VMEM, HBM],
-        out_specs=VMEM,
-    )(out_weight, own)
+        in_specs=[VMEM, VMEM, VMEM, SMEM, HBM],
+        out_specs=(VMEM,) * 4,
+    )(*near(next_pair), coarse_weight, context_weight, crops, own)
 
     shape = (peers * 16, LANES)
     de, back = call(
@@ -380,21 +438,16 @@
         6 * count * width * width,
         (pltpu.HBM((width, count), F32), jax.ShapeDtypeStruct(shape, F32)),
         limit=ROOM,
-        in_specs=[SMEM, VMEM, VMEM] + [HBM] * 5,
+        in_specs=[SMEM] + [VMEM] * 6 + [HBM] * 2,
         out_specs=(HBM, VMEM),
         scratch_shapes=[
             pltpu.VMEM((width, count), F32),
             pltpu.VMEM((width, count), F32),
-            pltpu.VMEM((width, width), F32),
-            pltpu.VMEM((pixels, width), F32),
-            pltpu.VMEM((width, width), F32),
             pltpu.VMEM((patches * 16, pixels), F32),
-            pltpu.VMEM((patches * 16, count), BF16),
-            pltpu.SemaphoreType.DMA((3,)),
             pltpu.SemaphoreType.DMA((2,)),
             pltpu.SemaphoreType.DMA((len(chunks),)),
         ],
-    )(crops.T, own, other, *fixed(xw, tw, gram, coarse_weight, context_weight))
+    )(crops, own, other, *near(*prepared), *fixed(xw, tw))
     returned = lax.all_to_all(back, patch, 0, 0, tiled=True)
 
     fine_grad = call(
@@ -408,7 +461,6 @@
             pltpu.VMEM((width, count), F32),
             pltpu.VMEM((count, values), F32),
             pltpu.VMEM((3 * width, values), BF16),
-            pltpu.VMEM((2, 3 * width, ROWS), BF16),
             pltpu.SemaphoreType.DMA((len(chunks),)),
             pltpu.SemaphoreType.DMA((len(chunks),)),
             pltpu.SemaphoreType.DMA((2,)),
@@ -419,7 +471,7 @@
         scatter_kernel,
         "scatter",
         10000,
-        (pltpu.HBM(part, F32), jax.ShapeDtypeStruct(part, F32)),
+        (jax.ShapeDtypeStruct(part, F32), jax.ShapeDtypeStruct(part, F32)),
         limit=ROOM,
         in_specs=[VMEM, HBM],
         out_specs=(VMEM, VMEM),

time: 58.7 us -> 60.6 us (1.032)
  Pallas kernels: 34.4 us -> 37.9 us
  other arithmetic: 1.38 us -> 0.62 us
  waiting for transfers between devices: 4.98 us -> 4.34 us
    pallas_call x4, Pallas kernels: 18.1 us -> 20.3 us  [the longest x1 9.52 us: body(): call(functools.partial(input_kernel, edges), 'input', 6 * count * values...]
    add x1, other arithmetic: 1.38 us -> 0.62 us  [body(): coarse_grad = mine + lax.ppermute(theirs, 'lvl', swap)]
    pallas_call x1, Pallas kernels: 8.73 us -> 9.47 us  [body(): call(functools.partial(middle_kernel, patches, peers), 'middle', 6 * coun...]
    pallas_call x1, Pallas kernels: 7.48 us -> 8.09 us  [body(): call(functools.partial(last_kernel, chunks), 'last', 6 * count * values *...]
    all_to_all x1, waiting for transfers between devices: 2.51 us -> 1.91 us  [body(): returned = lax.all_to_all(back, patch, 0, 0, tiled=True)]
  transfers between devices with their start and end apart: 9 -> 9, of which waited for: 2 -> 2; matrix products, arithmetic and copies ran while one was open for 0% -> 0% of each run, Pallas kernels for 42% -> 47%
where the time goes in v8:
time: 60.6 us; the launch traced here: 60.3 us
  Pallas kernels  37.9 us (63%)
  starting transfers between devices  16.7 us (28%)
  waiting for transfers between devices  4.34 us (7%)
  between operations  0.8 us (1%)
  other arithmetic  0.62 us (1%)
    pallas_call x1, Pallas kernels, body(): call(functools.partial(input_kernel, edges), 'input', 6 * count * values...  9.52 us
    pallas_call x1, Pallas kernels, body(): call(functools.partial(middle_kernel, patches, peers), 'middle', 6 * coun...  9.47 us
    pallas_call x1, Pallas kernels, body(): call(functools.partial(target_kernel, edges), 'target', 6 * count * value...  8.37 us
    pallas_call x1, Pallas kernels, body(): call(functools.partial(last_kernel, chunks), 'last', 6 * count * values *...  8.09 us
    ppermute x3, starting transfers between devices, body(): lax.ppermute(coarse_input, 'far', [(p, (p + k) % far) for p in range(far)])  7.93 us
    ppermute x3, starting transfers between devices, body(): lax.ppermute(column, ('lvl', 'y'), [(p, p ^ flip) for p in range(4)])  3.55 us
    all_to_all x1, starting transfers between devices, body(): returned = lax.all_to_all(back, patch, 0, 0, tiled=True)  3.54 us
    ppermute x1, waiting for transfers between devices, body(): coarse_grad = mine + lax.ppermute(theirs, 'lvl', swap)  2.42 us
  transfers between devices with their start and end apart: 9, of which 2 were waited for; matrix products, arithmetic and copies ran while one was open for 0% of the time, Pallas kernels for 47%

profile of v8, /device:TPU:0, one launch (start us, length us, event | category | flops | bytes accessed | tf_op | source)
XLA Modules:
  0.0 60.3 jit_solution(2507816904325113740)
XLA Ops:
  0.6 4.1 %collective-permute-start.1 = (f32[1,32,192]{2,1,0:T(8,128)}, f32[1,32,192]{2,1,0:T(8,128)S(1)}, u32[]{:S(2)}, u32[]{:S(2)}) collective-permute-start(f32[1,32,192]{2,1,0:T(8,128)} %refs_0_.1), channel_id=1, source_target_pairs={{0,8},{4,12},{8,0},{12,4},{1,9},{5,13},{9,1},{13,5},{2,10},{6,14},... | collective-permute-start | bytes 73736 | tf_op jit(solution)/shard_map/ppermute | solution.py:368
  4.7 1.6 %collective-permute-start = (f32[1,32,192]{2,1,0:T(8,128)}, f32[1,32,192]{2,1,0:T(8,128)S(1)}, u32[]{:S(2)}, u32[]{:S(2)}) collective-permute-start(f32[1,32,192]{2,1,0:T(8,128)} %refs_0_.1), channel_id=1, source_target_pairs={{0,4},{4,8},{8,12},{12,0},{1,5},{5,9},{9,13},{13,1},{2,6},{6,10},{... | collective-permute-start | bytes 73736 | tf_op jit(solution)/shard_map/ppermute | solution.py:368
  6.3 2.2 %collective-permute-start.2 = (f32[1,32,192]{2,1,0:T(8,128)}, f32[1,32,192]{2,1,0:T(8,128)S(1)}, u32[]{:S(2)}, u32[]{:S(2)}) collective-permute-start(f32[1,32,192]{2,1,0:T(8,128)} %refs_0_.1), channel_id=1, source_target_pairs={{0,12},{4,0},{8,4},{12,8},{1,13},{5,1},{9,5},{13,9},{2,14},{6,2},{... | collective-permute-start | bytes 73736 | tf_op jit(solution)/shard_map/ppermute | solution.py:368
  8.6 0.0 copy-start
  8.6 9.5 %input.1 = (f32[320,2048]{1,0:T(8,128)}, bf16[640,768]{1,0:T(8,128)(2,1)}, f32[256,768]{1,0:T(8,128)S(1)}, bf16[640,768]{1,0:T(8,128)(2,1)S(1)}) custom-call(f32[2048,768]{1,0:T(8,128)} %bitcast.14, f32[320,768]{1,0:T(8,128)} %bitcast.18, f32[2048,768]{1,0:T(8,128)} %bitcast.15, f32[320,768]{1,0:T(8,128)} %next_weight_hbm.1), custom_call_target="tpu_custom_call" | custom-call | flops 3019898880 | bytes 14680064 | tf_op jit(solution)/shard_map/input/pallas_call | solution.py:374
  18.1 0.0 collective-permute-done.1.refs_2_
  18.1 0.0 collective-permute-done.refs_1_
  18.1 0.0 collective-permute-done.2.refs_3_
  18.1 0.0 copy-done
  18.1 2.5 %collective-permute-start.5 = (f32[4,32,192]{2,1,0:T(8,128)S(1)}, f32[4,32,192]{2,1,0:T(8,128)S(1)}, u32[]{:S(2)}, u32[]{:S(2)}) collective-permute-start(f32[4,32,192]{2,1,0:T(8,128)S(1)} %stack.2.refs_0_), channel_id=1, source_target_pairs={{0,18},{2,16},{16,2},{18,0},{1,19},{3,17},{17,3},{19,1},{4,22},{6,... | collective-permute-start | bytes 294920 | tf_op jit(solution)/shard_map/ppermute | solution.py:400
  20.7 0.5 collective-permute-start.4
  21.2 0.5 collective-permute-start.3
  21.7 0.0 copy-start.1
  21.7 0.0 copy-start.2
  21.7 0.0 copy-start.3
  21.7 8.4 %target.1.refs_4_.tw_hbm = f32[320,2048]{1,0:T(8,128)} custom-call(f32[2048,768]{1,0:T(8,128)} %bitcast.16, f32[256,768]{1,0:T(8,128)S(1)} %get-tuple-element.15.rows, bf16[640,768]{1,0:T(8,128)(2,1)S(1)} %get-tuple-element.16.pair), custom_call_target="tpu_custom_call" | custom-call | flops 3019898880 | bytes 5242880 | tf_op jit(solution)/shard_map/target/pallas_call | solution.py:401
  30.1 0.0 collective-permute-done.5.refs_3_
  30.1 0.0 collective-permute-done.4.refs_2_
  30.1 0.0 collective-permute-done.3.refs_1_
  30.2 0.1 collective-permute-start.6
  30.2 0.0 copy-done.1
  30.3 0.0 copy-done.2
  30.3 0.0 copy-done.3
  30.3 2.1 %prepare.1 = (bf16[320,960]{1,0:T(8,128)(2,1)S(1)}, bf16[320,960]{1,0:T(8,128)(2,1)S(1)}, bf16[192,960]{1,0:T(8,128)(2,1)S(1)}, bf16[128,2048]{1,0:T(8,128)(2,1)S(1)}) custom-call(bf16[640,768]{1,0:T(8,128)(2,1)S(1)} %get-tuple-element.16.pair, f32[192,320]{1,0:T(8,128)S(1)} %copy-done.3, f32[320,320]{1,0:T(8,128)S(1)} %copy-done.2, s32[4,8]{1,0:T(4,128)S(1)} %bitcast.12, ...), custom_call_target="tpu_custom_call" | custom-call | flops 629145600 | bytes 8486912 | tf_op jit(solution)/shard_map/prepare/pallas_call | solution.py:419
  32.4 0.0 collective-permute-done.6.other_ref
  32.4 9.5 %middle.1 = (f32[320,2048]{1,0:T(8,128)}, f32[256,256]{1,0:T(8,128)}) custom-call(s32[4,8]{1,0:T(4,128)S(1)} %bitcast.13, f32[512,192]{1,0:T(8,128)S(1)} %bitcast.10, f32[512,192]{1,0:T(8,128)S(1)} %collective-permute-done.6.other_ref, bf16[320,960]{1,0:T(8,128)(2,1)S(1)} %get-tuple-element.17.grams, bf16[320,960]{1,0:T(8,128)(2,1)S(1)} %get-tuple-element.18.projects, ...), custom_call_target="tpu_custom_call" | custom-call | flops 1258291200 | bytes 5767168 | tf_op jit(solution)/shard_map/middle/pallas_call | solution.py:435
  41.9 3.5 %all-to-all-start = ((f32[16,16,256]{2,1,0:T(8,128)}), f32[16,16,256]{2,1,0:T(8,128)S(1)}, u32[]{:S(2)}, u32[]{:S(2)}) async-start(f32[16,16,256]{2,1,0:T(8,128)} %bitcast.5), calls=%async_computation | async-start | bytes 524288 | tf_op jit(solution)/shard_map/all_to_all | solution.py:451
  45.4 8.1 %last.1.done_ref = f32[2048,768]{1,0:T(8,128)} custom-call(f32[320,2048]{1,0:T(8,128)} %get-tuple-element.22.de_hbm, bf16[640,768]{1,0:T(8,128)(2,1)} %get-tuple-element.23.pair_hbm), custom_call_target="tpu_custom_call" | custom-call | flops 3019898880 | bytes 12582912 | tf_op jit(solution)/shard_map/last/pallas_call | solution.py:453
  53.5 1.9 %all-to-all-done = f32[16,16,256]{2,1,0:T(8,128)S(1)} async-done(((f32[16,16,256]{2,1,0:T(8,128)}), f32[16,16,256]{2,1,0:T(8,128)S(1)}, u32[]{:S(2)}, u32[]{:S(2)}) %all-to-all-start) | async-done | bytes 262176 | tf_op jit(solution)/shard_map/all_to_all | solution.py:451
  55.5 0.3 scatter.1
  55.7 1.6 %collective-permute-start.7 = (f32[1,32,192]{2,1,0:T(8,128)S(1)}, f32[1,32,192]{2,1,0:T(8,128)S(1)}, u32[]{:S(2)}, u32[]{:S(2)}) collective-permute-start(f32[1,32,192]{2,1,0:T(8,128)S(1)} %get-tuple-element.25), channel_id=1, source_target_pairs={{0,16},{16,0},{1,17},{17,1},{2,18},{18,2},{3,19},{19,3},{4,20},{20... | collective-permute-start | bytes 73736 | tf_op jit(solution)/shard_map/ppermute | solution.py:480
  57.3 2.4 %collective-permute-done.7 = f32[1,32,192]{2,1,0:T(8,128)S(1)} collective-permute-done((f32[1,32,192]{2,1,0:T(8,128)S(1)}, f32[1,32,192]{2,1,0:T(8,128)S(1)}, u32[]{:S(2)}, u32[]{:S(2)}) %collective-permute-start.7) | collective-permute-done | bytes 24608 | tf_op jit(solution)/shard_map/ppermute | solution.py:480
  59.7 0.6 %add.3 = f32[1,32,192]{2,1,0:T(8,128)} add(f32[1,32,192]{2,1,0:T(8,128)S(1)} %get-tuple-element.24, f32[1,32,192]{2,1,0:T(8,128)S(1)} %collective-permute-done.7) | non-fusion elementwise | flops 6144 | bytes 73728 | tf_op jit(solution)/shard_map/add | solution.py:480
  (2 shorter events, 0.0 us)
Async XLA Ops:
  0.6 17.5 %collective-permute-start.1 = (f32[1,32,192]{2,1,0:T(8,128)}, f32[1,32,192]{2,1,0:T(8,128)S(1)}, u32[]{:S(2)}, u32[]{:S(2)}) collective-permute-start(f32[1,32,192]{2,1,0:T(8,128)} %refs_0_.1), channel_id=1, source_target_pairs={{0,8},{4,12},{8,0},{12,4},{1,9},{5,13},{9,1},{13,5},{2,10},{6,14},... | collective-permute-start | bytes 73736 | tf_op jit(solution)/shard_map/ppermute | solution.py:368
  4.7 13.4 %collective-permute-start = (f32[1,32,192]{2,1,0:T(8,128)}, f32[1,32,192]{2,1,0:T(8,128)S(1)}, u32[]{:S(2)}, u32[]{:S(2)}) collective-permute-start(f32[1,32,192]{2,1,0:T(8,128)} %refs_0_.1), channel_id=1, source_target_pairs={{0,4},{4,8},{8,12},{12,0},{1,5},{5,9},{9,13},{13,1},{2,6},{6,10},{... | collective-permute-start | bytes 73736 | tf_op jit(solution)/shard_map/ppermute | solution.py:368
  6.3 11.8 %collective-permute-start.2 = (f32[1,32,192]{2,1,0:T(8,128)}, f32[1,32,192]{2,1,0:T(8,128)S(1)}, u32[]{:S(2)}, u32[]{:S(2)}) collective-permute-start(f32[1,32,192]{2,1,0:T(8,128)} %refs_0_.1), channel_id=1, source_target_pairs={{0,12},{4,0},{8,4},{12,8},{1,13},{5,1},{9,5},{13,9},{2,14},{6,2},{... | collective-permute-start | bytes 73736 | tf_op jit(solution)/shard_map/ppermute | solution.py:368
  8.6 9.6 %copy-start = (f32[1,32,192]{2,1,0:T(8,128)S(1)}, f32[1,32,192]{2,1,0:T(8,128)}, u32[]{:S(2)}) copy-start(f32[1,32,192]{2,1,0:T(8,128)} %refs_0_.1) | copy-start | bytes 73732
  18.1 11.9 %collective-permute-start.5 = (f32[4,32,192]{2,1,0:T(8,128)S(1)}, f32[4,32,192]{2,1,0:T(8,128)S(1)}, u32[]{:S(2)}, u32[]{:S(2)}) collective-permute-start(f32[4,32,192]{2,1,0:T(8,128)S(1)} %stack.2.refs_0_), channel_id=1, source_target_pairs={{0,18},{2,16},{16,2},{18,0},{1,19},{3,17},{17,3},{19,1},{4,22},{6,... | collective-permute-start | bytes 294920 | tf_op jit(solution)/shard_map/ppermute | solution.py:400
  20.7 9.4 %collective-permute-start.4 = (f32[4,32,192]{2,1,0:T(8,128)S(1)}, f32[4,32,192]{2,1,0:T(8,128)S(1)}, u32[]{:S(2)}, u32[]{:S(2)}) collective-permute-start(f32[4,32,192]{2,1,0:T(8,128)S(1)} %stack.2.refs_0_), channel_id=1, source_target_pairs={{0,16},{2,18},{16,0},{18,2},{1,17},{3,19},{17,1},{19,3},{4,20},{6,... | collective-permute-start | bytes 294920 | tf_op jit(solution)/shard_map/ppermute | solution.py:400
  21.2 8.9 %collective-permute-start.3 = (f32[4,32,192]{2,1,0:T(8,128)S(1)}, f32[4,32,192]{2,1,0:T(8,128)S(1)}, u32[]{:S(2)}, u32[]{:S(2)}) collective-permute-start(f32[4,32,192]{2,1,0:T(8,128)S(1)} %stack.2.refs_0_), channel_id=1, source_target_pairs={{0,2},{2,0},{16,18},{18,16},{1,3},{3,1},{17,19},{19,17},{4,6},{6,4... | collective-permute-start | bytes 294920 | tf_op jit(solution)/shard_map/ppermute | solution.py:400
  21.7 8.5 %copy-start.1 = (s32[8,4]{0,1:T(4,128)S(1)}, s32[8,4]{0,1:T(4,128)}, u32[]{:S(2)}) copy-start(s32[8,4]{0,1:T(4,128)} %param.12) | copy-start | bytes 388
  21.7 8.5 %copy-start.2 = (f32[320,320]{1,0:T(8,128)S(1)}, f32[320,320]{1,0:T(8,128)}, u32[]{:S(2)}) copy-start(f32[320,320]{1,0:T(8,128)} %xwgt.1) | copy-start | bytes 1228804
  21.7 8.6 %copy-start.3 = (f32[192,320]{1,0:T(8,128)S(1)}, f32[192,320]{1,0:T(8,128)}, u32[]{:S(2)}) copy-start(f32[192,320]{1,0:T(8,128)} %cwgt.1) | copy-start | bytes 737284
  30.2 2.2 %collective-permute-start.6 = (f32[512,192]{1,0:T(8,128)S(1)}, f32[512,192]{1,0:T(8,128)S(1)}, u32[]{:S(2)}, u32[]{:S(2)}) collective-permute-start(f32[512,192]{1,0:T(8,128)S(1)} %bitcast.8), channel_id=1, source_target_pairs={{0,1},{1,0},{2,3},{3,2},{4,5},{5,4},{6,7},{7,6},{8,9},{9,8},{10,11... | collective-permute-start | bytes 1179656 | tf_op jit(solution)/shard_map/ppermute | solution.py:417
  41.9 13.6 %all-to-all-start = ((f32[16,16,256]{2,1,0:T(8,128)}), f32[16,16,256]{2,1,0:T(8,128)S(1)}, u32[]{:S(2)}, u32[]{:S(2)}) async-start(f32[16,16,256]{2,1,0:T(8,128)} %bitcast.5), calls=%async_computation | async-start | bytes 524288 | tf_op jit(solution)/shard_map/all_to_all | solution.py:451
  55.7 4.0 %collective-permute-start.7 = (f32[1,32,192]{2,1,0:T(8,128)S(1)}, f32[1,32,192]{2,1,0:T(8,128)S(1)}, u32[]{:S(2)}, u32[]{:S(2)}) collective-permute-start(f32[1,32,192]{2,1,0:T(8,128)S(1)} %get-tuple-element.25), channel_id=1, source_target_pairs={{0,16},{16,0},{1,17},{17,1},{2,18},{18,2},{3,19},{19,3},{4,20},{20... | collective-permute-start | bytes 73736 | tf_op jit(solution)/shard_map/ppermute | solution.py:480

commit v9 on v8

--- a/solution.py
+++ b/solution.py
@@ -79,11 +79,11 @@
         copy.wait()
 
 
-def wide_product(pair, value):
-    width = pair.shape[0] // 2
+def pair_product(pair, value, dims):
+    rows = pair.shape[0] // 2
     high, low = split(value)
-    both = dot(pair[...], high, NT)
-    return both[:width] + (both[width:] + dot(pair[:width], low, NT))
+    both = dot(pair[...], high, dims)
+    return both[:rows] + (both[rows:] + dot(pair[:rows], low, dims))
 
 
 def input_kernel(
@@ -130,7 +130,7 @@
         if i == len(chunks) - 1:
             fetch_next.wait()
             next_pair[:width], next_pair[width:] = split(next_weight[...])
-        out[:, chunks[i]] = wide_product(pair, x[chunks[i], :])
+        out[:, chunks[i]] = pair_product(pair, x[chunks[i], :], NT)
 
     stream(loads, stores, product)
     keep.wait()
@@ -148,14 +148,14 @@
     ]
     for copy in loads[:AHEAD]:
         copy.start()
-    out[:, chunks[0]] = wide_product(pair, rows[...])
+    out[:, chunks[0]] = pair_product(pair, rows[...], NT)
     stores[0].start()
     for i, copy in enumerate(loads):
         copy.wait()
         if i + AHEAD < len(loads):
             loads[i + AHEAD].start()
         here = chunks[i + 1]
-        out[:, here] = wide_product(pair, t[here, :])
+        out[:, here] = pair_product(pair, t[here, :], NT)
         stores[i + 1].start()
     for copy in stores:
         copy.wait()
@@ -166,8 +166,8 @@
     width = xwgt.shape[0]
     high, low = pair[:width], pair[width:]
     grams[...] = side_by_side(dot3((high, low), (high, low), NT) + dot(low, low, NT))
-    projects[...] = side_by_side(xwgt[...])
-    coarses[...] = side_by_side(cwgt[...])
+    projects[...] = jnp.concatenate(split(xwgt[...]), axis=0)
+    coarses[...] = jnp.concatenate(split(cwgt[...]), axis=0)
     pick[...] = chosen(crops_ref, patches, pick.shape[1] // patches)
 
 
@@ -215,7 +215,7 @@
     in_sems,
     out_sems,
 ):
-    pixels = coarses.shape[0]
+    pixels = coarses.shape[0] // 2
     width, count = xw.shape
     slots = patches * 16
     far = peers // 4
@@ -239,10 +239,10 @@
             start = pl.ds(pl.multiple_of((shard * 4 + row % 4) * SIDE, SIDE), SIDE)
             line = jnp.where(near % 2 == 0, own_ref[start, :], other_ref[start, :])
             rows[j * 16 + a * 4 : j * 16 + a * 4 + 4, :] = pltpu.roll(line, SIDE - left, 0)[:4, :]
-    pre = dot3(split(rows[...]), (coarses[:, :width], coarses[:, width : 2 * width]))
+    pre = dot3(split(rows[...]), (coarses[:pixels], coarses[pixels:]))
     gate = sigmoid(pre)
     slope = (gate * (1.0 + pre * (1.0 - gate))).T
-    projected = dot3(split(pre * gate), (projects[:, :width], projects[:, width : 2 * width])).T
+    projected = dot3(split(pre * gate), (projects[:width], projects[width:])).T
     projected = jnp.concatenate(split(projected), axis=1)
     for copy in large:
         copy.wait()
@@ -267,8 +267,8 @@
     for copy in stores:
         copy.start()
 
-    dcontext = dot(projects[...], stacked(dslot[:width] + dslot[width:]))
-    grad = dot(coarses[...], stacked(dcontext * slope)).T
+    dcontext = pair_product(projects, dslot[:width] + dslot[width:], NN)
+    grad = pair_product(coarses, dcontext * slope, NN).T
     shape = (patches * 16, LANES - pixels)
     slot = lax.broadcasted_iota(jnp.int32, shape, 0) % 16
     top = row_value(crops_ref, 1, patches, shape, 0, 16)
@@ -298,7 +298,7 @@
 
 
 def last_kernel(chunks, de_hbm, pair_hbm, *refs):
-    out_hbm, de, out, deep, in_sems, out_sems, sems = refs
+    out_hbm, de, out, deep, cat, in_sems, out_sems, sems = refs
     width = de.shape[0]
     fetches = [
         pltpu.make_async_copy(pair_hbm, deep.at[: 2 * width], sems.at[0]),
@@ -315,20 +315,26 @@
         for i, here in enumerate(chunks)
     ]
 
-    def product(i):
-        if i == 0:
-            for copy in fetches:
-                copy.wait()
-        out[chunks[i], :] = dot(stacked(de[:, chunks[i]]), deep[...], TN)
-
-    stream(loads, stores, product)
-
-
-def chunk_rows(first, last, edge=ROWS):
-    cuts = [first] + list(range(first + edge, last, ROWS))
-    if cuts[-1] != last - edge:
-        cuts.append(last - edge)
-    return [slice(low, high) for low, high in zip(cuts, cuts[1:] + [last])]
+    def prepare(i):
+        loads[i].wait()
+        cat[i % 2] = stacked(de[:, chunks[i]])
+
+    for copy in loads:
+        copy.start()
+    prepare(0)
+    for copy in fetches:
+        copy.wait()
+    for i, here in enumerate(chunks):
+        out[here, :] = dot(cat[i % 2], deep[...], TN)
+        if i + 1 < len(chunks):
+            prepare(i + 1)
+        stores[i].start()
+    for copy in stores:
+        copy.wait()
+
+
+def chunk_rows(first, last):
+    return [slice(start, start + ROWS) for start in range(first, last, ROWS)]
 
 
 def fixed(*values):
@@ -368,17 +374,16 @@
         column.append(lax.ppermute(coarse_input, "far", [(p, (p + k) % far) for p in range(far)]))
 
     chunks = chunk_rows(0, count)
-    edges = chunk_rows(0, count, ROWS // 2)
     pair_shape = (2 * width, values)
     x, t = fine_input.reshape(count, values), fine_target.reshape(count, values)
     xw, pair, rows, next_pair = call(
-        functools.partial(input_kernel, edges),
+        functools.partial(input_kernel, chunks),
         "input",
         6 * count * values * width,
         (
             pltpu.HBM((width, count), F32),
             pltpu.HBM(pair_shape, BF16),
-            pltpu.VMEM((ROWS // 2, values), F32),
+            pltpu.VMEM((ROWS, values), F32),
             pltpu.VMEM(pair_shape, BF16),
         ),
         in_specs=[HBM] * 4,
@@ -389,8 +394,8 @@
             pltpu.VMEM((width, values), F32),
             pltpu.VMEM((width, values), F32),
             pltpu.VMEM(pair_shape, BF16),
-            pltpu.SemaphoreType.DMA((len(edges),)),
-            pltpu.SemaphoreType.DMA((len(edges),)),
+            pltpu.SemaphoreType.DMA((len(chunks),)),
+            pltpu.SemaphoreType.DMA((len(chunks),)),
             pltpu.SemaphoreType.DMA((4,)),
         ],
     )(*fixed(x, in_weight.T, t, out_weight))
@@ -399,7 +404,7 @@
     for flip in range(1, 4):
         own.append(lax.ppermute(column, ("lvl", "y"), [(p, p ^ flip) for p in range(4)]))
     tw = call(
-        functools.partial(target_kernel, edges),
+        functools.partial(target_kernel, chunks),
         "target",
         6 * count * values * width,
         pltpu.HBM((width, count), F32),
@@ -409,8 +414,8 @@
         scratch_shapes=[
             pltpu.VMEM((count, values), F32),
             pltpu.VMEM((width, count), F32),
-            pltpu.SemaphoreType.DMA((len(edges),)),
-            pltpu.SemaphoreType.DMA((len(edges),)),
+            pltpu.SemaphoreType.DMA((len(chunks),)),
+            pltpu.SemaphoreType.DMA((len(chunks),)),
         ],
     )(*fixed(t), *near(rows, next_pair))
     own = stack(own, tw).reshape(-1, pixels)
@@ -422,8 +427,8 @@
         8 * values * width * width,
         (
             pltpu.VMEM((width, 3 * width), BF16),
-            pltpu.VMEM((width, 3 * width), BF16),
-            pltpu.VMEM((pixels, 3 * width), BF16),
+            pltpu.VMEM((2 * width, width), BF16),
+            pltpu.VMEM((2 * pixels, width), BF16),
             pltpu.VMEM((patches * 16, count), BF16),
         ),
         limit=ROOM,
@@ -461,6 +466,7 @@
             pltpu.VMEM((width, count), F32),
             pltpu.VMEM((count, values), F32),
             pltpu.VMEM((3 * width, values), BF16),
+            pltpu.VMEM((2, 3 * width, ROWS), BF16),
             pltpu.SemaphoreType.DMA((len(chunks),)),
             pltpu.SemaphoreType.DMA((len(chunks),)),
             pltpu.SemaphoreType.DMA((2,)),

time: 60.6 us -> 56.4 us (0.931)
  Pallas kernels: 37.9 us -> 32.9 us
  local copies, waits for them, and re-layouts: 0.01 us -> 0.95 us
    pallas_call x2, Pallas kernels: 17.9 us -> 12 us  [the longest x1 6.72 us: body(): call(functools.partial(input_kernel, chunks), 'input', 6 * count * values...]
    unnamed x8, local copies, waits for them, and re-layouts: 0.01 us -> 0.95 us
  transfers between devices with their start and end apart: 9 -> 9, of which waited for: 2 -> 2; matrix products, arithmetic and copies ran while one was open for 0% -> 0% of each run, Pallas kernels for 47% -> 41%
where the time goes in v9:
time: 56.4 us; the launch traced here: 56.1 us
  Pallas kernels  32.9 us (58%)
  starting transfers between devices  16.8 us (30%)
  waiting for transfers between devices  3.95 us (7%)
  local copies, waits for them, and re-layouts  0.95 us (2%)
  between operations  0.8 us (1%)
  other arithmetic  0.62 us (1%)
    pallas_call x1, Pallas kernels, body(): call(functools.partial(middle_kernel, patches, peers), 'middle', 6 * coun...  9.83 us
    pallas_call x1, Pallas kernels, body(): call(functools.partial(last_kernel, chunks), 'last', 6 * count * values *...  8.48 us
    ppermute x3, starting transfers between devices, body(): lax.ppermute(coarse_input, 'far', [(p, (p + k) % far) for p in range(far)])  7.93 us
    pallas_call x1, Pallas kernels, body(): call(functools.partial(input_kernel, chunks), 'input', 6 * count * values...  6.72 us
    pallas_call x1, Pallas kernels, body(): call(functools.partial(target_kernel, chunks), 'target', 6 * count * valu...  5.28 us
    all_to_all x1, starting transfers between devices, body(): returned = lax.all_to_all(back, patch, 0, 0, tiled=True)  3.72 us
    ppermute x3, starting transfers between devices, body(): lax.ppermute(column, ('lvl', 'y'), [(p, p ^ flip) for p in range(4)])  3.55 us
    ppermute x1, waiting for transfers between devices, body(): coarse_grad = mine + lax.ppermute(theirs, 'lvl', swap)  2.42 us
  transfers between devices with their start and end apart: 9, of which 2 were waited for; matrix products, arithmetic and copies ran while one was open for 0% of the time, Pallas kernels for 41%

profile of v9, /device:TPU:0, one launch (start us, length us, event | category | flops | bytes accessed | tf_op | source)
XLA Modules:
  0.0 56.1 jit_solution(3206102818942935143)
XLA Ops:
  0.6 4.1 %collective-permute-start.1 = (f32[1,32,192]{2,1,0:T(8,128)}, f32[1,32,192]{2,1,0:T(8,128)S(1)}, u32[]{:S(2)}, u32[]{:S(2)}) collective-permute-start(f32[1,32,192]{2,1,0:T(8,128)} %refs_0_.1), channel_id=1, source_target_pairs={{0,8},{4,12},{8,0},{12,4},{1,9},{5,13},{9,1},{13,5},{2,10},{6,14},... | collective-permute-start | bytes 73736 | tf_op jit(solution)/shard_map/ppermute | solution.py:374
  4.7 1.6 %collective-permute-start = (f32[1,32,192]{2,1,0:T(8,128)}, f32[1,32,192]{2,1,0:T(8,128)S(1)}, u32[]{:S(2)}, u32[]{:S(2)}) collective-permute-start(f32[1,32,192]{2,1,0:T(8,128)} %refs_0_.1), channel_id=1, source_target_pairs={{0,4},{4,8},{8,12},{12,0},{1,5},{5,9},{9,13},{13,1},{2,6},{6,10},{... | collective-permute-start | bytes 73736 | tf_op jit(solution)/shard_map/ppermute | solution.py:374
  6.3 2.2 %collective-permute-start.2 = (f32[1,32,192]{2,1,0:T(8,128)}, f32[1,32,192]{2,1,0:T(8,128)S(1)}, u32[]{:S(2)}, u32[]{:S(2)}) collective-permute-start(f32[1,32,192]{2,1,0:T(8,128)} %refs_0_.1), channel_id=1, source_target_pairs={{0,12},{4,0},{8,4},{12,8},{1,13},{5,1},{9,5},{13,9},{2,14},{6,2},{... | collective-permute-start | bytes 73736 | tf_op jit(solution)/shard_map/ppermute | solution.py:374
  8.6 0.0 copy-start
  8.6 6.7 %input.1 = (f32[320,2048]{1,0:T(8,128)}, bf16[640,768]{1,0:T(8,128)(2,1)}, f32[512,768]{1,0:T(8,128)S(1)}, bf16[640,768]{1,0:T(8,128)(2,1)S(1)}) custom-call(f32[2048,768]{1,0:T(8,128)} %bitcast.16, f32[320,768]{1,0:T(8,128)} %bitcast.18, f32[2048,768]{1,0:T(8,128)} %bitcast.14, f32[320,768]{1,0:T(8,128)} %next_weight_hbm.1), custom_call_target="tpu_custom_call" | custom-call | flops 3019898880 | bytes 16252928 | tf_op jit(solution)/shard_map/input/pallas_call | solution.py:379
  15.3 0.0 collective-permute-done.1.refs_2_
  15.3 0.0 collective-permute-done.refs_1_
  15.3 0.0 collective-permute-done.2.refs_3_
  15.3 0.0 copy-done
  15.3 2.5 %collective-permute-start.5 = (f32[4,32,192]{2,1,0:T(8,128)S(1)}, f32[4,32,192]{2,1,0:T(8,128)S(1)}, u32[]{:S(2)}, u32[]{:S(2)}) collective-permute-start(f32[4,32,192]{2,1,0:T(8,128)S(1)} %stack.2.refs_0_), channel_id=1, source_target_pairs={{0,18},{2,16},{16,2},{18,0},{1,19},{3,17},{17,3},{19,1},{4,22},{6,... | collective-permute-start | bytes 294920 | tf_op jit(solution)/shard_map/ppermute | solution.py:405
  17.9 0.5 collective-permute-start.4
  18.4 0.5 collective-permute-start.3
  18.9 5.3 %target.1.refs_4_.tw_hbm = f32[320,2048]{1,0:T(8,128)} custom-call(f32[2048,768]{1,0:T(8,128)} %bitcast.15, f32[512,768]{1,0:T(8,128)S(1)} %get-tuple-element.15.rows, bf16[640,768]{1,0:T(8,128)(2,1)S(1)} %get-tuple-element.16.pair), custom_call_target="tpu_custom_call" | custom-call | flops 3019898880 | bytes 5242880 | tf_op jit(solution)/shard_map/target/pallas_call | solution.py:406
  24.2 0.0 copy-start.1
  24.2 0.0 copy-start.2
  24.2 0.0 copy-start.3
  24.2 0.0 collective-permute-done.5.refs_3_
  24.2 0.0 collective-permute-done.4.refs_2_
  24.3 0.0 collective-permute-done.3.refs_1_
  24.3 0.1 collective-permute-start.6
  24.4 0.5 copy-done.1
  24.9 0.4 copy-done.2
  25.2 0.1 copy-done.3
  25.3 2.3 %prepare.1 = (bf16[320,960]{1,0:T(8,128)(2,1)S(1)}, bf16[640,320]{1,0:T(8,128)(2,1)S(1)}, bf16[384,320]{1,0:T(8,128)(2,1)S(1)}, bf16[128,2048]{1,0:T(8,128)(2,1)S(1)}) custom-call(bf16[640,768]{1,0:T(8,128)(2,1)S(1)} %get-tuple-element.16.pair, f32[192,320]{1,0:T(8,128)S(1)} %copy-done.3, f32[320,320]{1,0:T(8,128)S(1)} %copy-done.2, s32[4,8]{1,0:T(4,128)S(1)} %bitcast.12, ...), custom_call_target="tpu_custom_call" | custom-call | flops 629145600 | bytes 7176192 | tf_op jit(solution)/shard_map/prepare/pallas_call | solution.py:424
  27.6 0.0 collective-permute-done.6.other_ref
  27.6 9.8 %middle.1 = (f32[320,2048]{1,0:T(8,128)}, f32[256,256]{1,0:T(8,128)}) custom-call(s32[4,8]{1,0:T(4,128)S(1)} %bitcast.13, f32[512,192]{1,0:T(8,128)S(1)} %bitcast.10, f32[512,192]{1,0:T(8,128)S(1)} %collective-permute-done.6.other_ref, bf16[320,960]{1,0:T(8,128)(2,1)S(1)} %get-tuple-element.17.grams, bf16[640,320]{1,0:T(8,128)(2,1)S(1)} %get-tuple-element.18.projects, ...), custom_call_target="tpu_custom_call" | custom-call | flops 1258291200 | bytes 5767168 | tf_op jit(solution)/shard_map/middle/pallas_call | solution.py:440
  37.5 3.7 %all-to-all-start = ((f32[16,16,256]{2,1,0:T(8,128)}), f32[16,16,256]{2,1,0:T(8,128)S(1)}, u32[]{:S(2)}, u32[]{:S(2)}) async-start(f32[16,16,256]{2,1,0:T(8,128)} %bitcast.5), calls=%async_computation | async-start | bytes 524288 | tf_op jit(solution)/shard_map/all_to_all | solution.py:456
  41.2 8.5 %last.1.done_ref = f32[2048,768]{1,0:T(8,128)} custom-call(f32[320,2048]{1,0:T(8,128)} %get-tuple-element.22.de_hbm, bf16[640,768]{1,0:T(8,128)(2,1)} %get-tuple-element.23.pair_hbm), custom_call_target="tpu_custom_call" | custom-call | flops 3019898880 | bytes 12582912 | tf_op jit(solution)/shard_map/last/pallas_call | solution.py:458
  49.7 1.5 %all-to-all-done = f32[16,16,256]{2,1,0:T(8,128)S(1)} async-done(((f32[16,16,256]{2,1,0:T(8,128)}), f32[16,16,256]{2,1,0:T(8,128)S(1)}, u32[]{:S(2)}, u32[]{:S(2)}) %all-to-all-start) | async-done | bytes 262176 | tf_op jit(solution)/shard_map/all_to_all | solution.py:456
  51.2 0.3 scatter.1
  51.5 1.6 %collective-permute-start.7 = (f32[1,32,192]{2,1,0:T(8,128)S(1)}, f32[1,32,192]{2,1,0:T(8,128)S(1)}, u32[]{:S(2)}, u32[]{:S(2)}) collective-permute-start(f32[1,32,192]{2,1,0:T(8,128)S(1)} %get-tuple-element.25), channel_id=1, source_target_pairs={{0,16},{16,0},{1,17},{17,1},{2,18},{18,2},{3,19},{19,3},{4,20},{20... | collective-permute-start | bytes 73736 | tf_op jit(solution)/shard_map/ppermute | solution.py:486
  53.1 2.4 %collective-permute-done.7 = f32[1,32,192]{2,1,0:T(8,128)S(1)} collective-permute-done((f32[1,32,192]{2,1,0:T(8,128)S(1)}, f32[1,32,192]{2,1,0:T(8,128)S(1)}, u32[]{:S(2)}, u32[]{:S(2)}) %collective-permute-start.7) | collective-permute-done | bytes 24608 | tf_op jit(solution)/shard_map/ppermute | solution.py:486
  55.5 0.6 %add.3 = f32[1,32,192]{2,1,0:T(8,128)} add(f32[1,32,192]{2,1,0:T(8,128)S(1)} %get-tuple-element.24, f32[1,32,192]{2,1,0:T(8,128)S(1)} %collective-permute-done.7) | non-fusion elementwise | flops 6144 | bytes 73728 | tf_op jit(solution)/shard_map/add | solution.py:486
  (2 shorter events, 0.0 us)
Async XLA Ops:
  0.6 14.7 %collective-permute-start.1 = (f32[1,32,192]{2,1,0:T(8,128)}, f32[1,32,192]{2,1,0:T(8,128)S(1)}, u32[]{:S(2)}, u32[]{:S(2)}) collective-permute-start(f32[1,32,192]{2,1,0:T(8,128)} %refs_0_.1), channel_id=1, source_target_pairs={{0,8},{4,12},{8,0},{12,4},{1,9},{5,13},{9,1},{13,5},{2,10},{6,14},... | collective-permute-start | bytes 73736 | tf_op jit(solution)/shard_map/ppermute | solution.py:374
  4.7 10.6 %collective-permute-start = (f32[1,32,192]{2,1,0:T(8,128)}, f32[1,32,192]{2,1,0:T(8,128)S(1)}, u32[]{:S(2)}, u32[]{:S(2)}) collective-permute-start(f32[1,32,192]{2,1,0:T(8,128)} %refs_0_.1), channel_id=1, source_target_pairs={{0,4},{4,8},{8,12},{12,0},{1,5},{5,9},{9,13},{13,1},{2,6},{6,10},{... | collective-permute-start | bytes 73736 | tf_op jit(solution)/shard_map/ppermute | solution.py:374
  6.3 9.0 %collective-permute-start.2 = (f32[1,32,192]{2,1,0:T(8,128)}, f32[1,32,192]{2,1,0:T(8,128)S(1)}, u32[]{:S(2)}, u32[]{:S(2)}) collective-permute-start(f32[1,32,192]{2,1,0:T(8,128)} %refs_0_.1), channel_id=1, source_target_pairs={{0,12},{4,0},{8,4},{12,8},{1,13},{5,1},{9,5},{13,9},{2,14},{6,2},{... | collective-permute-start | bytes 73736 | tf_op jit(solution)/shard_map/ppermute | solution.py:374
  8.6 6.8 %copy-start = (f32[1,32,192]{2,1,0:T(8,128)S(1)}, f32[1,32,192]{2,1,0:T(8,128)}, u32[]{:S(2)}) copy-start(f32[1,32,192]{2,1,0:T(8,128)} %refs_0_.1) | copy-start | bytes 73732
  15.3 8.9 %collective-permute-start.5 = (f32[4,32,192]{2,1,0:T(8,128)S(1)}, f32[4,32,192]{2,1,0:T(8,128)S(1)}, u32[]{:S(2)}, u32[]{:S(2)}) collective-permute-start(f32[4,32,192]{2,1,0:T(8,128)S(1)} %stack.2.refs_0_), channel_id=1, source_target_pairs={{0,18},{2,16},{16,2},{18,0},{1,19},{3,17},{17,3},{19,1},{4,22},{6,... | collective-permute-start | bytes 294920 | tf_op jit(solution)/shard_map/ppermute | solution.py:405
  17.9 6.4 %collective-permute-start.4 = (f32[4,32,192]{2,1,0:T(8,128)S(1)}, f32[4,32,192]{2,1,0:T(8,128)S(1)}, u32[]{:S(2)}, u32[]{:S(2)}) collective-permute-start(f32[4,32,192]{2,1,0:T(8,128)S(1)} %stack.2.refs_0_), channel_id=1, source_target_pairs={{0,16},{2,18},{16,0},{18,2},{1,17},{3,19},{17,1},{19,3},{4,20},{6,... | collective-permute-start | bytes 294920 | tf_op jit(solution)/shard_map/ppermute | solution.py:405
  18.4 5.8 %collective-permute-start.3 = (f32[4,32,192]{2,1,0:T(8,128)S(1)}, f32[4,32,192]{2,1,0:T(8,128)S(1)}, u32[]{:S(2)}, u32[]{:S(2)}) collective-permute-start(f32[4,32,192]{2,1,0:T(8,128)S(1)} %stack.2.refs_0_), channel_id=1, source_target_pairs={{0,2},{2,0},{16,18},{18,16},{1,3},{3,1},{17,19},{19,17},{4,6},{6,4... | collective-permute-start | bytes 294920 | tf_op jit(solution)/shard_map/ppermute | solution.py:405
  24.2 0.7 %copy-start.1 = (s32[8,4]{0,1:T(4,128)S(1)}, s32[8,4]{0,1:T(4,128)}, u32[]{:S(2)}) copy-start(s32[8,4]{0,1:T(4,128)} %param.12) | copy-start | bytes 388
  24.2 1.0 %copy-start.2 = (f32[320,320]{1,0:T(8,128)S(1)}, f32[320,320]{1,0:T(8,128)}, u32[]{:S(2)}) copy-start(f32[320,320]{1,0:T(8,128)} %xwgt.1) | copy-start | bytes 1228804
  24.2 1.1 %copy-start.3 = (f32[192,320]{1,0:T(8,128)S(1)}, f32[192,320]{1,0:T(8,128)}, u32[]{:S(2)}) copy-start(f32[192,320]{1,0:T(8,128)} %cwgt.1) | copy-start | bytes 737284
  24.3 3.3 %collective-permute-start.6 = (f32[512,192]{1,0:T(8,128)S(1)}, f32[512,192]{1,0:T(8,128)S(1)}, u32[]{:S(2)}, u32[]{:S(2)}) collective-permute-start(f32[512,192]{1,0:T(8,128)S(1)} %bitcast.8), channel_id=1, source_target_pairs={{0,1},{1,0},{2,3},{3,2},{4,5},{5,4},{6,7},{7,6},{8,9},{9,8},{10,11... | collective-permute-start | bytes 1179656 | tf_op jit(solution)/shard_map/ppermute | solution.py:422
  37.5 13.7 %all-to-all-start = ((f32[16,16,256]{2,1,0:T(8,128)}), f32[16,16,256]{2,1,0:T(8,128)S(1)}, u32[]{:S(2)}, u32[]{:S(2)}) async-start(f32[16,16,256]{2,1,0:T(8,128)} %bitcast.5), calls=%async_computation | async-start | bytes 524288 | tf_op jit(solution)/shard_map/all_to_all | solution.py:456
  51.5 4.0 %collective-permute-start.7 = (f32[1,32,192]{2,1,0:T(8,128)S(1)}, f32[1,32,192]{2,1,0:T(8,128)S(1)}, u32[]{:S(2)}, u32[]{:S(2)}) collective-permute-start(f32[1,32,192]{2,1,0:T(8,128)S(1)} %get-tuple-element.25), channel_id=1, source_target_pairs={{0,16},{16,0},{1,17},{17,1},{2,18},{18,2},{3,19},{19,3},{4,20},{20... | collective-permute-start | bytes 73736 | tf_op jit(solution)/shard_map/ppermute | solution.py:486

commit v10 on v9

--- a/solution.py
+++ b/solution.py
@@ -40,11 +40,6 @@
     )
 
 
-def stacked(value):
-    high, low = split(value)
-    return jnp.concatenate([high, high, low], axis=0)
-
-
 def side_by_side(value):
     high, low = split(value)
     return jnp.concatenate([high, low, high], axis=1)
@@ -79,11 +74,29 @@
         copy.wait()
 
 
+def blocks(rows, size):
+    return [slice(start, start + size) for start in range(0, rows, size)]
+
+
+def shift(here, by):
+    return slice(here.start + by, here.stop + by)
+
+
 def pair_product(pair, value, dims):
     rows = pair.shape[0] // 2
     high, low = split(value)
     both = dot(pair[...], high, dims)
     return both[:rows] + (both[rows:] + dot(pair[:rows], low, dims))
+
+
+def wide_product(pair, value, high, low, out, tokens):
+    width = pair.shape[0] // 2
+    for here in blocks(high.shape[0], 16):
+        high[here], low[here] = split(value[here])
+    both = dot(pair[...], high[...], NT)
+    rest = dot(pair[:width], low[...], NT)
+    for here in blocks(width, 32):
+        out[here, tokens] = both[here] + (both[shift(here, width)] + rest[here])
 
 
 def input_kernel(
@@ -101,6 +114,8 @@
     weight,
     next_weight,
     pair,
+    high,
+    low,
     in_sems,
     out_sems,
     sems,
@@ -130,14 +145,14 @@
         if i == len(chunks) - 1:
             fetch_next.wait()
             next_pair[:width], next_pair[width:] = split(next_weight[...])
-        out[:, chunks[i]] = pair_product(pair, x[chunks[i], :], NT)
+        wide_product(pair, x.at[chunks[i]], high, low, out, chunks[i])
 
     stream(loads, stores, product)
     keep.wait()
     fetch_rows.wait()
 
 
-def target_kernel(chunks, t_hbm, rows, pair, out_hbm, t, out, in_sems, out_sems):
+def target_kernel(chunks, t_hbm, rows, pair, out_hbm, t, out, high, low, in_sems, out_sems):
     loads = [
         pltpu.make_async_copy(t_hbm.at[here], t.at[here], in_sems.at[i])
         for i, here in enumerate(chunks[1:])
@@ -148,14 +163,14 @@
     ]
     for copy in loads[:AHEAD]:
         copy.start()
-    out[:, chunks[0]] = pair_product(pair, rows[...], NT)
+    wide_product(pair, rows, high, low, out, chunks[0])
     stores[0].start()
     for i, copy in enumerate(loads):
         copy.wait()
         if i + AHEAD < len(loads):
             loads[i + AHEAD].start()
         here = chunks[i + 1]
-        out[:, here] = pair_product(pair, t[here, :], NT)
+        wide_product(pair, t.at[here], high, low, out, here)
         stores[i + 1].start()
     for copy in stores:
         copy.wait()
@@ -212,6 +227,10 @@
     xw,
     tw,
     rows,
+    taken,
+    factor,
+    deep,
+    parts,
     in_sems,
     out_sems,
 ):
@@ -247,23 +266,23 @@
     for copy in large:
         copy.wait()
 
-    def first(i):
-        taken = pick[:, chunks[i]]
-        pre = xw[:, chunks[i]] + dot(projected, jnp.concatenate([taken, taken], axis=0))
-        gate = sigmoid(pre)
-        hidden = pre * gate
-        return gate + hidden * (1.0 - gate), stacked(hidden)
-
     dslot = jnp.zeros((2 * width, slots), F32)
-    ready = first(0)
-    for i, here in enumerate(chunks):
-        factor, stack = ready
-        product = dot(grams[...], stack)
-        if i + 1 < len(chunks):
-            ready = first(i + 1)
-        de = (product - tw[:, here]) * factor
-        xw[:, here] = de
-        dslot = dslot + dot(jnp.concatenate(split(de), axis=0), pick[:, here], NT)
+    for tokens in chunks:
+        taken[:slots], taken[slots:] = pick[:, tokens], pick[:, tokens]
+        spread = dot(projected, taken[...])
+        for here in blocks(width, 32):
+            pre = xw[here, tokens] + spread[here]
+            gate = sigmoid(pre)
+            hidden = pre * gate
+            factor[here] = gate + hidden * (1.0 - gate)
+            high, low = split(hidden)
+            deep[here], deep[shift(here, width)], deep[shift(here, 2 * width)] = high, high, low
+        product = dot(grams[...], deep[...])
+        for here in blocks(width, 32):
+            de = (product[here] - tw[here, tokens]) * factor[here]
+            xw[here, tokens] = de
+            parts[here], parts[shift(here, width)] = split(de)
+        dslot = dslot + dot(parts[...], pick[:, tokens], NT)
     for copy in stores:
         copy.start()
 
@@ -317,7 +336,9 @@
 
     def prepare(i):
         loads[i].wait()
-        cat[i % 2] = stacked(de[:, chunks[i]])
+        for here in blocks(width, 32):
+            high, low = split(de[here, chunks[i]])
+            cat[i % 2, here], cat[i % 2, shift(here, width)], cat[i % 2, shift(here, 2 * width)] = high, high, low
 
     for copy in loads:
         copy.start()
@@ -394,6 +415,8 @@
             pltpu.VMEM((width, values), F32),
             pltpu.VMEM((width, values), F32),
             pltpu.VMEM(pair_shape, BF16),
+            pltpu.VMEM((ROWS, values), BF16),
+            pltpu.VMEM((ROWS, values), BF16),
             pltpu.SemaphoreType.DMA((len(chunks),)),
             pltpu.SemaphoreType.DMA((len(chunks),)),
             pltpu.SemaphoreType.DMA((4,)),
@@ -414,6 +437,8 @@
         scratch_shapes=[
             pltpu.VMEM((count, values), F32),
             pltpu.VMEM((width, count), F32),
+            pltpu.VMEM((ROWS, values), BF16),
+            pltpu.VMEM((ROWS, values), BF16),
             pltpu.SemaphoreType.DMA((len(chunks),)),
             pltpu.SemaphoreType.DMA((len(chunks),)),
         ],
@@ -449,6 +474,10 @@
             pltpu.VMEM((width, count), F32),
             pltpu.VMEM((width, count), F32),
             pltpu.VMEM((patches * 16, pixels), F32),
+            pltpu.VMEM((2 * patches * 16, ROWS), BF16),
+            pltpu.VMEM((width, ROWS), F32),
+            pltpu.VMEM((3 * width, ROWS), BF16),
+            pltpu.VMEM((2 * width, ROWS), BF16),
             pltpu.SemaphoreType.DMA((2,)),
             pltpu.SemaphoreType.DMA((len(chunks),)),
         ],

time: 56.4 us -> 56.1 us (level)
  no operation moved by 1% of the time
where the time goes in v10:
time: 56.1 us; the launch traced here: 55.8 us
  Pallas kernels  32.8 us (58%)
  starting transfers between devices  16.8 us (30%)
  waiting for transfers between devices  3.76 us (7%)
  local copies, waits for them, and re-layouts  0.95 us (2%)
  between operations  0.8 us (1%)
  other arithmetic  0.62 us (1%)
    pallas_call x1, Pallas kernels, body(): call(functools.partial(middle_kernel, patches, peers), 'middle', 6 * coun...  9.67 us
    pallas_call x1, Pallas kernels, body(): call(functools.partial(last_kernel, chunks), 'last', 6 * count * values *...  8.49 us
    ppermute x3, starting transfers between devices, body(): lax.ppermute(coarse_input, 'far', [(p, (p + k) % far) for p in range(far)])  7.93 us
    pallas_call x1, Pallas kernels, body(): call(functools.partial(input_kernel, chunks), 'input', 6 * count * values...  6.72 us
    pallas_call x1, Pallas kernels, body(): call(functools.partial(target_kernel, chunks), 'target', 6 * count * valu...  5.28 us
    all_to_all x1, starting transfers between devices, body(): returned = lax.all_to_all(back, patch, 0, 0, tiled=True)  3.72 us
    ppermute x3, starting transfers between devices, body(): lax.ppermute(column, ('lvl', 'y'), [(p, p ^ flip) for p in range(4)])  3.55 us
    ppermute x1, waiting for transfers between devices, body(): coarse_grad = mine + lax.ppermute(theirs, 'lvl', swap)  2.42 us
  transfers between devices with their start and end apart: 9, of which 2 were waited for; matrix products, arithmetic and copies ran while one was open for 0% of the time, Pallas kernels for 41%

profile of v10, /device:TPU:0, one launch (start us, length us, event | category | flops | bytes accessed | tf_op | source)
XLA Modules:
  0.0 55.8 jit_solution(14551699789981965575)
XLA Ops:
  0.6 4.1 %collective-permute-start.1 = (f32[1,32,192]{2,1,0:T(8,128)}, f32[1,32,192]{2,1,0:T(8,128)S(1)}, u32[]{:S(2)}, u32[]{:S(2)}) collective-permute-start(f32[1,32,192]{2,1,0:T(8,128)} %refs_0_.1), channel_id=1, source_target_pairs={{0,8},{4,12},{8,0},{12,4},{1,9},{5,13},{9,1},{13,5},{2,10},{6,14},... | collective-permute-start | bytes 73736 | tf_op jit(solution)/shard_map/ppermute | solution.py:395
  4.7 1.6 %collective-permute-start = (f32[1,32,192]{2,1,0:T(8,128)}, f32[1,32,192]{2,1,0:T(8,128)S(1)}, u32[]{:S(2)}, u32[]{:S(2)}) collective-permute-start(f32[1,32,192]{2,1,0:T(8,128)} %refs_0_.1), channel_id=1, source_target_pairs={{0,4},{4,8},{8,12},{12,0},{1,5},{5,9},{9,13},{13,1},{2,6},{6,10},{... | collective-permute-start | bytes 73736 | tf_op jit(solution)/shard_map/ppermute | solution.py:395
  6.3 2.2 %collective-permute-start.2 = (f32[1,32,192]{2,1,0:T(8,128)}, f32[1,32,192]{2,1,0:T(8,128)S(1)}, u32[]{:S(2)}, u32[]{:S(2)}) collective-permute-start(f32[1,32,192]{2,1,0:T(8,128)} %refs_0_.1), channel_id=1, source_target_pairs={{0,12},{4,0},{8,4},{12,8},{1,13},{5,1},{9,5},{13,9},{2,14},{6,2},{... | collective-permute-start | bytes 73736 | tf_op jit(solution)/shard_map/ppermute | solution.py:395
  8.6 0.0 copy-start
  8.6 6.7 %input.1 = (f32[320,2048]{1,0:T(8,128)}, bf16[640,768]{1,0:T(8,128)(2,1)}, f32[512,768]{1,0:T(8,128)S(1)}, bf16[640,768]{1,0:T(8,128)(2,1)S(1)}) custom-call(f32[2048,768]{1,0:T(8,128)} %bitcast.16, f32[320,768]{1,0:T(8,128)} %bitcast.18, f32[2048,768]{1,0:T(8,128)} %bitcast.14, f32[320,768]{1,0:T(8,128)} %next_weight_hbm.1), custom_call_target="tpu_custom_call" | custom-call | flops 3019898880 | bytes 16252928 | tf_op jit(solution)/shard_map/input/pallas_call | solution.py:400
  15.3 0.0 collective-permute-done.1.refs_2_
  15.3 0.0 collective-permute-done.refs_1_
  15.3 0.0 collective-permute-done.2.refs_3_
  15.3 0.0 copy-done
  15.3 2.5 %collective-permute-start.5 = (f32[4,32,192]{2,1,0:T(8,128)S(1)}, f32[4,32,192]{2,1,0:T(8,128)S(1)}, u32[]{:S(2)}, u32[]{:S(2)}) collective-permute-start(f32[4,32,192]{2,1,0:T(8,128)S(1)} %stack.2.refs_0_), channel_id=1, source_target_pairs={{0,18},{2,16},{16,2},{18,0},{1,19},{3,17},{17,3},{19,1},{4,22},{6,... | collective-permute-start | bytes 294920 | tf_op jit(solution)/shard_map/ppermute | solution.py:428
  17.9 0.5 collective-permute-start.4
  18.4 0.5 collective-permute-start.3
  18.9 5.3 %target.1.refs_4_.tw_hbm = f32[320,2048]{1,0:T(8,128)} custom-call(f32[2048,768]{1,0:T(8,128)} %bitcast.15, f32[512,768]{1,0:T(8,128)S(1)} %get-tuple-element.15.rows, bf16[640,768]{1,0:T(8,128)(2,1)S(1)} %get-tuple-element.16.pair), custom_call_target="tpu_custom_call" | custom-call | flops 3019898880 | bytes 5242880 | tf_op jit(solution)/shard_map/target/pallas_call | solution.py:429
  24.2 0.0 copy-start.1
  24.2 0.0 copy-start.2
  24.2 0.0 copy-start.3
  24.2 0.0 collective-permute-done.5.refs_3_
  24.2 0.0 collective-permute-done.4.refs_2_
  24.3 0.0 collective-permute-done.3.refs_1_
  24.3 0.1 collective-permute-start.6
  24.4 0.5 copy-done.1
  24.9 0.4 copy-done.2
  25.2 0.1 copy-done.3
  25.3 2.3 %prepare.1 = (bf16[320,960]{1,0:T(8,128)(2,1)S(1)}, bf16[640,320]{1,0:T(8,128)(2,1)S(1)}, bf16[384,320]{1,0:T(8,128)(2,1)S(1)}, bf16[128,2048]{1,0:T(8,128)(2,1)S(1)}) custom-call(bf16[640,768]{1,0:T(8,128)(2,1)S(1)} %get-tuple-element.16.pair, f32[192,320]{1,0:T(8,128)S(1)} %copy-done.3, f32[320,320]{1,0:T(8,128)S(1)} %copy-done.2, s32[4,8]{1,0:T(4,128)S(1)} %bitcast.12, ...), custom_call_target="tpu_custom_call" | custom-call | flops 629145600 | bytes 7176192 | tf_op jit(solution)/shard_map/prepare/pallas_call | solution.py:449
  27.6 0.0 collective-permute-done.6.other_ref
  27.6 9.7 %middle.1 = (f32[320,2048]{1,0:T(8,128)}, f32[256,256]{1,0:T(8,128)}) custom-call(s32[4,8]{1,0:T(4,128)S(1)} %bitcast.13, f32[512,192]{1,0:T(8,128)S(1)} %bitcast.10, f32[512,192]{1,0:T(8,128)S(1)} %collective-permute-done.6.other_ref, bf16[320,960]{1,0:T(8,128)(2,1)S(1)} %get-tuple-element.17.grams, bf16[640,320]{1,0:T(8,128)(2,1)S(1)} %get-tuple-element.18.projects, ...), custom_call_target="tpu_custom_call" | custom-call | flops 1258291200 | bytes 5767168 | tf_op jit(solution)/shard_map/middle/pallas_call | solution.py:465
  37.3 3.7 %all-to-all-start = ((f32[16,16,256]{2,1,0:T(8,128)}), f32[16,16,256]{2,1,0:T(8,128)S(1)}, u32[]{:S(2)}, u32[]{:S(2)}) async-start(f32[16,16,256]{2,1,0:T(8,128)} %bitcast.5), calls=%async_computation | async-start | bytes 524288 | tf_op jit(solution)/shard_map/all_to_all | solution.py:485
  41.0 8.5 %last.1.done_ref = f32[2048,768]{1,0:T(8,128)} custom-call(f32[320,2048]{1,0:T(8,128)} %get-tuple-element.22.de_hbm, bf16[640,768]{1,0:T(8,128)(2,1)} %get-tuple-element.23.pair_hbm), custom_call_target="tpu_custom_call" | custom-call | flops 3019898880 | bytes 12582912 | tf_op jit(solution)/shard_map/last/pallas_call | solution.py:487
  49.5 1.3 %all-to-all-done = f32[16,16,256]{2,1,0:T(8,128)S(1)} async-done(((f32[16,16,256]{2,1,0:T(8,128)}), f32[16,16,256]{2,1,0:T(8,128)S(1)}, u32[]{:S(2)}, u32[]{:S(2)}) %all-to-all-start) | async-done | bytes 262176 | tf_op jit(solution)/shard_map/all_to_all | solution.py:485
  50.9 0.3 scatter.1
  51.2 1.6 %collective-permute-start.7 = (f32[1,32,192]{2,1,0:T(8,128)S(1)}, f32[1,32,192]{2,1,0:T(8,128)S(1)}, u32[]{:S(2)}, u32[]{:S(2)}) collective-permute-start(f32[1,32,192]{2,1,0:T(8,128)S(1)} %get-tuple-element.25), channel_id=1, source_target_pairs={{0,16},{16,0},{1,17},{17,1},{2,18},{18,2},{3,19},{19,3},{4,20},{20... | collective-permute-start | bytes 73736 | tf_op jit(solution)/shard_map/ppermute | solution.py:515
  52.7 2.4 %collective-permute-done.7 = f32[1,32,192]{2,1,0:T(8,128)S(1)} collective-permute-done((f32[1,32,192]{2,1,0:T(8,128)S(1)}, f32[1,32,192]{2,1,0:T(8,128)S(1)}, u32[]{:S(2)}, u32[]{:S(2)}) %collective-permute-start.7) | collective-permute-done | bytes 24608 | tf_op jit(solution)/shard_map/ppermute | solution.py:515
  55.1 0.6 %add.3 = f32[1,32,192]{2,1,0:T(8,128)} add(f32[1,32,192]{2,1,0:T(8,128)S(1)} %get-tuple-element.24, f32[1,32,192]{2,1,0:T(8,128)S(1)} %collective-permute-done.7) | non-fusion elementwise | flops 6144 | bytes 73728 | tf_op jit(solution)/shard_map/add | solution.py:515
  (2 shorter events, 0.0 us)
Async XLA Ops:
  0.6 14.7 %collective-permute-start.1 = (f32[1,32,192]{2,1,0:T(8,128)}, f32[1,32,192]{2,1,0:T(8,128)S(1)}, u32[]{:S(2)}, u32[]{:S(2)}) collective-permute-start(f32[1,32,192]{2,1,0:T(8,128)} %refs_0_.1), channel_id=1, source_target_pairs={{0,8},{4,12},{8,0},{12,4},{1,9},{5,13},{9,1},{13,5},{2,10},{6,14},... | collective-permute-start | bytes 73736 | tf_op jit(solution)/shard_map/ppermute | solution.py:395
  4.7 10.6 %collective-permute-start = (f32[1,32,192]{2,1,0:T(8,128)}, f32[1,32,192]{2,1,0:T(8,128)S(1)}, u32[]{:S(2)}, u32[]{:S(2)}) collective-permute-start(f32[1,32,192]{2,1,0:T(8,128)} %refs_0_.1), channel_id=1, source_target_pairs={{0,4},{4,8},{8,12},{12,0},{1,5},{5,9},{9,13},{13,1},{2,6},{6,10},{... | collective-permute-start | bytes 73736 | tf_op jit(solution)/shard_map/ppermute | solution.py:395
  6.3 9.0 %collective-permute-start.2 = (f32[1,32,192]{2,1,0:T(8,128)}, f32[1,32,192]{2,1,0:T(8,128)S(1)}, u32[]{:S(2)}, u32[]{:S(2)}) collective-permute-start(f32[1,32,192]{2,1,0:T(8,128)} %refs_0_.1), channel_id=1, source_target_pairs={{0,12},{4,0},{8,4},{12,8},{1,13},{5,1},{9,5},{13,9},{2,14},{6,2},{... | collective-permute-start | bytes 73736 | tf_op jit(solution)/shard_map/ppermute | solution.py:395
  8.6 6.8 %copy-start = (f32[1,32,192]{2,1,0:T(8,128)S(1)}, f32[1,32,192]{2,1,0:T(8,128)}, u32[]{:S(2)}) copy-start(f32[1,32,192]{2,1,0:T(8,128)} %refs_0_.1) | copy-start | bytes 73732
  15.3 8.9 %collective-permute-start.5 = (f32[4,32,192]{2,1,0:T(8,128)S(1)}, f32[4,32,192]{2,1,0:T(8,128)S(1)}, u32[]{:S(2)}, u32[]{:S(2)}) collective-permute-start(f32[4,32,192]{2,1,0:T(8,128)S(1)} %stack.2.refs_0_), channel_id=1, source_target_pairs={{0,18},{2,16},{16,2},{18,0},{1,19},{3,17},{17,3},{19,1},{4,22},{6,... | collective-permute-start | bytes 294920 | tf_op jit(solution)/shard_map/ppermute | solution.py:428
  17.9 6.4 %collective-permute-start.4 = (f32[4,32,192]{2,1,0:T(8,128)S(1)}, f32[4,32,192]{2,1,0:T(8,128)S(1)}, u32[]{:S(2)}, u32[]{:S(2)}) collective-permute-start(f32[4,32,192]{2,1,0:T(8,128)S(1)} %stack.2.refs_0_), channel_id=1, source_target_pairs={{0,16},{2,18},{16,0},{18,2},{1,17},{3,19},{17,1},{19,3},{4,20},{6,... | collective-permute-start | bytes 294920 | tf_op jit(solution)/shard_map/ppermute | solution.py:428
  18.4 5.8 %collective-permute-start.3 = (f32[4,32,192]{2,1,0:T(8,128)S(1)}, f32[4,32,192]{2,1,0:T(8,128)S(1)}, u32[]{:S(2)}, u32[]{:S(2)}) collective-permute-start(f32[4,32,192]{2,1,0:T(8,128)S(1)} %stack.2.refs_0_), channel_id=1, source_target_pairs={{0,2},{2,0},{16,18},{18,16},{1,3},{3,1},{17,19},{19,17},{4,6},{6,4... | collective-permute-start | bytes 294920 | tf_op jit(solution)/shard_map/ppermute | solution.py:428
  24.2 0.7 %copy-start.1 = (s32[8,4]{0,1:T(4,128)S(1)}, s32[8,4]{0,1:T(4,128)}, u32[]{:S(2)}) copy-start(s32[8,4]{0,1:T(4,128)} %param.12) | copy-start | bytes 388
  24.2 1.0 %copy-start.2 = (f32[320,320]{1,0:T(8,128)S(1)}, f32[320,320]{1,0:T(8,128)}, u32[]{:S(2)}) copy-start(f32[320,320]{1,0:T(8,128)} %xwgt.1) | copy-start | bytes 1228804
  24.2 1.1 %copy-start.3 = (f32[192,320]{1,0:T(8,128)S(1)}, f32[192,320]{1,0:T(8,128)}, u32[]{:S(2)}) copy-start(f32[192,320]{1,0:T(8,128)} %cwgt.1) | copy-start | bytes 737284
  24.3 3.3 %collective-permute-start.6 = (f32[512,192]{1,0:T(8,128)S(1)}, f32[512,192]{1,0:T(8,128)S(1)}, u32[]{:S(2)}, u32[]{:S(2)}) collective-permute-start(f32[512,192]{1,0:T(8,128)S(1)} %bitcast.8), channel_id=1, source_target_pairs={{0,1},{1,0},{2,3},{3,2},{4,5},{5,4},{6,7},{7,6},{8,9},{9,8},{10,11... | collective-permute-start | bytes 1179656 | tf_op jit(solution)/shard_map/ppermute | solution.py:447
  37.3 13.6 %all-to-all-start = ((f32[16,16,256]{2,1,0:T(8,128)}), f32[16,16,256]{2,1,0:T(8,128)S(1)}, u32[]{:S(2)}, u32[]{:S(2)}) async-start(f32[16,16,256]{2,1,0:T(8,128)} %bitcast.5), calls=%async_computation | async-start | bytes 524288 | tf_op jit(solution)/shard_map/all_to_all | solution.py:485
  51.2 4.0 %collective-permute-start.7 = (f32[1,32,192]{2,1,0:T(8,128)S(1)}, f32[1,32,192]{2,1,0:T(8,128)S(1)}, u32[]{:S(2)}, u32[]{:S(2)}) collective-permute-start(f32[1,32,192]{2,1,0:T(8,128)S(1)} %get-tuple-element.25), channel_id=1, source_target_pairs={{0,16},{16,0},{1,17},{17,1},{2,18},{18,2},{3,19},{19,3},{4,20},{20... | collective-permute-start | bytes 73736 | tf_op jit(solution)/shard_map/ppermute | solution.py:515

commit v11 on v10

--- a/solution.py
+++ b/solution.py
@@ -105,10 +105,12 @@
     weight_hbm,
     t_hbm,
     next_weight_hbm,
+    crops_hbm,
     out_hbm,
     pair_hbm,
     next_rows,
     next_pair,
+    crops,
     x,
     out,
     weight,
@@ -125,6 +127,7 @@
     keep = pltpu.make_async_copy(pair, pair_hbm, sems.at[1])
     fetch_next = pltpu.make_async_copy(next_weight_hbm, next_weight, sems.at[2])
     fetch_rows = pltpu.make_async_copy(t_hbm.at[: next_rows.shape[0]], next_rows, sems.at[3])
+    fetch_crops = pltpu.make_async_copy(crops_hbm, crops, sems.at[4])
     fetch.start()
     loads = [
         pltpu.make_async_copy(x_hbm.at[here], x.at[here], in_sems.at[i]) for i, here in enumerate(chunks)
@@ -142,6 +145,7 @@
             fetch_next.start()
         if i == 1:
             fetch_rows.start()
+            fetch_crops.start()
         if i == len(chunks) - 1:
             fetch_next.wait()
             next_pair[:width], next_pair[width:] = split(next_weight[...])
@@ -150,9 +154,33 @@
     stream(loads, stores, product)
     keep.wait()
     fetch_rows.wait()
-
-
-def target_kernel(chunks, t_hbm, rows, pair, out_hbm, t, out, high, low, in_sems, out_sems):
+    fetch_crops.wait()
+
+
+def target_kernel(
+    chunks,
+    t_hbm,
+    cwgt_hbm,
+    xwgt_hbm,
+    rows,
+    pair,
+    out_hbm,
+    coarses,
+    projects,
+    t,
+    out,
+    high,
+    low,
+    cwgt,
+    xwgt,
+    in_sems,
+    out_sems,
+    sems,
+):
+    fetches = [
+        pltpu.make_async_copy(cwgt_hbm, cwgt, sems.at[0]),
+        pltpu.make_async_copy(xwgt_hbm, xwgt, sems.at[1]),
+    ]
     loads = [
         pltpu.make_async_copy(t_hbm.at[here], t.at[here], in_sems.at[i])
         for i, here in enumerate(chunks[1:])
@@ -161,7 +189,7 @@
         pltpu.make_async_copy(out.at[:, here], out_hbm.at[:, here], out_sems.at[i])
         for i, here in enumerate(chunks)
     ]
-    for copy in loads[:AHEAD]:
+    for copy in loads[:AHEAD] + fetches:
         copy.start()
     wide_product(pair, rows, high, low, out, chunks[0])
     stores[0].start()
@@ -169,6 +197,11 @@
         copy.wait()
         if i + AHEAD < len(loads):
             loads[i + AHEAD].start()
+        if i == 0:
+            for fetch in fetches:
+                fetch.wait()
+            coarses[...] = jnp.concatenate(split(cwgt[...]), axis=0)
+            projects[...] = jnp.concatenate(split(xwgt[...]), axis=0)
         here = chunks[i + 1]
         wide_product(pair, t.at[here], high, low, out, here)
         stores[i + 1].start()
@@ -176,13 +209,11 @@
         copy.wait()
 
 
-def prepare_kernel(patches, pair, cwgt, xwgt, crops_ref, before_ref, grams, projects, coarses, pick):
+def prepare_kernel(patches, pair, crops_ref, before_ref, grams, pick):
     del before_ref
-    width = xwgt.shape[0]
+    width = grams.shape[0]
     high, low = pair[:width], pair[width:]
     grams[...] = side_by_side(dot3((high, low), (high, low), NT) + dot(low, low, NT))
-    projects[...] = jnp.concatenate(split(xwgt[...]), axis=0)
-    coarses[...] = jnp.concatenate(split(cwgt[...]), axis=0)
     pick[...] = chosen(crops_ref, patches, pick.shape[1] // patches)
 
 
@@ -210,43 +241,26 @@
     return jnp.where(slot == wanted, 1.0, 0.0).astype(BF16)
 
 
-def middle_kernel(
+def context_kernel(
     patches,
     peers,
     crops_ref,
     own_ref,
     other_ref,
-    grams,
+    coarses,
     projects,
-    coarses,
-    pick,
     xw_hbm,
-    tw_hbm,
-    de_hbm,
-    send_ref,
-    xw,
-    tw,
+    projected_ref,
+    slope_ref,
+    first_ref,
     rows,
-    taken,
-    factor,
-    deep,
-    parts,
-    in_sems,
-    out_sems,
+    sem,
 ):
+    fetch = pltpu.make_async_copy(xw_hbm.at[:, : first_ref.shape[1]], first_ref, sem)
+    fetch.start()
     pixels = coarses.shape[0] // 2
-    width, count = xw.shape
-    slots = patches * 16
+    width = projects.shape[1]
     far = peers // 4
-    chunks = chunk_rows(0, count)
-    large = [pltpu.make_async_copy(xw_hbm, xw, in_sems.at[0]), pltpu.make_async_copy(tw_hbm, tw, in_sems.at[1])]
-    stores = [
-        pltpu.make_async_copy(xw.at[:, here], de_hbm.at[:, here], out_sems.at[i])
-        for i, here in enumerate(chunks)
-    ]
-    for copy in large:
-        copy.start()
-
     me, side = lax.axis_index(("far", "y", "core")), lax.axis_index("lvl")
     for j in range(patches):
         frame, top, left = crops_ref[0, j], crops_ref[1, j], crops_ref[2, j]
@@ -260,34 +274,96 @@
             rows[j * 16 + a * 4 : j * 16 + a * 4 + 4, :] = pltpu.roll(line, SIDE - left, 0)[:4, :]
     pre = dot3(split(rows[...]), (coarses[:pixels], coarses[pixels:]))
     gate = sigmoid(pre)
-    slope = (gate * (1.0 + pre * (1.0 - gate))).T
+    slope_ref[...] = gate * (1.0 + pre * (1.0 - gate))
     projected = dot3(split(pre * gate), (projects[:width], projects[width:])).T
-    projected = jnp.concatenate(split(projected), axis=1)
-    for copy in large:
-        copy.wait()
-
-    dslot = jnp.zeros((2 * width, slots), F32)
-    for tokens in chunks:
+    projected_ref[...] = jnp.concatenate(split(projected), axis=1)
+    fetch.wait()
+
+
+def middle_kernel(
+    chunks,
+    projected,
+    grams,
+    pick,
+    first,
+    xw_hbm,
+    tw_hbm,
+    pair_hbm,
+    de_hbm,
+    de_ref,
+    deep_ref,
+    dslot_ref,
+    xw,
+    tw,
+    taken,
+    factor,
+    deep,
+    parts,
+    xw_sems,
+    tw_sems,
+    out_sems,
+    sems,
+):
+    width = grams.shape[0]
+    slots = pick.shape[0]
+    each = slots // len(chunks)
+    tw_loads = [
+        pltpu.make_async_copy(tw_hbm.at[:, here], tw.at[:, here], tw_sems.at[i]) for i, here in enumerate(chunks)
+    ]
+    xw_loads = [
+        pltpu.make_async_copy(xw_hbm.at[:, here], xw.at[:, here], xw_sems.at[i])
+        for i, here in enumerate(chunks[1:])
+    ]
+    stores = [
+        pltpu.make_async_copy(xw.at[:, here], de_hbm.at[:, here], out_sems.at[i])
+        for i, here in enumerate(chunks[:-1])
+    ]
+    fetches = [
+        pltpu.make_async_copy(pair_hbm, deep_ref.at[: 2 * width], sems.at[0]),
+        pltpu.make_async_copy(pair_hbm.at[:width], deep_ref.at[2 * width :], sems.at[1]),
+    ]
+    tw_loads[0].start()
+    for pair in zip(xw_loads, tw_loads[1:]):
+        for copy in pair:
+            copy.start()
+    for copy in fetches:
+        copy.start()
+    for i, tokens in enumerate(chunks):
+        if i > 0:
+            xw_loads[i - 1].wait()
+            tw_loads[i].wait()
+        source = first if i == 0 else xw.at[:, tokens]
+        target = de_ref if i == len(chunks) - 1 else xw.at[:, tokens]
         taken[:slots], taken[slots:] = pick[:, tokens], pick[:, tokens]
-        spread = dot(projected, taken[...])
+        spread = dot(projected[...], taken[...])
         for here in blocks(width, 32):
-            pre = xw[here, tokens] + spread[here]
+            pre = source[here] + spread[here]
             gate = sigmoid(pre)
             hidden = pre * gate
             factor[here] = gate + hidden * (1.0 - gate)
             high, low = split(hidden)
             deep[here], deep[shift(here, width)], deep[shift(here, 2 * width)] = high, high, low
         product = dot(grams[...], deep[...])
+        if i == 0:
+            tw_loads[0].wait()
         for here in blocks(width, 32):
             de = (product[here] - tw[here, tokens]) * factor[here]
-            xw[here, tokens] = de
+            target[here] = de
             parts[here], parts[shift(here, width)] = split(de)
-        dslot = dslot + dot(parts[...], pick[:, tokens], NT)
-    for copy in stores:
-        copy.start()
-
-    dcontext = pair_product(projects, dslot[:width] + dslot[width:], NN)
-    grad = pair_product(coarses, dcontext * slope, NN).T
+        mine = slice(i * each, (i + 1) * each)
+        dslot_ref[mine] = dot(pick[mine, tokens], parts[...], NT)
+        if i < len(stores):
+            stores[i].start()
+    for copy in stores + fetches:
+        copy.wait()
+
+
+def closing_kernel(patches, crops_ref, dslot_ref, slope_ref, coarses, projects, send_ref):
+    pixels = coarses.shape[0] // 2
+    width = projects.shape[1]
+    dslot = dslot_ref[:, :width] + dslot_ref[:, width:]
+    dcontext = dot3(split(dslot), (projects[:width], projects[width:]), NT)
+    grad = dot3(split(dcontext * slope_ref[...]), (coarses[:pixels], coarses[pixels:]), NT)
     shape = (patches * 16, LANES - pixels)
     slot = lax.broadcasted_iota(jnp.int32, shape, 0) % 16
     top = row_value(crops_ref, 1, patches, shape, 0, 16)
@@ -298,8 +374,6 @@
         start = pl.ds(pl.multiple_of(crops_ref[0, j] * 16, 16), 16)
         send_ref[start, :pixels] = grad[j * 16 : j * 16 + 16, :]
         send_ref[start, pixels:] = number[j * 16 : j * 16 + 16, :]
-    for copy in stores:
-        copy.wait()
 
 
 def scatter_kernel(message_ref, done_ref, mine_ref, other_ref, total):
@@ -316,39 +390,31 @@
     other_ref[0] = total[pl.ds(pl.multiple_of((1 - side) * half, half), half), :]
 
 
-def last_kernel(chunks, de_hbm, pair_hbm, *refs):
-    out_hbm, de, out, deep, cat, in_sems, out_sems, sems = refs
+def last_kernel(chunks, de_hbm, first, deep, out_hbm, de, out, cat, in_sems, out_sems):
     width = de.shape[0]
-    fetches = [
-        pltpu.make_async_copy(pair_hbm, deep.at[: 2 * width], sems.at[0]),
-        pltpu.make_async_copy(pair_hbm.at[:width], deep.at[2 * width :], sems.at[1]),
-    ]
-    for copy in fetches:
-        copy.start()
+    order = chunks[-1:] + chunks[:-1]
     loads = [
         pltpu.make_async_copy(de_hbm.at[:, here], de.at[:, here], in_sems.at[i])
-        for i, here in enumerate(chunks)
+        for i, here in enumerate(order[1:])
     ]
     stores = [
-        pltpu.make_async_copy(out.at[here], out_hbm.at[here], out_sems.at[i])
-        for i, here in enumerate(chunks)
-    ]
-
-    def prepare(i):
-        loads[i].wait()
+        pltpu.make_async_copy(out.at[here], out_hbm.at[here], out_sems.at[i]) for i, here in enumerate(order)
+    ]
+
+    def prepare(i, source):
         for here in blocks(width, 32):
-            high, low = split(de[here, chunks[i]])
+            high, low = split(source[here])
             cat[i % 2, here], cat[i % 2, shift(here, width)], cat[i % 2, shift(here, 2 * width)] = high, high, low
 
     for copy in loads:
         copy.start()
-    prepare(0)
-    for copy in fetches:
-        copy.wait()
-    for i, here in enumerate(chunks):
+    prepare(0, first)
+    for i, here in enumerate(order):
+        if i < len(loads):
+            loads[i].wait()
         out[here, :] = dot(cat[i % 2], deep[...], TN)
-        if i + 1 < len(chunks):
-            prepare(i + 1)
+        if i < len(loads):
+            prepare(i + 1, de.at[:, order[i + 1]])
         stores[i].start()
     for copy in stores:
         copy.wait()
@@ -397,7 +463,7 @@
     chunks = chunk_rows(0, count)
     pair_shape = (2 * width, values)
     x, t = fine_input.reshape(count, values), fine_target.reshape(count, values)
-    xw, pair, rows, next_pair = call(
+    xw, pair, rows, next_pair, crops = call(
         functools.partial(input_kernel, chunks),
         "input",
         6 * count * values * width,
@@ -406,9 +472,10 @@
             pltpu.HBM(pair_shape, BF16),
             pltpu.VMEM((ROWS, values), F32),
             pltpu.VMEM(pair_shape, BF16),
+            pltpu.VMEM((4, patches), jnp.int32),
         ),
-        in_specs=[HBM] * 4,
-        out_specs=(HBM, HBM, VMEM, VMEM),
+        in_specs=[HBM] * 5,
+        out_specs=(HBM, HBM, VMEM, VMEM, VMEM),
         scratch_shapes=[
             pltpu.VMEM((count, values), F32),
             pltpu.VMEM((width, count), F32),
@@ -419,69 +486,99 @@
             pltpu.VMEM((ROWS, values), BF16),
             pltpu.SemaphoreType.DMA((len(chunks),)),
             pltpu.SemaphoreType.DMA((len(chunks),)),
-            pltpu.SemaphoreType.DMA((4,)),
+            pltpu.SemaphoreType.DMA((5,)),
         ],
-    )(*fixed(x, in_weight.T, t, out_weight))
+    )(*fixed(x, in_weight.T, t, out_weight, crops.T))
     column = stack(column, xw)
     own = [column]
     for flip in range(1, 4):
         own.append(lax.ppermute(column, ("lvl", "y"), [(p, p ^ flip) for p in range(4)]))
-    tw = call(
+    tw, coarses, projects = call(
         functools.partial(target_kernel, chunks),
         "target",
         6 * count * values * width,
-        pltpu.HBM((width, count), F32),
-        limit=ROOM,
-        in_specs=[HBM, VMEM, VMEM],
-        out_specs=HBM,
+        (
+            pltpu.HBM((width, count), F32),
+            pltpu.VMEM((2 * pixels, width), BF16),
+            pltpu.VMEM((2 * width, width), BF16),
+        ),
+        limit=ROOM,
+        in_specs=[HBM] * 3 + [VMEM] * 2,
+        out_specs=(HBM, VMEM, VMEM),
         scratch_shapes=[
             pltpu.VMEM((count, values), F32),
             pltpu.VMEM((width, count), F32),
             pltpu.VMEM((ROWS, values), BF16),
             pltpu.VMEM((ROWS, values), BF16),
-            pltpu.SemaphoreType.DMA((len(chunks),)),
-            pltpu.SemaphoreType.DMA((len(chunks),)),
+            pltpu.VMEM((pixels, width), F32),
+            pltpu.VMEM((width, width), F32),
+            pltpu.SemaphoreType.DMA((len(chunks),)),
+            pltpu.SemaphoreType.DMA((len(chunks),)),
+            pltpu.SemaphoreType.DMA((2,)),
         ],
-    )(*fixed(t), *near(rows, next_pair))
+    )(*fixed(t, coarse_weight, context_weight), *near(rows, next_pair))
     own = stack(own, tw).reshape(-1, pixels)
     other = lax.ppermute(own, "core", swap)
-    crops = crops.T
-    prepared = call(
+    (crops,) = near(crops)
+    grams, pick = call(
         functools.partial(prepare_kernel, patches),
         "prepare",
         8 * values * width * width,
+        (pltpu.VMEM((width, 3 * width), BF16), pltpu.VMEM((patches * 16, count), BF16)),
+        limit=ROOM,
+        in_specs=[VMEM, SMEM, HBM],
+        out_specs=(VMEM, VMEM),
+    )(*near(next_pair), crops, own)
+
+    projected, slope, first = call(
+        functools.partial(context_kernel, patches, peers),
+        "context",
+        6 * patches * 16 * width * width,
         (
-            pltpu.VMEM((width, 3 * width), BF16),
-            pltpu.VMEM((2 * width, width), BF16),
-            pltpu.VMEM((2 * pixels, width), BF16),
-            pltpu.VMEM((patches * 16, count), BF16),
+            pltpu.VMEM((width, 2 * patches * 16), BF16),
+            pltpu.VMEM((patches * 16, width), F32),
+            pltpu.VMEM((width, ROWS), F32),
         ),
         limit=ROOM,
-        in_specs=[VMEM, VMEM, VMEM, SMEM, HBM],
-        out_specs=(VMEM,) * 4,
-    )(*near(next_pair), coarse_weight, context_weight, crops, own)
-
-    shape = (peers * 16, LANES)
-    de, back = call(
-        functools.partial(middle_kernel, patches, peers),
+        in_specs=[SMEM] + [VMEM] * 4 + [HBM],
+        out_specs=(VMEM,) * 3,
+        scratch_shapes=[pltpu.VMEM((patches * 16, pixels), F32), pltpu.SemaphoreType.DMA],
+    )(crops, own, other, *near(coarses, projects), *fixed(xw))
+    de, last_de, deep, dslot = call(
+        functools.partial(middle_kernel, chunks),
         "middle",
         6 * count * width * width,
-        (pltpu.HBM((width, count), F32), jax.ShapeDtypeStruct(shape, F32)),
-        limit=ROOM,
-        in_specs=[SMEM] + [VMEM] * 6 + [HBM] * 2,
-        out_specs=(HBM, VMEM),
+        (
+            pltpu.HBM((width, count), F32),
+            pltpu.VMEM((width, ROWS), F32),
+            pltpu.VMEM((3 * width, values), BF16),
+            pltpu.VMEM((patches * 16, 2 * width), F32),
+        ),
+        limit=ROOM,
+        in_specs=[VMEM] * 4 + [HBM] * 3,
+        out_specs=(HBM,) + (VMEM,) * 3,
         scratch_shapes=[
             pltpu.VMEM((width, count), F32),
             pltpu.VMEM((width, count), F32),
-            pltpu.VMEM((patches * 16, pixels), F32),
             pltpu.VMEM((2 * patches * 16, ROWS), BF16),
             pltpu.VMEM((width, ROWS), F32),
             pltpu.VMEM((3 * width, ROWS), BF16),
             pltpu.VMEM((2 * width, ROWS), BF16),
+            pltpu.SemaphoreType.DMA((len(chunks),)),
+            pltpu.SemaphoreType.DMA((len(chunks),)),
+            pltpu.SemaphoreType.DMA((len(chunks),)),
             pltpu.SemaphoreType.DMA((2,)),
-            pltpu.SemaphoreType.DMA((len(chunks),)),
         ],
-    )(crops, own, other, *near(*prepared), *fixed(xw, tw))
+    )(*near(projected, grams, pick, first), *fixed(xw, tw, pair))
+    back = call(
+        functools.partial(closing_kernel, patches),
+        "closing",
+        6 * patches * 16 * width * width,
+        jax.ShapeDtypeStruct((peers * 16, LANES), F32),
+        limit=ROOM,
+        in_specs=[SMEM] + [VMEM] * 4,
+        out_specs=VMEM,
+    )(crops, *near(dslot, slope, coarses, projects))
     returned = lax.all_to_all(back, patch, 0, 0, tiled=True)
 
     fine_grad = call(
@@ -489,18 +586,17 @@
         "last",
         6 * count * values * width,
         pltpu.HBM((count, values), F32),
-        in_specs=[HBM, HBM],
+        limit=ROOM,
+        in_specs=[HBM, VMEM, VMEM],
         out_specs=HBM,
         scratch_shapes=[
             pltpu.VMEM((width, count), F32),
             pltpu.VMEM((count, values), F32),
-            pltpu.VMEM((3 * width, values), BF16),
             pltpu.VMEM((2, 3 * width, ROWS), BF16),
             pltpu.SemaphoreType.DMA((len(chunks),)),
             pltpu.SemaphoreType.DMA((len(chunks),)),
-            pltpu.SemaphoreType.DMA((2,)),
         ],
-    )(*fixed(de, pair))
+    )(*fixed(de), *near(last_de, deep))
     part = (1, half, pixels)
     mine, theirs = call(
         scatter_kernel,

time: 56.1 us -> 56 us (level)
  waiting for transfers between devices: 3.76 us -> 5.65 us
  Pallas kernels: 32.8 us -> 31.8 us
  local copies, waits for them, and re-layouts: 0.95 us -> 0.01 us
    all_to_all x1, waiting for transfers between devices: 1.33 us -> 3.2 us  [body(): returned = lax.all_to_all(back, patch, 0, 0, tiled=True)]
    pallas_call x1, Pallas kernels: 8.49 us -> 6.8 us  [body(): call(functools.partial(last_kernel, chunks), 'last', 6 * count * values *...]
    pallas_call x1, Pallas kernels: 5.28 us -> 6.5 us  [body(): call(functools.partial(target_kernel, chunks), 'target', 6 * count * valu...]
    unnamed x8 -> x2, local copies, waits for them, and re-layouts: 0.95 us -> 0.01 us
    pallas_call x1 -> x3, Pallas kernels: 9.67 us -> 9.31 us  [the longest x1 5.06 us: body(): call(functools.partial(middle_kernel, chunks), 'middle', 6 * count * widt...]
  transfers between devices with their start and end apart: 9 -> 9, of which waited for: 2 -> 2; matrix products, arithmetic and copies ran while one was open for 0% -> 0% of each run, Pallas kernels for 41% -> 40%
where the time goes in v11:
time: 56 us; the launch traced here: 55.7 us
  Pallas kernels  31.8 us (57%)
  starting transfers between devices  16.8 us (30%)
  waiting for transfers between devices  5.65 us (10%)
  between operations  0.78 us (1%)
  other arithmetic  0.62 us (1%)
    ppermute x3, starting transfers between devices, body(): lax.ppermute(coarse_input, 'far', [(p, (p + k) % far) for p in range(far)])  7.93 us
    pallas_call x1, Pallas kernels, body(): call(functools.partial(last_kernel, chunks), 'last', 6 * count * values *...  6.8 us
    pallas_call x1, Pallas kernels, body(): call(functools.partial(input_kernel, chunks), 'input', 6 * count * values...  6.74 us
    pallas_call x1, Pallas kernels, body(): call(functools.partial(target_kernel, chunks), 'target', 6 * count * valu...  6.5 us
    pallas_call x1, Pallas kernels, body(): call(functools.partial(middle_kernel, chunks), 'middle', 6 * count * widt...  5.06 us
    all_to_all x1, starting transfers between devices, body(): returned = lax.all_to_all(back, patch, 0, 0, tiled=True)  3.71 us
    ppermute x3, starting transfers between devices, body(): lax.ppermute(column, ('lvl', 'y'), [(p, p ^ flip) for p in range(4)])  3.55 us
    all_to_all x1, waiting for transfers between devices, body(): returned = lax.all_to_all(back, patch, 0, 0, tiled=True)  3.2 us
  transfers between devices with their start and end apart: 9, of which 2 were waited for; matrix products, arithmetic and copies ran while one was open for 0% of the time, Pallas kernels for 40%

profile of v11, /device:TPU:0, one launch (start us, length us, event | category | flops | bytes accessed | tf_op | source)
XLA Modules:
  0.0 55.7 jit_solution(7638829836610580780)
XLA Ops:
  0.6 4.1 %collective-permute-start.1 = (f32[1,32,192]{2,1,0:T(8,128)}, f32[1,32,192]{2,1,0:T(8,128)S(1)}, u32[]{:S(2)}, u32[]{:S(2)}) collective-permute-start(f32[1,32,192]{2,1,0:T(8,128)} %refs_0_.1), channel_id=1, source_target_pairs={{0,8},{4,12},{8,0},{12,4},{1,9},{5,13},{9,1},{13,5},{2,10},{6,14},... | collective-permute-start | bytes 73736 | tf_op jit(solution)/shard_map/ppermute | solution.py:461
  4.7 1.6 %collective-permute-start = (f32[1,32,192]{2,1,0:T(8,128)}, f32[1,32,192]{2,1,0:T(8,128)S(1)}, u32[]{:S(2)}, u32[]{:S(2)}) collective-permute-start(f32[1,32,192]{2,1,0:T(8,128)} %refs_0_.1), channel_id=1, source_target_pairs={{0,4},{4,8},{8,12},{12,0},{1,5},{5,9},{9,13},{13,1},{2,6},{6,10},{... | collective-permute-start | bytes 73736 | tf_op jit(solution)/shard_map/ppermute | solution.py:461
  6.3 2.2 %collective-permute-start.2 = (f32[1,32,192]{2,1,0:T(8,128)}, f32[1,32,192]{2,1,0:T(8,128)S(1)}, u32[]{:S(2)}, u32[]{:S(2)}) collective-permute-start(f32[1,32,192]{2,1,0:T(8,128)} %refs_0_.1), channel_id=1, source_target_pairs={{0,12},{4,0},{8,4},{12,8},{1,13},{5,1},{9,5},{13,9},{2,14},{6,2},{... | collective-permute-start | bytes 73736 | tf_op jit(solution)/shard_map/ppermute | solution.py:461
  8.6 0.0 copy-start
  8.6 6.7 %input.1 = (f32[320,2048]{1,0:T(8,128)}, bf16[640,768]{1,0:T(8,128)(2,1)}, f32[512,768]{1,0:T(8,128)S(1)}, bf16[640,768]{1,0:T(8,128)(2,1)S(1)}, s32[4,8]{1,0:T(4,128)S(1)}) custom-call(f32[2048,768]{1,0:T(8,128)} %bitcast.13, f32[320,768]{1,0:T(8,128)} %bitcast.16, f32[2048,768]{1,0:T(8,128)} %bitcast.14, f32[320,768]{1,0:T(8,128)} %next_weight_hbm.1, ...), custom_call_target="tpu_custom_call" | custom-call | flops 3019898880 | bytes 16253184 | tf_op jit(solution)/shard_map/input/pallas_call | solution.py:466
  15.3 0.0 collective-permute-done.1.refs_2_
  15.3 0.0 collective-permute-done.refs_1_
  15.3 0.0 collective-permute-done.2.refs_3_
  15.3 0.0 copy-done
  15.4 2.5 %collective-permute-start.5 = (f32[4,32,192]{2,1,0:T(8,128)S(1)}, f32[4,32,192]{2,1,0:T(8,128)S(1)}, u32[]{:S(2)}, u32[]{:S(2)}) collective-permute-start(f32[4,32,192]{2,1,0:T(8,128)S(1)} %stack.2.refs_0_), channel_id=1, source_target_pairs={{0,18},{2,16},{16,2},{18,0},{1,19},{3,17},{17,3},{19,1},{4,22},{6,... | collective-permute-start | bytes 294920 | tf_op jit(solution)/shard_map/ppermute | solution.py:495
  17.9 0.5 collective-permute-start.4
  18.4 0.5 collective-permute-start.3
  18.9 6.5 %target.1 = (f32[320,2048]{1,0:T(8,128)}, bf16[384,320]{1,0:T(8,128)(2,1)S(1)}, bf16[640,320]{1,0:T(8,128)(2,1)S(1)}) custom-call(f32[2048,768]{1,0:T(8,128)} %bitcast.15, f32[192,320]{1,0:T(8,128)} %cwgt_hbm.1, f32[320,320]{1,0:T(8,128)} %xwgt_hbm.1, f32[512,768]{1,0:T(8,128)S(1)} %get-tuple-element.23.rows, bf16[640,768]{1,0:T(8,128)(2,1)S(1)} %get-tuple-element.24.pair), custom_call_target="tpu_custom_call" | custom-call | flops 3019898880 | bytes 7864320 | tf_op jit(solution)/shard_map/target/pallas_call | solution.py:496
  25.4 0.0 collective-permute-done.5.refs_3_
  25.4 0.0 collective-permute-done.4.refs_2_
  25.5 0.0 collective-permute-done.3.refs_1_
  25.5 0.1 collective-permute-start.6
  25.6 2.1 %prepare.1 = (bf16[320,960]{1,0:T(8,128)(2,1)S(1)}, bf16[128,2048]{1,0:T(8,128)(2,1)S(1)}) custom-call(bf16[640,768]{1,0:T(8,128)(2,1)S(1)} %get-tuple-element.24.pair, s32[4,8]{1,0:T(4,128)S(1)} %get-tuple-element.21.crops_ref, f32[512,192]{1,0:T(8,128)S(1)} %bitcast.9), custom_call_target="tpu_custom_call" | custom-call | flops 629145600 | bytes 4554752 | tf_op jit(solution)/shard_map/prepare/pallas_call | solution.py:523
  27.7 0.0 collective-permute-done.6.other_ref
  27.7 2.1 %context.1 = (bf16[320,256]{1,0:T(8,128)(2,1)S(1)}, f32[128,320]{1,0:T(8,128)S(1)}, f32[320,512]{1,0:T(8,128)S(1)}) custom-call(s32[4,8]{1,0:T(4,128)S(1)} %get-tuple-element.21.crops_ref, f32[512,192]{1,0:T(8,128)S(1)} %bitcast.10, f32[512,192]{1,0:T(8,128)S(1)} %collective-permute-done.6.other_ref, bf16[384,320]{1,0:T(8,128)(2,1)S(1)} %get-tuple-element.26.coarses, ...), custom_call_target="tpu_custom_call" | custom-call | flops 78643200 | bytes 2293760 | tf_op jit(solution)/shard_map/context/pallas_call | solution.py:533
  29.9 5.1 %middle.1 = (f32[320,2048]{1,0:T(8,128)}, f32[320,512]{1,0:T(8,128)S(1)}, bf16[960,768]{1,0:T(8,128)(2,1)S(1)}, f32[128,640]{1,0:T(8,128)S(1)}) custom-call(bf16[320,256]{1,0:T(8,128)(2,1)S(1)} %get-tuple-element.28.projected, bf16[320,960]{1,0:T(8,128)(2,1)S(1)} %get-tuple-element.29.grams, bf16[128,2048]{1,0:T(8,128)(2,1)S(1)} %get-tuple-element.30.pick, ...), custom_call_target="tpu_custom_call" | custom-call | flops 1258291200 | bytes 13107200 | tf_op jit(solution)/shard_map/middle/pallas_call | solution.py:547
  34.9 2.1 %closing.1 = f32[256,256]{1,0:T(8,128)} custom-call(s32[4,8]{1,0:T(4,128)S(1)} %get-tuple-element.21.crops_ref, f32[128,640]{1,0:T(8,128)S(1)} %get-tuple-element.33.dslot_ref, f32[128,320]{1,0:T(8,128)S(1)} %get-tuple-element.34.slope_ref, bf16[384,320]{1,0:T(8,128)(2,1)S(1)} %get-tuple-element.26.coarses, bf16[640,320]{1,0:T(8,128)(2,1)S(1)} %get-tuple-element.27.projects), custom_call_target="tpu_custom_call" | custom-call | flops 78643200 | bytes 524288 | tf_op jit(solution)/shard_map/closing/pallas_call | solution.py:573
  37.1 3.7 %all-to-all-start = ((f32[16,16,256]{2,1,0:T(8,128)}), f32[16,16,256]{2,1,0:T(8,128)S(1)}, u32[]{:S(2)}, u32[]{:S(2)}) async-start(f32[16,16,256]{2,1,0:T(8,128)} %bitcast.5), calls=%async_computation | async-start | bytes 524288 | tf_op jit(solution)/shard_map/all_to_all | solution.py:582
  40.8 6.8 %last.1.done_ref = f32[2048,768]{1,0:T(8,128)} custom-call(f32[320,2048]{1,0:T(8,128)} %get-tuple-element.35.de_hbm, f32[320,512]{1,0:T(8,128)S(1)} %get-tuple-element.36.first, bf16[960,768]{1,0:T(8,128)(2,1)S(1)} %get-tuple-element.37.deep), custom_call_target="tpu_custom_call" | custom-call | flops 3019898880 | bytes 12582912 | tf_op jit(solution)/shard_map/last/pallas_call | solution.py:584
  47.6 3.2 %all-to-all-done = f32[16,16,256]{2,1,0:T(8,128)S(1)} async-done(((f32[16,16,256]{2,1,0:T(8,128)}), f32[16,16,256]{2,1,0:T(8,128)S(1)}, u32[]{:S(2)}, u32[]{:S(2)}) %all-to-all-start) | async-done | bytes 262176 | tf_op jit(solution)/shard_map/all_to_all | solution.py:582
  50.8 0.3 scatter.1
  51.1 1.5 %collective-permute-start.7 = (f32[1,32,192]{2,1,0:T(8,128)S(1)}, f32[1,32,192]{2,1,0:T(8,128)S(1)}, u32[]{:S(2)}, u32[]{:S(2)}) collective-permute-start(f32[1,32,192]{2,1,0:T(8,128)S(1)} %get-tuple-element.39), channel_id=1, source_target_pairs={{0,16},{16,0},{1,17},{17,1},{2,18},{18,2},{3,19},{19,3},{4,20},{20... | collective-permute-start | bytes 73736 | tf_op jit(solution)/shard_map/ppermute | solution.py:611
  52.6 2.4 %collective-permute-done.7 = f32[1,32,192]{2,1,0:T(8,128)S(1)} collective-permute-done((f32[1,32,192]{2,1,0:T(8,128)S(1)}, f32[1,32,192]{2,1,0:T(8,128)S(1)}, u32[]{:S(2)}, u32[]{:S(2)}) %collective-permute-start.7) | collective-permute-done | bytes 24608 | tf_op jit(solution)/shard_map/ppermute | solution.py:611
  55.0 0.6 %add.3 = f32[1,32,192]{2,1,0:T(8,128)} add(f32[1,32,192]{2,1,0:T(8,128)S(1)} %get-tuple-element.38, f32[1,32,192]{2,1,0:T(8,128)S(1)} %collective-permute-done.7) | non-fusion elementwise | flops 6144 | bytes 73728 | tf_op jit(solution)/shard_map/add | solution.py:611
  (2 shorter events, 0.0 us)
Async XLA Ops:
  0.6 14.7 %collective-permute-start.1 = (f32[1,32,192]{2,1,0:T(8,128)}, f32[1,32,192]{2,1,0:T(8,128)S(1)}, u32[]{:S(2)}, u32[]{:S(2)}) collective-permute-start(f32[1,32,192]{2,1,0:T(8,128)} %refs_0_.1), channel_id=1, source_target_pairs={{0,8},{4,12},{8,0},{12,4},{1,9},{5,13},{9,1},{13,5},{2,10},{6,14},... | collective-permute-start | bytes 73736 | tf_op jit(solution)/shard_map/ppermute | solution.py:461
  4.7 10.6 %collective-permute-start = (f32[1,32,192]{2,1,0:T(8,128)}, f32[1,32,192]{2,1,0:T(8,128)S(1)}, u32[]{:S(2)}, u32[]{:S(2)}) collective-permute-start(f32[1,32,192]{2,1,0:T(8,128)} %refs_0_.1), channel_id=1, source_target_pairs={{0,4},{4,8},{8,12},{12,0},{1,5},{5,9},{9,13},{13,1},{2,6},{6,10},{... | collective-permute-start | bytes 73736 | tf_op jit(solution)/shard_map/ppermute | solution.py:461
  6.3 9.0 %collective-permute-start.2 = (f32[1,32,192]{2,1,0:T(8,128)}, f32[1,32,192]{2,1,0:T(8,128)S(1)}, u32[]{:S(2)}, u32[]{:S(2)}) collective-permute-start(f32[1,32,192]{2,1,0:T(8,128)} %refs_0_.1), channel_id=1, source_target_pairs={{0,12},{4,0},{8,4},{12,8},{1,13},{5,1},{9,5},{13,9},{2,14},{6,2},{... | collective-permute-start | bytes 73736 | tf_op jit(solution)/shard_map/ppermute | solution.py:461
  8.6 6.8 %copy-start = (f32[1,32,192]{2,1,0:T(8,128)S(1)}, f32[1,32,192]{2,1,0:T(8,128)}, u32[]{:S(2)}) copy-start(f32[1,32,192]{2,1,0:T(8,128)} %refs_0_.1) | copy-start | bytes 73732
  15.4 10.1 %collective-permute-start.5 = (f32[4,32,192]{2,1,0:T(8,128)S(1)}, f32[4,32,192]{2,1,0:T(8,128)S(1)}, u32[]{:S(2)}, u32[]{:S(2)}) collective-permute-start(f32[4,32,192]{2,1,0:T(8,128)S(1)} %stack.2.refs_0_), channel_id=1, source_target_pairs={{0,18},{2,16},{16,2},{18,0},{1,19},{3,17},{17,3},{19,1},{4,22},{6,... | collective-permute-start | bytes 294920 | tf_op jit(solution)/shard_map/ppermute | solution.py:495
  17.9 7.6 %collective-permute-start.4 = (f32[4,32,192]{2,1,0:T(8,128)S(1)}, f32[4,32,192]{2,1,0:T(8,128)S(1)}, u32[]{:S(2)}, u32[]{:S(2)}) collective-permute-start(f32[4,32,192]{2,1,0:T(8,128)S(1)} %stack.2.refs_0_), channel_id=1, source_target_pairs={{0,16},{2,18},{16,0},{18,2},{1,17},{3,19},{17,1},{19,3},{4,20},{6,... | collective-permute-start | bytes 294920 | tf_op jit(solution)/shard_map/ppermute | solution.py:495
  18.4 7.0 %collective-permute-start.3 = (f32[4,32,192]{2,1,0:T(8,128)S(1)}, f32[4,32,192]{2,1,0:T(8,128)S(1)}, u32[]{:S(2)}, u32[]{:S(2)}) collective-permute-start(f32[4,32,192]{2,1,0:T(8,128)S(1)} %stack.2.refs_0_), channel_id=1, source_target_pairs={{0,2},{2,0},{16,18},{18,16},{1,3},{3,1},{17,19},{19,17},{4,6},{6,4... | collective-permute-start | bytes 294920 | tf_op jit(solution)/shard_map/ppermute | solution.py:495
  25.5 2.2 %collective-permute-start.6 = (f32[512,192]{1,0:T(8,128)S(1)}, f32[512,192]{1,0:T(8,128)S(1)}, u32[]{:S(2)}, u32[]{:S(2)}) collective-permute-start(f32[512,192]{1,0:T(8,128)S(1)} %bitcast.8), channel_id=1, source_target_pairs={{0,1},{1,0},{2,3},{3,2},{4,5},{5,4},{6,7},{7,6},{8,9},{9,8},{10,11... | collective-permute-start | bytes 1179656 | tf_op jit(solution)/shard_map/ppermute | solution.py:521
  37.1 13.7 %all-to-all-start = ((f32[16,16,256]{2,1,0:T(8,128)}), f32[16,16,256]{2,1,0:T(8,128)S(1)}, u32[]{:S(2)}, u32[]{:S(2)}) async-start(f32[16,16,256]{2,1,0:T(8,128)} %bitcast.5), calls=%async_computation | async-start | bytes 524288 | tf_op jit(solution)/shard_map/all_to_all | solution.py:582
  51.1 4.0 %collective-permute-start.7 = (f32[1,32,192]{2,1,0:T(8,128)S(1)}, f32[1,32,192]{2,1,0:T(8,128)S(1)}, u32[]{:S(2)}, u32[]{:S(2)}) collective-permute-start(f32[1,32,192]{2,1,0:T(8,128)S(1)} %get-tuple-element.39), channel_id=1, source_target_pairs={{0,16},{16,0},{1,17},{17,1},{2,18},{18,2},{3,19},{19,3},{4,20},{20... | collective-permute-start | bytes 73736 | tf_op jit(solution)/shard_map/ppermute | solution.py:611

commit v12 on v11

--- a/solution.py
+++ b/solution.py
@@ -197,7 +197,7 @@
         copy.wait()
         if i + AHEAD < len(loads):
             loads[i + AHEAD].start()
-        if i == 0:
+        if i == len(loads) - 1:
             for fetch in fetches:
                 fetch.wait()
             coarses[...] = jnp.concatenate(split(cwgt[...]), axis=0)
@@ -209,12 +209,20 @@
         copy.wait()
 
 
-def prepare_kernel(patches, pair, crops_ref, before_ref, grams, pick):
+def prepare_kernel(patches, pair, crops_ref, before_ref, grams, pick, lay, number):
     del before_ref
     width = grams.shape[0]
-    high, low = pair[:width], pair[width:]
-    grams[...] = side_by_side(dot3((high, low), (high, low), NT) + dot(low, low, NT))
+    both = dot(pair[...], pair[:width], NT)
+    grams[...] = side_by_side(both[:width] + (both[width:] + both[width:].T))
     pick[...] = chosen(crops_ref, patches, pick.shape[1] // patches)
+    frame = row_value(crops_ref, 0, patches, (1, patches * 16), 1, 16)
+    slot = lax.broadcasted_iota(jnp.int32, (1, patches * 16), 1) % 16
+    line = lax.broadcasted_iota(jnp.int32, lay.shape, 0)
+    lay[...] = jnp.where(line == frame * 16 + slot, 1.0, 0.0).astype(BF16)
+    slot = lax.broadcasted_iota(jnp.int32, number.shape, 0) % 16
+    top = row_value(crops_ref, 1, patches, number.shape, 0, 16)
+    left = row_value(crops_ref, 2, patches, number.shape, 0, 16)
+    number[...] = ((top + slot // 4) * SIDE + left + slot % 4).astype(F32)
 
 
 def stack_kernel(*refs):
@@ -328,52 +336,54 @@
             copy.start()
     for copy in fetches:
         copy.start()
-    for i, tokens in enumerate(chunks):
-        if i > 0:
-            xw_loads[i - 1].wait()
-            tw_loads[i].wait()
+
+    def begin(i):
+        tokens = chunks[i]
         source = first if i == 0 else xw.at[:, tokens]
-        target = de_ref if i == len(chunks) - 1 else xw.at[:, tokens]
         taken[:slots], taken[slots:] = pick[:, tokens], pick[:, tokens]
         spread = dot(projected[...], taken[...])
         for here in blocks(width, 32):
             pre = source[here] + spread[here]
             gate = sigmoid(pre)
             hidden = pre * gate
-            factor[here] = gate + hidden * (1.0 - gate)
+            factor[i % 2, here] = gate + hidden * (1.0 - gate)
             high, low = split(hidden)
-            deep[here], deep[shift(here, width)], deep[shift(here, 2 * width)] = high, high, low
-        product = dot(grams[...], deep[...])
-        if i == 0:
-            tw_loads[0].wait()
+            for part, value in enumerate((high, high, low)):
+                deep[i % 2, shift(here, part * width)] = value
+
+    begin(0)
+    for i, tokens in enumerate(chunks):
+        tw_loads[i].wait()
+        if i + 1 < len(chunks):
+            xw_loads[i].wait()
+        target = de_ref if i == len(chunks) - 1 else xw.at[:, tokens]
+        product = dot(grams[...], deep[i % 2])
+        if i + 1 < len(chunks):
+            begin(i + 1)
         for here in blocks(width, 32):
-            de = (product[here] - tw[here, tokens]) * factor[here]
+            de = (product[here] - tw[here, tokens]) * factor[i % 2, here]
             target[here] = de
             parts[here], parts[shift(here, width)] = split(de)
         mine = slice(i * each, (i + 1) * each)
-        dslot_ref[mine] = dot(pick[mine, tokens], parts[...], NT)
+        both = dot(pick[mine, tokens], parts[...], NT)
+        dslot_ref[mine] = both[:, :width] + both[:, width:]
         if i < len(stores):
             stores[i].start()
     for copy in stores + fetches:
         copy.wait()
 
 
-def closing_kernel(patches, crops_ref, dslot_ref, slope_ref, coarses, projects, send_ref):
-    pixels = coarses.shape[0] // 2
-    width = projects.shape[1]
-    dslot = dslot_ref[:, :width] + dslot_ref[:, width:]
-    dcontext = dot3(split(dslot), (projects[:width], projects[width:]), NT)
-    grad = dot3(split(dcontext * slope_ref[...]), (coarses[:pixels], coarses[pixels:]), NT)
-    shape = (patches * 16, LANES - pixels)
-    slot = lax.broadcasted_iota(jnp.int32, shape, 0) % 16
-    top = row_value(crops_ref, 1, patches, shape, 0, 16)
-    left = row_value(crops_ref, 2, patches, shape, 0, 16)
-    number = ((top + slot // 4) * SIDE + left + slot % 4).astype(F32)
-    send_ref[...] = jnp.zeros_like(send_ref)
-    for j in range(patches):
-        start = pl.ds(pl.multiple_of(crops_ref[0, j] * 16, 16), 16)
-        send_ref[start, :pixels] = grad[j * 16 : j * 16 + 16, :]
-        send_ref[start, pixels:] = number[j * 16 : j * 16 + 16, :]
+def through(value, pair):
+    count, rows = value.shape[0], pair.shape[0] // 2
+    high, low = split(value)
+    both = dot(jnp.concatenate([high, low], axis=0), pair[:rows], NT)
+    return both[:count] + (both[count:] + dot(high, pair[rows:], NT))
+
+
+def closing_kernel(dslot_ref, slope_ref, coarses, projects, lay, number, send_ref):
+    grad = through(through(dslot_ref[...], projects) * slope_ref[...], coarses)
+    high, low = split(jnp.concatenate([grad, number[...]], axis=1))
+    send_ref[...] = dot(lay[...], high) + dot(lay[...], low)
 
 
 def scatter_kernel(message_ref, done_ref, mine_ref, other_ref, total):
@@ -520,14 +530,19 @@
     own = stack(own, tw).reshape(-1, pixels)
     other = lax.ppermute(own, "core", swap)
     (crops,) = near(crops)
-    grams, pick = call(
+    grams, pick, lay, number = call(
         functools.partial(prepare_kernel, patches),
         "prepare",
         8 * values * width * width,
-        (pltpu.VMEM((width, 3 * width), BF16), pltpu.VMEM((patches * 16, count), BF16)),
+        (
+            pltpu.VMEM((width, 3 * width), BF16),
+            pltpu.VMEM((patches * 16, count), BF16),
+            pltpu.VMEM((peers * 16, patches * 16), BF16),
+            pltpu.VMEM((patches * 16, LANES - pixels), F32),
+        ),
         limit=ROOM,
         in_specs=[VMEM, SMEM, HBM],
-        out_specs=(VMEM, VMEM),
+        out_specs=(VMEM,) * 4,
     )(*near(next_pair), crops, own)
 
     projected, slope, first = call(
@@ -552,7 +567,7 @@
             pltpu.HBM((width, count), F32),
             pltpu.VMEM((width, ROWS), F32),
             pltpu.VMEM((3 * width, values), BF16),
-            pltpu.VMEM((patches * 16, 2 * width), F32),
+            pltpu.VMEM((patches * 16, width), F32),
         ),
         limit=ROOM,
         in_specs=[VMEM] * 4 + [HBM] * 3,
@@ -561,8 +576,8 @@
             pltpu.VMEM((width, count), F32),
             pltpu.VMEM((width, count), F32),
             pltpu.VMEM((2 * patches * 16, ROWS), BF16),
-            pltpu.VMEM((width, ROWS), F32),
-            pltpu.VMEM((3 * width, ROWS), BF16),
+            pltpu.VMEM((2, width, ROWS), F32),
+            pltpu.VMEM((2, 3 * width, ROWS), BF16),
             pltpu.VMEM((2 * width, ROWS), BF16),
             pltpu.SemaphoreType.DMA((len(chunks),)),
             pltpu.SemaphoreType.DMA((len(chunks),)),
@@ -571,14 +586,14 @@
         ],
     )(*near(projected, grams, pick, first), *fixed(xw, tw, pair))
     back = call(
-        functools.partial(closing_kernel, patches),
+        closing_kernel,
         "closing",
         6 * patches * 16 * width * width,
         jax.ShapeDtypeStruct((peers * 16, LANES), F32),
         limit=ROOM,
-        in_specs=[SMEM] + [VMEM] * 4,
+        in_specs=[VMEM] * 6,
         out_specs=VMEM,
-    )(crops, *near(dslot, slope, coarses, projects))
+    )(*near(dslot, slope, coarses, projects, lay, number))
     returned = lax.all_to_all(back, patch, 0, 0, tiled=True)
 
     fine_grad = call(

time: 56 us -> 54.4 us (0.971)
  Pallas kernels: 31.8 us -> 30.3 us
    pallas_call x1, Pallas kernels: 6.5 us -> 5.44 us  [body(): call(functools.partial(target_kernel, chunks), 'target', 6 * count * valu...]
  transfers between devices with their start and end apart: 9 -> 9, of which waited for: 2 -> 2; matrix products, arithmetic and copies ran while one was open for 0% -> 0% of each run, Pallas kernels for 40% -> 39%
where the time goes in v12:
time: 54.4 us; the launch traced here: 54.1 us
  Pallas kernels  30.3 us (56%)
  starting transfers between devices  16.8 us (31%)
  waiting for transfers between devices  5.67 us (10%)
  between operations  0.78 us (1%)
  other arithmetic  0.62 us (1%)
    ppermute x3, starting transfers between devices, body(): lax.ppermute(coarse_input, 'far', [(p, (p + k) % far) for p in range(far)])  7.93 us
    pallas_call x1, Pallas kernels, body(): call(functools.partial(last_kernel, chunks), 'last', 6 * count * values *...  6.8 us
    pallas_call x1, Pallas kernels, body(): call(functools.partial(input_kernel, chunks), 'input', 6 * count * values...  6.74 us
    pallas_call x1, Pallas kernels, body(): call(functools.partial(target_kernel, chunks), 'target', 6 * count * valu...  5.44 us
    pallas_call x1, Pallas kernels, body(): call(functools.partial(middle_kernel, chunks), 'middle', 6 * count * widt...  5.3 us
    all_to_all x1, starting transfers between devices, body(): returned = lax.all_to_all(back, patch, 0, 0, tiled=True)  3.71 us
    ppermute x3, starting transfers between devices, body(): lax.ppermute(column, ('lvl', 'y'), [(p, p ^ flip) for p in range(4)])  3.55 us
    all_to_all x1, waiting for transfers between devices, body(): returned = lax.all_to_all(back, patch, 0, 0, tiled=True)  3.2 us
  transfers between devices with their start and end apart: 9, of which 2 were waited for; matrix products, arithmetic and copies ran while one was open for 0% of the time, Pallas kernels for 39%

profile of v12, /device:TPU:0, one launch (start us, length us, event | category | flops | bytes accessed | tf_op | source)
XLA Modules:
  0.0 54.1 jit_solution(11782259205620240296)
XLA Ops:
  0.6 4.1 %collective-permute-start.1 = (f32[1,32,192]{2,1,0:T(8,128)}, f32[1,32,192]{2,1,0:T(8,128)S(1)}, u32[]{:S(2)}, u32[]{:S(2)}) collective-permute-start(f32[1,32,192]{2,1,0:T(8,128)} %refs_0_.1), channel_id=1, source_target_pairs={{0,8},{4,12},{8,0},{12,4},{1,9},{5,13},{9,1},{13,5},{2,10},{6,14},... | collective-permute-start | bytes 73736 | tf_op jit(solution)/shard_map/ppermute | solution.py:471
  4.7 1.6 %collective-permute-start = (f32[1,32,192]{2,1,0:T(8,128)}, f32[1,32,192]{2,1,0:T(8,128)S(1)}, u32[]{:S(2)}, u32[]{:S(2)}) collective-permute-start(f32[1,32,192]{2,1,0:T(8,128)} %refs_0_.1), channel_id=1, source_target_pairs={{0,4},{4,8},{8,12},{12,0},{1,5},{5,9},{9,13},{13,1},{2,6},{6,10},{... | collective-permute-start | bytes 73736 | tf_op jit(solution)/shard_map/ppermute | solution.py:471
  6.3 2.2 %collective-permute-start.2 = (f32[1,32,192]{2,1,0:T(8,128)}, f32[1,32,192]{2,1,0:T(8,128)S(1)}, u32[]{:S(2)}, u32[]{:S(2)}) collective-permute-start(f32[1,32,192]{2,1,0:T(8,128)} %refs_0_.1), channel_id=1, source_target_pairs={{0,12},{4,0},{8,4},{12,8},{1,13},{5,1},{9,5},{13,9},{2,14},{6,2},{... | collective-permute-start | bytes 73736 | tf_op jit(solution)/shard_map/ppermute | solution.py:471
  8.6 0.0 copy-start
  8.6 6.7 %input.1 = (f32[320,2048]{1,0:T(8,128)}, bf16[640,768]{1,0:T(8,128)(2,1)}, f32[512,768]{1,0:T(8,128)S(1)}, bf16[640,768]{1,0:T(8,128)(2,1)S(1)}, s32[4,8]{1,0:T(4,128)S(1)}) custom-call(f32[2048,768]{1,0:T(8,128)} %bitcast.13, f32[320,768]{1,0:T(8,128)} %bitcast.16, f32[2048,768]{1,0:T(8,128)} %bitcast.14, f32[320,768]{1,0:T(8,128)} %next_weight_hbm.1, ...), custom_call_target="tpu_custom_call" | custom-call | flops 3019898880 | bytes 16253184 | tf_op jit(solution)/shard_map/input/pallas_call | solution.py:476
  15.3 0.0 collective-permute-done.1.refs_2_
  15.3 0.0 collective-permute-done.refs_1_
  15.3 0.0 collective-permute-done.2.refs_3_
  15.3 0.0 copy-done
  15.4 2.5 %collective-permute-start.5 = (f32[4,32,192]{2,1,0:T(8,128)S(1)}, f32[4,32,192]{2,1,0:T(8,128)S(1)}, u32[]{:S(2)}, u32[]{:S(2)}) collective-permute-start(f32[4,32,192]{2,1,0:T(8,128)S(1)} %stack.2.refs_0_), channel_id=1, source_target_pairs={{0,18},{2,16},{16,2},{18,0},{1,19},{3,17},{17,3},{19,1},{4,22},{6,... | collective-permute-start | bytes 294920 | tf_op jit(solution)/shard_map/ppermute | solution.py:505
  17.9 0.5 collective-permute-start.4
  18.4 0.5 collective-permute-start.3
  18.9 5.4 %target.1 = (f32[320,2048]{1,0:T(8,128)}, bf16[384,320]{1,0:T(8,128)(2,1)S(1)}, bf16[640,320]{1,0:T(8,128)(2,1)S(1)}) custom-call(f32[2048,768]{1,0:T(8,128)} %bitcast.15, f32[192,320]{1,0:T(8,128)} %cwgt_hbm.1, f32[320,320]{1,0:T(8,128)} %xwgt_hbm.1, f32[512,768]{1,0:T(8,128)S(1)} %get-tuple-element.25.rows, bf16[640,768]{1,0:T(8,128)(2,1)S(1)} %get-tuple-element.26.pair), custom_call_target="tpu_custom_call" | custom-call | flops 3019898880 | bytes 7864320 | tf_op jit(solution)/shard_map/target/pallas_call | solution.py:506
  24.4 0.0 collective-permute-done.5.refs_3_
  24.4 0.0 collective-permute-done.4.refs_2_
  24.4 0.0 collective-permute-done.3.refs_1_
  24.4 0.1 collective-permute-start.6
  24.5 1.9 %prepare.1 = (bf16[320,960]{1,0:T(8,128)(2,1)S(1)}, bf16[128,2048]{1,0:T(8,128)(2,1)S(1)}, bf16[256,128]{1,0:T(8,128)(2,1)S(1)}, f32[128,64]{1,0:T(8,128)S(1)}) custom-call(bf16[640,768]{1,0:T(8,128)(2,1)S(1)} %get-tuple-element.26.pair, s32[4,8]{1,0:T(4,128)S(1)} %get-tuple-element.23.crops_ref, f32[512,192]{1,0:T(8,128)S(1)} %bitcast.9), custom_call_target="tpu_custom_call" | custom-call | flops 629145600 | bytes 4882432 | tf_op jit(solution)/shard_map/prepare/pallas_call | solution.py:533
  26.4 0.0 collective-permute-done.6.other_ref
  26.4 2.1 %context.1 = (bf16[320,256]{1,0:T(8,128)(2,1)S(1)}, f32[128,320]{1,0:T(8,128)S(1)}, f32[320,512]{1,0:T(8,128)S(1)}) custom-call(s32[4,8]{1,0:T(4,128)S(1)} %get-tuple-element.23.crops_ref, f32[512,192]{1,0:T(8,128)S(1)} %bitcast.10, f32[512,192]{1,0:T(8,128)S(1)} %collective-permute-done.6.other_ref, bf16[384,320]{1,0:T(8,128)(2,1)S(1)} %get-tuple-element.28.coarses, ...), custom_call_target="tpu_custom_call" | custom-call | flops 78643200 | bytes 2293760 | tf_op jit(solution)/shard_map/context/pallas_call | solution.py:548
  28.5 5.3 %middle.1 = (f32[320,2048]{1,0:T(8,128)}, f32[320,512]{1,0:T(8,128)S(1)}, bf16[960,768]{1,0:T(8,128)(2,1)S(1)}, f32[128,320]{1,0:T(8,128)S(1)}) custom-call(bf16[320,256]{1,0:T(8,128)(2,1)S(1)} %get-tuple-element.30.projected, bf16[320,960]{1,0:T(8,128)(2,1)S(1)} %get-tuple-element.31.grams, bf16[128,2048]{1,0:T(8,128)(2,1)S(1)} %get-tuple-element.32.pick, ...), custom_call_target="tpu_custom_call" | custom-call | flops 1258291200 | bytes 12779520 | tf_op jit(solution)/shard_map/middle/pallas_call | solution.py:562
  33.8 1.7 %closing.1 = f32[256,256]{1,0:T(8,128)} custom-call(f32[128,320]{1,0:T(8,128)S(1)} %get-tuple-element.35.dslot_ref, f32[128,320]{1,0:T(8,128)S(1)} %get-tuple-element.36.slope_ref, bf16[384,320]{1,0:T(8,128)(2,1)S(1)} %get-tuple-element.28.coarses, bf16[640,320]{1,0:T(8,128)(2,1)S(1)} %get-tuple-element.29.projects, ...), custom_call_target="tpu_custom_call" | custom-call | flops 78643200 | bytes 524288 | tf_op jit(solution)/shard_map/closing/pallas_call | solution.py:588
  35.5 3.7 %all-to-all-start = ((f32[16,16,256]{2,1,0:T(8,128)}), f32[16,16,256]{2,1,0:T(8,128)S(1)}, u32[]{:S(2)}, u32[]{:S(2)}) async-start(f32[16,16,256]{2,1,0:T(8,128)} %bitcast.5), calls=%async_computation | async-start | bytes 524288 | tf_op jit(solution)/shard_map/all_to_all | solution.py:597
  39.2 6.8 %last.1.done_ref = f32[2048,768]{1,0:T(8,128)} custom-call(f32[320,2048]{1,0:T(8,128)} %get-tuple-element.39.de_hbm, f32[320,512]{1,0:T(8,128)S(1)} %get-tuple-element.40.first, bf16[960,768]{1,0:T(8,128)(2,1)S(1)} %get-tuple-element.41.deep), custom_call_target="tpu_custom_call" | custom-call | flops 3019898880 | bytes 12582912 | tf_op jit(solution)/shard_map/last/pallas_call | solution.py:599
  46.1 3.2 %all-to-all-done = f32[16,16,256]{2,1,0:T(8,128)S(1)} async-done(((f32[16,16,256]{2,1,0:T(8,128)}), f32[16,16,256]{2,1,0:T(8,128)S(1)}, u32[]{:S(2)}, u32[]{:S(2)}) %all-to-all-start) | async-done | bytes 262176 | tf_op jit(solution)/shard_map/all_to_all | solution.py:597
  49.3 0.3 scatter.1
  49.5 1.5 %collective-permute-start.7 = (f32[1,32,192]{2,1,0:T(8,128)S(1)}, f32[1,32,192]{2,1,0:T(8,128)S(1)}, u32[]{:S(2)}, u32[]{:S(2)}) collective-permute-start(f32[1,32,192]{2,1,0:T(8,128)S(1)} %get-tuple-element.43), channel_id=1, source_target_pairs={{0,16},{16,0},{1,17},{17,1},{2,18},{18,2},{3,19},{19,3},{4,20},{20... | collective-permute-start | bytes 73736 | tf_op jit(solution)/shard_map/ppermute | solution.py:626
  51.1 2.4 %collective-permute-done.7 = f32[1,32,192]{2,1,0:T(8,128)S(1)} collective-permute-done((f32[1,32,192]{2,1,0:T(8,128)S(1)}, f32[1,32,192]{2,1,0:T(8,128)S(1)}, u32[]{:S(2)}, u32[]{:S(2)}) %collective-permute-start.7) | collective-permute-done | bytes 24608 | tf_op jit(solution)/shard_map/ppermute | solution.py:626
  53.5 0.6 %add.3 = f32[1,32,192]{2,1,0:T(8,128)} add(f32[1,32,192]{2,1,0:T(8,128)S(1)} %get-tuple-element.42, f32[1,32,192]{2,1,0:T(8,128)S(1)} %collective-permute-done.7) | non-fusion elementwise | flops 6144 | bytes 73728 | tf_op jit(solution)/shard_map/add | solution.py:626
  (2 shorter events, 0.0 us)
Async XLA Ops:
  0.6 14.7 %collective-permute-start.1 = (f32[1,32,192]{2,1,0:T(8,128)}, f32[1,32,192]{2,1,0:T(8,128)S(1)}, u32[]{:S(2)}, u32[]{:S(2)}) collective-permute-start(f32[1,32,192]{2,1,0:T(8,128)} %refs_0_.1), channel_id=1, source_target_pairs={{0,8},{4,12},{8,0},{12,4},{1,9},{5,13},{9,1},{13,5},{2,10},{6,14},... | collective-permute-start | bytes 73736 | tf_op jit(solution)/shard_map/ppermute | solution.py:471
  4.7 10.6 %collective-permute-start = (f32[1,32,192]{2,1,0:T(8,128)}, f32[1,32,192]{2,1,0:T(8,128)S(1)}, u32[]{:S(2)}, u32[]{:S(2)}) collective-permute-start(f32[1,32,192]{2,1,0:T(8,128)} %refs_0_.1), channel_id=1, source_target_pairs={{0,4},{4,8},{8,12},{12,0},{1,5},{5,9},{9,13},{13,1},{2,6},{6,10},{... | collective-permute-start | bytes 73736 | tf_op jit(solution)/shard_map/ppermute | solution.py:471
  6.3 9.0 %collective-permute-start.2 = (f32[1,32,192]{2,1,0:T(8,128)}, f32[1,32,192]{2,1,0:T(8,128)S(1)}, u32[]{:S(2)}, u32[]{:S(2)}) collective-permute-start(f32[1,32,192]{2,1,0:T(8,128)} %refs_0_.1), channel_id=1, source_target_pairs={{0,12},{4,0},{8,4},{12,8},{1,13},{5,1},{9,5},{13,9},{2,14},{6,2},{... | collective-permute-start | bytes 73736 | tf_op jit(solution)/shard_map/ppermute | solution.py:471
  8.6 6.8 %copy-start = (f32[1,32,192]{2,1,0:T(8,128)S(1)}, f32[1,32,192]{2,1,0:T(8,128)}, u32[]{:S(2)}) copy-start(f32[1,32,192]{2,1,0:T(8,128)} %refs_0_.1) | copy-start | bytes 73732
  15.4 9.0 %collective-permute-start.5 = (f32[4,32,192]{2,1,0:T(8,128)S(1)}, f32[4,32,192]{2,1,0:T(8,128)S(1)}, u32[]{:S(2)}, u32[]{:S(2)}) collective-permute-start(f32[4,32,192]{2,1,0:T(8,128)S(1)} %stack.2.refs_0_), channel_id=1, source_target_pairs={{0,18},{2,16},{16,2},{18,0},{1,19},{3,17},{17,3},{19,1},{4,22},{6,... | collective-permute-start | bytes 294920 | tf_op jit(solution)/shard_map/ppermute | solution.py:505
  17.9 6.5 %collective-permute-start.4 = (f32[4,32,192]{2,1,0:T(8,128)S(1)}, f32[4,32,192]{2,1,0:T(8,128)S(1)}, u32[]{:S(2)}, u32[]{:S(2)}) collective-permute-start(f32[4,32,192]{2,1,0:T(8,128)S(1)} %stack.2.refs_0_), channel_id=1, source_target_pairs={{0,16},{2,18},{16,0},{18,2},{1,17},{3,19},{17,1},{19,3},{4,20},{6,... | collective-permute-start | bytes 294920 | tf_op jit(solution)/shard_map/ppermute | solution.py:505
  18.4 6.0 %collective-permute-start.3 = (f32[4,32,192]{2,1,0:T(8,128)S(1)}, f32[4,32,192]{2,1,0:T(8,128)S(1)}, u32[]{:S(2)}, u32[]{:S(2)}) collective-permute-start(f32[4,32,192]{2,1,0:T(8,128)S(1)} %stack.2.refs_0_), channel_id=1, source_target_pairs={{0,2},{2,0},{16,18},{18,16},{1,3},{3,1},{17,19},{19,17},{4,6},{6,4... | collective-permute-start | bytes 294920 | tf_op jit(solution)/shard_map/ppermute | solution.py:505
  24.4 2.0 %collective-permute-start.6 = (f32[512,192]{1,0:T(8,128)S(1)}, f32[512,192]{1,0:T(8,128)S(1)}, u32[]{:S(2)}, u32[]{:S(2)}) collective-permute-start(f32[512,192]{1,0:T(8,128)S(1)} %bitcast.8), channel_id=1, source_target_pairs={{0,1},{1,0},{2,3},{3,2},{4,5},{5,4},{6,7},{7,6},{8,9},{9,8},{10,11... | collective-permute-start | bytes 1179656 | tf_op jit(solution)/shard_map/ppermute | solution.py:531
  35.5 13.7 %all-to-all-start = ((f32[16,16,256]{2,1,0:T(8,128)}), f32[16,16,256]{2,1,0:T(8,128)S(1)}, u32[]{:S(2)}, u32[]{:S(2)}) async-start(f32[16,16,256]{2,1,0:T(8,128)} %bitcast.5), calls=%async_computation | async-start | bytes 524288 | tf_op jit(solution)/shard_map/all_to_all | solution.py:597
  49.5 4.0 %collective-permute-start.7 = (f32[1,32,192]{2,1,0:T(8,128)S(1)}, f32[1,32,192]{2,1,0:T(8,128)S(1)}, u32[]{:S(2)}, u32[]{:S(2)}) collective-permute-start(f32[1,32,192]{2,1,0:T(8,128)S(1)} %get-tuple-element.43), channel_id=1, source_target_pairs={{0,16},{16,0},{1,17},{17,1},{2,18},{18,2},{3,19},{19,3},{4,20},{20... | collective-permute-start | bytes 73736 | tf_op jit(solution)/shard_map/ppermute | solution.py:626

commit v13 on v12

--- a/solution.py
+++ b/solution.py
@@ -15,7 +15,6 @@
 TN = (((0,), (0,)), ((), ()))
 ROWS = 512
 SIDE = 8
-AHEAD = 2
 LANES = 256
 LIMIT = 60 * 1024 * 1024
 ROOM = 40 * 1024 * 1024
@@ -61,19 +60,6 @@
     )
 
 
-def stream(loads, stores, product):
-    for copy in loads[:AHEAD]:
-        copy.start()
-    for i, store in enumerate(stores):
-        loads[i].wait()
-        if i + AHEAD < len(loads):
-            loads[i + AHEAD].start()
-        product(i)
-        store.start()
-    for copy in stores:
-        copy.wait()
-
-
 def blocks(rows, size):
     return [slice(start, start + size) for start in range(0, rows, size)]
 
@@ -89,10 +75,17 @@
     return both[:rows] + (both[rows:] + dot(pair[:rows], low, dims))
 
 
-def wide_product(pair, value, high, low, out, tokens):
+def chunk(i):
+    return pl.ds(pl.multiple_of(i * ROWS, ROWS), ROWS)
+
+
+def split_rows(source, high, low):
+    for here in blocks(high.shape[0], 16):
+        high[here], low[here] = split(source[here])
+
+
+def wide_chunk(pair, high, low, out, tokens):
     width = pair.shape[0] // 2
-    for here in blocks(high.shape[0], 16):
-        high[here], low[here] = split(value[here])
     both = dot(pair[...], high[...], NT)
     rest = dot(pair[:width], low[...], NT)
     for here in blocks(width, 32):
@@ -100,7 +93,6 @@
 
 
 def input_kernel(
-    chunks,
     x_hbm,
     weight_hbm,
     t_hbm,
@@ -123,52 +115,62 @@
     sems,
 ):
     width = weight.shape[0]
+    steps = x.shape[0] // ROWS
     fetch = pltpu.make_async_copy(weight_hbm, weight, sems.at[0])
     keep = pltpu.make_async_copy(pair, pair_hbm, sems.at[1])
     fetch_next = pltpu.make_async_copy(next_weight_hbm, next_weight, sems.at[2])
     fetch_rows = pltpu.make_async_copy(t_hbm.at[: next_rows.shape[0]], next_rows, sems.at[3])
     fetch_crops = pltpu.make_async_copy(crops_hbm, crops, sems.at[4])
+
+    def load(i):
+        return pltpu.make_async_copy(x_hbm.at[chunk(i)], x.at[chunk(i)], in_sems.at[i])
+
+    def store(i):
+        return pltpu.make_async_copy(out.at[:, chunk(i)], out_hbm.at[:, chunk(i)], out_sems.at[i])
+
     fetch.start()
-    loads = [
-        pltpu.make_async_copy(x_hbm.at[here], x.at[here], in_sems.at[i]) for i, here in enumerate(chunks)
-    ]
-    stores = [
-        pltpu.make_async_copy(out.at[:, here], out_hbm.at[:, here], out_sems.at[i])
-        for i, here in enumerate(chunks)
-    ]
-
-    def product(i):
-        if i == 0:
-            fetch.wait()
-            pair[:width], pair[width:] = split(weight[...])
-            keep.start()
-            fetch_next.start()
-        if i == 1:
-            fetch_rows.start()
-            fetch_crops.start()
-        if i == len(chunks) - 1:
-            fetch_next.wait()
-            next_pair[:width], next_pair[width:] = split(next_weight[...])
-        wide_product(pair, x.at[chunks[i]], high, low, out, chunks[i])
-
-    stream(loads, stores, product)
-    keep.wait()
-    fetch_rows.wait()
-    fetch_crops.wait()
+    load(0).start()
+    fetch.wait()
+    for i in range(1, steps):
+        load(i).start()
+    for copy in (fetch_next, fetch_crops, fetch_rows):
+        copy.start()
+    pair[:width], pair[width:] = split(weight[...])
+    keep.start()
+    load(0).wait()
+    split_rows(x.at[chunk(0)], high, low)
+
+    def step(i, _):
+        wide_chunk(pair, high, low, out, chunk(i))
+        store(i).start()
+
+        @pl.when(i + 1 < steps)
+        def _():
+            load(i + 1).wait()
+            split_rows(x.at[chunk(i + 1)], high, low)
+
+        return 0
+
+    lax.fori_loop(0, steps, step, 0)
+    fetch_next.wait()
+    next_pair[:width], next_pair[width:] = split(next_weight[...])
+    for copy in (keep, fetch_rows, fetch_crops):
+        copy.wait()
+    for i in range(steps):
+        store(i).wait()
 
 
 def target_kernel(
-    chunks,
     t_hbm,
     cwgt_hbm,
     xwgt_hbm,
     rows,
     pair,
     out_hbm,
+    out,
     coarses,
     projects,
     t,
-    out,
     high,
     low,
     cwgt,
@@ -177,44 +179,52 @@
     out_sems,
     sems,
 ):
+    steps = t.shape[0] // ROWS
     fetches = [
         pltpu.make_async_copy(cwgt_hbm, cwgt, sems.at[0]),
         pltpu.make_async_copy(xwgt_hbm, xwgt, sems.at[1]),
     ]
-    loads = [
-        pltpu.make_async_copy(t_hbm.at[here], t.at[here], in_sems.at[i])
-        for i, here in enumerate(chunks[1:])
-    ]
-    stores = [
-        pltpu.make_async_copy(out.at[:, here], out_hbm.at[:, here], out_sems.at[i])
-        for i, here in enumerate(chunks)
-    ]
-    for copy in loads[:AHEAD] + fetches:
+
+    def load(i):
+        return pltpu.make_async_copy(t_hbm.at[chunk(i)], t.at[chunk(i)], in_sems.at[i])
+
+    def store(i):
+        return pltpu.make_async_copy(out, out_hbm.at[:, chunk(i)], out_sems.at[i])
+
+    for i in range(1, steps):
+        load(i).start()
+    for copy in fetches:
         copy.start()
-    wide_product(pair, rows, high, low, out, chunks[0])
-    stores[0].start()
-    for i, copy in enumerate(loads):
+    split_rows(rows, high, low)
+
+    def step(i, _):
+        @pl.when(i > 0)
+        def _():
+            store(i - 1).wait()
+
+        wide_chunk(pair, high, low, out, slice(None))
+
+        @pl.when(i + 1 < steps)
+        def _():
+            store(i).start()
+            load(i + 1).wait()
+            split_rows(t.at[chunk(i + 1)], high, low)
+
+        return 0
+
+    lax.fori_loop(0, steps, step, 0)
+    for copy in fetches:
         copy.wait()
-        if i + AHEAD < len(loads):
-            loads[i + AHEAD].start()
-        if i == len(loads) - 1:
-            for fetch in fetches:
-                fetch.wait()
-            coarses[...] = jnp.concatenate(split(cwgt[...]), axis=0)
-            projects[...] = jnp.concatenate(split(xwgt[...]), axis=0)
-        here = chunks[i + 1]
-        wide_product(pair, t.at[here], high, low, out, here)
-        stores[i + 1].start()
-    for copy in stores:
-        copy.wait()
-
-
-def prepare_kernel(patches, pair, crops_ref, before_ref, grams, pick, lay, number):
+    coarses[...] = jnp.concatenate(split(cwgt[...]), axis=0)
+    projects[...] = jnp.concatenate(split(xwgt[...]), axis=0)
+
+
+def prepare_kernel(patches, pair, crops_ref, before_ref, grams, wanted, lay, number):
     del before_ref
     width = grams.shape[0]
     both = dot(pair[...], pair[:width], NT)
     grams[...] = side_by_side(both[:width] + (both[width:] + both[width:].T))
-    pick[...] = chosen(crops_ref, patches, pick.shape[1] // patches)
+    wanted[...] = slot_row(crops_ref, patches, wanted.shape[1] // patches)
     frame = row_value(crops_ref, 0, patches, (1, patches * 16), 1, 16)
     slot = lax.broadcasted_iota(jnp.int32, (1, patches * 16), 1) % 16
     line = lax.broadcasted_iota(jnp.int32, lay.shape, 0)
@@ -240,12 +250,15 @@
     return found
 
 
-def chosen(crops_ref, patches, tokens):
+def slot_row(crops_ref, patches, tokens):
     scale = row_value(crops_ref, 3, patches, (1, patches * tokens), 1, tokens)
     token = lax.broadcasted_iota(jnp.int32, (1, patches * tokens), 1)
     row, column = (token % tokens) // 16, token % 16
-    wanted = token // tokens * 16 + (row * scale // 8) * 4 + column * scale // 8
-    slot = lax.broadcasted_iota(jnp.int32, (patches * 16, patches * tokens), 0)
+    return token // tokens * 16 + (row * scale // 8) * 4 + column * scale // 8
+
+
+def taking(wanted, slots, first):
+    slot = lax.broadcasted_iota(jnp.int32, (slots, wanted.shape[1]), 0) + first
     return jnp.where(slot == wanted, 1.0, 0.0).astype(BF16)
 
 
@@ -289,11 +302,11 @@
 
 
 def middle_kernel(
-    chunks,
     projected,
     grams,
-    pick,
+    wanted,
     first,
+    tw_last,
     xw_hbm,
     tw_hbm,
     pair_hbm,
@@ -312,64 +325,76 @@
     out_sems,
     sems,
 ):
-    width = grams.shape[0]
-    slots = pick.shape[0]
-    each = slots // len(chunks)
-    tw_loads = [
-        pltpu.make_async_copy(tw_hbm.at[:, here], tw.at[:, here], tw_sems.at[i]) for i, here in enumerate(chunks)
-    ]
-    xw_loads = [
-        pltpu.make_async_copy(xw_hbm.at[:, here], xw.at[:, here], xw_sems.at[i])
-        for i, here in enumerate(chunks[1:])
-    ]
-    stores = [
-        pltpu.make_async_copy(xw.at[:, here], de_hbm.at[:, here], out_sems.at[i])
-        for i, here in enumerate(chunks[:-1])
-    ]
+    width, count = xw.shape
+    slots = dslot_ref.shape[0]
+    steps = count // ROWS
+    each = slots // steps
+
+    def load_xw(i):
+        return pltpu.make_async_copy(xw_hbm.at[:, chunk(i)], xw.at[:, chunk(i)], xw_sems.at[i])
+
+    def load_tw(i):
+        return pltpu.make_async_copy(tw_hbm.at[:, chunk(i)], tw.at[:, chunk(i)], tw_sems.at[i])
+
+    def store(i):
+        return pltpu.make_async_copy(de_ref, de_hbm.at[:, chunk(i)], out_sems.at[i])
+
     fetches = [
         pltpu.make_async_copy(pair_hbm, deep_ref.at[: 2 * width], sems.at[0]),
         pltpu.make_async_copy(pair_hbm.at[:width], deep_ref.at[2 * width :], sems.at[1]),
     ]
-    tw_loads[0].start()
-    for pair in zip(xw_loads, tw_loads[1:]):
-        for copy in pair:
-            copy.start()
+    for i in range(steps):
+        if i < steps - 1:
+            load_tw(i).start()
+            load_xw(i + 1).start()
     for copy in fetches:
         copy.start()
-
-    def begin(i):
-        tokens = chunks[i]
-        source = first if i == 0 else xw.at[:, tokens]
-        taken[:slots], taken[slots:] = pick[:, tokens], pick[:, tokens]
+    tw[:, (steps - 1) * ROWS :] = tw_last[...]
+
+    def begin(i, source):
+        here = taking(wanted[:, chunk(i)], slots, 0)
+        taken[:slots], taken[slots:] = here, here
         spread = dot(projected[...], taken[...])
         for here in blocks(width, 32):
             pre = source[here] + spread[here]
             gate = sigmoid(pre)
             hidden = pre * gate
-            factor[i % 2, here] = gate + hidden * (1.0 - gate)
+            factor[here] = gate + hidden * (1.0 - gate)
             high, low = split(hidden)
-            for part, value in enumerate((high, high, low)):
-                deep[i % 2, shift(here, part * width)] = value
-
-    begin(0)
-    for i, tokens in enumerate(chunks):
-        tw_loads[i].wait()
-        if i + 1 < len(chunks):
-            xw_loads[i].wait()
-        target = de_ref if i == len(chunks) - 1 else xw.at[:, tokens]
-        product = dot(grams[...], deep[i % 2])
-        if i + 1 < len(chunks):
-            begin(i + 1)
+            deep[here], deep[shift(here, width)], deep[shift(here, 2 * width)] = high, high, low
+
+    begin(0, first)
+
+    def step(i, _):
+        product = dot(grams[...], deep[...])
+
+        @pl.when(i + 1 < steps)
+        def _():
+            load_tw(i).wait()
+
+        @pl.when(i > 0)
+        def _():
+            store(i - 1).wait()
+
+        tokens = chunk(i)
         for here in blocks(width, 32):
-            de = (product[here] - tw[here, tokens]) * factor[i % 2, here]
-            target[here] = de
+            de = (product[here] - tw[here, tokens]) * factor[here]
+            de_ref[here] = de
             parts[here], parts[shift(here, width)] = split(de)
-        mine = slice(i * each, (i + 1) * each)
-        both = dot(pick[mine, tokens], parts[...], NT)
-        dslot_ref[mine] = both[:, :width] + both[:, width:]
-        if i < len(stores):
-            stores[i].start()
-    for copy in stores + fetches:
+        mine = taking(wanted[:, tokens], each, i * each)
+        both = dot(mine, parts[...], NT)
+        dslot_ref[pl.ds(pl.multiple_of(i * each, each), each)] = both[:, :width] + both[:, width:]
+
+        @pl.when(i + 1 < steps)
+        def _():
+            store(i).start()
+            load_xw(i + 1).wait()
+            begin(i + 1, xw.at[:, chunk(i + 1)])
+
+        return 0
+
+    lax.fori_loop(0, steps, step, 0)
+    for copy in fetches:
         copy.wait()
 
 
@@ -400,38 +425,40 @@
     other_ref[0] = total[pl.ds(pl.multiple_of((1 - side) * half, half), half), :]
 
 
-def last_kernel(chunks, de_hbm, first, deep, out_hbm, de, out, cat, in_sems, out_sems):
+def last_kernel(de_hbm, first, deep, out_hbm, de, out, cat, in_sems, out_sems):
     width = de.shape[0]
-    order = chunks[-1:] + chunks[:-1]
-    loads = [
-        pltpu.make_async_copy(de_hbm.at[:, here], de.at[:, here], in_sems.at[i])
-        for i, here in enumerate(order[1:])
-    ]
-    stores = [
-        pltpu.make_async_copy(out.at[here], out_hbm.at[here], out_sems.at[i]) for i, here in enumerate(order)
-    ]
-
-    def prepare(i, source):
+    steps = de.shape[1] // ROWS
+
+    def load(i):
+        return pltpu.make_async_copy(de_hbm.at[:, chunk(i)], de.at[:, chunk(i)], in_sems.at[i])
+
+    def store(i):
+        return pltpu.make_async_copy(out.at[chunk(i)], out_hbm.at[chunk(i)], out_sems.at[i])
+
+    def prepare(source):
         for here in blocks(width, 32):
             high, low = split(source[here])
-            cat[i % 2, here], cat[i % 2, shift(here, width)], cat[i % 2, shift(here, 2 * width)] = high, high, low
-
-    for copy in loads:
-        copy.start()
-    prepare(0, first)
-    for i, here in enumerate(order):
-        if i < len(loads):
-            loads[i].wait()
-        out[here, :] = dot(cat[i % 2], deep[...], TN)
-        if i < len(loads):
-            prepare(i + 1, de.at[:, order[i + 1]])
-        stores[i].start()
-    for copy in stores:
-        copy.wait()
-
-
-def chunk_rows(first, last):
-    return [slice(start, start + ROWS) for start in range(first, last, ROWS)]
+            cat[here], cat[shift(here, width)], cat[shift(here, 2 * width)] = high, high, low
+
+    for i in range(steps - 1):
+        load(i).start()
+    prepare(first)
+
+    def step(i, _):
+        mine = lax.rem(i + steps - 1, steps)
+        out[chunk(mine), :] = dot(cat[...], deep[...], TN)
+        store(mine).start()
+
+        @pl.when(i + 1 < steps)
+        def _():
+            load(i).wait()
+            prepare(de.at[:, chunk(i)])
+
+        return 0
+
+    lax.fori_loop(0, steps, step, 0)
+    for i in range(steps):
+        store(i).wait()
 
 
 def fixed(*values):
@@ -470,11 +497,11 @@
     for k in range(1, far):
         column.append(lax.ppermute(coarse_input, "far", [(p, (p + k) % far) for p in range(far)]))
 
-    chunks = chunk_rows(0, count)
+    steps = count // ROWS
     pair_shape = (2 * width, values)
     x, t = fine_input.reshape(count, values), fine_target.reshape(count, values)
     xw, pair, rows, next_pair, crops = call(
-        functools.partial(input_kernel, chunks),
+        input_kernel,
         "input",
         6 * count * values * width,
         (
@@ -494,8 +521,8 @@
             pltpu.VMEM(pair_shape, BF16),
             pltpu.VMEM((ROWS, values), BF16),
             pltpu.VMEM((ROWS, values), BF16),
-            pltpu.SemaphoreType.DMA((len(chunks),)),
-            pltpu.SemaphoreType.DMA((len(chunks),)),
+            pltpu.SemaphoreType.DMA((steps,)),
+            pltpu.SemaphoreType.DMA((steps,)),
             pltpu.SemaphoreType.DMA((5,)),
         ],
     )(*fixed(x, in_weight.T, t, out_weight, crops.T))
@@ -503,40 +530,40 @@
     own = [column]
     for flip in range(1, 4):
         own.append(lax.ppermute(column, ("lvl", "y"), [(p, p ^ flip) for p in range(4)]))
-    tw, coarses, projects = call(
-        functools.partial(target_kernel, chunks),
+    tw, tw_last, coarses, projects = call(
+        target_kernel,
         "target",
         6 * count * values * width,
         (
             pltpu.HBM((width, count), F32),
+            pltpu.VMEM((width, ROWS), F32),
             pltpu.VMEM((2 * pixels, width), BF16),
             pltpu.VMEM((2 * width, width), BF16),
         ),
         limit=ROOM,
         in_specs=[HBM] * 3 + [VMEM] * 2,
-        out_specs=(HBM, VMEM, VMEM),
+        out_specs=(HBM, VMEM, VMEM, VMEM),
         scratch_shapes=[
             pltpu.VMEM((count, values), F32),
-            pltpu.VMEM((width, count), F32),
             pltpu.VMEM((ROWS, values), BF16),
             pltpu.VMEM((ROWS, values), BF16),
             pltpu.VMEM((pixels, width), F32),
             pltpu.VMEM((width, width), F32),
-            pltpu.SemaphoreType.DMA((len(chunks),)),
-            pltpu.SemaphoreType.DMA((len(chunks),)),
+            pltpu.SemaphoreType.DMA((steps,)),
+            pltpu.SemaphoreType.DMA((steps,)),
             pltpu.SemaphoreType.DMA((2,)),
         ],
     )(*fixed(t, coarse_weight, context_weight), *near(rows, next_pair))
     own = stack(own, tw).reshape(-1, pixels)
     other = lax.ppermute(own, "core", swap)
     (crops,) = near(crops)
-    grams, pick, lay, number = call(
+    grams, wanted, lay, number = call(
         functools.partial(prepare_kernel, patches),
         "prepare",
         8 * values * width * width,
         (
             pltpu.VMEM((width, 3 * width), BF16),
-            pltpu.VMEM((patches * 16, count), BF16),
+            pltpu.VMEM((1, count), jnp.int32),
             pltpu.VMEM((peers * 16, patches * 16), BF16),
             pltpu.VMEM((patches * 16, LANES - pixels), F32),
         ),
@@ -560,7 +587,7 @@
         scratch_shapes=[pltpu.VMEM((patches * 16, pixels), F32), pltpu.SemaphoreType.DMA],
     )(crops, own, other, *near(coarses, projects), *fixed(xw))
     de, last_de, deep, dslot = call(
-        functools.partial(middle_kernel, chunks),
+        middle_kernel,
         "middle",
         6 * count * width * width,
         (
@@ -570,21 +597,21 @@
             pltpu.VMEM((patches * 16, width), F32),
         ),
         limit=ROOM,
-        in_specs=[VMEM] * 4 + [HBM] * 3,
+        in_specs=[VMEM] * 5 + [HBM] * 3,
         out_specs=(HBM,) + (VMEM,) * 3,
         scratch_shapes=[
             pltpu.VMEM((width, count), F32),
             pltpu.VMEM((width, count), F32),
             pltpu.VMEM((2 * patches * 16, ROWS), BF16),
-            pltpu.VMEM((2, width, ROWS), F32),
-            pltpu.VMEM((2, 3 * width, ROWS), BF16),
+            pltpu.VMEM((width, ROWS), F32),
+            pltpu.VMEM((3 * width, ROWS), BF16),
             pltpu.VMEM((2 * width, ROWS), BF16),
-            pltpu.SemaphoreType.DMA((len(chunks),)),
-            pltpu.SemaphoreType.DMA((len(chunks),)),
-            pltpu.SemaphoreType.DMA((len(chunks),)),
+            pltpu.SemaphoreType.DMA((steps,)),
+            pltpu.SemaphoreType.DMA((steps,)),
+            pltpu.SemaphoreType.DMA((steps,)),
             pltpu.SemaphoreType.DMA((2,)),
         ],
-    )(*near(projected, grams, pick, first), *fixed(xw, tw, pair))
+    )(*near(projected, grams, wanted, first, tw_last), *fixed(xw, tw, pair))
     back = call(
         closing_kernel,
         "closing",
@@ -597,7 +624,7 @@
     returned = lax.all_to_all(back, patch, 0, 0, tiled=True)
 
     fine_grad = call(
-        functools.partial(last_kernel, chunks),
+        last_kernel,
         "last",
         6 * count * values * width,
         pltpu.HBM((count, values), F32),
@@ -607,9 +634,9 @@
         scratch_shapes=[
             pltpu.VMEM((width, count), F32),
             pltpu.VMEM((count, values), F32),
-            pltpu.VMEM((2, 3 * width, ROWS), BF16),
-            pltpu.SemaphoreType.DMA((len(chunks),)),
-            pltpu.SemaphoreType.DMA((len(chunks),)),
+            pltpu.VMEM((3 * width, ROWS), BF16),
+            pltpu.SemaphoreType.DMA((steps,)),
+            pltpu.SemaphoreType.DMA((steps,)),
         ],
     )(*fixed(de), *near(last_de, deep))
     part = (1, half, pixels)

time: 54.4 us -> 57.4 us (1.055)
  Pallas kernels: 30.3 us -> 32 us
  waiting for transfers between devices: 5.67 us -> 7.04 us
    pallas_call x4, Pallas kernels: 24.3 us -> 26.3 us  [the longest x1 7.77 us: body(): call(input_kernel, 'input', 6 * count * values * width, (pltpu.HBM((width...]
    all_to_all x1, waiting for transfers between devices: 3.2 us -> 4.33 us  [body(): returned = lax.all_to_all(back, patch, 0, 0, tiled=True)]
  transfers between devices with their start and end apart: 9 -> 9, of which waited for: 2 -> 3; matrix products, arithmetic and copies ran while one was open for 0% -> 0% of each run, Pallas kernels for 39% -> 38%
where the time goes in v13:
time: 57.4 us; the launch traced here: 57.1 us
  Pallas kernels  32 us (56%)
  starting transfers between devices  16.6 us (29%)
  waiting for transfers between devices  7.04 us (12%)
  between operations  0.78 us (1%)
  other arithmetic  0.62 us (1%)
    ppermute x3, starting transfers between devices, body(): lax.ppermute(coarse_input, 'far', [(p, (p + k) % far) for p in range(far)])  7.93 us
    pallas_call x1, Pallas kernels, body(): call(input_kernel, 'input', 6 * count * values * width, (pltpu.HBM((width...  7.77 us
    pallas_call x1, Pallas kernels, body(): call(target_kernel, 'target', 6 * count * values * width, (pltpu.HBM((wid...  6.87 us
    pallas_call x1, Pallas kernels, body(): call(middle_kernel, 'middle', 6 * count * width * width, (pltpu.HBM((widt...  5.96 us
    pallas_call x1, Pallas kernels, body(): call(last_kernel, 'last', 6 * count * values * width, pltpu.HBM((count, v...  5.66 us
    all_to_all x1, waiting for transfers between devices, body(): returned = lax.all_to_all(back, patch, 0, 0, tiled=True)  4.33 us
    ppermute x3, starting transfers between devices, body(): lax.ppermute(column, ('lvl', 'y'), [(p, p ^ flip) for p in range(4)])  3.55 us
    all_to_all x1, starting transfers between devices, body(): returned = lax.all_to_all(back, patch, 0, 0, tiled=True)  3.53 us
  transfers between devices with their start and end apart: 9, of which 3 were waited for; matrix products, arithmetic and copies ran while one was open for 0% of the time, Pallas kernels for 38%

profile of v13, /device:TPU:0, one launch (start us, length us, event | category | flops | bytes accessed | tf_op | source)
XLA Modules:
  0.0 57.1 jit_solution(8064556058577539224)
XLA Ops:
  0.6 4.1 %collective-permute-start.1 = (f32[1,32,192]{2,1,0:T(8,128)}, f32[1,32,192]{2,1,0:T(8,128)S(1)}, u32[]{:S(2)}, u32[]{:S(2)}) collective-permute-start(f32[1,32,192]{2,1,0:T(8,128)} %refs_0_.1), channel_id=1, source_target_pairs={{0,8},{4,12},{8,0},{12,4},{1,9},{5,13},{9,1},{13,5},{2,10},{6,14},... | collective-permute-start | bytes 73736 | tf_op jit(solution)/shard_map/ppermute | solution.py:498
  4.7 1.6 %collective-permute-start = (f32[1,32,192]{2,1,0:T(8,128)}, f32[1,32,192]{2,1,0:T(8,128)S(1)}, u32[]{:S(2)}, u32[]{:S(2)}) collective-permute-start(f32[1,32,192]{2,1,0:T(8,128)} %refs_0_.1), channel_id=1, source_target_pairs={{0,4},{4,8},{8,12},{12,0},{1,5},{5,9},{9,13},{13,1},{2,6},{6,10},{... | collective-permute-start | bytes 73736 | tf_op jit(solution)/shard_map/ppermute | solution.py:498
  6.3 2.2 %collective-permute-start.2 = (f32[1,32,192]{2,1,0:T(8,128)}, f32[1,32,192]{2,1,0:T(8,128)S(1)}, u32[]{:S(2)}, u32[]{:S(2)}) collective-permute-start(f32[1,32,192]{2,1,0:T(8,128)} %refs_0_.1), channel_id=1, source_target_pairs={{0,12},{4,0},{8,4},{12,8},{1,13},{5,1},{9,5},{13,9},{2,14},{6,2},{... | collective-permute-start | bytes 73736 | tf_op jit(solution)/shard_map/ppermute | solution.py:498
  8.6 0.0 copy-start
  8.6 7.8 %input.1 = (f32[320,2048]{1,0:T(8,128)}, bf16[640,768]{1,0:T(8,128)(2,1)}, f32[512,768]{1,0:T(8,128)S(1)}, bf16[640,768]{1,0:T(8,128)(2,1)S(1)}, s32[4,8]{1,0:T(4,128)S(1)}) custom-call(f32[2048,768]{1,0:T(8,128)} %bitcast.13, f32[320,768]{1,0:T(8,128)} %bitcast.16, f32[2048,768]{1,0:T(8,128)} %bitcast.14, f32[320,768]{1,0:T(8,128)} %next_weight_hbm.1, ...), custom_call_target="tpu_custom_call" | custom-call | flops 3019898880 | bytes 16253184 | tf_op jit(solution)/shard_map/input/pallas_call | solution.py:503
  16.3 0.0 collective-permute-done.1.refs_2_
  16.3 0.0 collective-permute-done.refs_1_
  16.4 0.0 collective-permute-done.2.refs_3_
  16.4 0.0 copy-done
  16.4 2.5 %collective-permute-start.5 = (f32[4,32,192]{2,1,0:T(8,128)S(1)}, f32[4,32,192]{2,1,0:T(8,128)S(1)}, u32[]{:S(2)}, u32[]{:S(2)}) collective-permute-start(f32[4,32,192]{2,1,0:T(8,128)S(1)} %stack.2.refs_0_), channel_id=1, source_target_pairs={{0,18},{2,16},{16,2},{18,0},{1,19},{3,17},{17,3},{19,1},{4,22},{6,... | collective-permute-start | bytes 294920 | tf_op jit(solution)/shard_map/ppermute | solution.py:532
  18.9 0.5 collective-permute-start.4
  19.4 0.5 collective-permute-start.3
  20.0 6.9 %target.1 = (f32[320,2048]{1,0:T(8,128)}, f32[320,512]{1,0:T(8,128)S(1)}, bf16[384,320]{1,0:T(8,128)(2,1)S(1)}, bf16[640,320]{1,0:T(8,128)(2,1)S(1)}) custom-call(f32[2048,768]{1,0:T(8,128)} %bitcast.15, f32[192,320]{1,0:T(8,128)} %cwgt_hbm.1, f32[320,320]{1,0:T(8,128)} %xwgt_hbm.1, f32[512,768]{1,0:T(8,128)S(1)} %get-tuple-element.26.rows, ...), custom_call_target="tpu_custom_call" | custom-call | flops 3019898880 | bytes 9175040 | tf_op jit(solution)/shard_map/target/pallas_call | solution.py:533
  26.8 0.0 collective-permute-done.5.refs_3_
  26.8 0.0 collective-permute-done.4.refs_2_
  26.9 0.0 collective-permute-done.3.refs_1_
  26.9 0.1 collective-permute-start.6
  27.0 1.6 %prepare.1 = (bf16[320,960]{1,0:T(8,128)(2,1)S(1)}, s32[1,2048]{1,0:T(1,128)S(1)}, bf16[256,128]{1,0:T(8,128)(2,1)S(1)}, f32[128,64]{1,0:T(8,128)S(1)}) custom-call(bf16[640,768]{1,0:T(8,128)(2,1)S(1)} %get-tuple-element.27.pair, s32[4,8]{1,0:T(4,128)S(1)} %get-tuple-element.24.crops_ref, f32[512,192]{1,0:T(8,128)S(1)} %bitcast.9), custom_call_target="tpu_custom_call" | custom-call | flops 629145600 | bytes 2801664 | tf_op jit(solution)/shard_map/prepare/pallas_call | solution.py:560
  28.6 0.3 collective-permute-done.6.other_ref
  28.9 2.1 %context.1 = (bf16[320,256]{1,0:T(8,128)(2,1)S(1)}, f32[128,320]{1,0:T(8,128)S(1)}, f32[320,512]{1,0:T(8,128)S(1)}) custom-call(s32[4,8]{1,0:T(4,128)S(1)} %get-tuple-element.24.crops_ref, f32[512,192]{1,0:T(8,128)S(1)} %bitcast.10, f32[512,192]{1,0:T(8,128)S(1)} %collective-permute-done.6.other_ref, bf16[384,320]{1,0:T(8,128)(2,1)S(1)} %get-tuple-element.29.coarses, ...), custom_call_target="tpu_custom_call" | custom-call | flops 78643200 | bytes 2293760 | tf_op jit(solution)/shard_map/context/pallas_call | solution.py:575
  31.0 6.0 %middle.1 = (f32[320,2048]{1,0:T(8,128)}, f32[320,512]{1,0:T(8,128)S(1)}, bf16[960,768]{1,0:T(8,128)(2,1)S(1)}, f32[128,320]{1,0:T(8,128)S(1)}) custom-call(bf16[320,256]{1,0:T(8,128)(2,1)S(1)} %get-tuple-element.31.projected, bf16[320,960]{1,0:T(8,128)(2,1)S(1)} %get-tuple-element.32.grams, s32[1,2048]{1,0:T(1,128)S(1)} %get-tuple-element.33.wanted, ...), custom_call_target="tpu_custom_call" | custom-call | flops 1258291200 | bytes 12779520 | tf_op jit(solution)/shard_map/middle/pallas_call | solution.py:589
  37.0 1.7 %closing.1 = f32[256,256]{1,0:T(8,128)} custom-call(f32[128,320]{1,0:T(8,128)S(1)} %get-tuple-element.37.dslot_ref, f32[128,320]{1,0:T(8,128)S(1)} %get-tuple-element.38.slope_ref, bf16[384,320]{1,0:T(8,128)(2,1)S(1)} %get-tuple-element.29.coarses, bf16[640,320]{1,0:T(8,128)(2,1)S(1)} %get-tuple-element.30.projects, ...), custom_call_target="tpu_custom_call" | custom-call | flops 78643200 | bytes 524288 | tf_op jit(solution)/shard_map/closing/pallas_call | solution.py:615
  38.7 3.5 %all-to-all-start = ((f32[16,16,256]{2,1,0:T(8,128)}), f32[16,16,256]{2,1,0:T(8,128)S(1)}, u32[]{:S(2)}, u32[]{:S(2)}) async-start(f32[16,16,256]{2,1,0:T(8,128)} %bitcast.5), calls=%async_computation | async-start | bytes 524288 | tf_op jit(solution)/shard_map/all_to_all | solution.py:624
  42.2 5.7 %last.1.done_ref = f32[2048,768]{1,0:T(8,128)} custom-call(f32[320,2048]{1,0:T(8,128)} %get-tuple-element.41.de_hbm, f32[320,512]{1,0:T(8,128)S(1)} %get-tuple-element.42.first, bf16[960,768]{1,0:T(8,128)(2,1)S(1)} %get-tuple-element.43.deep), custom_call_target="tpu_custom_call" | custom-call | flops 3019898880 | bytes 12582912 | tf_op jit(solution)/shard_map/last/pallas_call | solution.py:626
  47.9 4.3 %all-to-all-done = f32[16,16,256]{2,1,0:T(8,128)S(1)} async-done(((f32[16,16,256]{2,1,0:T(8,128)}), f32[16,16,256]{2,1,0:T(8,128)S(1)}, u32[]{:S(2)}, u32[]{:S(2)}) %all-to-all-start) | async-done | bytes 262176 | tf_op jit(solution)/shard_map/all_to_all | solution.py:624
  52.2 0.3 scatter.1
  52.5 1.5 %collective-permute-start.7 = (f32[1,32,192]{2,1,0:T(8,128)S(1)}, f32[1,32,192]{2,1,0:T(8,128)S(1)}, u32[]{:S(2)}, u32[]{:S(2)}) collective-permute-start(f32[1,32,192]{2,1,0:T(8,128)S(1)} %get-tuple-element.45), channel_id=1, source_target_pairs={{0,16},{16,0},{1,17},{17,1},{2,18},{18,2},{3,19},{19,3},{4,20},{20... | collective-permute-start | bytes 73736 | tf_op jit(solution)/shard_map/ppermute | solution.py:653
  54.0 2.4 %collective-permute-done.7 = f32[1,32,192]{2,1,0:T(8,128)S(1)} collective-permute-done((f32[1,32,192]{2,1,0:T(8,128)S(1)}, f32[1,32,192]{2,1,0:T(8,128)S(1)}, u32[]{:S(2)}, u32[]{:S(2)}) %collective-permute-start.7) | collective-permute-done | bytes 24608 | tf_op jit(solution)/shard_map/ppermute | solution.py:653
  56.5 0.6 %add.3 = f32[1,32,192]{2,1,0:T(8,128)} add(f32[1,32,192]{2,1,0:T(8,128)S(1)} %get-tuple-element.44, f32[1,32,192]{2,1,0:T(8,128)S(1)} %collective-permute-done.7) | non-fusion elementwise | flops 6144 | bytes 73728 | tf_op jit(solution)/shard_map/add | solution.py:653
  (2 shorter events, 0.0 us)
Async XLA Ops:
  0.6 15.7 %collective-permute-start.1 = (f32[1,32,192]{2,1,0:T(8,128)}, f32[1,32,192]{2,1,0:T(8,128)S(1)}, u32[]{:S(2)}, u32[]{:S(2)}) collective-permute-start(f32[1,32,192]{2,1,0:T(8,128)} %refs_0_.1), channel_id=1, source_target_pairs={{0,8},{4,12},{8,0},{12,4},{1,9},{5,13},{9,1},{13,5},{2,10},{6,14},... | collective-permute-start | bytes 73736 | tf_op jit(solution)/shard_map/ppermute | solution.py:498
  4.7 11.6 %collective-permute-start = (f32[1,32,192]{2,1,0:T(8,128)}, f32[1,32,192]{2,1,0:T(8,128)S(1)}, u32[]{:S(2)}, u32[]{:S(2)}) collective-permute-start(f32[1,32,192]{2,1,0:T(8,128)} %refs_0_.1), channel_id=1, source_target_pairs={{0,4},{4,8},{8,12},{12,0},{1,5},{5,9},{9,13},{13,1},{2,6},{6,10},{... | collective-permute-start | bytes 73736 | tf_op jit(solution)/shard_map/ppermute | solution.py:498
  6.3 10.1 %collective-permute-start.2 = (f32[1,32,192]{2,1,0:T(8,128)}, f32[1,32,192]{2,1,0:T(8,128)S(1)}, u32[]{:S(2)}, u32[]{:S(2)}) collective-permute-start(f32[1,32,192]{2,1,0:T(8,128)} %refs_0_.1), channel_id=1, source_target_pairs={{0,12},{4,0},{8,4},{12,8},{1,13},{5,1},{9,5},{13,9},{2,14},{6,2},{... | collective-permute-start | bytes 73736 | tf_op jit(solution)/shard_map/ppermute | solution.py:498
  8.6 7.8 %copy-start = (f32[1,32,192]{2,1,0:T(8,128)S(1)}, f32[1,32,192]{2,1,0:T(8,128)}, u32[]{:S(2)}) copy-start(f32[1,32,192]{2,1,0:T(8,128)} %refs_0_.1) | copy-start | bytes 73732
  16.4 10.4 %collective-permute-start.5 = (f32[4,32,192]{2,1,0:T(8,128)S(1)}, f32[4,32,192]{2,1,0:T(8,128)S(1)}, u32[]{:S(2)}, u32[]{:S(2)}) collective-permute-start(f32[4,32,192]{2,1,0:T(8,128)S(1)} %stack.2.refs_0_), channel_id=1, source_target_pairs={{0,18},{2,16},{16,2},{18,0},{1,19},{3,17},{17,3},{19,1},{4,22},{6,... | collective-permute-start | bytes 294920 | tf_op jit(solution)/shard_map/ppermute | solution.py:532
  18.9 7.9 %collective-permute-start.4 = (f32[4,32,192]{2,1,0:T(8,128)S(1)}, f32[4,32,192]{2,1,0:T(8,128)S(1)}, u32[]{:S(2)}, u32[]{:S(2)}) collective-permute-start(f32[4,32,192]{2,1,0:T(8,128)S(1)} %stack.2.refs_0_), channel_id=1, source_target_pairs={{0,16},{2,18},{16,0},{18,2},{1,17},{3,19},{17,1},{19,3},{4,20},{6,... | collective-permute-start | bytes 294920 | tf_op jit(solution)/shard_map/ppermute | solution.py:532
  19.4 7.4 %collective-permute-start.3 = (f32[4,32,192]{2,1,0:T(8,128)S(1)}, f32[4,32,192]{2,1,0:T(8,128)S(1)}, u32[]{:S(2)}, u32[]{:S(2)}) collective-permute-start(f32[4,32,192]{2,1,0:T(8,128)S(1)} %stack.2.refs_0_), channel_id=1, source_target_pairs={{0,2},{2,0},{16,18},{18,16},{1,3},{3,1},{17,19},{19,17},{4,6},{6,4... | collective-permute-start | bytes 294920 | tf_op jit(solution)/shard_map/ppermute | solution.py:532
  26.9 2.0 %collective-permute-start.6 = (f32[512,192]{1,0:T(8,128)S(1)}, f32[512,192]{1,0:T(8,128)S(1)}, u32[]{:S(2)}, u32[]{:S(2)}) collective-permute-start(f32[512,192]{1,0:T(8,128)S(1)} %bitcast.8), channel_id=1, source_target_pairs={{0,1},{1,0},{2,3},{3,2},{4,5},{5,4},{6,7},{7,6},{8,9},{9,8},{10,11... | collective-permute-start | bytes 1179656 | tf_op jit(solution)/shard_map/ppermute | solution.py:558
  38.7 13.5 %all-to-all-start = ((f32[16,16,256]{2,1,0:T(8,128)}), f32[16,16,256]{2,1,0:T(8,128)S(1)}, u32[]{:S(2)}, u32[]{:S(2)}) async-start(f32[16,16,256]{2,1,0:T(8,128)} %bitcast.5), calls=%async_computation | async-start | bytes 524288 | tf_op jit(solution)/shard_map/all_to_all | solution.py:624
  52.5 4.0 %collective-permute-start.7 = (f32[1,32,192]{2,1,0:T(8,128)S(1)}, f32[1,32,192]{2,1,0:T(8,128)S(1)}, u32[]{:S(2)}, u32[]{:S(2)}) collective-permute-start(f32[1,32,192]{2,1,0:T(8,128)S(1)} %get-tuple-element.45), channel_id=1, source_target_pairs={{0,16},{16,0},{1,17},{17,1},{2,18},{18,2},{3,19},{19,3},{4,20},{20... | collective-permute-start | bytes 73736 | tf_op jit(solution)/shard_map/ppermute | solution.py:653

commit v14 on v13

--- a/solution.py
+++ b/solution.py
@@ -84,12 +84,21 @@
         high[here], low[here] = split(source[here])
 
 
-def wide_chunk(pair, high, low, out, tokens):
+def wide_product(pair, value, high, low, out):
     width = pair.shape[0] // 2
+    split_rows(value, high, low)
     both = dot(pair[...], high[...], NT)
     rest = dot(pair[:width], low[...], NT)
     for here in blocks(width, 32):
-        out[here, tokens] = both[here] + (both[shift(here, width)] + rest[here])
+        out[here] = both[here] + (both[shift(here, width)] + rest[here])
+
+
+def deep_product(wide, value, deep, out):
+    values = value.shape[1]
+    for here in blocks(deep.shape[0], 16):
+        high, low = split(value[here])
+        deep[here, :values], deep[here, values : 2 * values], deep[here, 2 * values :] = high, high, low
+    out[...] = dot(wide[...], deep[...], NT)
 
 
 def input_kernel(
@@ -101,7 +110,7 @@
     out_hbm,
     pair_hbm,
     next_rows,
-    next_pair,
+    next_wide,
     crops,
     x,
     out,
@@ -114,50 +123,36 @@
     out_sems,
     sems,
 ):
-    width = weight.shape[0]
-    steps = x.shape[0] // ROWS
+    width, values = weight.shape
+    chunks = chunk_rows(x.shape[0])
     fetch = pltpu.make_async_copy(weight_hbm, weight, sems.at[0])
     keep = pltpu.make_async_copy(pair, pair_hbm, sems.at[1])
     fetch_next = pltpu.make_async_copy(next_weight_hbm, next_weight, sems.at[2])
     fetch_rows = pltpu.make_async_copy(t_hbm.at[: next_rows.shape[0]], next_rows, sems.at[3])
     fetch_crops = pltpu.make_async_copy(crops_hbm, crops, sems.at[4])
-
-    def load(i):
-        return pltpu.make_async_copy(x_hbm.at[chunk(i)], x.at[chunk(i)], in_sems.at[i])
-
-    def store(i):
-        return pltpu.make_async_copy(out.at[:, chunk(i)], out_hbm.at[:, chunk(i)], out_sems.at[i])
-
+    loads = [
+        pltpu.make_async_copy(x_hbm.at[here], x.at[here], in_sems.at[i]) for i, here in enumerate(chunks)
+    ]
+    stores = [
+        pltpu.make_async_copy(out.at[:, here], out_hbm.at[:, here], out_sems.at[i])
+        for i, here in enumerate(chunks)
+    ]
     fetch.start()
-    load(0).start()
+    loads[0].start()
     fetch.wait()
-    for i in range(1, steps):
-        load(i).start()
-    for copy in (fetch_next, fetch_crops, fetch_rows):
+    for copy in loads[1:] + [fetch_next, fetch_crops, fetch_rows]:
         copy.start()
     pair[:width], pair[width:] = split(weight[...])
     keep.start()
-    load(0).wait()
-    split_rows(x.at[chunk(0)], high, low)
-
-    def step(i, _):
-        wide_chunk(pair, high, low, out, chunk(i))
-        store(i).start()
-
-        @pl.when(i + 1 < steps)
-        def _():
-            load(i + 1).wait()
-            split_rows(x.at[chunk(i + 1)], high, low)
-
-        return 0
-
-    lax.fori_loop(0, steps, step, 0)
+    for i, here in enumerate(chunks):
+        loads[i].wait()
+        wide_product(pair, x.at[here], high, low, out.at[:, here])
+        stores[i].start()
     fetch_next.wait()
-    next_pair[:width], next_pair[width:] = split(next_weight[...])
-    for copy in (keep, fetch_rows, fetch_crops):
+    high_part, low_part = split(next_weight[...])
+    next_wide[:, :values], next_wide[:, values : 2 * values], next_wide[:, 2 * values :] = high_part, low_part, high_part
+    for copy in [keep, fetch_rows, fetch_crops] + stores:
         copy.wait()
-    for i in range(steps):
-        store(i).wait()
 
 
 def target_kernel(
@@ -165,65 +160,63 @@
     cwgt_hbm,
     xwgt_hbm,
     rows,
-    pair,
+    wide,
     out_hbm,
-    out,
+    out_last,
     coarses,
     projects,
     t,
-    high,
-    low,
+    out,
+    deep,
     cwgt,
     xwgt,
     in_sems,
     out_sems,
     sems,
 ):
-    steps = t.shape[0] // ROWS
+    chunks = chunk_rows(t.shape[0])
     fetches = [
         pltpu.make_async_copy(cwgt_hbm, cwgt, sems.at[0]),
         pltpu.make_async_copy(xwgt_hbm, xwgt, sems.at[1]),
     ]
-
-    def load(i):
-        return pltpu.make_async_copy(t_hbm.at[chunk(i)], t.at[chunk(i)], in_sems.at[i])
-
-    def store(i):
-        return pltpu.make_async_copy(out, out_hbm.at[:, chunk(i)], out_sems.at[i])
-
-    for i in range(1, steps):
-        load(i).start()
-    for copy in fetches:
+    loads = [
+        pltpu.make_async_copy(t_hbm.at[here], t.at[here], in_sems.at[i])
+        for i, here in enumerate(chunks[1:])
+    ]
+    stores = [
+        pltpu.make_async_copy(out.at[:, here], out_hbm.at[:, here], out_sems.at[i])
+        for i, here in enumerate(chunks[:-1])
+    ]
+    for copy in loads + fetches:
         copy.start()
-    split_rows(rows, high, low)
-
-    def step(i, _):
-        @pl.when(i > 0)
-        def _():
-            store(i - 1).wait()
-
-        wide_chunk(pair, high, low, out, slice(None))
-
-        @pl.when(i + 1 < steps)
-        def _():
-            store(i).start()
-            load(i + 1).wait()
-            split_rows(t.at[chunk(i + 1)], high, low)
-
-        return 0
-
-    lax.fori_loop(0, steps, step, 0)
+    for i, here in enumerate(chunks):
+        if i > 0:
+            loads[i - 1].wait()
+        source = rows if i == 0 else t.at[here]
+        if i < len(stores):
+            deep_product(wide, source, deep, out.at[:, here])
+            stores[i].start()
+        else:
+            deep_product(wide, source, deep, out_last)
     for copy in fetches:
         copy.wait()
     coarses[...] = jnp.concatenate(split(cwgt[...]), axis=0)
     projects[...] = jnp.concatenate(split(xwgt[...]), axis=0)
-
-
-def prepare_kernel(patches, pair, crops_ref, before_ref, grams, wanted, lay, number):
+    for copy in stores:
+        copy.wait()
+
+
+def chunk_rows(count):
+    return [slice(start, start + ROWS) for start in range(0, count, ROWS)]
+
+
+def prepare_kernel(patches, wide, crops_ref, before_ref, grams, wanted, lay, number):
     del before_ref
     width = grams.shape[0]
-    both = dot(pair[...], pair[:width], NT)
-    grams[...] = side_by_side(both[:width] + (both[width:] + both[width:].T))
+    values = wide.shape[1] // 3
+    high = wide[:, :values]
+    mixed = dot(wide[:, values : 2 * values], high, NT)
+    grams[...] = side_by_side(dot(high, high, NT) + (mixed + mixed.T))
     wanted[...] = slot_row(crops_ref, patches, wanted.shape[1] // patches)
     frame = row_value(crops_ref, 0, patches, (1, patches * 16), 1, 16)
     slot = lax.broadcasted_iota(jnp.int32, (1, patches * 16), 1) % 16
@@ -327,74 +320,65 @@
 ):
     width, count = xw.shape
     slots = dslot_ref.shape[0]
-    steps = count // ROWS
-    each = slots // steps
-
-    def load_xw(i):
-        return pltpu.make_async_copy(xw_hbm.at[:, chunk(i)], xw.at[:, chunk(i)], xw_sems.at[i])
-
-    def load_tw(i):
-        return pltpu.make_async_copy(tw_hbm.at[:, chunk(i)], tw.at[:, chunk(i)], tw_sems.at[i])
-
-    def store(i):
-        return pltpu.make_async_copy(de_ref, de_hbm.at[:, chunk(i)], out_sems.at[i])
-
+    chunks = chunk_rows(count)
+    each = slots // len(chunks)
+    tw_loads = [
+        pltpu.make_async_copy(tw_hbm.at[:, here], tw.at[:, here], tw_sems.at[i])
+        for i, here in enumerate(chunks[:-1])
+    ]
+    xw_loads = [
+        pltpu.make_async_copy(xw_hbm.at[:, here], xw.at[:, here], xw_sems.at[i])
+        for i, here in enumerate(chunks[1:])
+    ]
+    stores = [
+        pltpu.make_async_copy(xw.at[:, here], de_hbm.at[:, here], out_sems.at[i])
+        for i, here in enumerate(chunks[:-1])
+    ]
     fetches = [
         pltpu.make_async_copy(pair_hbm, deep_ref.at[: 2 * width], sems.at[0]),
         pltpu.make_async_copy(pair_hbm.at[:width], deep_ref.at[2 * width :], sems.at[1]),
     ]
-    for i in range(steps):
-        if i < steps - 1:
-            load_tw(i).start()
-            load_xw(i + 1).start()
+    for pair in zip(tw_loads, xw_loads):
+        for copy in pair:
+            copy.start()
     for copy in fetches:
         copy.start()
-    tw[:, (steps - 1) * ROWS :] = tw_last[...]
-
-    def begin(i, source):
-        here = taking(wanted[:, chunk(i)], slots, 0)
+
+    def begin(i):
+        tokens = chunks[i]
+        source = first if i == 0 else xw.at[:, tokens]
+        here = taking(wanted[:, tokens], slots, 0)
         taken[:slots], taken[slots:] = here, here
         spread = dot(projected[...], taken[...])
         for here in blocks(width, 32):
             pre = source[here] + spread[here]
             gate = sigmoid(pre)
             hidden = pre * gate
-            factor[here] = gate + hidden * (1.0 - gate)
+            factor[i % 2, here] = gate + hidden * (1.0 - gate)
             high, low = split(hidden)
-            deep[here], deep[shift(here, width)], deep[shift(here, 2 * width)] = high, high, low
-
-    begin(0, first)
-
-    def step(i, _):
-        product = dot(grams[...], deep[...])
-
-        @pl.when(i + 1 < steps)
-        def _():
-            load_tw(i).wait()
-
-        @pl.when(i > 0)
-        def _():
-            store(i - 1).wait()
-
-        tokens = chunk(i)
+            for part, value in enumerate((high, high, low)):
+                deep[i % 2, shift(here, part * width)] = value
+
+    begin(0)
+    for i, tokens in enumerate(chunks):
+        if i + 1 < len(chunks):
+            tw_loads[i].wait()
+            xw_loads[i].wait()
+        minus = tw_last if i == len(chunks) - 1 else tw.at[:, tokens]
+        target = de_ref if i == len(chunks) - 1 else xw.at[:, tokens]
+        product = dot(grams[...], deep[i % 2])
+        if i + 1 < len(chunks):
+            begin(i + 1)
         for here in blocks(width, 32):
-            de = (product[here] - tw[here, tokens]) * factor[here]
-            de_ref[here] = de
+            de = (product[here] - minus[here]) * factor[i % 2, here]
+            target[here] = de
             parts[here], parts[shift(here, width)] = split(de)
-        mine = taking(wanted[:, tokens], each, i * each)
-        both = dot(mine, parts[...], NT)
-        dslot_ref[pl.ds(pl.multiple_of(i * each, each), each)] = both[:, :width] + both[:, width:]
-
-        @pl.when(i + 1 < steps)
-        def _():
-            store(i).start()
-            load_xw(i + 1).wait()
-            begin(i + 1, xw.at[:, chunk(i + 1)])
-
-        return 0
-
-    lax.fori_loop(0, steps, step, 0)
-    for copy in fetches:
+        mine = slice(i * each, (i + 1) * each)
+        both = dot(taking(wanted[:, tokens], each, i * each), parts[...], NT)
+        dslot_ref[mine] = both[:, :width] + both[:, width:]
+        if i < len(stores):
+            stores[i].start()
+    for copy in stores + fetches:
         copy.wait()
 
 
@@ -500,7 +484,7 @@
     steps = count // ROWS
     pair_shape = (2 * width, values)
     x, t = fine_input.reshape(count, values), fine_target.reshape(count, values)
-    xw, pair, rows, next_pair, crops = call(
+    xw, pair, rows, next_wide, crops = call(
         input_kernel,
         "input",
         6 * count * values * width,
@@ -508,7 +492,7 @@
             pltpu.HBM((width, count), F32),
             pltpu.HBM(pair_shape, BF16),
             pltpu.VMEM((ROWS, values), F32),
-            pltpu.VMEM(pair_shape, BF16),
+            pltpu.VMEM((width, 3 * values), BF16),
             pltpu.VMEM((4, patches), jnp.int32),
         ),
         in_specs=[HBM] * 5,
@@ -545,15 +529,15 @@
         out_specs=(HBM, VMEM, VMEM, VMEM),
         scratch_shapes=[
             pltpu.VMEM((count, values), F32),
-            pltpu.VMEM((ROWS, values), BF16),
-            pltpu.VMEM((ROWS, values), BF16),
+            pltpu.VMEM((width, count), F32),
+            pltpu.VMEM((ROWS, 3 * values), BF16),
             pltpu.VMEM((pixels, width), F32),
             pltpu.VMEM((width, width), F32),
             pltpu.SemaphoreType.DMA((steps,)),
             pltpu.SemaphoreType.DMA((steps,)),
             pltpu.SemaphoreType.DMA((2,)),
         ],
-    )(*fixed(t, coarse_weight, context_weight), *near(rows, next_pair))
+    )(*fixed(t, coarse_weight, context_weight), *near(rows, next_wide))
     own = stack(own, tw).reshape(-1, pixels)
     other = lax.ppermute(own, "core", swap)
     (crops,) = near(crops)
@@ -570,7 +554,7 @@
         limit=ROOM,
         in_specs=[VMEM, SMEM, HBM],
         out_specs=(VMEM,) * 4,
-    )(*near(next_pair), crops, own)
+    )(*near(next_wide), crops, own)
 
     projected, slope, first = call(
         functools.partial(context_kernel, patches, peers),
@@ -603,8 +587,8 @@
             pltpu.VMEM((width, count), F32),
             pltpu.VMEM((width, count), F32),
             pltpu.VMEM((2 * patches * 16, ROWS), BF16),
-            pltpu.VMEM((width, ROWS), F32),
-            pltpu.VMEM((3 * width, ROWS), BF16),
+            pltpu.VMEM((2, width, ROWS), F32),
+            pltpu.VMEM((2, 3 * width, ROWS), BF16),
             pltpu.VMEM((2 * width, ROWS), BF16),
             pltpu.SemaphoreType.DMA((steps,)),
             pltpu.SemaphoreType.DMA((steps,)),

time: 57.4 us -> 53.6 us (0.934)
  Pallas kernels: 32 us -> 27.9 us
    pallas_call x1, Pallas kernels: 6.87 us -> 4.55 us  [body(): call(target_kernel, 'target', 6 * count * values * width, (pltpu.HBM((wid...]
    pallas_call x1, Pallas kernels: 5.96 us -> 4.87 us  [body(): call(middle_kernel, 'middle', 6 * count * width * width, (pltpu.HBM((widt...]
  transfers between devices with their start and end apart: 9 -> 9, of which waited for: 3 -> 5; matrix products, arithmetic and copies ran while one was open for 0% -> 0% of each run, Pallas kernels for 38% -> 35%
where the time goes in v14:
time: 53.6 us; the launch traced here: 53.3 us
  Pallas kernels  27.9 us (52%)
  starting transfers between devices  16.6 us (31%)
  waiting for transfers between devices  7.41 us (14%)
  between operations  0.76 us (1%)
  other arithmetic  0.62 us (1%)
    ppermute x3, starting transfers between devices, body(): lax.ppermute(coarse_input, 'far', [(p, (p + k) % far) for p in range(far)])  7.93 us
    pallas_call x1, Pallas kernels, body(): call(input_kernel, 'input', 6 * count * values * width, (pltpu.HBM((width...  7.23 us
    pallas_call x1, Pallas kernels, body(): call(last_kernel, 'last', 6 * count * values * width, pltpu.HBM((count, v...  5.66 us
    pallas_call x1, Pallas kernels, body(): call(middle_kernel, 'middle', 6 * count * width * width, (pltpu.HBM((widt...  4.87 us
    pallas_call x1, Pallas kernels, body(): call(target_kernel, 'target', 6 * count * values * width, (pltpu.HBM((wid...  4.55 us
    all_to_all x1, waiting for transfers between devices, body(): returned = lax.all_to_all(back, patch, 0, 0, tiled=True)  4.33 us
    ppermute x3, starting transfers between devices, body(): lax.ppermute(column, ('lvl', 'y'), [(p, p ^ flip) for p in range(4)])  3.55 us
    all_to_all x1, starting transfers between devices, body(): returned = lax.all_to_all(back, patch, 0, 0, tiled=True)  3.53 us
  transfers between devices with their start and end apart: 9, of which 5 were waited for; matrix products, arithmetic and copies ran while one was open for 0% of the time, Pallas kernels for 35%

profile of v14, /device:TPU:0, one launch (start us, length us, event | category | flops | bytes accessed | tf_op | source)
XLA Modules:
  0.0 53.3 jit_solution(4632476330334182567)
XLA Ops:
  0.6 4.1 %collective-permute-start.1 = (f32[1,32,192]{2,1,0:T(8,128)}, f32[1,32,192]{2,1,0:T(8,128)S(1)}, u32[]{:S(2)}, u32[]{:S(2)}) collective-permute-start(f32[1,32,192]{2,1,0:T(8,128)} %refs_0_.1), channel_id=1, source_target_pairs={{0,8},{4,12},{8,0},{12,4},{1,9},{5,13},{9,1},{13,5},{2,10},{6,14},... | collective-permute-start | bytes 73736 | tf_op jit(solution)/shard_map/ppermute | solution.py:482
  4.7 1.6 %collective-permute-start = (f32[1,32,192]{2,1,0:T(8,128)}, f32[1,32,192]{2,1,0:T(8,128)S(1)}, u32[]{:S(2)}, u32[]{:S(2)}) collective-permute-start(f32[1,32,192]{2,1,0:T(8,128)} %refs_0_.1), channel_id=1, source_target_pairs={{0,4},{4,8},{8,12},{12,0},{1,5},{5,9},{9,13},{13,1},{2,6},{6,10},{... | collective-permute-start | bytes 73736 | tf_op jit(solution)/shard_map/ppermute | solution.py:482
  6.3 2.2 %collective-permute-start.2 = (f32[1,32,192]{2,1,0:T(8,128)}, f32[1,32,192]{2,1,0:T(8,128)S(1)}, u32[]{:S(2)}, u32[]{:S(2)}) collective-permute-start(f32[1,32,192]{2,1,0:T(8,128)} %refs_0_.1), channel_id=1, source_target_pairs={{0,12},{4,0},{8,4},{12,8},{1,13},{5,1},{9,5},{13,9},{2,14},{6,2},{... | collective-permute-start | bytes 73736 | tf_op jit(solution)/shard_map/ppermute | solution.py:482
  8.6 0.0 copy-start
  8.6 7.2 %input.1 = (f32[320,2048]{1,0:T(8,128)}, bf16[640,768]{1,0:T(8,128)(2,1)}, f32[512,768]{1,0:T(8,128)S(1)}, bf16[320,2304]{1,0:T(8,128)(2,1)S(1)}, s32[4,8]{1,0:T(4,128)S(1)}) custom-call(f32[2048,768]{1,0:T(8,128)} %bitcast.13, f32[320,768]{1,0:T(8,128)} %bitcast.16, f32[2048,768]{1,0:T(8,128)} %bitcast.14, f32[320,768]{1,0:T(8,128)} %next_weight_hbm.1, ...), custom_call_target="tpu_custom_call" | custom-call | flops 3019898880 | bytes 18219264 | tf_op jit(solution)/shard_map/input/pallas_call | solution.py:487
  15.8 0.0 collective-permute-done.1.refs_2_
  15.8 0.0 collective-permute-done.refs_1_
  15.8 0.0 collective-permute-done.2.refs_3_
  15.8 0.0 copy-done
  15.9 2.5 %collective-permute-start.5 = (f32[4,32,192]{2,1,0:T(8,128)S(1)}, f32[4,32,192]{2,1,0:T(8,128)S(1)}, u32[]{:S(2)}, u32[]{:S(2)}) collective-permute-start(f32[4,32,192]{2,1,0:T(8,128)S(1)} %stack.2.refs_0_), channel_id=1, source_target_pairs={{0,18},{2,16},{16,2},{18,0},{1,19},{3,17},{17,3},{19,1},{4,22},{6,... | collective-permute-start | bytes 294920 | tf_op jit(solution)/shard_map/ppermute | solution.py:516
  18.4 0.5 %collective-permute-start.4 = (f32[4,32,192]{2,1,0:T(8,128)S(1)}, f32[4,32,192]{2,1,0:T(8,128)S(1)}, u32[]{:S(2)}, u32[]{:S(2)}) collective-permute-start(f32[4,32,192]{2,1,0:T(8,128)S(1)} %stack.2.refs_0_), channel_id=1, source_target_pairs={{0,16},{2,18},{16,0},{18,2},{1,17},{3,19},{17,1},{19,3},{4,20},{6,... | collective-permute-start | bytes 294920 | tf_op jit(solution)/shard_map/ppermute | solution.py:516
  18.9 0.5 collective-permute-start.3
  19.4 4.5 %target.1 = (f32[320,2048]{1,0:T(8,128)}, f32[320,512]{1,0:T(8,128)S(1)}, bf16[384,320]{1,0:T(8,128)(2,1)S(1)}, bf16[640,320]{1,0:T(8,128)(2,1)S(1)}) custom-call(f32[2048,768]{1,0:T(8,128)} %bitcast.15, f32[192,320]{1,0:T(8,128)} %cwgt_hbm.1, f32[320,320]{1,0:T(8,128)} %xwgt_hbm.1, f32[512,768]{1,0:T(8,128)S(1)} %get-tuple-element.26.rows, ...), custom_call_target="tpu_custom_call" | custom-call | flops 3019898880 | bytes 9175040 | tf_op jit(solution)/shard_map/target/pallas_call | solution.py:517
  24.0 0.0 collective-permute-done.5.refs_3_
  24.0 0.1 collective-permute-done.4.refs_2_
  24.1 0.1 collective-permute-done.3.refs_1_
  24.2 0.1 collective-permute-start.6
  24.3 1.4 %prepare.1 = (bf16[320,960]{1,0:T(8,128)(2,1)S(1)}, s32[1,2048]{1,0:T(1,128)S(1)}, bf16[256,128]{1,0:T(8,128)(2,1)S(1)}, f32[128,64]{1,0:T(8,128)S(1)}) custom-call(bf16[320,2304]{1,0:T(8,128)(2,1)S(1)} %get-tuple-element.27.wide, s32[4,8]{1,0:T(4,128)S(1)} %get-tuple-element.24.crops_ref, f32[512,192]{1,0:T(8,128)S(1)} %bitcast.9), custom_call_target="tpu_custom_call" | custom-call | flops 629145600 | bytes 2801664 | tf_op jit(solution)/shard_map/prepare/pallas_call | solution.py:544
  25.7 0.4 collective-permute-done.6.other_ref
  26.2 2.1 %context.1 = (bf16[320,256]{1,0:T(8,128)(2,1)S(1)}, f32[128,320]{1,0:T(8,128)S(1)}, f32[320,512]{1,0:T(8,128)S(1)}) custom-call(s32[4,8]{1,0:T(4,128)S(1)} %get-tuple-element.24.crops_ref, f32[512,192]{1,0:T(8,128)S(1)} %bitcast.10, f32[512,192]{1,0:T(8,128)S(1)} %collective-permute-done.6.other_ref, bf16[384,320]{1,0:T(8,128)(2,1)S(1)} %get-tuple-element.29.coarses, ...), custom_call_target="tpu_custom_call" | custom-call | flops 78643200 | bytes 2293760 | tf_op jit(solution)/shard_map/context/pallas_call | solution.py:559
  28.3 4.9 %middle.1 = (f32[320,2048]{1,0:T(8,128)}, f32[320,512]{1,0:T(8,128)S(1)}, bf16[960,768]{1,0:T(8,128)(2,1)S(1)}, f32[128,320]{1,0:T(8,128)S(1)}) custom-call(bf16[320,256]{1,0:T(8,128)(2,1)S(1)} %get-tuple-element.31.projected, bf16[320,960]{1,0:T(8,128)(2,1)S(1)} %get-tuple-element.32.grams, s32[1,2048]{1,0:T(1,128)S(1)} %get-tuple-element.33.wanted, ...), custom_call_target="tpu_custom_call" | custom-call | flops 1258291200 | bytes 12779520 | tf_op jit(solution)/shard_map/middle/pallas_call | solution.py:573
  33.2 1.7 %closing.1 = f32[256,256]{1,0:T(8,128)} custom-call(f32[128,320]{1,0:T(8,128)S(1)} %get-tuple-element.37.dslot_ref, f32[128,320]{1,0:T(8,128)S(1)} %get-tuple-element.38.slope_ref, bf16[384,320]{1,0:T(8,128)(2,1)S(1)} %get-tuple-element.29.coarses, bf16[640,320]{1,0:T(8,128)(2,1)S(1)} %get-tuple-element.30.projects, ...), custom_call_target="tpu_custom_call" | custom-call | flops 78643200 | bytes 524288 | tf_op jit(solution)/shard_map/closing/pallas_call | solution.py:599
  34.9 3.5 %all-to-all-start = ((f32[16,16,256]{2,1,0:T(8,128)}), f32[16,16,256]{2,1,0:T(8,128)S(1)}, u32[]{:S(2)}, u32[]{:S(2)}) async-start(f32[16,16,256]{2,1,0:T(8,128)} %bitcast.5), calls=%async_computation | async-start | bytes 524288 | tf_op jit(solution)/shard_map/all_to_all | solution.py:608
  38.4 5.7 %last.1.done_ref = f32[2048,768]{1,0:T(8,128)} custom-call(f32[320,2048]{1,0:T(8,128)} %get-tuple-element.41.de_hbm, f32[320,512]{1,0:T(8,128)S(1)} %get-tuple-element.42.first, bf16[960,768]{1,0:T(8,128)(2,1)S(1)} %get-tuple-element.43.deep), custom_call_target="tpu_custom_call" | custom-call | flops 3019898880 | bytes 12582912 | tf_op jit(solution)/shard_map/last/pallas_call | solution.py:610
  44.1 4.3 %all-to-all-done = f32[16,16,256]{2,1,0:T(8,128)S(1)} async-done(((f32[16,16,256]{2,1,0:T(8,128)}), f32[16,16,256]{2,1,0:T(8,128)S(1)}, u32[]{:S(2)}, u32[]{:S(2)}) %all-to-all-start) | async-done | bytes 262176 | tf_op jit(solution)/shard_map/all_to_all | solution.py:608
  48.4 0.3 scatter.1
  48.7 1.5 %collective-permute-start.7 = (f32[1,32,192]{2,1,0:T(8,128)S(1)}, f32[1,32,192]{2,1,0:T(8,128)S(1)}, u32[]{:S(2)}, u32[]{:S(2)}) collective-permute-start(f32[1,32,192]{2,1,0:T(8,128)S(1)} %get-tuple-element.45), channel_id=1, source_target_pairs={{0,16},{16,0},{1,17},{17,1},{2,18},{18,2},{3,19},{19,3},{4,20},{20... | collective-permute-start | bytes 73736 | tf_op jit(solution)/shard_map/ppermute | solution.py:637
  50.2 2.4 %collective-permute-done.7 = f32[1,32,192]{2,1,0:T(8,128)S(1)} collective-permute-done((f32[1,32,192]{2,1,0:T(8,128)S(1)}, f32[1,32,192]{2,1,0:T(8,128)S(1)}, u32[]{:S(2)}, u32[]{:S(2)}) %collective-permute-start.7) | collective-permute-done | bytes 24608 | tf_op jit(solution)/shard_map/ppermute | solution.py:637
  52.7 0.6 %add.3 = f32[1,32,192]{2,1,0:T(8,128)} add(f32[1,32,192]{2,1,0:T(8,128)S(1)} %get-tuple-element.44, f32[1,32,192]{2,1,0:T(8,128)S(1)} %collective-permute-done.7) | non-fusion elementwise | flops 6144 | bytes 73728 | tf_op jit(solution)/shard_map/add | solution.py:637
  (2 shorter events, 0.0 us)
Async XLA Ops:
  0.6 15.2 %collective-permute-start.1 = (f32[1,32,192]{2,1,0:T(8,128)}, f32[1,32,192]{2,1,0:T(8,128)S(1)}, u32[]{:S(2)}, u32[]{:S(2)}) collective-permute-start(f32[1,32,192]{2,1,0:T(8,128)} %refs_0_.1), channel_id=1, source_target_pairs={{0,8},{4,12},{8,0},{12,4},{1,9},{5,13},{9,1},{13,5},{2,10},{6,14},... | collective-permute-start | bytes 73736 | tf_op jit(solution)/shard_map/ppermute | solution.py:482
  4.7 11.1 %collective-permute-start = (f32[1,32,192]{2,1,0:T(8,128)}, f32[1,32,192]{2,1,0:T(8,128)S(1)}, u32[]{:S(2)}, u32[]{:S(2)}) collective-permute-start(f32[1,32,192]{2,1,0:T(8,128)} %refs_0_.1), channel_id=1, source_target_pairs={{0,4},{4,8},{8,12},{12,0},{1,5},{5,9},{9,13},{13,1},{2,6},{6,10},{... | collective-permute-start | bytes 73736 | tf_op jit(solution)/shard_map/ppermute | solution.py:482
  6.3 9.5 %collective-permute-start.2 = (f32[1,32,192]{2,1,0:T(8,128)}, f32[1,32,192]{2,1,0:T(8,128)S(1)}, u32[]{:S(2)}, u32[]{:S(2)}) collective-permute-start(f32[1,32,192]{2,1,0:T(8,128)} %refs_0_.1), channel_id=1, source_target_pairs={{0,12},{4,0},{8,4},{12,8},{1,13},{5,1},{9,5},{13,9},{2,14},{6,2},{... | collective-permute-start | bytes 73736 | tf_op jit(solution)/shard_map/ppermute | solution.py:482
  8.6 7.3 %copy-start = (f32[1,32,192]{2,1,0:T(8,128)S(1)}, f32[1,32,192]{2,1,0:T(8,128)}, u32[]{:S(2)}) copy-start(f32[1,32,192]{2,1,0:T(8,128)} %refs_0_.1) | copy-start | bytes 73732
  15.9 8.1 %collective-permute-start.5 = (f32[4,32,192]{2,1,0:T(8,128)S(1)}, f32[4,32,192]{2,1,0:T(8,128)S(1)}, u32[]{:S(2)}, u32[]{:S(2)}) collective-permute-start(f32[4,32,192]{2,1,0:T(8,128)S(1)} %stack.2.refs_0_), channel_id=1, source_target_pairs={{0,18},{2,16},{16,2},{18,0},{1,19},{3,17},{17,3},{19,1},{4,22},{6,... | collective-permute-start | bytes 294920 | tf_op jit(solution)/shard_map/ppermute | solution.py:516
  18.4 5.7 %collective-permute-start.4 = (f32[4,32,192]{2,1,0:T(8,128)S(1)}, f32[4,32,192]{2,1,0:T(8,128)S(1)}, u32[]{:S(2)}, u32[]{:S(2)}) collective-permute-start(f32[4,32,192]{2,1,0:T(8,128)S(1)} %stack.2.refs_0_), channel_id=1, source_target_pairs={{0,16},{2,18},{16,0},{18,2},{1,17},{3,19},{17,1},{19,3},{4,20},{6,... | collective-permute-start | bytes 294920 | tf_op jit(solution)/shard_map/ppermute | solution.py:516
  18.9 5.3 %collective-permute-start.3 = (f32[4,32,192]{2,1,0:T(8,128)S(1)}, f32[4,32,192]{2,1,0:T(8,128)S(1)}, u32[]{:S(2)}, u32[]{:S(2)}) collective-permute-start(f32[4,32,192]{2,1,0:T(8,128)S(1)} %stack.2.refs_0_), channel_id=1, source_target_pairs={{0,2},{2,0},{16,18},{18,16},{1,3},{3,1},{17,19},{19,17},{4,6},{6,4... | collective-permute-start | bytes 294920 | tf_op jit(solution)/shard_map/ppermute | solution.py:516
  24.2 2.0 %collective-permute-start.6 = (f32[512,192]{1,0:T(8,128)S(1)}, f32[512,192]{1,0:T(8,128)S(1)}, u32[]{:S(2)}, u32[]{:S(2)}) collective-permute-start(f32[512,192]{1,0:T(8,128)S(1)} %bitcast.8), channel_id=1, source_target_pairs={{0,1},{1,0},{2,3},{3,2},{4,5},{5,4},{6,7},{7,6},{8,9},{9,8},{10,11... | collective-permute-start | bytes 1179656 | tf_op jit(solution)/shard_map/ppermute | solution.py:542
  34.9 13.5 %all-to-all-start = ((f32[16,16,256]{2,1,0:T(8,128)}), f32[16,16,256]{2,1,0:T(8,128)S(1)}, u32[]{:S(2)}, u32[]{:S(2)}) async-start(f32[16,16,256]{2,1,0:T(8,128)} %bitcast.5), calls=%async_computation | async-start | bytes 524288 | tf_op jit(solution)/shard_map/all_to_all | solution.py:608
  48.7 4.0 %collective-permute-start.7 = (f32[1,32,192]{2,1,0:T(8,128)S(1)}, f32[1,32,192]{2,1,0:T(8,128)S(1)}, u32[]{:S(2)}, u32[]{:S(2)}) collective-permute-start(f32[1,32,192]{2,1,0:T(8,128)S(1)} %get-tuple-element.45), channel_id=1, source_target_pairs={{0,16},{16,0},{1,17},{17,1},{2,18},{18,2},{3,19},{19,3},{4,20},{20... | collective-permute-start | bytes 73736 | tf_op jit(solution)/shard_map/ppermute | solution.py:637

commit v15 on v14

--- a/solution.py
+++ b/solution.py
@@ -79,18 +79,9 @@
     return pl.ds(pl.multiple_of(i * ROWS, ROWS), ROWS)
 
 
-def split_rows(source, high, low):
-    for here in blocks(high.shape[0], 16):
-        high[here], low[here] = split(source[here])
-
-
-def wide_product(pair, value, high, low, out):
-    width = pair.shape[0] // 2
-    split_rows(value, high, low)
-    both = dot(pair[...], high[...], NT)
-    rest = dot(pair[:width], low[...], NT)
-    for here in blocks(width, 32):
-        out[here] = both[here] + (both[shift(here, width)] + rest[here])
+def fill_wide(ref, high, low):
+    values = high.shape[1]
+    ref[:, :values], ref[:, values : 2 * values], ref[:, 2 * values :] = high, low, high
 
 
 def deep_product(wide, value, deep, out):
@@ -117,13 +108,13 @@
     weight,
     next_weight,
     pair,
-    high,
-    low,
+    wide,
+    deep,
     in_sems,
     out_sems,
     sems,
 ):
-    width, values = weight.shape
+    width = weight.shape[0]
     chunks = chunk_rows(x.shape[0])
     fetch = pltpu.make_async_copy(weight_hbm, weight, sems.at[0])
     keep = pltpu.make_async_copy(pair, pair_hbm, sems.at[1])
@@ -142,15 +133,17 @@
     fetch.wait()
     for copy in loads[1:] + [fetch_next, fetch_crops, fetch_rows]:
         copy.start()
-    pair[:width], pair[width:] = split(weight[...])
+    high, low = split(weight[...])
+    fill_wide(wide, high, low)
+    pair[:width], pair[width:] = high, low
     keep.start()
     for i, here in enumerate(chunks):
         loads[i].wait()
-        wide_product(pair, x.at[here], high, low, out.at[:, here])
+        if i == len(chunks) - 1:
+            fetch_next.wait()
+            fill_wide(next_wide, *split(next_weight[...]))
+        deep_product(wide, x.at[here], deep, out.at[:, here])
         stores[i].start()
-    fetch_next.wait()
-    high_part, low_part = split(next_weight[...])
-    next_wide[:, :values], next_wide[:, values : 2 * values], next_wide[:, 2 * values :] = high_part, low_part, high_part
     for copy in [keep, fetch_rows, fetch_crops] + stores:
         copy.wait()
 
@@ -235,6 +228,16 @@
         out_ref[k * size : (k + 1) * size] = ref[...]
 
 
+def pack_kernel(*refs):
+    *block_refs, _, out_ref = refs
+    tokens = block_refs[0].shape[1]
+    size = tokens * 3 // 2
+    for k, ref in enumerate(block_refs):
+        out_ref[k * size : k * size + tokens] = ref[0, :, :128]
+        tails = [ref[0, : tokens // 2, 128:], ref[0, tokens // 2 :, 128:]]
+        out_ref[k * size + tokens : (k + 1) * size] = jnp.concatenate(tails, axis=1)
+
+
 def row_value(crops_ref, column, patches, shape, axis, each):
     index = lax.broadcasted_iota(jnp.int32, shape, axis) // each
     found = jnp.zeros(shape, jnp.int32)
@@ -278,18 +281,25 @@
     me, side = lax.axis_index(("far", "y", "core")), lax.axis_index("lvl")
     for j in range(patches):
         frame, top, left = crops_ref[0, j], crops_ref[1, j], crops_ref[2, j]
-        near = lax.bitwise_xor(frame % 4, me % 4)
+        near_by = lax.bitwise_xor(frame % 4, me % 4)
         k = (me // 4 - frame // 4 + far) % far
+        here = near_by % 2 == 0
         for a in range(4):
             row = jnp.minimum(top + a, SIDE - 1)
-            shard = (lax.bitwise_xor(row // 4, side) * 2 + near // 2) * far + k
-            start = pl.ds(pl.multiple_of((shard * 4 + row % 4) * SIDE, SIDE), SIDE)
-            line = jnp.where(near % 2 == 0, own_ref[start, :], other_ref[start, :])
-            rows[j * 16 + a * 4 : j * 16 + a * 4 + 4, :] = pltpu.roll(line, SIDE - left, 0)[:4, :]
-    pre = dot3(split(rows[...]), (coarses[:pixels], coarses[pixels:]))
+            shard = (lax.bitwise_xor(row // 4, side) * 2 + near_by // 2) * far + k
+            row = row % 4
+            start = shard * (6 * SIDE)
+            wide = pl.ds(pl.multiple_of(start + row * SIDE, SIDE), SIDE)
+            tail = pl.ds(pl.multiple_of(start + (4 + row % 2) * SIDE, SIDE), SIDE)
+            into = slice(j * 16 + a * 4, j * 16 + a * 4 + 4)
+            line = jnp.where(here, own_ref[wide, :], other_ref[wide, :])
+            rows[into, :128] = pltpu.roll(line, SIDE - left, 0)[:4, :]
+            line = pltpu.roll(jnp.where(here, own_ref[tail, :], other_ref[tail, :]), SIDE - left, 0)[:4, :]
+            rows[into, 128:] = jnp.where(row >= 2, line[:, 64:], line[:, :64])
+    pre = through(rows[...], coarses, NN)
     gate = sigmoid(pre)
     slope_ref[...] = gate * (1.0 + pre * (1.0 - gate))
-    projected = dot3(split(pre * gate), (projects[:width], projects[width:])).T
+    projected = through(pre * gate, projects, NN).T
     projected_ref[...] = jnp.concatenate(split(projected), axis=1)
     fetch.wait()
 
@@ -382,15 +392,15 @@
         copy.wait()
 
 
-def through(value, pair):
+def through(value, pair, dims):
     count, rows = value.shape[0], pair.shape[0] // 2
     high, low = split(value)
-    both = dot(jnp.concatenate([high, low], axis=0), pair[:rows], NT)
-    return both[:count] + (both[count:] + dot(high, pair[rows:], NT))
+    both = dot(jnp.concatenate([high, low], axis=0), pair[:rows], dims)
+    return both[:count] + (both[count:] + dot(high, pair[rows:], dims))
 
 
 def closing_kernel(dslot_ref, slope_ref, coarses, projects, lay, number, send_ref):
-    grad = through(through(dslot_ref[...], projects) * slope_ref[...], coarses)
+    grad = through(through(dslot_ref[...], projects, NT) * slope_ref[...], coarses, NT)
     high, low = split(jnp.concatenate([grad, number[...]], axis=1))
     send_ref[...] = dot(lay[...], high) + dot(lay[...], low)
 
@@ -453,10 +463,10 @@
     return [pltpu.with_memory_space_constraint(value, pltpu.VMEM) for value in values]
 
 
-def stack(blocks, before):
-    shape = (len(blocks) * blocks[0].shape[0],) + blocks[0].shape[1:]
+def stack(kernel, blocks, before, rows):
+    shape = (len(blocks) * rows, 128)
     return call(
-        stack_kernel,
+        kernel,
         "stack",
         1000,
         jax.ShapeDtypeStruct(shape, F32),
@@ -503,14 +513,14 @@
             pltpu.VMEM((width, values), F32),
             pltpu.VMEM((width, values), F32),
             pltpu.VMEM(pair_shape, BF16),
-            pltpu.VMEM((ROWS, values), BF16),
-            pltpu.VMEM((ROWS, values), BF16),
+            pltpu.VMEM((width, 3 * values), BF16),
+            pltpu.VMEM((ROWS, 3 * values), BF16),
             pltpu.SemaphoreType.DMA((steps,)),
             pltpu.SemaphoreType.DMA((steps,)),
             pltpu.SemaphoreType.DMA((5,)),
         ],
     )(*fixed(x, in_weight.T, t, out_weight, crops.T))
-    column = stack(column, xw)
+    column = stack(pack_kernel, column, xw, half * 3 // 2)
     own = [column]
     for flip in range(1, 4):
         own.append(lax.ppermute(column, ("lvl", "y"), [(p, p ^ flip) for p in range(4)]))
@@ -538,7 +548,7 @@
             pltpu.SemaphoreType.DMA((2,)),
         ],
     )(*fixed(t, coarse_weight, context_weight), *near(rows, next_wide))
-    own = stack(own, tw).reshape(-1, pixels)
+    own = stack(stack_kernel, own, tw, column.shape[0])
     other = lax.ppermute(own, "core", swap)
     (crops,) = near(crops)
     grams, wanted, lay, number = call(

time: 53.6 us -> 53.6 us (level)
  transfers between devices with their start and end apart: 9 -> 9, of which waited for: 5 -> 3; matrix products, arithmetic and copies ran while one was open for 0% -> 0% of each run, Pallas kernels for 35% -> 36%
where the time goes in v15:
time: 53.6 us; the launch traced here: 53.3 us
  Pallas kernels  28.3 us (53%)
  starting transfers between devices  16.6 us (31%)
  waiting for transfers between devices  7.03 us (13%)
  between operations  0.77 us (1%)
  other arithmetic  0.62 us (1%)
    ppermute x3, starting transfers between devices, body(): lax.ppermute(coarse_input, 'far', [(p, (p + k) % far) for p in range(far)])  7.93 us
    pallas_call x1, Pallas kernels, body(): call(input_kernel, 'input', 6 * count * values * width, (pltpu.HBM((width...  7.46 us
    pallas_call x1, Pallas kernels, body(): call(last_kernel, 'last', 6 * count * values * width, pltpu.HBM((count, v...  5.67 us
    pallas_call x1, Pallas kernels, body(): call(middle_kernel, 'middle', 6 * count * width * width, (pltpu.HBM((widt...  4.86 us
    pallas_call x1, Pallas kernels, body(): call(target_kernel, 'target', 6 * count * values * width, (pltpu.HBM((wid...  4.54 us
    all_to_all x1, waiting for transfers between devices, body(): returned = lax.all_to_all(back, patch, 0, 0, tiled=True)  4.33 us
    ppermute x3, starting transfers between devices, body(): lax.ppermute(column, ('lvl', 'y'), [(p, p ^ flip) for p in range(4)])  3.55 us
    all_to_all x1, starting transfers between devices, body(): returned = lax.all_to_all(back, patch, 0, 0, tiled=True)  3.53 us
  transfers between devices with their start and end apart: 9, of which 3 were waited for; matrix products, arithmetic and copies ran while one was open for 0% of the time, Pallas kernels for 36%

profile of v15, /device:TPU:0, one launch (start us, length us, event | category | flops | bytes accessed | tf_op | source)
XLA Modules:
  0.0 53.3 jit_solution(3106325177432849600)
XLA Ops:
  0.6 4.1 %collective-permute-start.1 = (f32[1,32,192]{2,1,0:T(8,128)}, f32[1,32,192]{2,1,0:T(8,128)S(1)}, u32[]{:S(2)}, u32[]{:S(2)}) collective-permute-start(f32[1,32,192]{2,1,0:T(8,128)} %refs_0_.1), channel_id=1, source_target_pairs={{0,8},{4,12},{8,0},{12,4},{1,9},{5,13},{9,1},{13,5},{2,10},{6,14},... | collective-permute-start | bytes 73736 | tf_op jit(solution)/shard_map/ppermute | solution.py:492
  4.7 1.6 %collective-permute-start = (f32[1,32,192]{2,1,0:T(8,128)}, f32[1,32,192]{2,1,0:T(8,128)S(1)}, u32[]{:S(2)}, u32[]{:S(2)}) collective-permute-start(f32[1,32,192]{2,1,0:T(8,128)} %refs_0_.1), channel_id=1, source_target_pairs={{0,4},{4,8},{8,12},{12,0},{1,5},{5,9},{9,13},{13,1},{2,6},{6,10},{... | collective-permute-start | bytes 73736 | tf_op jit(solution)/shard_map/ppermute | solution.py:492
  6.3 2.2 %collective-permute-start.2 = (f32[1,32,192]{2,1,0:T(8,128)}, f32[1,32,192]{2,1,0:T(8,128)S(1)}, u32[]{:S(2)}, u32[]{:S(2)}) collective-permute-start(f32[1,32,192]{2,1,0:T(8,128)} %refs_0_.1), channel_id=1, source_target_pairs={{0,12},{4,0},{8,4},{12,8},{1,13},{5,1},{9,5},{13,9},{2,14},{6,2},{... | collective-permute-start | bytes 73736 | tf_op jit(solution)/shard_map/ppermute | solution.py:492
  8.6 0.0 copy-start
  8.6 7.5 %input.1 = (f32[320,2048]{1,0:T(8,128)}, bf16[640,768]{1,0:T(8,128)(2,1)}, f32[512,768]{1,0:T(8,128)S(1)}, bf16[320,2304]{1,0:T(8,128)(2,1)S(1)}, s32[4,8]{1,0:T(4,128)S(1)}) custom-call(f32[2048,768]{1,0:T(8,128)} %bitcast.9, f32[320,768]{1,0:T(8,128)} %bitcast.12, f32[2048,768]{1,0:T(8,128)} %bitcast.10, f32[320,768]{1,0:T(8,128)} %next_weight_hbm.1, ...), custom_call_target="tpu_custom_call" | custom-call | flops 3019898880 | bytes 18219264 | tf_op jit(solution)/shard_map/input/pallas_call | solution.py:497
  16.0 0.0 collective-permute-done.1.refs_2_
  16.0 0.0 collective-permute-done.refs_1_
  16.0 0.0 collective-permute-done.2.refs_3_
  16.1 0.0 copy-done
  16.1 0.1 stack.2.refs_0_
  16.1 2.5 %collective-permute-start.5 = (f32[192,128]{1,0:T(8,128)S(1)}, f32[192,128]{1,0:T(8,128)S(1)}, u32[]{:S(2)}, u32[]{:S(2)}) collective-permute-start(f32[192,128]{1,0:T(8,128)S(1)} %stack.2.refs_0_), channel_id=1, source_target_pairs={{0,18},{2,16},{16,2},{18,0},{1,19},{3,17},{17,3},{19,1},{4,22},{6,... | collective-permute-start | bytes 294920 | tf_op jit(solution)/shard_map/ppermute | solution.py:526
  18.7 0.5 %collective-permute-start.4 = (f32[192,128]{1,0:T(8,128)S(1)}, f32[192,128]{1,0:T(8,128)S(1)}, u32[]{:S(2)}, u32[]{:S(2)}) collective-permute-start(f32[192,128]{1,0:T(8,128)S(1)} %stack.2.refs_0_), channel_id=1, source_target_pairs={{0,16},{2,18},{16,0},{18,2},{1,17},{3,19},{17,1},{19,3},{4,20},{6,... | collective-permute-start | bytes 294920 | tf_op jit(solution)/shard_map/ppermute | solution.py:526
  19.2 0.5 collective-permute-start.3
  19.7 4.5 %target.1 = (f32[320,2048]{1,0:T(8,128)}, f32[320,512]{1,0:T(8,128)S(1)}, bf16[384,320]{1,0:T(8,128)(2,1)S(1)}, bf16[640,320]{1,0:T(8,128)(2,1)S(1)}) custom-call(f32[2048,768]{1,0:T(8,128)} %bitcast.11, f32[192,320]{1,0:T(8,128)} %cwgt_hbm.1, f32[320,320]{1,0:T(8,128)} %xwgt_hbm.1, f32[512,768]{1,0:T(8,128)S(1)} %get-tuple-element.26.rows, ...), custom_call_target="tpu_custom_call" | custom-call | flops 3019898880 | bytes 9175040 | tf_op jit(solution)/shard_map/target/pallas_call | solution.py:527
  24.3 0.0 collective-permute-done.5.refs_3_
  24.3 0.0 collective-permute-done.4.refs_2_
  24.3 0.0 collective-permute-done.3.refs_1_
  24.3 0.1 collective-permute-start.6
  24.4 1.4 %prepare.1 = (bf16[320,960]{1,0:T(8,128)(2,1)S(1)}, s32[1,2048]{1,0:T(1,128)S(1)}, bf16[256,128]{1,0:T(8,128)(2,1)S(1)}, f32[128,64]{1,0:T(8,128)S(1)}) custom-call(bf16[320,2304]{1,0:T(8,128)(2,1)S(1)} %get-tuple-element.27.wide, s32[4,8]{1,0:T(4,128)S(1)} %get-tuple-element.24.crops_ref, f32[768,128]{1,0:T(8,128)S(1)} %stack.3.own_ref.before_ref), custom_call_target="tpu_custom_call" | custom-call | flops 629145600 | bytes 2801664 | tf_op jit(solution)/shard_map/prepare/pallas_call | solution.py:554
  25.8 0.3 collective-permute-done.6.other_ref
  26.1 2.2 %context.1 = (bf16[320,256]{1,0:T(8,128)(2,1)S(1)}, f32[128,320]{1,0:T(8,128)S(1)}, f32[320,512]{1,0:T(8,128)S(1)}) custom-call(s32[4,8]{1,0:T(4,128)S(1)} %get-tuple-element.24.crops_ref, f32[768,128]{1,0:T(8,128)S(1)} %stack.3.own_ref.before_ref, f32[768,128]{1,0:T(8,128)S(1)} %collective-permute-done.6.other_ref, ...), custom_call_target="tpu_custom_call" | custom-call | flops 78643200 | bytes 2293760 | tf_op jit(solution)/shard_map/context/pallas_call | solution.py:569
  28.4 4.9 %middle.1 = (f32[320,2048]{1,0:T(8,128)}, f32[320,512]{1,0:T(8,128)S(1)}, bf16[960,768]{1,0:T(8,128)(2,1)S(1)}, f32[128,320]{1,0:T(8,128)S(1)}) custom-call(bf16[320,256]{1,0:T(8,128)(2,1)S(1)} %get-tuple-element.31.projected, bf16[320,960]{1,0:T(8,128)(2,1)S(1)} %get-tuple-element.32.grams, s32[1,2048]{1,0:T(1,128)S(1)} %get-tuple-element.33.wanted, ...), custom_call_target="tpu_custom_call" | custom-call | flops 1258291200 | bytes 12779520 | tf_op jit(solution)/shard_map/middle/pallas_call | solution.py:583
  33.2 1.7 %closing.1 = f32[256,256]{1,0:T(8,128)} custom-call(f32[128,320]{1,0:T(8,128)S(1)} %get-tuple-element.37.dslot_ref, f32[128,320]{1,0:T(8,128)S(1)} %get-tuple-element.38.slope_ref, bf16[384,320]{1,0:T(8,128)(2,1)S(1)} %get-tuple-element.29.coarses, bf16[640,320]{1,0:T(8,128)(2,1)S(1)} %get-tuple-element.30.projects, ...), custom_call_target="tpu_custom_call" | custom-call | flops 78643200 | bytes 524288 | tf_op jit(solution)/shard_map/closing/pallas_call | solution.py:609
  34.9 3.5 %all-to-all-start = ((f32[16,16,256]{2,1,0:T(8,128)}), f32[16,16,256]{2,1,0:T(8,128)S(1)}, u32[]{:S(2)}, u32[]{:S(2)}) async-start(f32[16,16,256]{2,1,0:T(8,128)} %bitcast.4), calls=%async_computation | async-start | bytes 524288 | tf_op jit(solution)/shard_map/all_to_all | solution.py:618
  38.4 5.7 %last.1.done_ref = f32[2048,768]{1,0:T(8,128)} custom-call(f32[320,2048]{1,0:T(8,128)} %get-tuple-element.41.de_hbm, f32[320,512]{1,0:T(8,128)S(1)} %get-tuple-element.42.first, bf16[960,768]{1,0:T(8,128)(2,1)S(1)} %get-tuple-element.43.deep), custom_call_target="tpu_custom_call" | custom-call | flops 3019898880 | bytes 12582912 | tf_op jit(solution)/shard_map/last/pallas_call | solution.py:620
  44.1 4.3 %all-to-all-done = f32[16,16,256]{2,1,0:T(8,128)S(1)} async-done(((f32[16,16,256]{2,1,0:T(8,128)}), f32[16,16,256]{2,1,0:T(8,128)S(1)}, u32[]{:S(2)}, u32[]{:S(2)}) %all-to-all-start) | async-done | bytes 262176 | tf_op jit(solution)/shard_map/all_to_all | solution.py:618
  48.5 0.3 scatter.1
  48.7 1.6 %collective-permute-start.7 = (f32[1,32,192]{2,1,0:T(8,128)S(1)}, f32[1,32,192]{2,1,0:T(8,128)S(1)}, u32[]{:S(2)}, u32[]{:S(2)}) collective-permute-start(f32[1,32,192]{2,1,0:T(8,128)S(1)} %get-tuple-element.45), channel_id=1, source_target_pairs={{0,16},{16,0},{1,17},{17,1},{2,18},{18,2},{3,19},{19,3},{4,20},{20... | collective-permute-start | bytes 73736 | tf_op jit(solution)/shard_map/ppermute | solution.py:647
  50.3 2.4 %collective-permute-done.7 = f32[1,32,192]{2,1,0:T(8,128)S(1)} collective-permute-done((f32[1,32,192]{2,1,0:T(8,128)S(1)}, f32[1,32,192]{2,1,0:T(8,128)S(1)}, u32[]{:S(2)}, u32[]{:S(2)}) %collective-permute-start.7) | collective-permute-done | bytes 24608 | tf_op jit(solution)/shard_map/ppermute | solution.py:647
  52.7 0.6 %add.3 = f32[1,32,192]{2,1,0:T(8,128)} add(f32[1,32,192]{2,1,0:T(8,128)S(1)} %get-tuple-element.44, f32[1,32,192]{2,1,0:T(8,128)S(1)} %collective-permute-done.7) | non-fusion elementwise | flops 6144 | bytes 73728 | tf_op jit(solution)/shard_map/add | solution.py:647
  (1 shorter events, 0.0 us)
Async XLA Ops:
  0.6 15.4 %collective-permute-start.1 = (f32[1,32,192]{2,1,0:T(8,128)}, f32[1,32,192]{2,1,0:T(8,128)S(1)}, u32[]{:S(2)}, u32[]{:S(2)}) collective-permute-start(f32[1,32,192]{2,1,0:T(8,128)} %refs_0_.1), channel_id=1, source_target_pairs={{0,8},{4,12},{8,0},{12,4},{1,9},{5,13},{9,1},{13,5},{2,10},{6,14},... | collective-permute-start | bytes 73736 | tf_op jit(solution)/shard_map/ppermute | solution.py:492
  4.7 11.3 %collective-permute-start = (f32[1,32,192]{2,1,0:T(8,128)}, f32[1,32,192]{2,1,0:T(8,128)S(1)}, u32[]{:S(2)}, u32[]{:S(2)}) collective-permute-start(f32[1,32,192]{2,1,0:T(8,128)} %refs_0_.1), channel_id=1, source_target_pairs={{0,4},{4,8},{8,12},{12,0},{1,5},{5,9},{9,13},{13,1},{2,6},{6,10},{... | collective-permute-start | bytes 73736 | tf_op jit(solution)/shard_map/ppermute | solution.py:492
  6.3 9.7 %collective-permute-start.2 = (f32[1,32,192]{2,1,0:T(8,128)}, f32[1,32,192]{2,1,0:T(8,128)S(1)}, u32[]{:S(2)}, u32[]{:S(2)}) collective-permute-start(f32[1,32,192]{2,1,0:T(8,128)} %refs_0_.1), channel_id=1, source_target_pairs={{0,12},{4,0},{8,4},{12,8},{1,13},{5,1},{9,5},{13,9},{2,14},{6,2},{... | collective-permute-start | bytes 73736 | tf_op jit(solution)/shard_map/ppermute | solution.py:492
  8.6 7.5 %copy-start = (f32[1,32,192]{2,1,0:T(8,128)S(1)}, f32[1,32,192]{2,1,0:T(8,128)}, u32[]{:S(2)}) copy-start(f32[1,32,192]{2,1,0:T(8,128)} %refs_0_.1) | copy-start | bytes 73732
  16.1 8.1 %collective-permute-start.5 = (f32[192,128]{1,0:T(8,128)S(1)}, f32[192,128]{1,0:T(8,128)S(1)}, u32[]{:S(2)}, u32[]{:S(2)}) collective-permute-start(f32[192,128]{1,0:T(8,128)S(1)} %stack.2.refs_0_), channel_id=1, source_target_pairs={{0,18},{2,16},{16,2},{18,0},{1,19},{3,17},{17,3},{19,1},{4,22},{6,... | collective-permute-start | bytes 294920 | tf_op jit(solution)/shard_map/ppermute | solution.py:526
  18.7 5.6 %collective-permute-start.4 = (f32[192,128]{1,0:T(8,128)S(1)}, f32[192,128]{1,0:T(8,128)S(1)}, u32[]{:S(2)}, u32[]{:S(2)}) collective-permute-start(f32[192,128]{1,0:T(8,128)S(1)} %stack.2.refs_0_), channel_id=1, source_target_pairs={{0,16},{2,18},{16,0},{18,2},{1,17},{3,19},{17,1},{19,3},{4,20},{6,... | collective-permute-start | bytes 294920 | tf_op jit(solution)/shard_map/ppermute | solution.py:526
  19.2 5.1 %collective-permute-start.3 = (f32[192,128]{1,0:T(8,128)S(1)}, f32[192,128]{1,0:T(8,128)S(1)}, u32[]{:S(2)}, u32[]{:S(2)}) collective-permute-start(f32[192,128]{1,0:T(8,128)S(1)} %stack.2.refs_0_), channel_id=1, source_target_pairs={{0,2},{2,0},{16,18},{18,16},{1,3},{3,1},{17,19},{19,17},{4,6},{6,4... | collective-permute-start | bytes 294920 | tf_op jit(solution)/shard_map/ppermute | solution.py:526
  24.3 1.8 %collective-permute-start.6 = (f32[768,128]{1,0:T(8,128)S(1)}, f32[768,128]{1,0:T(8,128)S(1)}, u32[]{:S(2)}, u32[]{:S(2)}) collective-permute-start(f32[768,128]{1,0:T(8,128)S(1)} %stack.3.own_ref.before_ref), channel_id=1, source_target_pairs={{0,1},{1,0},{2,3},{3,2},{4,5},{5,4},{6,7},{7,6},{8,9},{9,8},{10,11... | collective-permute-start | bytes 1179656 | tf_op jit(solution)/shard_map/ppermute | solution.py:552
  34.9 13.5 %all-to-all-start = ((f32[16,16,256]{2,1,0:T(8,128)}), f32[16,16,256]{2,1,0:T(8,128)S(1)}, u32[]{:S(2)}, u32[]{:S(2)}) async-start(f32[16,16,256]{2,1,0:T(8,128)} %bitcast.4), calls=%async_computation | async-start | bytes 524288 | tf_op jit(solution)/shard_map/all_to_all | solution.py:618
  48.7 4.0 %collective-permute-start.7 = (f32[1,32,192]{2,1,0:T(8,128)S(1)}, f32[1,32,192]{2,1,0:T(8,128)S(1)}, u32[]{:S(2)}, u32[]{:S(2)}) collective-permute-start(f32[1,32,192]{2,1,0:T(8,128)S(1)} %get-tuple-element.45), channel_id=1, source_target_pairs={{0,16},{16,0},{1,17},{17,1},{2,18},{18,2},{3,19},{19,3},{4,20},{20... | collective-permute-start | bytes 73736 | tf_op jit(solution)/shard_map/ppermute | solution.py:647

commit v16 on v15

--- a/solution.py
+++ b/solution.py
@@ -84,11 +84,13 @@
     ref[:, :values], ref[:, values : 2 * values], ref[:, 2 * values :] = high, low, high
 
 
-def deep_product(wide, value, deep, out):
+def deep_product(wide, value, deep, out, following=()):
     values = value.shape[1]
     for here in blocks(deep.shape[0], 16):
         high, low = split(value[here])
         deep[here, :values], deep[here, values : 2 * values], deep[here, 2 * values :] = high, high, low
+    for copy in following:
+        copy.start()
     out[...] = dot(wide[...], deep[...], NT)
 
 
@@ -131,8 +133,9 @@
     fetch.start()
     loads[0].start()
     fetch.wait()
-    for copy in loads[1:] + [fetch_next, fetch_crops, fetch_rows]:
-        copy.start()
+    loads[1].start()
+    later = [[load] for load in loads[2:]] + [[fetch_rows, fetch_crops], []]
+    later[0].append(fetch_next)
     high, low = split(weight[...])
     fill_wide(wide, high, low)
     pair[:width], pair[width:] = high, low
@@ -142,7 +145,7 @@
         if i == len(chunks) - 1:
             fetch_next.wait()
             fill_wide(next_wide, *split(next_weight[...]))
-        deep_product(wide, x.at[here], deep, out.at[:, here])
+        deep_product(wide, x.at[here], deep, out.at[:, here], later[i])
         stores[i].start()
     for copy in [keep, fetch_rows, fetch_crops] + stores:
         copy.wait()
@@ -180,14 +183,14 @@
         pltpu.make_async_copy(out.at[:, here], out_hbm.at[:, here], out_sems.at[i])
         for i, here in enumerate(chunks[:-1])
     ]
-    for copy in loads + fetches:
-        copy.start()
+    loads[0].start()
+    later = [[load] for load in loads[1:]] + [fetches, []]
     for i, here in enumerate(chunks):
         if i > 0:
             loads[i - 1].wait()
         source = rows if i == 0 else t.at[here]
         if i < len(stores):
-            deep_product(wide, source, deep, out.at[:, here])
+            deep_product(wide, source, deep, out.at[:, here], later[i])
             stores[i].start()
         else:
             deep_product(wide, source, deep, out_last)
@@ -267,14 +270,20 @@
     coarses,
     projects,
     xw_hbm,
+    tw_hbm,
     projected_ref,
     slope_ref,
-    first_ref,
+    xw,
+    tw,
     rows,
-    sem,
+    sems,
 ):
-    fetch = pltpu.make_async_copy(xw_hbm.at[:, : first_ref.shape[1]], first_ref, sem)
-    fetch.start()
+    fetches = [
+        pltpu.make_async_copy(xw_hbm, xw, sems.at[0]),
+        pltpu.make_async_copy(tw_hbm.at[:, : tw.shape[1]], tw, sems.at[1]),
+    ]
+    for copy in fetches:
+        copy.start()
     pixels = coarses.shape[0] // 2
     width = projects.shape[1]
     far = peers // 4
@@ -282,7 +291,7 @@
     for j in range(patches):
         frame, top, left = crops_ref[0, j], crops_ref[1, j], crops_ref[2, j]
         near_by = lax.bitwise_xor(frame % 4, me % 4)
-        k = (me // 4 - frame // 4 + far) % far
+        k = lax.bitwise_xor(frame // 4, me // 4)
         here = near_by % 2 == 0
         for a in range(4):
             row = jnp.minimum(top + a, SIDE - 1)
@@ -301,30 +310,27 @@
     slope_ref[...] = gate * (1.0 + pre * (1.0 - gate))
     projected = through(pre * gate, projects, NN).T
     projected_ref[...] = jnp.concatenate(split(projected), axis=1)
-    fetch.wait()
+    for copy in fetches:
+        copy.wait()
 
 
 def middle_kernel(
     projected,
     grams,
     wanted,
-    first,
+    xw,
+    tw,
     tw_last,
-    xw_hbm,
-    tw_hbm,
     pair_hbm,
     de_hbm,
     de_ref,
     deep_ref,
     dslot_ref,
-    xw,
-    tw,
+    des,
     taken,
     factor,
     deep,
     parts,
-    xw_sems,
-    tw_sems,
     out_sems,
     sems,
 ):
@@ -332,36 +338,24 @@
     slots = dslot_ref.shape[0]
     chunks = chunk_rows(count)
     each = slots // len(chunks)
-    tw_loads = [
-        pltpu.make_async_copy(tw_hbm.at[:, here], tw.at[:, here], tw_sems.at[i])
-        for i, here in enumerate(chunks[:-1])
-    ]
-    xw_loads = [
-        pltpu.make_async_copy(xw_hbm.at[:, here], xw.at[:, here], xw_sems.at[i])
-        for i, here in enumerate(chunks[1:])
-    ]
     stores = [
-        pltpu.make_async_copy(xw.at[:, here], de_hbm.at[:, here], out_sems.at[i])
+        pltpu.make_async_copy(des.at[:, here], de_hbm.at[:, here], out_sems.at[i])
         for i, here in enumerate(chunks[:-1])
     ]
     fetches = [
         pltpu.make_async_copy(pair_hbm, deep_ref.at[: 2 * width], sems.at[0]),
         pltpu.make_async_copy(pair_hbm.at[:width], deep_ref.at[2 * width :], sems.at[1]),
     ]
-    for pair in zip(tw_loads, xw_loads):
-        for copy in pair:
-            copy.start()
     for copy in fetches:
         copy.start()
 
     def begin(i):
         tokens = chunks[i]
-        source = first if i == 0 else xw.at[:, tokens]
         here = taking(wanted[:, tokens], slots, 0)
         taken[:slots], taken[slots:] = here, here
         spread = dot(projected[...], taken[...])
         for here in blocks(width, 32):
-            pre = source[here] + spread[here]
+            pre = xw[here, tokens] + spread[here]
             gate = sigmoid(pre)
             hidden = pre * gate
             factor[i % 2, here] = gate + hidden * (1.0 - gate)
@@ -371,11 +365,8 @@
 
     begin(0)
     for i, tokens in enumerate(chunks):
-        if i + 1 < len(chunks):
-            tw_loads[i].wait()
-            xw_loads[i].wait()
         minus = tw_last if i == len(chunks) - 1 else tw.at[:, tokens]
-        target = de_ref if i == len(chunks) - 1 else xw.at[:, tokens]
+        target = de_ref if i == len(chunks) - 1 else des.at[:, tokens]
         product = dot(grams[...], deep[i % 2])
         if i + 1 < len(chunks):
             begin(i + 1)
@@ -489,7 +480,7 @@
 
     column = [coarse_input]
     for k in range(1, far):
-        column.append(lax.ppermute(coarse_input, "far", [(p, (p + k) % far) for p in range(far)]))
+        column.append(lax.ppermute(coarse_input, "far", [(p, p ^ k) for p in range(far)]))
 
     steps = count // ROWS
     pair_shape = (2 * width, values)
@@ -566,20 +557,21 @@
         out_specs=(VMEM,) * 4,
     )(*near(next_wide), crops, own)
 
-    projected, slope, first = call(
+    projected, slope, xw, tw = call(
         functools.partial(context_kernel, patches, peers),
         "context",
         6 * patches * 16 * width * width,
         (
             pltpu.VMEM((width, 2 * patches * 16), BF16),
             pltpu.VMEM((patches * 16, width), F32),
-            pltpu.VMEM((width, ROWS), F32),
+            pltpu.VMEM((width, count), F32),
+            pltpu.VMEM((width, count - ROWS), F32),
         ),
         limit=ROOM,
-        in_specs=[SMEM] + [VMEM] * 4 + [HBM],
-        out_specs=(VMEM,) * 3,
-        scratch_shapes=[pltpu.VMEM((patches * 16, pixels), F32), pltpu.SemaphoreType.DMA],
-    )(crops, own, other, *near(coarses, projects), *fixed(xw))
+        in_specs=[SMEM] + [VMEM] * 4 + [HBM] * 2,
+        out_specs=(VMEM,) * 4,
+        scratch_shapes=[pltpu.VMEM((patches * 16, pixels), F32), pltpu.SemaphoreType.DMA((2,))],
+    )(crops, own, other, *near(coarses, projects), *fixed(xw, tw))
     de, last_de, deep, dslot = call(
         middle_kernel,
         "middle",
@@ -591,21 +583,18 @@
             pltpu.VMEM((patches * 16, width), F32),
         ),
         limit=ROOM,
-        in_specs=[VMEM] * 5 + [HBM] * 3,
+        in_specs=[VMEM] * 6 + [HBM],
         out_specs=(HBM,) + (VMEM,) * 3,
         scratch_shapes=[
-            pltpu.VMEM((width, count), F32),
             pltpu.VMEM((width, count), F32),
             pltpu.VMEM((2 * patches * 16, ROWS), BF16),
             pltpu.VMEM((2, width, ROWS), F32),
             pltpu.VMEM((2, 3 * width, ROWS), BF16),
             pltpu.VMEM((2 * width, ROWS), BF16),
             pltpu.SemaphoreType.DMA((steps,)),
-            pltpu.SemaphoreType.DMA((steps,)),
-            pltpu.SemaphoreType.DMA((steps,)),
             pltpu.SemaphoreType.DMA((2,)),
         ],
-    )(*near(projected, grams, wanted, first, tw_last), *fixed(xw, tw, pair))
+    )(*near(projected, grams, wanted, xw, tw, tw_last), *fixed(pair))
     back = call(
         closing_kernel,
         "closing",

time: 53.6 us -> 55.6 us (1.037)
  Pallas kernels: 28.3 us -> 29.8 us
    all_to_all x1, starting transfers between devices: 3.53 us -> 6.17 us  [body(): returned = lax.all_to_all(back, patch, 0, 0, tiled=True)]
    ppermute x3, starting transfers between devices: 7.93 us -> 5.68 us  [body(): lax.ppermute(coarse_input, 'far', [(p, p ^ k) for p in range(far)])]
    pallas_call x1, Pallas kernels: 2.24 us -> 3.47 us  [body(): call(functools.partial(context_kernel, patches, peers), 'context', 6 * pa...]
where the time goes in v16:
time: 55.6 us; the launch traced here: 55.3 us
  Pallas kernels  29.8 us (54%)
  starting transfers between devices  17 us (31%)
  waiting for transfers between devices  7.06 us (13%)
  between operations  0.77 us (1%)
  other arithmetic  0.62 us (1%)
    pallas_call x1, Pallas kernels, body(): call(input_kernel, 'input', 6 * count * values * width, (pltpu.HBM((width...  7.72 us
    all_to_all x1, starting transfers between devices, body(): returned = lax.all_to_all(back, patch, 0, 0, tiled=True)  6.17 us
    ppermute x3, starting transfers between devices, body(): lax.ppermute(coarse_input, 'far', [(p, p ^ k) for p in range(far)])  5.68 us
    pallas_call x1, Pallas kernels, body(): call(last_kernel, 'last', 6 * count * values * width, pltpu.HBM((count, v...  5.67 us
    pallas_call x1, Pallas kernels, body(): call(target_kernel, 'target', 6 * count * values * width, (pltpu.HBM((wid...  4.99 us
    pallas_call x1, Pallas kernels, body(): call(middle_kernel, 'middle', 6 * count * width * width, (pltpu.HBM((widt...  4.43 us
    all_to_all x1, waiting for transfers between devices, body(): returned = lax.all_to_all(back, patch, 0, 0, tiled=True)  4.37 us
    ppermute x3, starting transfers between devices, body(): lax.ppermute(column, ('lvl', 'y'), [(p, p ^ flip) for p in range(4)])  3.55 us
  transfers between devices with their start and end apart: 9, of which 3 were waited for; matrix products, arithmetic and copies ran while one was open for 0% of the time, Pallas kernels for 36%

profile of v16, /device:TPU:0, one launch (start us, length us, event | category | flops | bytes accessed | tf_op | source)
XLA Modules:
  0.0 55.3 jit_solution(9546431674257052920)
XLA Ops:
  0.6 4.1 %collective-permute-start.1 = (f32[1,32,192]{2,1,0:T(8,128)}, f32[1,32,192]{2,1,0:T(8,128)S(1)}, u32[]{:S(2)}, u32[]{:S(2)}) collective-permute-start(f32[1,32,192]{2,1,0:T(8,128)} %refs_0_.1), channel_id=1, source_target_pairs={{0,8},{4,12},{8,0},{12,4},{1,9},{5,13},{9,1},{13,5},{2,10},{6,14},... | collective-permute-start | bytes 73736 | tf_op jit(solution)/shard_map/ppermute | solution.py:483
  4.7 1.6 %collective-permute-start = (f32[1,32,192]{2,1,0:T(8,128)}, f32[1,32,192]{2,1,0:T(8,128)S(1)}, u32[]{:S(2)}, u32[]{:S(2)}) collective-permute-start(f32[1,32,192]{2,1,0:T(8,128)} %refs_0_.1), channel_id=1, source_target_pairs={{0,4},{4,0},{8,12},{12,8},{1,5},{5,1},{9,13},{13,9},{2,6},{6,2},{1... | collective-permute-start | bytes 73736 | tf_op jit(solution)/shard_map/ppermute | solution.py:483
  6.3 0.0 collective-permute-start.2
  6.3 0.0 copy-start
  6.3 7.7 %input.1 = (f32[320,2048]{1,0:T(8,128)}, bf16[640,768]{1,0:T(8,128)(2,1)}, f32[512,768]{1,0:T(8,128)S(1)}, bf16[320,2304]{1,0:T(8,128)(2,1)S(1)}, s32[4,8]{1,0:T(4,128)S(1)}) custom-call(f32[2048,768]{1,0:T(8,128)} %bitcast.9, f32[320,768]{1,0:T(8,128)} %bitcast.12, f32[2048,768]{1,0:T(8,128)} %bitcast.10, f32[320,768]{1,0:T(8,128)} %next_weight_hbm.1, ...), custom_call_target="tpu_custom_call" | custom-call | flops 3019898880 | bytes 18219264 | tf_op jit(solution)/shard_map/input/pallas_call | solution.py:488
  14.0 0.0 collective-permute-done.1.refs_2_
  14.1 0.0 collective-permute-done.refs_1_
  14.1 0.0 collective-permute-done.2.refs_3_
  14.1 0.0 copy-done
  14.1 0.1 stack.2.refs_0_
  14.2 2.7 %collective-permute-start.5 = (f32[192,128]{1,0:T(8,128)S(1)}, f32[192,128]{1,0:T(8,128)S(1)}, u32[]{:S(2)}, u32[]{:S(2)}) collective-permute-start(f32[192,128]{1,0:T(8,128)S(1)} %stack.2.refs_0_), channel_id=1, source_target_pairs={{0,18},{2,16},{16,2},{18,0},{1,19},{3,17},{17,3},{19,1},{4,22},{6,... | collective-permute-start | bytes 294920 | tf_op jit(solution)/shard_map/ppermute | solution.py:517
  16.9 0.5 collective-permute-start.4
  17.4 0.3 collective-permute-start.3
  17.7 5.0 %target.1 = (f32[320,2048]{1,0:T(8,128)}, f32[320,512]{1,0:T(8,128)S(1)}, bf16[384,320]{1,0:T(8,128)(2,1)S(1)}, bf16[640,320]{1,0:T(8,128)(2,1)S(1)}) custom-call(f32[2048,768]{1,0:T(8,128)} %bitcast.11, f32[192,320]{1,0:T(8,128)} %cwgt_hbm.1, f32[320,320]{1,0:T(8,128)} %xwgt_hbm.1, f32[512,768]{1,0:T(8,128)S(1)} %get-tuple-element.27.rows, ...), custom_call_target="tpu_custom_call" | custom-call | flops 3019898880 | bytes 9175040 | tf_op jit(solution)/shard_map/target/pallas_call | solution.py:518
  22.7 0.0 collective-permute-done.5.refs_3_
  22.7 0.0 collective-permute-done.4.refs_2_
  22.7 0.0 collective-permute-done.3.refs_1_
  22.8 0.1 collective-permute-start.6
  22.9 1.4 %prepare.1 = (bf16[320,960]{1,0:T(8,128)(2,1)S(1)}, s32[1,2048]{1,0:T(1,128)S(1)}, bf16[256,128]{1,0:T(8,128)(2,1)S(1)}, f32[128,64]{1,0:T(8,128)S(1)}) custom-call(bf16[320,2304]{1,0:T(8,128)(2,1)S(1)} %get-tuple-element.28.wide, s32[4,8]{1,0:T(4,128)S(1)} %get-tuple-element.25.crops_ref, f32[768,128]{1,0:T(8,128)S(1)} %stack.3.own_ref.before_ref), custom_call_target="tpu_custom_call" | custom-call | flops 629145600 | bytes 2801664 | tf_op jit(solution)/shard_map/prepare/pallas_call | solution.py:545
  24.3 0.3 collective-permute-done.6.other_ref
  24.6 3.5 %context.1 = (bf16[320,256]{1,0:T(8,128)(2,1)S(1)}, f32[128,320]{1,0:T(8,128)S(1)}, f32[320,2048]{1,0:T(8,128)S(1)}, f32[320,1536]{1,0:T(8,128)S(1)}) custom-call(s32[4,8]{1,0:T(4,128)S(1)} %get-tuple-element.25.crops_ref, f32[768,128]{1,0:T(8,128)S(1)} %stack.3.own_ref.before_ref, f32[768,128]{1,0:T(8,128)S(1)} %collective-permute-done.6.other_ref, ...), custom_call_target="tpu_custom_call" | custom-call | flops 78643200 | bytes 10158080 | tf_op jit(solution)/shard_map/context/pallas_call | solution.py:560
  28.1 4.4 %middle.1 = (f32[320,2048]{1,0:T(8,128)}, f32[320,512]{1,0:T(8,128)S(1)}, bf16[960,768]{1,0:T(8,128)(2,1)S(1)}, f32[128,320]{1,0:T(8,128)S(1)}) custom-call(bf16[320,256]{1,0:T(8,128)(2,1)S(1)} %get-tuple-element.32.projected, bf16[320,960]{1,0:T(8,128)(2,1)S(1)} %get-tuple-element.33.grams, s32[1,2048]{1,0:T(1,128)S(1)} %get-tuple-element.34.wanted, ...), custom_call_target="tpu_custom_call" | custom-call | flops 1258291200 | bytes 12779520 | tf_op jit(solution)/shard_map/middle/pallas_call | solution.py:575
  32.5 1.7 %closing.1 = f32[256,256]{1,0:T(8,128)} custom-call(f32[128,320]{1,0:T(8,128)S(1)} %get-tuple-element.39.dslot_ref, f32[128,320]{1,0:T(8,128)S(1)} %get-tuple-element.40.slope_ref, bf16[384,320]{1,0:T(8,128)(2,1)S(1)} %get-tuple-element.30.coarses, bf16[640,320]{1,0:T(8,128)(2,1)S(1)} %get-tuple-element.31.projects, ...), custom_call_target="tpu_custom_call" | custom-call | flops 78643200 | bytes 524288 | tf_op jit(solution)/shard_map/closing/pallas_call | solution.py:598
  34.2 6.2 %all-to-all-start = ((f32[16,16,256]{2,1,0:T(8,128)}), f32[16,16,256]{2,1,0:T(8,128)S(1)}, u32[]{:S(2)}, u32[]{:S(2)}) async-start(f32[16,16,256]{2,1,0:T(8,128)} %bitcast.4), calls=%async_computation | async-start | bytes 524288 | tf_op jit(solution)/shard_map/all_to_all | solution.py:607
  40.4 5.7 %last.1.done_ref = f32[2048,768]{1,0:T(8,128)} custom-call(f32[320,2048]{1,0:T(8,128)} %get-tuple-element.43.de_hbm, f32[320,512]{1,0:T(8,128)S(1)} %get-tuple-element.44.first, bf16[960,768]{1,0:T(8,128)(2,1)S(1)} %get-tuple-element.45.deep), custom_call_target="tpu_custom_call" | custom-call | flops 3019898880 | bytes 12582912 | tf_op jit(solution)/shard_map/last/pallas_call | solution.py:609
  46.0 4.4 %all-to-all-done = f32[16,16,256]{2,1,0:T(8,128)S(1)} async-done(((f32[16,16,256]{2,1,0:T(8,128)}), f32[16,16,256]{2,1,0:T(8,128)S(1)}, u32[]{:S(2)}, u32[]{:S(2)}) %all-to-all-start) | async-done | bytes 262176 | tf_op jit(solution)/shard_map/all_to_all | solution.py:607
  50.4 0.3 scatter.1
  50.7 1.6 %collective-permute-start.7 = (f32[1,32,192]{2,1,0:T(8,128)S(1)}, f32[1,32,192]{2,1,0:T(8,128)S(1)}, u32[]{:S(2)}, u32[]{:S(2)}) collective-permute-start(f32[1,32,192]{2,1,0:T(8,128)S(1)} %get-tuple-element.47), channel_id=1, source_target_pairs={{0,16},{16,0},{1,17},{17,1},{2,18},{18,2},{3,19},{19,3},{4,20},{20... | collective-permute-start | bytes 73736 | tf_op jit(solution)/shard_map/ppermute | solution.py:636
  52.3 2.4 %collective-permute-done.7 = f32[1,32,192]{2,1,0:T(8,128)S(1)} collective-permute-done((f32[1,32,192]{2,1,0:T(8,128)S(1)}, f32[1,32,192]{2,1,0:T(8,128)S(1)}, u32[]{:S(2)}, u32[]{:S(2)}) %collective-permute-start.7) | collective-permute-done | bytes 24608 | tf_op jit(solution)/shard_map/ppermute | solution.py:636
  54.7 0.6 %add.3 = f32[1,32,192]{2,1,0:T(8,128)} add(f32[1,32,192]{2,1,0:T(8,128)S(1)} %get-tuple-element.46, f32[1,32,192]{2,1,0:T(8,128)S(1)} %collective-permute-done.7) | non-fusion elementwise | flops 6144 | bytes 73728 | tf_op jit(solution)/shard_map/add | solution.py:636
  (1 shorter events, 0.0 us)
Async XLA Ops:
  0.6 13.4 %collective-permute-start.1 = (f32[1,32,192]{2,1,0:T(8,128)}, f32[1,32,192]{2,1,0:T(8,128)S(1)}, u32[]{:S(2)}, u32[]{:S(2)}) collective-permute-start(f32[1,32,192]{2,1,0:T(8,128)} %refs_0_.1), channel_id=1, source_target_pairs={{0,8},{4,12},{8,0},{12,4},{1,9},{5,13},{9,1},{13,5},{2,10},{6,14},... | collective-permute-start | bytes 73736 | tf_op jit(solution)/shard_map/ppermute | solution.py:483
  4.7 9.3 %collective-permute-start = (f32[1,32,192]{2,1,0:T(8,128)}, f32[1,32,192]{2,1,0:T(8,128)S(1)}, u32[]{:S(2)}, u32[]{:S(2)}) collective-permute-start(f32[1,32,192]{2,1,0:T(8,128)} %refs_0_.1), channel_id=1, source_target_pairs={{0,4},{4,0},{8,12},{12,8},{1,5},{5,1},{9,13},{13,9},{2,6},{6,2},{1... | collective-permute-start | bytes 73736 | tf_op jit(solution)/shard_map/ppermute | solution.py:483
  6.3 7.8 %collective-permute-start.2 = (f32[1,32,192]{2,1,0:T(8,128)}, f32[1,32,192]{2,1,0:T(8,128)S(1)}, u32[]{:S(2)}, u32[]{:S(2)}) collective-permute-start(f32[1,32,192]{2,1,0:T(8,128)} %refs_0_.1), channel_id=1, source_target_pairs={{0,12},{4,8},{8,4},{12,0},{1,13},{5,9},{9,5},{13,1},{2,14},{6,10},... | collective-permute-start | bytes 73736 | tf_op jit(solution)/shard_map/ppermute | solution.py:483
  6.3 7.8 %copy-start = (f32[1,32,192]{2,1,0:T(8,128)S(1)}, f32[1,32,192]{2,1,0:T(8,128)}, u32[]{:S(2)}) copy-start(f32[1,32,192]{2,1,0:T(8,128)} %refs_0_.1) | copy-start | bytes 73732
  14.2 8.6 %collective-permute-start.5 = (f32[192,128]{1,0:T(8,128)S(1)}, f32[192,128]{1,0:T(8,128)S(1)}, u32[]{:S(2)}, u32[]{:S(2)}) collective-permute-start(f32[192,128]{1,0:T(8,128)S(1)} %stack.2.refs_0_), channel_id=1, source_target_pairs={{0,18},{2,16},{16,2},{18,0},{1,19},{3,17},{17,3},{19,1},{4,22},{6,... | collective-permute-start | bytes 294920 | tf_op jit(solution)/shard_map/ppermute | solution.py:517
  16.9 5.8 %collective-permute-start.4 = (f32[192,128]{1,0:T(8,128)S(1)}, f32[192,128]{1,0:T(8,128)S(1)}, u32[]{:S(2)}, u32[]{:S(2)}) collective-permute-start(f32[192,128]{1,0:T(8,128)S(1)} %stack.2.refs_0_), channel_id=1, source_target_pairs={{0,16},{2,18},{16,0},{18,2},{1,17},{3,19},{17,1},{19,3},{4,20},{6,... | collective-permute-start | bytes 294920 | tf_op jit(solution)/shard_map/ppermute | solution.py:517
  17.4 5.3 %collective-permute-start.3 = (f32[192,128]{1,0:T(8,128)S(1)}, f32[192,128]{1,0:T(8,128)S(1)}, u32[]{:S(2)}, u32[]{:S(2)}) collective-permute-start(f32[192,128]{1,0:T(8,128)S(1)} %stack.2.refs_0_), channel_id=1, source_target_pairs={{0,2},{2,0},{16,18},{18,16},{1,3},{3,1},{17,19},{19,17},{4,6},{6,4... | collective-permute-start | bytes 294920 | tf_op jit(solution)/shard_map/ppermute | solution.py:517
  22.8 1.8 %collective-permute-start.6 = (f32[768,128]{1,0:T(8,128)S(1)}, f32[768,128]{1,0:T(8,128)S(1)}, u32[]{:S(2)}, u32[]{:S(2)}) collective-permute-start(f32[768,128]{1,0:T(8,128)S(1)} %stack.3.own_ref.before_ref), channel_id=1, source_target_pairs={{0,1},{1,0},{2,3},{3,2},{4,5},{5,4},{6,7},{7,6},{8,9},{9,8},{10,11... | collective-permute-start | bytes 1179656 | tf_op jit(solution)/shard_map/ppermute | solution.py:543
  34.2 16.2 %all-to-all-start = ((f32[16,16,256]{2,1,0:T(8,128)}), f32[16,16,256]{2,1,0:T(8,128)S(1)}, u32[]{:S(2)}, u32[]{:S(2)}) async-start(f32[16,16,256]{2,1,0:T(8,128)} %bitcast.4), calls=%async_computation | async-start | bytes 524288 | tf_op jit(solution)/shard_map/all_to_all | solution.py:607
  50.7 4.0 %collective-permute-start.7 = (f32[1,32,192]{2,1,0:T(8,128)S(1)}, f32[1,32,192]{2,1,0:T(8,128)S(1)}, u32[]{:S(2)}, u32[]{:S(2)}) collective-permute-start(f32[1,32,192]{2,1,0:T(8,128)S(1)} %get-tuple-element.47), channel_id=1, source_target_pairs={{0,16},{16,0},{1,17},{17,1},{2,18},{18,2},{3,19},{19,3},{4,20},{20... | collective-permute-start | bytes 73736 | tf_op jit(solution)/shard_map/ppermute | solution.py:636

commit v17 on v15

--- a/solution.py
+++ b/solution.py
@@ -79,17 +79,14 @@
     return pl.ds(pl.multiple_of(i * ROWS, ROWS), ROWS)
 
 
-def fill_wide(ref, high, low):
-    values = high.shape[1]
-    ref[:, :values], ref[:, values : 2 * values], ref[:, 2 * values :] = high, low, high
-
-
-def deep_product(wide, value, deep, out):
-    values = value.shape[1]
-    for here in blocks(deep.shape[0], 16):
-        high, low = split(value[here])
-        deep[here, :values], deep[here, values : 2 * values], deep[here, 2 * values :] = high, high, low
-    out[...] = dot(wide[...], deep[...], NT)
+def wide_product(pair, value, high, low, out):
+    width = pair.shape[0] // 2
+    for here in blocks(high.shape[0], 16):
+        high[here], low[here] = split(value[here])
+    both = dot(pair[...], high[...], NT)
+    rest = dot(pair[:width], low[...], NT)
+    for here in blocks(width, 32):
+        out[here] = both[here] + (both[shift(here, width)] + rest[here])
 
 
 def input_kernel(
@@ -101,15 +98,15 @@
     out_hbm,
     pair_hbm,
     next_rows,
-    next_wide,
+    next_pair,
     crops,
     x,
     out,
     weight,
     next_weight,
     pair,
-    wide,
-    deep,
+    high,
+    low,
     in_sems,
     out_sems,
     sems,
@@ -128,21 +125,24 @@
         pltpu.make_async_copy(out.at[:, here], out_hbm.at[:, here], out_sems.at[i])
         for i, here in enumerate(chunks)
     ]
-    fetch.start()
-    loads[0].start()
-    fetch.wait()
-    for copy in loads[1:] + [fetch_next, fetch_crops, fetch_rows]:
+    for copy in [fetch] + loads[:2]:
         copy.start()
-    high, low = split(weight[...])
-    fill_wide(wide, high, low)
-    pair[:width], pair[width:] = high, low
-    keep.start()
     for i, here in enumerate(chunks):
         loads[i].wait()
+        if i + 2 < len(chunks):
+            loads[i + 2].start()
+        if i == 0:
+            fetch.wait()
+            pair[:width], pair[width:] = split(weight[...])
+            keep.start()
+            fetch_next.start()
+        if i == 1:
+            fetch_rows.start()
+            fetch_crops.start()
         if i == len(chunks) - 1:
             fetch_next.wait()
-            fill_wide(next_wide, *split(next_weight[...]))
-        deep_product(wide, x.at[here], deep, out.at[:, here])
+            next_pair[:width], next_pair[width:] = split(next_weight[...])
+        wide_product(pair, x.at[here], high, low, out.at[:, here])
         stores[i].start()
     for copy in [keep, fetch_rows, fetch_crops] + stores:
         copy.wait()
@@ -153,14 +153,15 @@
     cwgt_hbm,
     xwgt_hbm,
     rows,
-    wide,
+    pair,
     out_hbm,
     out_last,
     coarses,
     projects,
     t,
     out,
-    deep,
+    high,
+    low,
     cwgt,
     xwgt,
     in_sems,
@@ -187,10 +188,10 @@
             loads[i - 1].wait()
         source = rows if i == 0 else t.at[here]
         if i < len(stores):
-            deep_product(wide, source, deep, out.at[:, here])
+            wide_product(pair, source, high, low, out.at[:, here])
             stores[i].start()
         else:
-            deep_product(wide, source, deep, out_last)
+            wide_product(pair, source, high, low, out_last)
     for copy in fetches:
         copy.wait()
     coarses[...] = jnp.concatenate(split(cwgt[...]), axis=0)
@@ -203,13 +204,11 @@
     return [slice(start, start + ROWS) for start in range(0, count, ROWS)]
 
 
-def prepare_kernel(patches, wide, crops_ref, before_ref, grams, wanted, lay, number):
+def prepare_kernel(patches, pair, crops_ref, before_ref, grams, wanted, lay, number):
     del before_ref
     width = grams.shape[0]
-    values = wide.shape[1] // 3
-    high = wide[:, :values]
-    mixed = dot(wide[:, values : 2 * values], high, NT)
-    grams[...] = side_by_side(dot(high, high, NT) + (mixed + mixed.T))
+    both = dot(pair[...], pair[:width], NT)
+    grams[...] = side_by_side(both[:width] + (both[width:] + both[width:].T))
     wanted[...] = slot_row(crops_ref, patches, wanted.shape[1] // patches)
     frame = row_value(crops_ref, 0, patches, (1, patches * 16), 1, 16)
     slot = lax.broadcasted_iota(jnp.int32, (1, patches * 16), 1) % 16
@@ -267,14 +266,20 @@
     coarses,
     projects,
     xw_hbm,
+    tw_hbm,
     projected_ref,
     slope_ref,
-    first_ref,
+    xw_first,
+    tw_first,
     rows,
-    sem,
+    sems,
 ):
-    fetch = pltpu.make_async_copy(xw_hbm.at[:, : first_ref.shape[1]], first_ref, sem)
-    fetch.start()
+    fetches = [
+        pltpu.make_async_copy(xw_hbm.at[:, : xw_first.shape[1]], xw_first, sems.at[0]),
+        pltpu.make_async_copy(tw_hbm.at[:, : tw_first.shape[1]], tw_first, sems.at[1]),
+    ]
+    for copy in fetches:
+        copy.start()
     pixels = coarses.shape[0] // 2
     width = projects.shape[1]
     far = peers // 4
@@ -301,14 +306,16 @@
     slope_ref[...] = gate * (1.0 + pre * (1.0 - gate))
     projected = through(pre * gate, projects, NN).T
     projected_ref[...] = jnp.concatenate(split(projected), axis=1)
-    fetch.wait()
+    for copy in fetches:
+        copy.wait()
 
 
 def middle_kernel(
     projected,
     grams,
     wanted,
-    first,
+    xw_first,
+    tw_first,
     tw_last,
     xw_hbm,
     tw_hbm,
@@ -334,11 +341,11 @@
     each = slots // len(chunks)
     tw_loads = [
         pltpu.make_async_copy(tw_hbm.at[:, here], tw.at[:, here], tw_sems.at[i])
-        for i, here in enumerate(chunks[:-1])
+        for i, here in enumerate(chunks[1:-1])
     ]
     xw_loads = [
         pltpu.make_async_copy(xw_hbm.at[:, here], xw.at[:, here], xw_sems.at[i])
-        for i, here in enumerate(chunks[1:])
+        for i, here in enumerate(chunks[2:])
     ]
     stores = [
         pltpu.make_async_copy(xw.at[:, here], de_hbm.at[:, here], out_sems.at[i])
@@ -356,7 +363,7 @@
 
     def begin(i):
         tokens = chunks[i]
-        source = first if i == 0 else xw.at[:, tokens]
+        source = xw_first.at[:, tokens] if i < 2 else xw.at[:, tokens]
         here = taking(wanted[:, tokens], slots, 0)
         taken[:slots], taken[slots:] = here, here
         spread = dot(projected[...], taken[...])
@@ -371,10 +378,10 @@
 
     begin(0)
     for i, tokens in enumerate(chunks):
-        if i + 1 < len(chunks):
-            tw_loads[i].wait()
-            xw_loads[i].wait()
-        minus = tw_last if i == len(chunks) - 1 else tw.at[:, tokens]
+        if 0 < i < len(chunks) - 1:
+            tw_loads[i - 1].wait()
+            xw_loads[i - 1].wait()
+        minus = tw_first if i == 0 else tw_last if i == len(chunks) - 1 else tw.at[:, tokens]
         target = de_ref if i == len(chunks) - 1 else xw.at[:, tokens]
         product = dot(grams[...], deep[i % 2])
         if i + 1 < len(chunks):
@@ -494,7 +501,7 @@
     steps = count // ROWS
     pair_shape = (2 * width, values)
     x, t = fine_input.reshape(count, values), fine_target.reshape(count, values)
-    xw, pair, rows, next_wide, crops = call(
+    xw, pair, rows, next_pair, crops = call(
         input_kernel,
         "input",
         6 * count * values * width,
@@ -502,7 +509,7 @@
             pltpu.HBM((width, count), F32),
             pltpu.HBM(pair_shape, BF16),
             pltpu.VMEM((ROWS, values), F32),
-            pltpu.VMEM((width, 3 * values), BF16),
+            pltpu.VMEM(pair_shape, BF16),
             pltpu.VMEM((4, patches), jnp.int32),
         ),
         in_specs=[HBM] * 5,
@@ -513,8 +520,8 @@
             pltpu.VMEM((width, values), F32),
             pltpu.VMEM((width, values), F32),
             pltpu.VMEM(pair_shape, BF16),
-            pltpu.VMEM((width, 3 * values), BF16),
-            pltpu.VMEM((ROWS, 3 * values), BF16),
+            pltpu.VMEM((ROWS, values), BF16),
+            pltpu.VMEM((ROWS, values), BF16),
             pltpu.SemaphoreType.DMA((steps,)),
             pltpu.SemaphoreType.DMA((steps,)),
             pltpu.SemaphoreType.DMA((5,)),
@@ -540,14 +547,15 @@
         scratch_shapes=[
             pltpu.VMEM((count, values), F32),
             pltpu.VMEM((width, count), F32),
-            pltpu.VMEM((ROWS, 3 * values), BF16),
+            pltpu.VMEM((ROWS, values), BF16),
+            pltpu.VMEM((ROWS, values), BF16),
             pltpu.VMEM((pixels, width), F32),
             pltpu.VMEM((width, width), F32),
             pltpu.SemaphoreType.DMA((steps,)),
             pltpu.SemaphoreType.DMA((steps,)),
             pltpu.SemaphoreType.DMA((2,)),
         ],
-    )(*fixed(t, coarse_weight, context_weight), *near(rows, next_wide))
+    )(*fixed(t, coarse_weight, context_weight), *near(rows, next_pair))
     own = stack(stack_kernel, own, tw, column.shape[0])
     other = lax.ppermute(own, "core", swap)
     (crops,) = near(crops)
@@ -564,22 +572,23 @@
         limit=ROOM,
         in_specs=[VMEM, SMEM, HBM],
         out_specs=(VMEM,) * 4,
-    )(*near(next_wide), crops, own)
-
-    projected, slope, first = call(
+    )(*near(next_pair), crops, own)
+
+    projected, slope, xw_first, tw_first = call(
         functools.partial(context_kernel, patches, peers),
         "context",
         6 * patches * 16 * width * width,
         (
             pltpu.VMEM((width, 2 * patches * 16), BF16),
             pltpu.VMEM((patches * 16, width), F32),
+            pltpu.VMEM((width, 2 * ROWS), F32),
             pltpu.VMEM((width, ROWS), F32),
         ),
         limit=ROOM,
-        in_specs=[SMEM] + [VMEM] * 4 + [HBM],
-        out_specs=(VMEM,) * 3,
-        scratch_shapes=[pltpu.VMEM((patches * 16, pixels), F32), pltpu.SemaphoreType.DMA],
-    )(crops, own, other, *near(coarses, projects), *fixed(xw))
+        in_specs=[SMEM] + [VMEM] * 4 + [HBM] * 2,
+        out_specs=(VMEM,) * 4,
+        scratch_shapes=[pltpu.VMEM((patches * 16, pixels), F32), pltpu.SemaphoreType.DMA((2,))],
+    )(crops, own, other, *near(coarses, projects), *fixed(xw, tw))
     de, last_de, deep, dslot = call(
         middle_kernel,
         "middle",
@@ -591,7 +600,7 @@
             pltpu.VMEM((patches * 16, width), F32),
         ),
         limit=ROOM,
-        in_specs=[VMEM] * 5 + [HBM] * 3,
+        in_specs=[VMEM] * 6 + [HBM] * 3,
         out_specs=(HBM,) + (VMEM,) * 3,
         scratch_shapes=[
             pltpu.VMEM((width, count), F32),
@@ -605,7 +614,7 @@
             pltpu.SemaphoreType.DMA((steps,)),
             pltpu.SemaphoreType.DMA((2,)),
         ],
-    )(*near(projected, grams, wanted, first, tw_last), *fixed(xw, tw, pair))
+    )(*near(projected, grams, wanted, xw_first, tw_first, tw_last), *fixed(xw, tw, pair))
     back = call(
         closing_kernel,
         "closing",

time: 53.6 us -> 52.6 us (0.981)
  Pallas kernels: 28.3 us -> 27.4 us
    pallas_call x1, Pallas kernels: 7.46 us -> 6.73 us  [body(): call(input_kernel, 'input', 6 * count * values * width, (pltpu.HBM((width...]
    pallas_call x1, Pallas kernels: 4.86 us -> 4.14 us  [body(): call(middle_kernel, 'middle', 6 * count * width * width, (pltpu.HBM((widt...]
  transfers between devices with their start and end apart: 9 -> 9, of which waited for: 3 -> 3; matrix products, arithmetic and copies ran while one was open for 0% -> 0% of each run, Pallas kernels for 36% -> 35%
where the time goes in v17:
time: 52.6 us; the launch traced here: 52.3 us
  Pallas kernels  27.4 us (52%)
  starting transfers between devices  16.6 us (32%)
  waiting for transfers between devices  6.85 us (13%)
  between operations  0.77 us (1%)
  other arithmetic  0.62 us (1%)
    ppermute x3, starting transfers between devices, body(): lax.ppermute(coarse_input, 'far', [(p, (p + k) % far) for p in range(far)])  7.93 us
    pallas_call x1, Pallas kernels, body(): call(input_kernel, 'input', 6 * count * values * width, (pltpu.HBM((width...  6.73 us
    pallas_call x1, Pallas kernels, body(): call(last_kernel, 'last', 6 * count * values * width, pltpu.HBM((count, v...  5.67 us
    pallas_call x1, Pallas kernels, body(): call(target_kernel, 'target', 6 * count * values * width, (pltpu.HBM((wid...  4.54 us
    all_to_all x1, waiting for transfers between devices, body(): returned = lax.all_to_all(back, patch, 0, 0, tiled=True)  4.33 us
    pallas_call x1, Pallas kernels, body(): call(middle_kernel, 'middle', 6 * count * width * width, (pltpu.HBM((widt...  4.14 us
    ppermute x3, starting transfers between devices, body(): lax.ppermute(column, ('lvl', 'y'), [(p, p ^ flip) for p in range(4)])  3.55 us
    all_to_all x1, starting transfers between devices, body(): returned = lax.all_to_all(back, patch, 0, 0, tiled=True)  3.53 us
  transfers between devices with their start and end apart: 9, of which 3 were waited for; matrix products, arithmetic and copies ran while one was open for 0% of the time, Pallas kernels for 35%

profile of v17, /device:TPU:0, one launch (start us, length us, event | category | flops | bytes accessed | tf_op | source)
XLA Modules:
  0.0 52.3 jit_solution(14091813559203821723)
XLA Ops:
  0.6 4.1 %collective-permute-start.1 = (f32[1,32,192]{2,1,0:T(8,128)}, f32[1,32,192]{2,1,0:T(8,128)S(1)}, u32[]{:S(2)}, u32[]{:S(2)}) collective-permute-start(f32[1,32,192]{2,1,0:T(8,128)} %refs_0_.1), channel_id=1, source_target_pairs={{0,8},{4,12},{8,0},{12,4},{1,9},{5,13},{9,1},{13,5},{2,10},{6,14},... | collective-permute-start | bytes 73736 | tf_op jit(solution)/shard_map/ppermute | solution.py:499
  4.7 1.6 %collective-permute-start = (f32[1,32,192]{2,1,0:T(8,128)}, f32[1,32,192]{2,1,0:T(8,128)S(1)}, u32[]{:S(2)}, u32[]{:S(2)}) collective-permute-start(f32[1,32,192]{2,1,0:T(8,128)} %refs_0_.1), channel_id=1, source_target_pairs={{0,4},{4,8},{8,12},{12,0},{1,5},{5,9},{9,13},{13,1},{2,6},{6,10},{... | collective-permute-start | bytes 73736 | tf_op jit(solution)/shard_map/ppermute | solution.py:499
  6.3 2.2 %collective-permute-start.2 = (f32[1,32,192]{2,1,0:T(8,128)}, f32[1,32,192]{2,1,0:T(8,128)S(1)}, u32[]{:S(2)}, u32[]{:S(2)}) collective-permute-start(f32[1,32,192]{2,1,0:T(8,128)} %refs_0_.1), channel_id=1, source_target_pairs={{0,12},{4,0},{8,4},{12,8},{1,13},{5,1},{9,5},{13,9},{2,14},{6,2},{... | collective-permute-start | bytes 73736 | tf_op jit(solution)/shard_map/ppermute | solution.py:499
  8.6 0.0 copy-start
  8.6 6.7 %input.1 = (f32[320,2048]{1,0:T(8,128)}, bf16[640,768]{1,0:T(8,128)(2,1)}, f32[512,768]{1,0:T(8,128)S(1)}, bf16[640,768]{1,0:T(8,128)(2,1)S(1)}, s32[4,8]{1,0:T(4,128)S(1)}) custom-call(f32[2048,768]{1,0:T(8,128)} %bitcast.9, f32[320,768]{1,0:T(8,128)} %bitcast.12, f32[2048,768]{1,0:T(8,128)} %bitcast.10, f32[320,768]{1,0:T(8,128)} %next_weight_hbm.1, ...), custom_call_target="tpu_custom_call" | custom-call | flops 3019898880 | bytes 16253184 | tf_op jit(solution)/shard_map/input/pallas_call | solution.py:504
  15.3 0.0 collective-permute-done.1.refs_2_
  15.3 0.0 collective-permute-done.refs_1_
  15.3 0.0 collective-permute-done.2.refs_3_
  15.3 0.0 copy-done
  15.3 0.1 stack.2.refs_0_
  15.4 2.5 %collective-permute-start.5 = (f32[192,128]{1,0:T(8,128)S(1)}, f32[192,128]{1,0:T(8,128)S(1)}, u32[]{:S(2)}, u32[]{:S(2)}) collective-permute-start(f32[192,128]{1,0:T(8,128)S(1)} %stack.2.refs_0_), channel_id=1, source_target_pairs={{0,18},{2,16},{16,2},{18,0},{1,19},{3,17},{17,3},{19,1},{4,22},{6,... | collective-permute-start | bytes 294920 | tf_op jit(solution)/shard_map/ppermute | solution.py:533
  17.9 0.5 %collective-permute-start.4 = (f32[192,128]{1,0:T(8,128)S(1)}, f32[192,128]{1,0:T(8,128)S(1)}, u32[]{:S(2)}, u32[]{:S(2)}) collective-permute-start(f32[192,128]{1,0:T(8,128)S(1)} %stack.2.refs_0_), channel_id=1, source_target_pairs={{0,16},{2,18},{16,0},{18,2},{1,17},{3,19},{17,1},{19,3},{4,20},{6,... | collective-permute-start | bytes 294920 | tf_op jit(solution)/shard_map/ppermute | solution.py:533
  18.5 0.5 collective-permute-start.3
  19.0 4.5 %target.1 = (f32[320,2048]{1,0:T(8,128)}, f32[320,512]{1,0:T(8,128)S(1)}, bf16[384,320]{1,0:T(8,128)(2,1)S(1)}, bf16[640,320]{1,0:T(8,128)(2,1)S(1)}) custom-call(f32[2048,768]{1,0:T(8,128)} %bitcast.11, f32[192,320]{1,0:T(8,128)} %cwgt_hbm.1, f32[320,320]{1,0:T(8,128)} %xwgt_hbm.1, f32[512,768]{1,0:T(8,128)S(1)} %get-tuple-element.27.rows, ...), custom_call_target="tpu_custom_call" | custom-call | flops 3019898880 | bytes 9175040 | tf_op jit(solution)/shard_map/target/pallas_call | solution.py:534
  23.5 0.0 collective-permute-done.5.refs_3_
  23.5 0.0 collective-permute-done.4.refs_2_
  23.5 0.0 collective-permute-done.3.refs_1_
  23.6 0.1 collective-permute-start.6
  23.7 1.6 %prepare.1 = (bf16[320,960]{1,0:T(8,128)(2,1)S(1)}, s32[1,2048]{1,0:T(1,128)S(1)}, bf16[256,128]{1,0:T(8,128)(2,1)S(1)}, f32[128,64]{1,0:T(8,128)S(1)}) custom-call(bf16[640,768]{1,0:T(8,128)(2,1)S(1)} %get-tuple-element.28.pair, s32[4,8]{1,0:T(4,128)S(1)} %get-tuple-element.25.crops_ref, f32[768,128]{1,0:T(8,128)S(1)} %stack.3.own_ref.before_ref), custom_call_target="tpu_custom_call" | custom-call | flops 629145600 | bytes 2801664 | tf_op jit(solution)/shard_map/prepare/pallas_call | solution.py:562
  25.3 0.1 collective-permute-done.6.other_ref
  25.4 2.7 %context.1 = (bf16[320,256]{1,0:T(8,128)(2,1)S(1)}, f32[128,320]{1,0:T(8,128)S(1)}, f32[320,1024]{1,0:T(8,128)S(1)}, f32[320,512]{1,0:T(8,128)S(1)}) custom-call(s32[4,8]{1,0:T(4,128)S(1)} %get-tuple-element.25.crops_ref, f32[768,128]{1,0:T(8,128)S(1)} %stack.3.own_ref.before_ref, f32[768,128]{1,0:T(8,128)S(1)} %collective-permute-done.6.other_ref, ...), custom_call_target="tpu_custom_call" | custom-call | flops 78643200 | bytes 4915200 | tf_op jit(solution)/shard_map/context/pallas_call | solution.py:577
  28.0 4.1 %middle.1 = (f32[320,2048]{1,0:T(8,128)}, f32[320,512]{1,0:T(8,128)S(1)}, bf16[960,768]{1,0:T(8,128)(2,1)S(1)}, f32[128,320]{1,0:T(8,128)S(1)}) custom-call(bf16[320,256]{1,0:T(8,128)(2,1)S(1)} %get-tuple-element.32.projected, bf16[320,960]{1,0:T(8,128)(2,1)S(1)} %get-tuple-element.33.grams, s32[1,2048]{1,0:T(1,128)S(1)} %get-tuple-element.34.wanted, ...), custom_call_target="tpu_custom_call" | custom-call | flops 1258291200 | bytes 12779520 | tf_op jit(solution)/shard_map/middle/pallas_call | solution.py:592
  32.2 1.7 %closing.1 = f32[256,256]{1,0:T(8,128)} custom-call(f32[128,320]{1,0:T(8,128)S(1)} %get-tuple-element.39.dslot_ref, f32[128,320]{1,0:T(8,128)S(1)} %get-tuple-element.40.slope_ref, bf16[384,320]{1,0:T(8,128)(2,1)S(1)} %get-tuple-element.30.coarses, bf16[640,320]{1,0:T(8,128)(2,1)S(1)} %get-tuple-element.31.projects, ...), custom_call_target="tpu_custom_call" | custom-call | flops 78643200 | bytes 524288 | tf_op jit(solution)/shard_map/closing/pallas_call | solution.py:618
  33.9 3.5 %all-to-all-start = ((f32[16,16,256]{2,1,0:T(8,128)}), f32[16,16,256]{2,1,0:T(8,128)S(1)}, u32[]{:S(2)}, u32[]{:S(2)}) async-start(f32[16,16,256]{2,1,0:T(8,128)} %bitcast.4), calls=%async_computation | async-start | bytes 524288 | tf_op jit(solution)/shard_map/all_to_all | solution.py:627
  37.4 5.7 %last.1.done_ref = f32[2048,768]{1,0:T(8,128)} custom-call(f32[320,2048]{1,0:T(8,128)} %get-tuple-element.43.de_hbm, f32[320,512]{1,0:T(8,128)S(1)} %get-tuple-element.44.first, bf16[960,768]{1,0:T(8,128)(2,1)S(1)} %get-tuple-element.45.deep), custom_call_target="tpu_custom_call" | custom-call | flops 3019898880 | bytes 12582912 | tf_op jit(solution)/shard_map/last/pallas_call | solution.py:629
  43.1 4.3 %all-to-all-done = f32[16,16,256]{2,1,0:T(8,128)S(1)} async-done(((f32[16,16,256]{2,1,0:T(8,128)}), f32[16,16,256]{2,1,0:T(8,128)S(1)}, u32[]{:S(2)}, u32[]{:S(2)}) %all-to-all-start) | async-done | bytes 262176 | tf_op jit(solution)/shard_map/all_to_all | solution.py:627
  47.4 0.3 scatter.1
  47.7 1.6 %collective-permute-start.7 = (f32[1,32,192]{2,1,0:T(8,128)S(1)}, f32[1,32,192]{2,1,0:T(8,128)S(1)}, u32[]{:S(2)}, u32[]{:S(2)}) collective-permute-start(f32[1,32,192]{2,1,0:T(8,128)S(1)} %get-tuple-element.47), channel_id=1, source_target_pairs={{0,16},{16,0},{1,17},{17,1},{2,18},{18,2},{3,19},{19,3},{4,20},{20... | collective-permute-start | bytes 73736 | tf_op jit(solution)/shard_map/ppermute | solution.py:656
  49.3 2.4 %collective-permute-done.7 = f32[1,32,192]{2,1,0:T(8,128)S(1)} collective-permute-done((f32[1,32,192]{2,1,0:T(8,128)S(1)}, f32[1,32,192]{2,1,0:T(8,128)S(1)}, u32[]{:S(2)}, u32[]{:S(2)}) %collective-permute-start.7) | collective-permute-done | bytes 24608 | tf_op jit(solution)/shard_map/ppermute | solution.py:656
  51.7 0.6 %add.3 = f32[1,32,192]{2,1,0:T(8,128)} add(f32[1,32,192]{2,1,0:T(8,128)S(1)} %get-tuple-element.46, f32[1,32,192]{2,1,0:T(8,128)S(1)} %collective-permute-done.7) | non-fusion elementwise | flops 6144 | bytes 73728 | tf_op jit(solution)/shard_map/add | solution.py:656
  (1 shorter events, 0.0 us)
Async XLA Ops:
  0.6 14.7 %collective-permute-start.1 = (f32[1,32,192]{2,1,0:T(8,128)}, f32[1,32,192]{2,1,0:T(8,128)S(1)}, u32[]{:S(2)}, u32[]{:S(2)}) collective-permute-start(f32[1,32,192]{2,1,0:T(8,128)} %refs_0_.1), channel_id=1, source_target_pairs={{0,8},{4,12},{8,0},{12,4},{1,9},{5,13},{9,1},{13,5},{2,10},{6,14},... | collective-permute-start | bytes 73736 | tf_op jit(solution)/shard_map/ppermute | solution.py:499
  4.7 10.6 %collective-permute-start = (f32[1,32,192]{2,1,0:T(8,128)}, f32[1,32,192]{2,1,0:T(8,128)S(1)}, u32[]{:S(2)}, u32[]{:S(2)}) collective-permute-start(f32[1,32,192]{2,1,0:T(8,128)} %refs_0_.1), channel_id=1, source_target_pairs={{0,4},{4,8},{8,12},{12,0},{1,5},{5,9},{9,13},{13,1},{2,6},{6,10},{... | collective-permute-start | bytes 73736 | tf_op jit(solution)/shard_map/ppermute | solution.py:499
  6.3 9.0 %collective-permute-start.2 = (f32[1,32,192]{2,1,0:T(8,128)}, f32[1,32,192]{2,1,0:T(8,128)S(1)}, u32[]{:S(2)}, u32[]{:S(2)}) collective-permute-start(f32[1,32,192]{2,1,0:T(8,128)} %refs_0_.1), channel_id=1, source_target_pairs={{0,12},{4,0},{8,4},{12,8},{1,13},{5,1},{9,5},{13,9},{2,14},{6,2},{... | collective-permute-start | bytes 73736 | tf_op jit(solution)/shard_map/ppermute | solution.py:499
  8.6 6.8 %copy-start = (f32[1,32,192]{2,1,0:T(8,128)S(1)}, f32[1,32,192]{2,1,0:T(8,128)}, u32[]{:S(2)}) copy-start(f32[1,32,192]{2,1,0:T(8,128)} %refs_0_.1) | copy-start | bytes 73732
  15.4 8.1 %collective-permute-start.5 = (f32[192,128]{1,0:T(8,128)S(1)}, f32[192,128]{1,0:T(8,128)S(1)}, u32[]{:S(2)}, u32[]{:S(2)}) collective-permute-start(f32[192,128]{1,0:T(8,128)S(1)} %stack.2.refs_0_), channel_id=1, source_target_pairs={{0,18},{2,16},{16,2},{18,0},{1,19},{3,17},{17,3},{19,1},{4,22},{6,... | collective-permute-start | bytes 294920 | tf_op jit(solution)/shard_map/ppermute | solution.py:533
  17.9 5.6 %collective-permute-start.4 = (f32[192,128]{1,0:T(8,128)S(1)}, f32[192,128]{1,0:T(8,128)S(1)}, u32[]{:S(2)}, u32[]{:S(2)}) collective-permute-start(f32[192,128]{1,0:T(8,128)S(1)} %stack.2.refs_0_), channel_id=1, source_target_pairs={{0,16},{2,18},{16,0},{18,2},{1,17},{3,19},{17,1},{19,3},{4,20},{6,... | collective-permute-start | bytes 294920 | tf_op jit(solution)/shard_map/ppermute | solution.py:533
  18.5 5.1 %collective-permute-start.3 = (f32[192,128]{1,0:T(8,128)S(1)}, f32[192,128]{1,0:T(8,128)S(1)}, u32[]{:S(2)}, u32[]{:S(2)}) collective-permute-start(f32[192,128]{1,0:T(8,128)S(1)} %stack.2.refs_0_), channel_id=1, source_target_pairs={{0,2},{2,0},{16,18},{18,16},{1,3},{3,1},{17,19},{19,17},{4,6},{6,4... | collective-permute-start | bytes 294920 | tf_op jit(solution)/shard_map/ppermute | solution.py:533
  23.6 1.8 %collective-permute-start.6 = (f32[768,128]{1,0:T(8,128)S(1)}, f32[768,128]{1,0:T(8,128)S(1)}, u32[]{:S(2)}, u32[]{:S(2)}) collective-permute-start(f32[768,128]{1,0:T(8,128)S(1)} %stack.3.own_ref.before_ref), channel_id=1, source_target_pairs={{0,1},{1,0},{2,3},{3,2},{4,5},{5,4},{6,7},{7,6},{8,9},{9,8},{10,11... | collective-permute-start | bytes 1179656 | tf_op jit(solution)/shard_map/ppermute | solution.py:560
  33.9 13.5 %all-to-all-start = ((f32[16,16,256]{2,1,0:T(8,128)}), f32[16,16,256]{2,1,0:T(8,128)S(1)}, u32[]{:S(2)}, u32[]{:S(2)}) async-start(f32[16,16,256]{2,1,0:T(8,128)} %bitcast.4), calls=%async_computation | async-start | bytes 524288 | tf_op jit(solution)/shard_map/all_to_all | solution.py:627
  47.7 4.0 %collective-permute-start.7 = (f32[1,32,192]{2,1,0:T(8,128)S(1)}, f32[1,32,192]{2,1,0:T(8,128)S(1)}, u32[]{:S(2)}, u32[]{:S(2)}) collective-permute-start(f32[1,32,192]{2,1,0:T(8,128)S(1)} %get-tuple-element.47), channel_id=1, source_target_pairs={{0,16},{16,0},{1,17},{17,1},{2,18},{18,2},{3,19},{19,3},{4,20},{20... | collective-permute-start | bytes 73736 | tf_op jit(solution)/shard_map/ppermute | solution.py:656

commit v18 on v17

--- a/solution.py
+++ b/solution.py
@@ -96,6 +96,7 @@
     next_weight_hbm,
     crops_hbm,
     out_hbm,
+    out_last,
     pair_hbm,
     next_rows,
     next_pair,
@@ -123,7 +124,7 @@
     ]
     stores = [
         pltpu.make_async_copy(out.at[:, here], out_hbm.at[:, here], out_sems.at[i])
-        for i, here in enumerate(chunks)
+        for i, here in enumerate(chunks[:-1])
     ]
     for copy in [fetch] + loads[:2]:
         copy.start()
@@ -142,8 +143,10 @@
         if i == len(chunks) - 1:
             fetch_next.wait()
             next_pair[:width], next_pair[width:] = split(next_weight[...])
-        wide_product(pair, x.at[here], high, low, out.at[:, here])
-        stores[i].start()
+        target = out.at[:, here] if i < len(stores) else out_last
+        wide_product(pair, x.at[here], high, low, target)
+        if i < len(stores):
+            stores[i].start()
     for copy in [keep, fetch_rows, fetch_crops] + stores:
         copy.wait()
 
@@ -154,7 +157,9 @@
     xwgt_hbm,
     rows,
     pair,
+    before_last,
     out_hbm,
+    before_hbm,
     out_last,
     coarses,
     projects,
@@ -181,7 +186,8 @@
         pltpu.make_async_copy(out.at[:, here], out_hbm.at[:, here], out_sems.at[i])
         for i, here in enumerate(chunks[:-1])
     ]
-    for copy in loads + fetches:
+    keep = pltpu.make_async_copy(before_last, before_hbm, sems.at[2])
+    for copy in loads + fetches + [keep]:
         copy.start()
     for i, here in enumerate(chunks):
         if i > 0:
@@ -196,7 +202,7 @@
         copy.wait()
     coarses[...] = jnp.concatenate(split(cwgt[...]), axis=0)
     projects[...] = jnp.concatenate(split(xwgt[...]), axis=0)
-    for copy in stores:
+    for copy in stores + [keep]:
         copy.wait()
 
 
@@ -318,6 +324,7 @@
     tw_first,
     tw_last,
     xw_hbm,
+    xw_last,
     tw_hbm,
     pair_hbm,
     de_hbm,
@@ -345,8 +352,9 @@
     ]
     xw_loads = [
         pltpu.make_async_copy(xw_hbm.at[:, here], xw.at[:, here], xw_sems.at[i])
-        for i, here in enumerate(chunks[2:])
-    ]
+        for i, here in enumerate(chunks[1:-1])
+    ]
+    xw_loads.append(pltpu.make_async_copy(xw_last, xw.at[:, chunks[-1]], xw_sems.at[len(xw_loads)]))
     stores = [
         pltpu.make_async_copy(xw.at[:, here], de_hbm.at[:, here], out_sems.at[i])
         for i, here in enumerate(chunks[:-1])
@@ -355,15 +363,11 @@
         pltpu.make_async_copy(pair_hbm, deep_ref.at[: 2 * width], sems.at[0]),
         pltpu.make_async_copy(pair_hbm.at[:width], deep_ref.at[2 * width :], sems.at[1]),
     ]
-    for pair in zip(tw_loads, xw_loads):
-        for copy in pair:
-            copy.start()
-    for copy in fetches:
-        copy.start()
+    xw_loads[0].start()
 
     def begin(i):
         tokens = chunks[i]
-        source = xw_first.at[:, tokens] if i < 2 else xw.at[:, tokens]
+        source = xw_first if i == 0 else xw.at[:, tokens]
         here = taking(wanted[:, tokens], slots, 0)
         taken[:slots], taken[slots:] = here, here
         spread = dot(projected[...], taken[...])
@@ -377,10 +381,17 @@
                 deep[i % 2, shift(here, part * width)] = value
 
     begin(0)
+    for pair in zip(tw_loads, xw_loads[1:]):
+        for copy in pair:
+            copy.start()
     for i, tokens in enumerate(chunks):
+        if i < len(xw_loads):
+            xw_loads[i].wait()
         if 0 < i < len(chunks) - 1:
             tw_loads[i - 1].wait()
-            xw_loads[i - 1].wait()
+        if i == 1:
+            for copy in fetches:
+                copy.start()
         minus = tw_first if i == 0 else tw_last if i == len(chunks) - 1 else tw.at[:, tokens]
         target = de_ref if i == len(chunks) - 1 else xw.at[:, tokens]
         product = dot(grams[...], deep[i % 2])
@@ -501,19 +512,20 @@
     steps = count // ROWS
     pair_shape = (2 * width, values)
     x, t = fine_input.reshape(count, values), fine_target.reshape(count, values)
-    xw, pair, rows, next_pair, crops = call(
+    xw, xw_last, pair, rows, next_pair, crops = call(
         input_kernel,
         "input",
         6 * count * values * width,
         (
-            pltpu.HBM((width, count), F32),
+            pltpu.HBM((width, count - ROWS), F32),
+            pltpu.VMEM((width, ROWS), F32),
             pltpu.HBM(pair_shape, BF16),
             pltpu.VMEM((ROWS, values), F32),
             pltpu.VMEM(pair_shape, BF16),
             pltpu.VMEM((4, patches), jnp.int32),
         ),
         in_specs=[HBM] * 5,
-        out_specs=(HBM, HBM, VMEM, VMEM, VMEM),
+        out_specs=(HBM, VMEM, HBM, VMEM, VMEM, VMEM),
         scratch_shapes=[
             pltpu.VMEM((count, values), F32),
             pltpu.VMEM((width, count), F32),
@@ -531,19 +543,20 @@
     own = [column]
     for flip in range(1, 4):
         own.append(lax.ppermute(column, ("lvl", "y"), [(p, p ^ flip) for p in range(4)]))
-    tw, tw_last, coarses, projects = call(
+    tw, xw_last, tw_last, coarses, projects = call(
         target_kernel,
         "target",
         6 * count * values * width,
         (
-            pltpu.HBM((width, count), F32),
+            pltpu.HBM((width, count - ROWS), F32),
+            pltpu.HBM((width, ROWS), F32),
             pltpu.VMEM((width, ROWS), F32),
             pltpu.VMEM((2 * pixels, width), BF16),
             pltpu.VMEM((2 * width, width), BF16),
         ),
         limit=ROOM,
-        in_specs=[HBM] * 3 + [VMEM] * 2,
-        out_specs=(HBM, VMEM, VMEM, VMEM),
+        in_specs=[HBM] * 3 + [VMEM] * 3,
+        out_specs=(HBM, HBM, VMEM, VMEM, VMEM),
         scratch_shapes=[
             pltpu.VMEM((count, values), F32),
             pltpu.VMEM((width, count), F32),
@@ -553,9 +566,9 @@
             pltpu.VMEM((width, width), F32),
             pltpu.SemaphoreType.DMA((steps,)),
             pltpu.SemaphoreType.DMA((steps,)),
-            pltpu.SemaphoreType.DMA((2,)),
+            pltpu.SemaphoreType.DMA((3,)),
         ],
-    )(*fixed(t, coarse_weight, context_weight), *near(rows, next_pair))
+    )(*fixed(t, coarse_weight, context_weight), *near(rows, next_pair, xw_last))
     own = stack(stack_kernel, own, tw, column.shape[0])
     other = lax.ppermute(own, "core", swap)
     (crops,) = near(crops)
@@ -581,7 +594,7 @@
         (
             pltpu.VMEM((width, 2 * patches * 16), BF16),
             pltpu.VMEM((patches * 16, width), F32),
-            pltpu.VMEM((width, 2 * ROWS), F32),
+            pltpu.VMEM((width, ROWS), F32),
             pltpu.VMEM((width, ROWS), F32),
         ),
         limit=ROOM,
@@ -600,7 +613,7 @@
             pltpu.VMEM((patches * 16, width), F32),
         ),
         limit=ROOM,
-        in_specs=[VMEM] * 6 + [HBM] * 3,
+        in_specs=[VMEM] * 6 + [HBM] * 4,
         out_specs=(HBM,) + (VMEM,) * 3,
         scratch_shapes=[
             pltpu.VMEM((width, count), F32),
@@ -614,7 +627,7 @@
             pltpu.SemaphoreType.DMA((steps,)),
             pltpu.SemaphoreType.DMA((2,)),
         ],
-    )(*near(projected, grams, wanted, xw_first, tw_first, tw_last), *fixed(xw, tw, pair))
+    )(*near(projected, grams, wanted, xw_first, tw_first, tw_last), *fixed(xw, xw_last, tw, pair))
     back = call(
         closing_kernel,
         "closing",

time: 52.6 us -> 52.4 us (level)
    pallas_call x1, Pallas kernels: 6.73 us -> 5.9 us  [body(): call(input_kernel, 'input', 6 * count * values * width, (pltpu.HBM((width...]
    pallas_call x1, Pallas kernels: 4.14 us -> 4.68 us  [body(): call(middle_kernel, 'middle', 6 * count * width * width, (pltpu.HBM((widt...]
where the time goes in v18:
time: 52.4 us; the launch traced here: 52.2 us
  Pallas kernels  27.3 us (52%)
  starting transfers between devices  16.6 us (32%)
  waiting for transfers between devices  6.85 us (13%)
  between operations  0.77 us (1%)
  other arithmetic  0.62 us (1%)
    ppermute x3, starting transfers between devices, body(): lax.ppermute(coarse_input, 'far', [(p, (p + k) % far) for p in range(far)])  7.93 us
    pallas_call x1, Pallas kernels, body(): call(input_kernel, 'input', 6 * count * values * width, (pltpu.HBM((width...  5.9 us
    pallas_call x1, Pallas kernels, body(): call(last_kernel, 'last', 6 * count * values * width, pltpu.HBM((count, v...  5.67 us
    pallas_call x1, Pallas kernels, body(): call(target_kernel, 'target', 6 * count * values * width, (pltpu.HBM((wid...  4.91 us
    pallas_call x1, Pallas kernels, body(): call(middle_kernel, 'middle', 6 * count * width * width, (pltpu.HBM((widt...  4.68 us
    all_to_all x1, waiting for transfers between devices, body(): returned = lax.all_to_all(back, patch, 0, 0, tiled=True)  4.33 us
    ppermute x3, starting transfers between devices, body(): lax.ppermute(column, ('lvl', 'y'), [(p, p ^ flip) for p in range(4)])  3.55 us
    all_to_all x1, starting transfers between devices, body(): returned = lax.all_to_all(back, patch, 0, 0, tiled=True)  3.53 us
  transfers between devices with their start and end apart: 9, of which 3 were waited for; matrix products, arithmetic and copies ran while one was open for 0% of the time, Pallas kernels for 35%

profile of v18, /device:TPU:0, one launch (start us, length us, event | category | flops | bytes accessed | tf_op | source)
XLA Modules:
  0.0 52.2 jit_solution(10237156907095050231)
XLA Ops:
  0.6 4.1 %collective-permute-start.1 = (f32[1,32,192]{2,1,0:T(8,128)}, f32[1,32,192]{2,1,0:T(8,128)S(1)}, u32[]{:S(2)}, u32[]{:S(2)}) collective-permute-start(f32[1,32,192]{2,1,0:T(8,128)} %refs_0_.1), channel_id=1, source_target_pairs={{0,8},{4,12},{8,0},{12,4},{1,9},{5,13},{9,1},{13,5},{2,10},{6,14},... | collective-permute-start | bytes 73736 | tf_op jit(solution)/shard_map/ppermute | solution.py:510
  4.7 1.6 %collective-permute-start = (f32[1,32,192]{2,1,0:T(8,128)}, f32[1,32,192]{2,1,0:T(8,128)S(1)}, u32[]{:S(2)}, u32[]{:S(2)}) collective-permute-start(f32[1,32,192]{2,1,0:T(8,128)} %refs_0_.1), channel_id=1, source_target_pairs={{0,4},{4,8},{8,12},{12,0},{1,5},{5,9},{9,13},{13,1},{2,6},{6,10},{... | collective-permute-start | bytes 73736 | tf_op jit(solution)/shard_map/ppermute | solution.py:510
  6.3 2.2 %collective-permute-start.2 = (f32[1,32,192]{2,1,0:T(8,128)}, f32[1,32,192]{2,1,0:T(8,128)S(1)}, u32[]{:S(2)}, u32[]{:S(2)}) collective-permute-start(f32[1,32,192]{2,1,0:T(8,128)} %refs_0_.1), channel_id=1, source_target_pairs={{0,12},{4,0},{8,4},{12,8},{1,13},{5,1},{9,5},{13,9},{2,14},{6,2},{... | collective-permute-start | bytes 73736 | tf_op jit(solution)/shard_map/ppermute | solution.py:510
  8.6 0.0 copy-start
  8.6 5.9 %input.1 = (f32[320,1536]{1,0:T(8,128)}, f32[320,512]{1,0:T(8,128)S(1)}, bf16[640,768]{1,0:T(8,128)(2,1)}, f32[512,768]{1,0:T(8,128)S(1)}, bf16[640,768]{1,0:T(8,128)(2,1)S(1)}, /*index=5*/s32[4,8]{1,0:T(4,128)S(1)}) custom-call(f32[2048,768]{1,0:T(8,128)} %bitcast.9, f32[320,768]{1,0:T(8,128)} %bitcast.12, f32[2048,768]{1,0:T(8,128)} %bitcast.10, ...), custom_call_target="tpu_custom_call" | custom-call | flops 3019898880 | bytes 16253184 | tf_op jit(solution)/shard_map/input/pallas_call | solution.py:515
  14.5 0.0 collective-permute-done.1.refs_2_
  14.5 0.0 collective-permute-done.refs_1_
  14.5 0.0 collective-permute-done.2.refs_3_
  14.5 0.0 copy-done
  14.5 0.1 stack.2.refs_0_
  14.6 2.5 %collective-permute-start.5 = (f32[192,128]{1,0:T(8,128)S(1)}, f32[192,128]{1,0:T(8,128)S(1)}, u32[]{:S(2)}, u32[]{:S(2)}) collective-permute-start(f32[192,128]{1,0:T(8,128)S(1)} %stack.2.refs_0_), channel_id=1, source_target_pairs={{0,18},{2,16},{16,2},{18,0},{1,19},{3,17},{17,3},{19,1},{4,22},{6,... | collective-permute-start | bytes 294920 | tf_op jit(solution)/shard_map/ppermute | solution.py:545
  17.1 0.5 %collective-permute-start.4 = (f32[192,128]{1,0:T(8,128)S(1)}, f32[192,128]{1,0:T(8,128)S(1)}, u32[]{:S(2)}, u32[]{:S(2)}) collective-permute-start(f32[192,128]{1,0:T(8,128)S(1)} %stack.2.refs_0_), channel_id=1, source_target_pairs={{0,16},{2,18},{16,0},{18,2},{1,17},{3,19},{17,1},{19,3},{4,20},{6,... | collective-permute-start | bytes 294920 | tf_op jit(solution)/shard_map/ppermute | solution.py:545
  17.6 0.5 collective-permute-start.3
  18.1 4.9 %target.1 = (f32[320,1536]{1,0:T(8,128)}, f32[320,512]{1,0:T(8,128)}, f32[320,512]{1,0:T(8,128)S(1)}, bf16[384,320]{1,0:T(8,128)(2,1)S(1)}, bf16[640,320]{1,0:T(8,128)(2,1)S(1)}) custom-call(f32[2048,768]{1,0:T(8,128)} %bitcast.11, f32[192,320]{1,0:T(8,128)} %cwgt_hbm.1, f32[320,320]{1,0:T(8,128)} %xwgt_hbm.1, f32[512,768]{1,0:T(8,128)S(1)} %get-tuple-element.29.rows, ...), custom_call_target="tpu_custom_call" | custom-call | flops 3019898880 | bytes 9175040 | tf_op jit(solution)/shard_map/target/pallas_call | solution.py:546
  23.1 0.0 collective-permute-done.5.refs_3_
  23.1 0.0 collective-permute-done.4.refs_2_
  23.1 0.0 collective-permute-done.3.refs_1_
  23.1 0.1 collective-permute-start.6
  23.2 1.6 %prepare.1 = (bf16[320,960]{1,0:T(8,128)(2,1)S(1)}, s32[1,2048]{1,0:T(1,128)S(1)}, bf16[256,128]{1,0:T(8,128)(2,1)S(1)}, f32[128,64]{1,0:T(8,128)S(1)}) custom-call(bf16[640,768]{1,0:T(8,128)(2,1)S(1)} %get-tuple-element.30.pair, s32[4,8]{1,0:T(4,128)S(1)} %get-tuple-element.27.crops_ref, f32[768,128]{1,0:T(8,128)S(1)} %stack.3.own_ref.before_ref), custom_call_target="tpu_custom_call" | custom-call | flops 629145600 | bytes 2801664 | tf_op jit(solution)/shard_map/prepare/pallas_call | solution.py:575
  24.8 0.1 collective-permute-done.6.other_ref
  24.9 2.4 %context.1 = (bf16[320,256]{1,0:T(8,128)(2,1)S(1)}, f32[128,320]{1,0:T(8,128)S(1)}, f32[320,512]{1,0:T(8,128)S(1)}, f32[320,512]{1,0:T(8,128)S(1)}) custom-call(s32[4,8]{1,0:T(4,128)S(1)} %get-tuple-element.27.crops_ref, f32[768,128]{1,0:T(8,128)S(1)} %stack.3.own_ref.before_ref, f32[768,128]{1,0:T(8,128)S(1)} %collective-permute-done.6.other_ref, ...), custom_call_target="tpu_custom_call" | custom-call | flops 78643200 | bytes 3604480 | tf_op jit(solution)/shard_map/context/pallas_call | solution.py:590
  27.4 4.7 %middle.1 = (f32[320,2048]{1,0:T(8,128)}, f32[320,512]{1,0:T(8,128)S(1)}, bf16[960,768]{1,0:T(8,128)(2,1)S(1)}, f32[128,320]{1,0:T(8,128)S(1)}) custom-call(bf16[320,256]{1,0:T(8,128)(2,1)S(1)} %get-tuple-element.35.projected, bf16[320,960]{1,0:T(8,128)(2,1)S(1)} %get-tuple-element.36.grams, s32[1,2048]{1,0:T(1,128)S(1)} %get-tuple-element.37.wanted, ...), custom_call_target="tpu_custom_call" | custom-call | flops 1258291200 | bytes 12779520 | tf_op jit(solution)/shard_map/middle/pallas_call | solution.py:605
  32.1 1.7 %closing.1 = f32[256,256]{1,0:T(8,128)} custom-call(f32[128,320]{1,0:T(8,128)S(1)} %get-tuple-element.43.dslot_ref, f32[128,320]{1,0:T(8,128)S(1)} %get-tuple-element.44.slope_ref, bf16[384,320]{1,0:T(8,128)(2,1)S(1)} %get-tuple-element.33.coarses, bf16[640,320]{1,0:T(8,128)(2,1)S(1)} %get-tuple-element.34.projects, ...), custom_call_target="tpu_custom_call" | custom-call | flops 78643200 | bytes 524288 | tf_op jit(solution)/shard_map/closing/pallas_call | solution.py:631
  33.7 3.5 %all-to-all-start = ((f32[16,16,256]{2,1,0:T(8,128)}), f32[16,16,256]{2,1,0:T(8,128)S(1)}, u32[]{:S(2)}, u32[]{:S(2)}) async-start(f32[16,16,256]{2,1,0:T(8,128)} %bitcast.4), calls=%async_computation | async-start | bytes 524288 | tf_op jit(solution)/shard_map/all_to_all | solution.py:640
  37.3 5.7 %last.1.done_ref = f32[2048,768]{1,0:T(8,128)} custom-call(f32[320,2048]{1,0:T(8,128)} %get-tuple-element.47.de_hbm, f32[320,512]{1,0:T(8,128)S(1)} %get-tuple-element.48.first, bf16[960,768]{1,0:T(8,128)(2,1)S(1)} %get-tuple-element.49.deep), custom_call_target="tpu_custom_call" | custom-call | flops 3019898880 | bytes 12582912 | tf_op jit(solution)/shard_map/last/pallas_call | solution.py:642
  43.0 4.3 %all-to-all-done = f32[16,16,256]{2,1,0:T(8,128)S(1)} async-done(((f32[16,16,256]{2,1,0:T(8,128)}), f32[16,16,256]{2,1,0:T(8,128)S(1)}, u32[]{:S(2)}, u32[]{:S(2)}) %all-to-all-start) | async-done | bytes 262176 | tf_op jit(solution)/shard_map/all_to_all | solution.py:640
  47.3 0.3 scatter.1
  47.6 1.6 %collective-permute-start.7 = (f32[1,32,192]{2,1,0:T(8,128)S(1)}, f32[1,32,192]{2,1,0:T(8,128)S(1)}, u32[]{:S(2)}, u32[]{:S(2)}) collective-permute-start(f32[1,32,192]{2,1,0:T(8,128)S(1)} %get-tuple-element.51), channel_id=1, source_target_pairs={{0,16},{16,0},{1,17},{17,1},{2,18},{18,2},{3,19},{19,3},{4,20},{20... | collective-permute-start | bytes 73736 | tf_op jit(solution)/shard_map/ppermute | solution.py:669
  49.1 2.4 %collective-permute-done.7 = f32[1,32,192]{2,1,0:T(8,128)S(1)} collective-permute-done((f32[1,32,192]{2,1,0:T(8,128)S(1)}, f32[1,32,192]{2,1,0:T(8,128)S(1)}, u32[]{:S(2)}, u32[]{:S(2)}) %collective-permute-start.7) | collective-permute-done | bytes 24608 | tf_op jit(solution)/shard_map/ppermute | solution.py:669
  51.6 0.6 %add.3 = f32[1,32,192]{2,1,0:T(8,128)} add(f32[1,32,192]{2,1,0:T(8,128)S(1)} %get-tuple-element.50, f32[1,32,192]{2,1,0:T(8,128)S(1)} %collective-permute-done.7) | non-fusion elementwise | flops 6144 | bytes 73728 | tf_op jit(solution)/shard_map/add | solution.py:669
  (1 shorter events, 0.0 us)
Async XLA Ops:
  0.6 13.8 %collective-permute-start.1 = (f32[1,32,192]{2,1,0:T(8,128)}, f32[1,32,192]{2,1,0:T(8,128)S(1)}, u32[]{:S(2)}, u32[]{:S(2)}) collective-permute-start(f32[1,32,192]{2,1,0:T(8,128)} %refs_0_.1), channel_id=1, source_target_pairs={{0,8},{4,12},{8,0},{12,4},{1,9},{5,13},{9,1},{13,5},{2,10},{6,14},... | collective-permute-start | bytes 73736 | tf_op jit(solution)/shard_map/ppermute | solution.py:510
  4.7 9.8 %collective-permute-start = (f32[1,32,192]{2,1,0:T(8,128)}, f32[1,32,192]{2,1,0:T(8,128)S(1)}, u32[]{:S(2)}, u32[]{:S(2)}) collective-permute-start(f32[1,32,192]{2,1,0:T(8,128)} %refs_0_.1), channel_id=1, source_target_pairs={{0,4},{4,8},{8,12},{12,0},{1,5},{5,9},{9,13},{13,1},{2,6},{6,10},{... | collective-permute-start | bytes 73736 | tf_op jit(solution)/shard_map/ppermute | solution.py:510
  6.3 8.2 %collective-permute-start.2 = (f32[1,32,192]{2,1,0:T(8,128)}, f32[1,32,192]{2,1,0:T(8,128)S(1)}, u32[]{:S(2)}, u32[]{:S(2)}) collective-permute-start(f32[1,32,192]{2,1,0:T(8,128)} %refs_0_.1), channel_id=1, source_target_pairs={{0,12},{4,0},{8,4},{12,8},{1,13},{5,1},{9,5},{13,9},{2,14},{6,2},{... | collective-permute-start | bytes 73736 | tf_op jit(solution)/shard_map/ppermute | solution.py:510
  8.6 5.9 %copy-start = (f32[1,32,192]{2,1,0:T(8,128)S(1)}, f32[1,32,192]{2,1,0:T(8,128)}, u32[]{:S(2)}) copy-start(f32[1,32,192]{2,1,0:T(8,128)} %refs_0_.1) | copy-start | bytes 73732
  14.6 8.5 %collective-permute-start.5 = (f32[192,128]{1,0:T(8,128)S(1)}, f32[192,128]{1,0:T(8,128)S(1)}, u32[]{:S(2)}, u32[]{:S(2)}) collective-permute-start(f32[192,128]{1,0:T(8,128)S(1)} %stack.2.refs_0_), channel_id=1, source_target_pairs={{0,18},{2,16},{16,2},{18,0},{1,19},{3,17},{17,3},{19,1},{4,22},{6,... | collective-permute-start | bytes 294920 | tf_op jit(solution)/shard_map/ppermute | solution.py:545
  17.1 6.0 %collective-permute-start.4 = (f32[192,128]{1,0:T(8,128)S(1)}, f32[192,128]{1,0:T(8,128)S(1)}, u32[]{:S(2)}, u32[]{:S(2)}) collective-permute-start(f32[192,128]{1,0:T(8,128)S(1)} %stack.2.refs_0_), channel_id=1, source_target_pairs={{0,16},{2,18},{16,0},{18,2},{1,17},{3,19},{17,1},{19,3},{4,20},{6,... | collective-permute-start | bytes 294920 | tf_op jit(solution)/shard_map/ppermute | solution.py:545
  17.6 5.4 %collective-permute-start.3 = (f32[192,128]{1,0:T(8,128)S(1)}, f32[192,128]{1,0:T(8,128)S(1)}, u32[]{:S(2)}, u32[]{:S(2)}) collective-permute-start(f32[192,128]{1,0:T(8,128)S(1)} %stack.2.refs_0_), channel_id=1, source_target_pairs={{0,2},{2,0},{16,18},{18,16},{1,3},{3,1},{17,19},{19,17},{4,6},{6,4... | collective-permute-start | bytes 294920 | tf_op jit(solution)/shard_map/ppermute | solution.py:545
  23.1 1.8 %collective-permute-start.6 = (f32[768,128]{1,0:T(8,128)S(1)}, f32[768,128]{1,0:T(8,128)S(1)}, u32[]{:S(2)}, u32[]{:S(2)}) collective-permute-start(f32[768,128]{1,0:T(8,128)S(1)} %stack.3.own_ref.before_ref), channel_id=1, source_target_pairs={{0,1},{1,0},{2,3},{3,2},{4,5},{5,4},{6,7},{7,6},{8,9},{9,8},{10,11... | collective-permute-start | bytes 1179656 | tf_op jit(solution)/shard_map/ppermute | solution.py:573
  33.7 13.5 %all-to-all-start = ((f32[16,16,256]{2,1,0:T(8,128)}), f32[16,16,256]{2,1,0:T(8,128)S(1)}, u32[]{:S(2)}, u32[]{:S(2)}) async-start(f32[16,16,256]{2,1,0:T(8,128)} %bitcast.4), calls=%async_computation | async-start | bytes 524288 | tf_op jit(solution)/shard_map/all_to_all | solution.py:640
  47.6 4.0 %collective-permute-start.7 = (f32[1,32,192]{2,1,0:T(8,128)S(1)}, f32[1,32,192]{2,1,0:T(8,128)S(1)}, u32[]{:S(2)}, u32[]{:S(2)}) collective-permute-start(f32[1,32,192]{2,1,0:T(8,128)S(1)} %get-tuple-element.51), channel_id=1, source_target_pairs={{0,16},{16,0},{1,17},{17,1},{2,18},{18,2},{3,19},{19,3},{4,20},{20... | collective-permute-start | bytes 73736 | tf_op jit(solution)/shard_map/ppermute | solution.py:669

commit v19 on v18

--- a/solution.py
+++ b/solution.py
@@ -187,11 +187,13 @@
         for i, here in enumerate(chunks[:-1])
     ]
     keep = pltpu.make_async_copy(before_last, before_hbm, sems.at[2])
-    for copy in loads + fetches + [keep]:
+    for copy in loads + fetches:
         copy.start()
     for i, here in enumerate(chunks):
         if i > 0:
             loads[i - 1].wait()
+        if i == 2:
+            keep.start()
         source = rows if i == 0 else t.at[here]
         if i < len(stores):
             wide_product(pair, source, high, low, out.at[:, here])
@@ -266,7 +268,7 @@
 def context_kernel(
     patches,
     peers,
-    crops_ref,
+    crops_vmem,
     own_ref,
     other_ref,
     coarses,
@@ -278,6 +280,7 @@
     xw_first,
     tw_first,
     rows,
+    crops_ref,
     sems,
 ):
     fetches = [
@@ -286,6 +289,9 @@
     ]
     for copy in fetches:
         copy.start()
+    take = pltpu.make_async_copy(crops_vmem, crops_ref, sems.at[2])
+    take.start()
+    take.wait()
     pixels = coarses.shape[0] // 2
     width = projects.shape[1]
     far = peers // 4
@@ -294,6 +300,7 @@
         frame, top, left = crops_ref[0, j], crops_ref[1, j], crops_ref[2, j]
         near_by = lax.bitwise_xor(frame % 4, me % 4)
         k = (me // 4 - frame // 4 + far) % far
+        k = jnp.where(k == 1, 2, jnp.where(k == 2, 1, k))
         here = near_by % 2 == 0
         for a in range(4):
             row = jnp.minimum(top + a, SIDE - 1)
@@ -352,7 +359,7 @@
     ]
     xw_loads = [
         pltpu.make_async_copy(xw_hbm.at[:, here], xw.at[:, here], xw_sems.at[i])
-        for i, here in enumerate(chunks[1:-1])
+        for i, here in enumerate(chunks[2:-1])
     ]
     xw_loads.append(pltpu.make_async_copy(xw_last, xw.at[:, chunks[-1]], xw_sems.at[len(xw_loads)]))
     stores = [
@@ -363,11 +370,15 @@
         pltpu.make_async_copy(pair_hbm, deep_ref.at[: 2 * width], sems.at[0]),
         pltpu.make_async_copy(pair_hbm.at[:width], deep_ref.at[2 * width :], sems.at[1]),
     ]
-    xw_loads[0].start()
+    for pair in zip(tw_loads, xw_loads):
+        for copy in pair:
+            copy.start()
+    for copy in fetches:
+        copy.start()
 
     def begin(i):
         tokens = chunks[i]
-        source = xw_first if i == 0 else xw.at[:, tokens]
+        source = xw_first.at[:, tokens] if i < 2 else xw.at[:, tokens]
         here = taking(wanted[:, tokens], slots, 0)
         taken[:slots], taken[slots:] = here, here
         spread = dot(projected[...], taken[...])
@@ -381,17 +392,10 @@
                 deep[i % 2, shift(here, part * width)] = value
 
     begin(0)
-    for pair in zip(tw_loads, xw_loads[1:]):
-        for copy in pair:
-            copy.start()
     for i, tokens in enumerate(chunks):
-        if i < len(xw_loads):
-            xw_loads[i].wait()
         if 0 < i < len(chunks) - 1:
             tw_loads[i - 1].wait()
-        if i == 1:
-            for copy in fetches:
-                copy.start()
+            xw_loads[i - 1].wait()
         minus = tw_first if i == 0 else tw_last if i == len(chunks) - 1 else tw.at[:, tokens]
         target = de_ref if i == len(chunks) - 1 else xw.at[:, tokens]
         product = dot(grams[...], deep[i % 2])
@@ -505,9 +509,10 @@
     count = patches * tokens
     swap = [(0, 1), (1, 0)]
 
-    column = [coarse_input]
+    column = {0: coarse_input}
     for k in range(1, far):
-        column.append(lax.ppermute(coarse_input, "far", [(p, (p + k) % far) for p in range(far)]))
+        column[k] = lax.ppermute(coarse_input, "far", [(p, (p + k) % far) for p in range(far)])
+    column = [column[k] for k in [0, 2, 1] + list(range(3, far))]
 
     steps = count // ROWS
     pair_shape = (2 * width, values)
@@ -594,13 +599,17 @@
         (
             pltpu.VMEM((width, 2 * patches * 16), BF16),
             pltpu.VMEM((patches * 16, width), F32),
-            pltpu.VMEM((width, ROWS), F32),
+            pltpu.VMEM((width, 2 * ROWS), F32),
             pltpu.VMEM((width, ROWS), F32),
         ),
         limit=ROOM,
-        in_specs=[SMEM] + [VMEM] * 4 + [HBM] * 2,
+        in_specs=[VMEM] * 5 + [HBM] * 2,
         out_specs=(VMEM,) * 4,
-        scratch_shapes=[pltpu.VMEM((patches * 16, pixels), F32), pltpu.SemaphoreType.DMA((2,))],
+        scratch_shapes=[
+            pltpu.VMEM((patches * 16, pixels), F32),
+            pltpu.SMEM((4, patches), jnp.int32),
+            pltpu.SemaphoreType.DMA((3,)),
+        ],
     )(crops, own, other, *near(coarses, projects), *fixed(xw, tw))
     de, last_de, deep, dslot = call(
         middle_kernel,

time: 52.4 us -> 50.3 us (0.960)
  Pallas kernels: 27.3 us -> 26.1 us
  starting transfers between devices: 16.6 us -> 15.7 us
    ppermute x3, starting transfers between devices: 7.93 us -> 7.01 us  [body(): lax.ppermute(coarse_input, 'far', [(p, (p + k) % far) for p in range(far)])]
where the time goes in v19:
time: 50.3 us; the launch traced here: 50 us
  Pallas kernels  26.1 us (52%)
  starting transfers between devices  15.7 us (31%)
  waiting for transfers between devices  6.84 us (14%)
  between operations  0.77 us (2%)
  other arithmetic  0.62 us (1%)
    ppermute x3, starting transfers between devices, body(): lax.ppermute(coarse_input, 'far', [(p, (p + k) % far) for p in range(far)])  7.01 us
    pallas_call x1, Pallas kernels, body(): call(input_kernel, 'input', 6 * count * values * width, (pltpu.HBM((width...  5.9 us
    pallas_call x1, Pallas kernels, body(): call(last_kernel, 'last', 6 * count * values * width, pltpu.HBM((count, v...  5.67 us
    pallas_call x1, Pallas kernels, body(): call(target_kernel, 'target', 6 * count * values * width, (pltpu.HBM((wid...  4.55 us
    all_to_all x1, waiting for transfers between devices, body(): returned = lax.all_to_all(back, patch, 0, 0, tiled=True)  4.33 us
    pallas_call x1, Pallas kernels, body(): call(middle_kernel, 'middle', 6 * count * width * width, (pltpu.HBM((widt...  4.29 us
    ppermute x3, starting transfers between devices, body(): lax.ppermute(column, ('lvl', 'y'), [(p, p ^ flip) for p in range(4)])  3.55 us
    all_to_all x1, starting transfers between devices, body(): returned = lax.all_to_all(back, patch, 0, 0, tiled=True)  3.53 us
  transfers between devices with their start and end apart: 9, of which 3 were waited for; matrix products, arithmetic and copies ran while one was open for 0% of the time, Pallas kernels for 35%

profile of v19, /device:TPU:0, one launch (start us, length us, event | category | flops | bytes accessed | tf_op | source)
XLA Modules:
  0.0 50.0 jit_solution(7765282730269490654)
XLA Ops:
  0.6 3.1 %collective-permute-start.1 = (f32[1,32,192]{2,1,0:T(8,128)}, f32[1,32,192]{2,1,0:T(8,128)S(1)}, u32[]{:S(2)}, u32[]{:S(2)}) collective-permute-start(f32[1,32,192]{2,1,0:T(8,128)} %refs_0_.1), channel_id=1, source_target_pairs={{0,4},{4,8},{8,12},{12,0},{1,5},{5,9},{9,13},{13,1},{2,6},{6,10},{... | collective-permute-start | bytes 73736 | tf_op jit(solution)/shard_map/ppermute | solution.py:514
  3.7 2.6 %collective-permute-start = (f32[1,32,192]{2,1,0:T(8,128)}, f32[1,32,192]{2,1,0:T(8,128)S(1)}, u32[]{:S(2)}, u32[]{:S(2)}) collective-permute-start(f32[1,32,192]{2,1,0:T(8,128)} %refs_0_.1), channel_id=1, source_target_pairs={{0,8},{4,12},{8,0},{12,4},{1,9},{5,13},{9,1},{13,5},{2,10},{6,14},... | collective-permute-start | bytes 73736 | tf_op jit(solution)/shard_map/ppermute | solution.py:514
  6.3 1.3 %collective-permute-start.2 = (f32[1,32,192]{2,1,0:T(8,128)}, f32[1,32,192]{2,1,0:T(8,128)S(1)}, u32[]{:S(2)}, u32[]{:S(2)}) collective-permute-start(f32[1,32,192]{2,1,0:T(8,128)} %refs_0_.1), channel_id=1, source_target_pairs={{0,12},{4,0},{8,4},{12,8},{1,13},{5,1},{9,5},{13,9},{2,14},{6,2},{... | collective-permute-start | bytes 73736 | tf_op jit(solution)/shard_map/ppermute | solution.py:514
  7.6 0.0 copy-start
  7.6 5.9 %input.1 = (f32[320,1536]{1,0:T(8,128)}, f32[320,512]{1,0:T(8,128)S(1)}, bf16[640,768]{1,0:T(8,128)(2,1)}, f32[512,768]{1,0:T(8,128)S(1)}, bf16[640,768]{1,0:T(8,128)(2,1)S(1)}, /*index=5*/s32[4,8]{1,0:T(4,128)S(1)}) custom-call(f32[2048,768]{1,0:T(8,128)} %bitcast.9, f32[320,768]{1,0:T(8,128)} %bitcast.12, f32[2048,768]{1,0:T(8,128)} %bitcast.10, ...), custom_call_target="tpu_custom_call" | custom-call | flops 3019898880 | bytes 16253184 | tf_op jit(solution)/shard_map/input/pallas_call | solution.py:520
  13.6 0.0 collective-permute-done.1.refs_2_
  13.6 0.0 collective-permute-done.refs_1_
  13.6 0.0 collective-permute-done.2.refs_3_
  13.6 0.0 copy-done
  13.6 0.1 stack.2.refs_0_
  13.7 2.5 %collective-permute-start.5 = (f32[192,128]{1,0:T(8,128)S(1)}, f32[192,128]{1,0:T(8,128)S(1)}, u32[]{:S(2)}, u32[]{:S(2)}) collective-permute-start(f32[192,128]{1,0:T(8,128)S(1)} %stack.2.refs_0_), channel_id=1, source_target_pairs={{0,18},{2,16},{16,2},{18,0},{1,19},{3,17},{17,3},{19,1},{4,22},{6,... | collective-permute-start | bytes 294920 | tf_op jit(solution)/shard_map/ppermute | solution.py:550
  16.2 0.5 %collective-permute-start.4 = (f32[192,128]{1,0:T(8,128)S(1)}, f32[192,128]{1,0:T(8,128)S(1)}, u32[]{:S(2)}, u32[]{:S(2)}) collective-permute-start(f32[192,128]{1,0:T(8,128)S(1)} %stack.2.refs_0_), channel_id=1, source_target_pairs={{0,16},{2,18},{16,0},{18,2},{1,17},{3,19},{17,1},{19,3},{4,20},{6,... | collective-permute-start | bytes 294920 | tf_op jit(solution)/shard_map/ppermute | solution.py:550
  16.7 0.5 %collective-permute-start.3 = (f32[192,128]{1,0:T(8,128)S(1)}, f32[192,128]{1,0:T(8,128)S(1)}, u32[]{:S(2)}, u32[]{:S(2)}) collective-permute-start(f32[192,128]{1,0:T(8,128)S(1)} %stack.2.refs_0_), channel_id=1, source_target_pairs={{0,2},{2,0},{16,18},{18,16},{1,3},{3,1},{17,19},{19,17},{4,6},{6,4... | collective-permute-start | bytes 294920 | tf_op jit(solution)/shard_map/ppermute | solution.py:550
  17.2 4.5 %target.1 = (f32[320,1536]{1,0:T(8,128)}, f32[320,512]{1,0:T(8,128)}, f32[320,512]{1,0:T(8,128)S(1)}, bf16[384,320]{1,0:T(8,128)(2,1)S(1)}, bf16[640,320]{1,0:T(8,128)(2,1)S(1)}) custom-call(f32[2048,768]{1,0:T(8,128)} %bitcast.11, f32[192,320]{1,0:T(8,128)} %cwgt_hbm.1, f32[320,320]{1,0:T(8,128)} %xwgt_hbm.1, f32[512,768]{1,0:T(8,128)S(1)} %get-tuple-element.29.rows, ...), custom_call_target="tpu_custom_call" | custom-call | flops 3019898880 | bytes 9175040 | tf_op jit(solution)/shard_map/target/pallas_call | solution.py:551
  21.8 0.0 collective-permute-done.5.refs_3_
  21.8 0.0 collective-permute-done.4.refs_2_
  21.8 0.0 collective-permute-done.3.refs_1_
  21.9 0.1 collective-permute-start.6
  21.9 1.6 %prepare.1 = (bf16[320,960]{1,0:T(8,128)(2,1)S(1)}, s32[1,2048]{1,0:T(1,128)S(1)}, bf16[256,128]{1,0:T(8,128)(2,1)S(1)}, f32[128,64]{1,0:T(8,128)S(1)}) custom-call(bf16[640,768]{1,0:T(8,128)(2,1)S(1)} %get-tuple-element.30.pair, s32[4,8]{1,0:T(4,128)S(1)} %get-tuple-element.27.crops_vmem.crops_ref, f32[768,128]{1,0:T(8,128)S(1)} %stack.3.own_ref.before_ref), custom_call_target="tpu_custom_call" | custom-call | flops 629145600 | bytes 2801664 | tf_op jit(solution)/shard_map/prepare/pallas_call | solution.py:580
  23.6 0.1 collective-permute-done.6.other_ref
  23.6 1.9 %context.1 = (bf16[320,256]{1,0:T(8,128)(2,1)S(1)}, f32[128,320]{1,0:T(8,128)S(1)}, f32[320,1024]{1,0:T(8,128)S(1)}, f32[320,512]{1,0:T(8,128)S(1)}) custom-call(s32[4,8]{1,0:T(4,128)S(1)} %get-tuple-element.27.crops_vmem.crops_ref, f32[768,128]{1,0:T(8,128)S(1)} %stack.3.own_ref.before_ref, f32[768,128]{1,0:T(8,128)S(1)} %collective-permute-done.6.other_ref, ...), custom_call_target="tpu_custom_call" | custom-call | flops 78643200 | bytes 4915200 | tf_op jit(solution)/shard_map/context/pallas_call | solution.py:595
  25.6 4.3 %middle.1 = (f32[320,2048]{1,0:T(8,128)}, f32[320,512]{1,0:T(8,128)S(1)}, bf16[960,768]{1,0:T(8,128)(2,1)S(1)}, f32[128,320]{1,0:T(8,128)S(1)}) custom-call(bf16[320,256]{1,0:T(8,128)(2,1)S(1)} %get-tuple-element.35.projected, bf16[320,960]{1,0:T(8,128)(2,1)S(1)} %get-tuple-element.36.grams, s32[1,2048]{1,0:T(1,128)S(1)} %get-tuple-element.37.wanted, ...), custom_call_target="tpu_custom_call" | custom-call | flops 1258291200 | bytes 12779520 | tf_op jit(solution)/shard_map/middle/pallas_call | solution.py:614
  29.9 1.7 %closing.1 = f32[256,256]{1,0:T(8,128)} custom-call(f32[128,320]{1,0:T(8,128)S(1)} %get-tuple-element.43.dslot_ref, f32[128,320]{1,0:T(8,128)S(1)} %get-tuple-element.44.slope_ref, bf16[384,320]{1,0:T(8,128)(2,1)S(1)} %get-tuple-element.33.coarses, bf16[640,320]{1,0:T(8,128)(2,1)S(1)} %get-tuple-element.34.projects, ...), custom_call_target="tpu_custom_call" | custom-call | flops 78643200 | bytes 524288 | tf_op jit(solution)/shard_map/closing/pallas_call | solution.py:640
  31.6 3.5 %all-to-all-start = ((f32[16,16,256]{2,1,0:T(8,128)}), f32[16,16,256]{2,1,0:T(8,128)S(1)}, u32[]{:S(2)}, u32[]{:S(2)}) async-start(f32[16,16,256]{2,1,0:T(8,128)} %bitcast.4), calls=%async_computation | async-start | bytes 524288 | tf_op jit(solution)/shard_map/all_to_all | solution.py:649
  35.1 5.7 %last.1.done_ref = f32[2048,768]{1,0:T(8,128)} custom-call(f32[320,2048]{1,0:T(8,128)} %get-tuple-element.47.de_hbm, f32[320,512]{1,0:T(8,128)S(1)} %get-tuple-element.48.first, bf16[960,768]{1,0:T(8,128)(2,1)S(1)} %get-tuple-element.49.deep), custom_call_target="tpu_custom_call" | custom-call | flops 3019898880 | bytes 12582912 | tf_op jit(solution)/shard_map/last/pallas_call | solution.py:651
  40.8 4.3 %all-to-all-done = f32[16,16,256]{2,1,0:T(8,128)S(1)} async-done(((f32[16,16,256]{2,1,0:T(8,128)}), f32[16,16,256]{2,1,0:T(8,128)S(1)}, u32[]{:S(2)}, u32[]{:S(2)}) %all-to-all-start) | async-done | bytes 262176 | tf_op jit(solution)/shard_map/all_to_all | solution.py:649
  45.1 0.3 scatter.1
  45.4 1.6 %collective-permute-start.7 = (f32[1,32,192]{2,1,0:T(8,128)S(1)}, f32[1,32,192]{2,1,0:T(8,128)S(1)}, u32[]{:S(2)}, u32[]{:S(2)}) collective-permute-start(f32[1,32,192]{2,1,0:T(8,128)S(1)} %get-tuple-element.51), channel_id=1, source_target_pairs={{0,16},{16,0},{1,17},{17,1},{2,18},{18,2},{3,19},{19,3},{4,20},{20... | collective-permute-start | bytes 73736 | tf_op jit(solution)/shard_map/ppermute | solution.py:678
  47.0 2.4 %collective-permute-done.7 = f32[1,32,192]{2,1,0:T(8,128)S(1)} collective-permute-done((f32[1,32,192]{2,1,0:T(8,128)S(1)}, f32[1,32,192]{2,1,0:T(8,128)S(1)}, u32[]{:S(2)}, u32[]{:S(2)}) %collective-permute-start.7) | collective-permute-done | bytes 24608 | tf_op jit(solution)/shard_map/ppermute | solution.py:678
  49.4 0.6 %add.3 = f32[1,32,192]{2,1,0:T(8,128)} add(f32[1,32,192]{2,1,0:T(8,128)S(1)} %get-tuple-element.50, f32[1,32,192]{2,1,0:T(8,128)S(1)} %collective-permute-done.7) | non-fusion elementwise | flops 6144 | bytes 73728 | tf_op jit(solution)/shard_map/add | solution.py:678
  (1 shorter events, 0.0 us)
Async XLA Ops:
  0.6 12.9 %collective-permute-start.1 = (f32[1,32,192]{2,1,0:T(8,128)}, f32[1,32,192]{2,1,0:T(8,128)S(1)}, u32[]{:S(2)}, u32[]{:S(2)}) collective-permute-start(f32[1,32,192]{2,1,0:T(8,128)} %refs_0_.1), channel_id=1, source_target_pairs={{0,4},{4,8},{8,12},{12,0},{1,5},{5,9},{9,13},{13,1},{2,6},{6,10},{... | collective-permute-start | bytes 73736 | tf_op jit(solution)/shard_map/ppermute | solution.py:514
  3.7 9.9 %collective-permute-start = (f32[1,32,192]{2,1,0:T(8,128)}, f32[1,32,192]{2,1,0:T(8,128)S(1)}, u32[]{:S(2)}, u32[]{:S(2)}) collective-permute-start(f32[1,32,192]{2,1,0:T(8,128)} %refs_0_.1), channel_id=1, source_target_pairs={{0,8},{4,12},{8,0},{12,4},{1,9},{5,13},{9,1},{13,5},{2,10},{6,14},... | collective-permute-start | bytes 73736 | tf_op jit(solution)/shard_map/ppermute | solution.py:514
  6.3 7.3 %collective-permute-start.2 = (f32[1,32,192]{2,1,0:T(8,128)}, f32[1,32,192]{2,1,0:T(8,128)S(1)}, u32[]{:S(2)}, u32[]{:S(2)}) collective-permute-start(f32[1,32,192]{2,1,0:T(8,128)} %refs_0_.1), channel_id=1, source_target_pairs={{0,12},{4,0},{8,4},{12,8},{1,13},{5,1},{9,5},{13,9},{2,14},{6,2},{... | collective-permute-start | bytes 73736 | tf_op jit(solution)/shard_map/ppermute | solution.py:514
  7.6 5.9 %copy-start = (f32[1,32,192]{2,1,0:T(8,128)S(1)}, f32[1,32,192]{2,1,0:T(8,128)}, u32[]{:S(2)}) copy-start(f32[1,32,192]{2,1,0:T(8,128)} %refs_0_.1) | copy-start | bytes 73732
  13.7 8.1 %collective-permute-start.5 = (f32[192,128]{1,0:T(8,128)S(1)}, f32[192,128]{1,0:T(8,128)S(1)}, u32[]{:S(2)}, u32[]{:S(2)}) collective-permute-start(f32[192,128]{1,0:T(8,128)S(1)} %stack.2.refs_0_), channel_id=1, source_target_pairs={{0,18},{2,16},{16,2},{18,0},{1,19},{3,17},{17,3},{19,1},{4,22},{6,... | collective-permute-start | bytes 294920 | tf_op jit(solution)/shard_map/ppermute | solution.py:550
  16.2 5.6 %collective-permute-start.4 = (f32[192,128]{1,0:T(8,128)S(1)}, f32[192,128]{1,0:T(8,128)S(1)}, u32[]{:S(2)}, u32[]{:S(2)}) collective-permute-start(f32[192,128]{1,0:T(8,128)S(1)} %stack.2.refs_0_), channel_id=1, source_target_pairs={{0,16},{2,18},{16,0},{18,2},{1,17},{3,19},{17,1},{19,3},{4,20},{6,... | collective-permute-start | bytes 294920 | tf_op jit(solution)/shard_map/ppermute | solution.py:550
  16.7 5.1 %collective-permute-start.3 = (f32[192,128]{1,0:T(8,128)S(1)}, f32[192,128]{1,0:T(8,128)S(1)}, u32[]{:S(2)}, u32[]{:S(2)}) collective-permute-start(f32[192,128]{1,0:T(8,128)S(1)} %stack.2.refs_0_), channel_id=1, source_target_pairs={{0,2},{2,0},{16,18},{18,16},{1,3},{3,1},{17,19},{19,17},{4,6},{6,4... | collective-permute-start | bytes 294920 | tf_op jit(solution)/shard_map/ppermute | solution.py:550
  21.9 1.8 %collective-permute-start.6 = (f32[768,128]{1,0:T(8,128)S(1)}, f32[768,128]{1,0:T(8,128)S(1)}, u32[]{:S(2)}, u32[]{:S(2)}) collective-permute-start(f32[768,128]{1,0:T(8,128)S(1)} %stack.3.own_ref.before_ref), channel_id=1, source_target_pairs={{0,1},{1,0},{2,3},{3,2},{4,5},{5,4},{6,7},{7,6},{8,9},{9,8},{10,11... | collective-permute-start | bytes 1179656 | tf_op jit(solution)/shard_map/ppermute | solution.py:578
  31.6 13.5 %all-to-all-start = ((f32[16,16,256]{2,1,0:T(8,128)}), f32[16,16,256]{2,1,0:T(8,128)S(1)}, u32[]{:S(2)}, u32[]{:S(2)}) async-start(f32[16,16,256]{2,1,0:T(8,128)} %bitcast.4), calls=%async_computation | async-start | bytes 524288 | tf_op jit(solution)/shard_map/all_to_all | solution.py:649
  45.4 4.0 %collective-permute-start.7 = (f32[1,32,192]{2,1,0:T(8,128)S(1)}, f32[1,32,192]{2,1,0:T(8,128)S(1)}, u32[]{:S(2)}, u32[]{:S(2)}) collective-permute-start(f32[1,32,192]{2,1,0:T(8,128)S(1)} %get-tuple-element.51), channel_id=1, source_target_pairs={{0,16},{16,0},{1,17},{17,1},{2,18},{18,2},{3,19},{19,3},{4,20},{20... | collective-permute-start | bytes 73736 | tf_op jit(solution)/shard_map/ppermute | solution.py:678

commit v20 on v19

--- a/solution.py
+++ b/solution.py
@@ -299,7 +299,7 @@
     for j in range(patches):
         frame, top, left = crops_ref[0, j], crops_ref[1, j], crops_ref[2, j]
         near_by = lax.bitwise_xor(frame % 4, me % 4)
-        k = (me // 4 - frame // 4 + far) % far
+        k = lax.bitwise_xor(frame // 4, me // 4)
         k = jnp.where(k == 1, 2, jnp.where(k == 2, 1, k))
         here = near_by % 2 == 0
         for a in range(4):
@@ -421,10 +421,17 @@
     return both[:count] + (both[count:] + dot(high, pair[rows:], dims))
 
 
+def back_through(value, pair):
+    count, rows = value.shape[0], pair.shape[0] // 2
+    both = dot(jnp.concatenate(split(value), axis=0), pair[...], NT)
+    return both[:count, :rows] + (both[count:, :rows] + both[:count, rows:])
+
+
 def closing_kernel(dslot_ref, slope_ref, coarses, projects, lay, number, send_ref):
-    grad = through(through(dslot_ref[...], projects, NT) * slope_ref[...], coarses, NT)
-    high, low = split(jnp.concatenate([grad, number[...]], axis=1))
-    send_ref[...] = dot(lay[...], high) + dot(lay[...], low)
+    grad = back_through(back_through(dslot_ref[...], projects) * slope_ref[...], coarses)
+    parts = jnp.concatenate(split(jnp.concatenate([grad, number[...]], axis=1)), axis=1)
+    both = dot(lay[...], parts)
+    send_ref[...] = both[:, :LANES] + both[:, LANES:]
 
 
 def scatter_kernel(message_ref, done_ref, mine_ref, other_ref, total):
@@ -511,7 +518,7 @@
 
     column = {0: coarse_input}
     for k in range(1, far):
-        column[k] = lax.ppermute(coarse_input, "far", [(p, (p + k) % far) for p in range(far)])
+        column[k] = lax.ppermute(coarse_input, "far", [(p, p ^ k) for p in range(far)])
     column = [column[k] for k in [0, 2, 1] + list(range(3, far))]
 
     steps = count // ROWS

time: 50.3 us -> 51.7 us (1.028)
  starting transfers between devices: 15.7 us -> 17.1 us
    all_to_all x1, starting transfers between devices: 3.53 us -> 6.2 us  [body(): returned = lax.all_to_all(back, patch, 0, 0, tiled=True)]
    ppermute x3, starting transfers between devices: 7.01 us -> 5.68 us  [body(): lax.ppermute(coarse_input, 'far', [(p, p ^ k) for p in range(far)])]
where the time goes in v20:
time: 51.7 us; the launch traced here: 51.4 us
  Pallas kernels  26.1 us (50%)
  starting transfers between devices  17.1 us (33%)
  waiting for transfers between devices  6.88 us (13%)
  between operations  0.77 us (1%)
  other arithmetic  0.62 us (1%)
    all_to_all x1, starting transfers between devices, body(): returned = lax.all_to_all(back, patch, 0, 0, tiled=True)  6.2 us
    pallas_call x1, Pallas kernels, body(): call(input_kernel, 'input', 6 * count * values * width, (pltpu.HBM((width...  5.91 us
    ppermute x3, starting transfers between devices, body(): lax.ppermute(coarse_input, 'far', [(p, p ^ k) for p in range(far)])  5.68 us
    pallas_call x1, Pallas kernels, body(): call(last_kernel, 'last', 6 * count * values * width, pltpu.HBM((count, v...  5.66 us
    pallas_call x1, Pallas kernels, body(): call(target_kernel, 'target', 6 * count * values * width, (pltpu.HBM((wid...  4.55 us
    all_to_all x1, waiting for transfers between devices, body(): returned = lax.all_to_all(back, patch, 0, 0, tiled=True)  4.38 us
    pallas_call x1, Pallas kernels, body(): call(middle_kernel, 'middle', 6 * count * width * width, (pltpu.HBM((widt...  4.29 us
    ppermute x3, starting transfers between devices, body(): lax.ppermute(column, ('lvl', 'y'), [(p, p ^ flip) for p in range(4)])  3.55 us
  transfers between devices with their start and end apart: 9, of which 3 were waited for; matrix products, arithmetic and copies ran while one was open for 0% of the time, Pallas kernels for 35%

profile of v20, /device:TPU:0, one launch (start us, length us, event | category | flops | bytes accessed | tf_op | source)
XLA Modules:
  0.0 51.4 jit_solution(18374718636581312073)
XLA Ops:
  0.6 3.1 %collective-permute-start.1 = (f32[1,32,192]{2,1,0:T(8,128)}, f32[1,32,192]{2,1,0:T(8,128)S(1)}, u32[]{:S(2)}, u32[]{:S(2)}) collective-permute-start(f32[1,32,192]{2,1,0:T(8,128)} %refs_0_.1), channel_id=1, source_target_pairs={{0,4},{4,0},{8,12},{12,8},{1,5},{5,1},{9,13},{13,9},{2,6},{6,2},{1... | collective-permute-start | bytes 73736 | tf_op jit(solution)/shard_map/ppermute | solution.py:521
  3.7 2.6 %collective-permute-start = (f32[1,32,192]{2,1,0:T(8,128)}, f32[1,32,192]{2,1,0:T(8,128)S(1)}, u32[]{:S(2)}, u32[]{:S(2)}) collective-permute-start(f32[1,32,192]{2,1,0:T(8,128)} %refs_0_.1), channel_id=1, source_target_pairs={{0,8},{4,12},{8,0},{12,4},{1,9},{5,13},{9,1},{13,5},{2,10},{6,14},... | collective-permute-start | bytes 73736 | tf_op jit(solution)/shard_map/ppermute | solution.py:521
  6.3 0.0 collective-permute-start.2
  6.3 0.0 copy-start
  6.3 5.9 %input.1 = (f32[320,1536]{1,0:T(8,128)}, f32[320,512]{1,0:T(8,128)S(1)}, bf16[640,768]{1,0:T(8,128)(2,1)}, f32[512,768]{1,0:T(8,128)S(1)}, bf16[640,768]{1,0:T(8,128)(2,1)S(1)}, /*index=5*/s32[4,8]{1,0:T(4,128)S(1)}) custom-call(f32[2048,768]{1,0:T(8,128)} %bitcast.9, f32[320,768]{1,0:T(8,128)} %bitcast.12, f32[2048,768]{1,0:T(8,128)} %bitcast.10, ...), custom_call_target="tpu_custom_call" | custom-call | flops 3019898880 | bytes 16253184 | tf_op jit(solution)/shard_map/input/pallas_call | solution.py:527
  12.2 0.0 collective-permute-done.1.refs_2_
  12.2 0.0 collective-permute-done.refs_1_
  12.3 0.0 collective-permute-done.2.refs_3_
  12.3 0.0 copy-done
  12.3 0.1 stack.2.refs_0_
  12.4 2.7 %collective-permute-start.5 = (f32[192,128]{1,0:T(8,128)S(1)}, f32[192,128]{1,0:T(8,128)S(1)}, u32[]{:S(2)}, u32[]{:S(2)}) collective-permute-start(f32[192,128]{1,0:T(8,128)S(1)} %stack.2.refs_0_), channel_id=1, source_target_pairs={{0,18},{2,16},{16,2},{18,0},{1,19},{3,17},{17,3},{19,1},{4,22},{6,... | collective-permute-start | bytes 294920 | tf_op jit(solution)/shard_map/ppermute | solution.py:557
  15.1 0.5 %collective-permute-start.4 = (f32[192,128]{1,0:T(8,128)S(1)}, f32[192,128]{1,0:T(8,128)S(1)}, u32[]{:S(2)}, u32[]{:S(2)}) collective-permute-start(f32[192,128]{1,0:T(8,128)S(1)} %stack.2.refs_0_), channel_id=1, source_target_pairs={{0,16},{2,18},{16,0},{18,2},{1,17},{3,19},{17,1},{19,3},{4,20},{6,... | collective-permute-start | bytes 294920 | tf_op jit(solution)/shard_map/ppermute | solution.py:557
  15.6 0.3 collective-permute-start.3
  15.9 4.6 %target.1 = (f32[320,1536]{1,0:T(8,128)}, f32[320,512]{1,0:T(8,128)}, f32[320,512]{1,0:T(8,128)S(1)}, bf16[384,320]{1,0:T(8,128)(2,1)S(1)}, bf16[640,320]{1,0:T(8,128)(2,1)S(1)}) custom-call(f32[2048,768]{1,0:T(8,128)} %bitcast.11, f32[192,320]{1,0:T(8,128)} %cwgt_hbm.1, f32[320,320]{1,0:T(8,128)} %xwgt_hbm.1, f32[512,768]{1,0:T(8,128)S(1)} %get-tuple-element.29.rows, ...), custom_call_target="tpu_custom_call" | custom-call | flops 3019898880 | bytes 9175040 | tf_op jit(solution)/shard_map/target/pallas_call | solution.py:558
  20.5 0.0 collective-permute-done.5.refs_3_
  20.5 0.0 collective-permute-done.4.refs_2_
  20.5 0.0 collective-permute-done.3.refs_1_
  20.5 0.1 collective-permute-start.6
  20.6 1.6 %prepare.1 = (bf16[320,960]{1,0:T(8,128)(2,1)S(1)}, s32[1,2048]{1,0:T(1,128)S(1)}, bf16[256,128]{1,0:T(8,128)(2,1)S(1)}, f32[128,64]{1,0:T(8,128)S(1)}) custom-call(bf16[640,768]{1,0:T(8,128)(2,1)S(1)} %get-tuple-element.30.pair, s32[4,8]{1,0:T(4,128)S(1)} %get-tuple-element.27.crops_vmem.crops_ref, f32[768,128]{1,0:T(8,128)S(1)} %stack.3.own_ref.before_ref), custom_call_target="tpu_custom_call" | custom-call | flops 629145600 | bytes 2801664 | tf_op jit(solution)/shard_map/prepare/pallas_call | solution.py:587
  22.2 0.1 collective-permute-done.6.other_ref
  22.3 1.9 %context.1 = (bf16[320,256]{1,0:T(8,128)(2,1)S(1)}, f32[128,320]{1,0:T(8,128)S(1)}, f32[320,1024]{1,0:T(8,128)S(1)}, f32[320,512]{1,0:T(8,128)S(1)}) custom-call(s32[4,8]{1,0:T(4,128)S(1)} %get-tuple-element.27.crops_vmem.crops_ref, f32[768,128]{1,0:T(8,128)S(1)} %stack.3.own_ref.before_ref, f32[768,128]{1,0:T(8,128)S(1)} %collective-permute-done.6.other_ref, ...), custom_call_target="tpu_custom_call" | custom-call | flops 78643200 | bytes 4915200 | tf_op jit(solution)/shard_map/context/pallas_call | solution.py:602
  24.2 4.3 %middle.1 = (f32[320,2048]{1,0:T(8,128)}, f32[320,512]{1,0:T(8,128)S(1)}, bf16[960,768]{1,0:T(8,128)(2,1)S(1)}, f32[128,320]{1,0:T(8,128)S(1)}) custom-call(bf16[320,256]{1,0:T(8,128)(2,1)S(1)} %get-tuple-element.35.projected, bf16[320,960]{1,0:T(8,128)(2,1)S(1)} %get-tuple-element.36.grams, s32[1,2048]{1,0:T(1,128)S(1)} %get-tuple-element.37.wanted, ...), custom_call_target="tpu_custom_call" | custom-call | flops 1258291200 | bytes 12779520 | tf_op jit(solution)/shard_map/middle/pallas_call | solution.py:621
  28.5 1.7 %closing.1 = f32[256,256]{1,0:T(8,128)} custom-call(f32[128,320]{1,0:T(8,128)S(1)} %get-tuple-element.43.dslot_ref, f32[128,320]{1,0:T(8,128)S(1)} %get-tuple-element.44.slope_ref, bf16[384,320]{1,0:T(8,128)(2,1)S(1)} %get-tuple-element.33.coarses, bf16[640,320]{1,0:T(8,128)(2,1)S(1)} %get-tuple-element.34.projects, ...), custom_call_target="tpu_custom_call" | custom-call | flops 78643200 | bytes 524288 | tf_op jit(solution)/shard_map/closing/pallas_call | solution.py:647
  30.3 6.2 %all-to-all-start = ((f32[16,16,256]{2,1,0:T(8,128)}), f32[16,16,256]{2,1,0:T(8,128)S(1)}, u32[]{:S(2)}, u32[]{:S(2)}) async-start(f32[16,16,256]{2,1,0:T(8,128)} %bitcast.4), calls=%async_computation | async-start | bytes 524288 | tf_op jit(solution)/shard_map/all_to_all | solution.py:656
  36.5 5.7 %last.1.done_ref = f32[2048,768]{1,0:T(8,128)} custom-call(f32[320,2048]{1,0:T(8,128)} %get-tuple-element.47.de_hbm, f32[320,512]{1,0:T(8,128)S(1)} %get-tuple-element.48.first, bf16[960,768]{1,0:T(8,128)(2,1)S(1)} %get-tuple-element.49.deep), custom_call_target="tpu_custom_call" | custom-call | flops 3019898880 | bytes 12582912 | tf_op jit(solution)/shard_map/last/pallas_call | solution.py:658
  42.2 4.4 %all-to-all-done = f32[16,16,256]{2,1,0:T(8,128)S(1)} async-done(((f32[16,16,256]{2,1,0:T(8,128)}), f32[16,16,256]{2,1,0:T(8,128)S(1)}, u32[]{:S(2)}, u32[]{:S(2)}) %all-to-all-start) | async-done | bytes 262176 | tf_op jit(solution)/shard_map/all_to_all | solution.py:656
  46.5 0.3 scatter.1
  46.8 1.6 %collective-permute-start.7 = (f32[1,32,192]{2,1,0:T(8,128)S(1)}, f32[1,32,192]{2,1,0:T(8,128)S(1)}, u32[]{:S(2)}, u32[]{:S(2)}) collective-permute-start(f32[1,32,192]{2,1,0:T(8,128)S(1)} %get-tuple-element.51), channel_id=1, source_target_pairs={{0,16},{16,0},{1,17},{17,1},{2,18},{18,2},{3,19},{19,3},{4,20},{20... | collective-permute-start | bytes 73736 | tf_op jit(solution)/shard_map/ppermute | solution.py:685
  48.4 2.4 %collective-permute-done.7 = f32[1,32,192]{2,1,0:T(8,128)S(1)} collective-permute-done((f32[1,32,192]{2,1,0:T(8,128)S(1)}, f32[1,32,192]{2,1,0:T(8,128)S(1)}, u32[]{:S(2)}, u32[]{:S(2)}) %collective-permute-start.7) | collective-permute-done | bytes 24608 | tf_op jit(solution)/shard_map/ppermute | solution.py:685
  50.8 0.6 %add.3 = f32[1,32,192]{2,1,0:T(8,128)} add(f32[1,32,192]{2,1,0:T(8,128)S(1)} %get-tuple-element.50, f32[1,32,192]{2,1,0:T(8,128)S(1)} %collective-permute-done.7) | non-fusion elementwise | flops 6144 | bytes 73728 | tf_op jit(solution)/shard_map/add | solution.py:685
  (1 shorter events, 0.0 us)
Async XLA Ops:
  0.6 11.6 %collective-permute-start.1 = (f32[1,32,192]{2,1,0:T(8,128)}, f32[1,32,192]{2,1,0:T(8,128)S(1)}, u32[]{:S(2)}, u32[]{:S(2)}) collective-permute-start(f32[1,32,192]{2,1,0:T(8,128)} %refs_0_.1), channel_id=1, source_target_pairs={{0,4},{4,0},{8,12},{12,8},{1,5},{5,1},{9,13},{13,9},{2,6},{6,2},{1... | collective-permute-start | bytes 73736 | tf_op jit(solution)/shard_map/ppermute | solution.py:521
  3.7 8.5 %collective-permute-start = (f32[1,32,192]{2,1,0:T(8,128)}, f32[1,32,192]{2,1,0:T(8,128)S(1)}, u32[]{:S(2)}, u32[]{:S(2)}) collective-permute-start(f32[1,32,192]{2,1,0:T(8,128)} %refs_0_.1), channel_id=1, source_target_pairs={{0,8},{4,12},{8,0},{12,4},{1,9},{5,13},{9,1},{13,5},{2,10},{6,14},... | collective-permute-start | bytes 73736 | tf_op jit(solution)/shard_map/ppermute | solution.py:521
  6.3 5.9 %collective-permute-start.2 = (f32[1,32,192]{2,1,0:T(8,128)}, f32[1,32,192]{2,1,0:T(8,128)S(1)}, u32[]{:S(2)}, u32[]{:S(2)}) collective-permute-start(f32[1,32,192]{2,1,0:T(8,128)} %refs_0_.1), channel_id=1, source_target_pairs={{0,12},{4,8},{8,4},{12,0},{1,13},{5,9},{9,5},{13,1},{2,14},{6,10},... | collective-permute-start | bytes 73736 | tf_op jit(solution)/shard_map/ppermute | solution.py:521
  6.3 6.0 %copy-start = (f32[1,32,192]{2,1,0:T(8,128)S(1)}, f32[1,32,192]{2,1,0:T(8,128)}, u32[]{:S(2)}) copy-start(f32[1,32,192]{2,1,0:T(8,128)} %refs_0_.1) | copy-start | bytes 73732
  12.4 8.1 %collective-permute-start.5 = (f32[192,128]{1,0:T(8,128)S(1)}, f32[192,128]{1,0:T(8,128)S(1)}, u32[]{:S(2)}, u32[]{:S(2)}) collective-permute-start(f32[192,128]{1,0:T(8,128)S(1)} %stack.2.refs_0_), channel_id=1, source_target_pairs={{0,18},{2,16},{16,2},{18,0},{1,19},{3,17},{17,3},{19,1},{4,22},{6,... | collective-permute-start | bytes 294920 | tf_op jit(solution)/shard_map/ppermute | solution.py:557
  15.1 5.4 %collective-permute-start.4 = (f32[192,128]{1,0:T(8,128)S(1)}, f32[192,128]{1,0:T(8,128)S(1)}, u32[]{:S(2)}, u32[]{:S(2)}) collective-permute-start(f32[192,128]{1,0:T(8,128)S(1)} %stack.2.refs_0_), channel_id=1, source_target_pairs={{0,16},{2,18},{16,0},{18,2},{1,17},{3,19},{17,1},{19,3},{4,20},{6,... | collective-permute-start | bytes 294920 | tf_op jit(solution)/shard_map/ppermute | solution.py:557
  15.6 4.9 %collective-permute-start.3 = (f32[192,128]{1,0:T(8,128)S(1)}, f32[192,128]{1,0:T(8,128)S(1)}, u32[]{:S(2)}, u32[]{:S(2)}) collective-permute-start(f32[192,128]{1,0:T(8,128)S(1)} %stack.2.refs_0_), channel_id=1, source_target_pairs={{0,2},{2,0},{16,18},{18,16},{1,3},{3,1},{17,19},{19,17},{4,6},{6,4... | collective-permute-start | bytes 294920 | tf_op jit(solution)/shard_map/ppermute | solution.py:557
  20.5 1.8 %collective-permute-start.6 = (f32[768,128]{1,0:T(8,128)S(1)}, f32[768,128]{1,0:T(8,128)S(1)}, u32[]{:S(2)}, u32[]{:S(2)}) collective-permute-start(f32[768,128]{1,0:T(8,128)S(1)} %stack.3.own_ref.before_ref), channel_id=1, source_target_pairs={{0,1},{1,0},{2,3},{3,2},{4,5},{5,4},{6,7},{7,6},{8,9},{9,8},{10,11... | collective-permute-start | bytes 1179656 | tf_op jit(solution)/shard_map/ppermute | solution.py:585
  30.3 16.3 %all-to-all-start = ((f32[16,16,256]{2,1,0:T(8,128)}), f32[16,16,256]{2,1,0:T(8,128)S(1)}, u32[]{:S(2)}, u32[]{:S(2)}) async-start(f32[16,16,256]{2,1,0:T(8,128)} %bitcast.4), calls=%async_computation | async-start | bytes 524288 | tf_op jit(solution)/shard_map/all_to_all | solution.py:656
  46.8 4.0 %collective-permute-start.7 = (f32[1,32,192]{2,1,0:T(8,128)S(1)}, f32[1,32,192]{2,1,0:T(8,128)S(1)}, u32[]{:S(2)}, u32[]{:S(2)}) collective-permute-start(f32[1,32,192]{2,1,0:T(8,128)S(1)} %get-tuple-element.51), channel_id=1, source_target_pairs={{0,16},{16,0},{1,17},{17,1},{2,18},{18,2},{3,19},{19,3},{4,20},{20... | collective-permute-start | bytes 73736 | tf_op jit(solution)/shard_map/ppermute | solution.py:685

commit v21 on v20

--- a/solution.py
+++ b/solution.py
@@ -299,8 +299,8 @@
     for j in range(patches):
         frame, top, left = crops_ref[0, j], crops_ref[1, j], crops_ref[2, j]
         near_by = lax.bitwise_xor(frame % 4, me % 4)
-        k = lax.bitwise_xor(frame // 4, me // 4)
-        k = jnp.where(k == 1, 2, jnp.where(k == 2, 1, k))
+        k = (me // 4 - frame // 4 + far) % far
+        k = jnp.where(k == 1, 2, jnp.where(k == 2, 3, jnp.where(k == 3, 1, k)))
         here = near_by % 2 == 0
         for a in range(4):
             row = jnp.minimum(top + a, SIDE - 1)
@@ -518,8 +518,8 @@
 
     column = {0: coarse_input}
     for k in range(1, far):
-        column[k] = lax.ppermute(coarse_input, "far", [(p, p ^ k) for p in range(far)])
-    column = [column[k] for k in [0, 2, 1] + list(range(3, far))]
+        column[k] = lax.ppermute(coarse_input, "far", [(p, (p + k) % far) for p in range(far)])
+    column = [column[k] for k in [0, 3, 1, 2] + list(range(4, far))]
 
     steps = count // ROWS
     pair_shape = (2 * width, values)
@@ -648,7 +648,7 @@
         closing_kernel,
         "closing",
         6 * patches * 16 * width * width,
-        jax.ShapeDtypeStruct((peers * 16, LANES), F32),
+        pltpu.VMEM((peers * 16, LANES), F32),
         limit=ROOM,
         in_specs=[VMEM] * 6,
         out_specs=VMEM,

time: 51.7 us -> 50.5 us (0.977)
  starting transfers between devices: 17.1 us -> 15.8 us
    all_to_all x1, starting transfers between devices: 6.2 us -> 4.52 us  [body(): returned = lax.all_to_all(back, patch, 0, 0, tiled=True)]
where the time goes in v21:
time: 50.5 us; the launch traced here: 50.2 us
  Pallas kernels  26.1 us (52%)
  starting transfers between devices  15.8 us (31%)
  waiting for transfers between devices  6.9 us (14%)
  between operations  0.77 us (2%)
  other arithmetic  0.62 us (1%)
    ppermute x3, starting transfers between devices, body(): lax.ppermute(coarse_input, 'far', [(p, (p + k) % far) for p in range(far)])  6.11 us
    pallas_call x1, Pallas kernels, body(): call(input_kernel, 'input', 6 * count * values * width, (pltpu.HBM((width...  5.9 us
    pallas_call x1, Pallas kernels, body(): call(last_kernel, 'last', 6 * count * values * width, pltpu.HBM((count, v...  5.67 us
    pallas_call x1, Pallas kernels, body(): call(target_kernel, 'target', 6 * count * values * width, (pltpu.HBM((wid...  4.55 us
    all_to_all x1, starting transfers between devices, body(): returned = lax.all_to_all(back, patch, 0, 0, tiled=True)  4.52 us
    all_to_all x1, waiting for transfers between devices, body(): returned = lax.all_to_all(back, patch, 0, 0, tiled=True)  4.37 us
    pallas_call x1, Pallas kernels, body(): call(middle_kernel, 'middle', 6 * count * width * width, (pltpu.HBM((widt...  4.29 us
    ppermute x3, starting transfers between devices, body(): lax.ppermute(column, ('lvl', 'y'), [(p, p ^ flip) for p in range(4)])  3.55 us
  transfers between devices with their start and end apart: 9, of which 3 were waited for; matrix products, arithmetic and copies ran while one was open for 0% of the time, Pallas kernels for 35%

profile of v21, /device:TPU:0, one launch (start us, length us, event | category | flops | bytes accessed | tf_op | source)
XLA Modules:
  0.0 50.2 jit_solution(12376523608206729998)
XLA Ops:
  0.6 3.1 %collective-permute-start.1 = (f32[1,32,192]{2,1,0:T(8,128)}, f32[1,32,192]{2,1,0:T(8,128)S(1)}, u32[]{:S(2)}, u32[]{:S(2)}) collective-permute-start(f32[1,32,192]{2,1,0:T(8,128)} %refs_0_.1), channel_id=1, source_target_pairs={{0,4},{4,8},{8,12},{12,0},{1,5},{5,9},{9,13},{13,1},{2,6},{6,10},{... | collective-permute-start | bytes 73736 | tf_op jit(solution)/shard_map/ppermute | solution.py:521
  3.7 2.1 %collective-permute-start = (f32[1,32,192]{2,1,0:T(8,128)}, f32[1,32,192]{2,1,0:T(8,128)S(1)}, u32[]{:S(2)}, u32[]{:S(2)}) collective-permute-start(f32[1,32,192]{2,1,0:T(8,128)} %refs_0_.1), channel_id=1, source_target_pairs={{0,12},{4,0},{8,4},{12,8},{1,13},{5,1},{9,5},{13,9},{2,14},{6,2},{... | collective-permute-start | bytes 73736 | tf_op jit(solution)/shard_map/ppermute | solution.py:521
  5.8 0.9 %collective-permute-start.2 = (f32[1,32,192]{2,1,0:T(8,128)}, f32[1,32,192]{2,1,0:T(8,128)S(1)}, u32[]{:S(2)}, u32[]{:S(2)}) collective-permute-start(f32[1,32,192]{2,1,0:T(8,128)} %refs_0_.1), channel_id=1, source_target_pairs={{0,8},{4,12},{8,0},{12,4},{1,9},{5,13},{9,1},{13,5},{2,10},{6,14},... | collective-permute-start | bytes 73736 | tf_op jit(solution)/shard_map/ppermute | solution.py:521
  6.7 0.0 copy-start
  6.7 5.9 %input.1 = (f32[320,1536]{1,0:T(8,128)}, f32[320,512]{1,0:T(8,128)S(1)}, bf16[640,768]{1,0:T(8,128)(2,1)}, f32[512,768]{1,0:T(8,128)S(1)}, bf16[640,768]{1,0:T(8,128)(2,1)S(1)}, /*index=5*/s32[4,8]{1,0:T(4,128)S(1)}) custom-call(f32[2048,768]{1,0:T(8,128)} %bitcast.9, f32[320,768]{1,0:T(8,128)} %bitcast.12, f32[2048,768]{1,0:T(8,128)} %bitcast.10, ...), custom_call_target="tpu_custom_call" | custom-call | flops 3019898880 | bytes 16253184 | tf_op jit(solution)/shard_map/input/pallas_call | solution.py:527
  12.7 0.0 collective-permute-done.1.refs_2_
  12.7 0.0 collective-permute-done.refs_1_
  12.7 0.0 collective-permute-done.2.refs_3_
  12.7 0.0 copy-done
  12.7 0.1 stack.2.refs_0_
  12.8 2.5 %collective-permute-start.5 = (f32[192,128]{1,0:T(8,128)S(1)}, f32[192,128]{1,0:T(8,128)S(1)}, u32[]{:S(2)}, u32[]{:S(2)}) collective-permute-start(f32[192,128]{1,0:T(8,128)S(1)} %stack.2.refs_0_), channel_id=1, source_target_pairs={{0,18},{2,16},{16,2},{18,0},{1,19},{3,17},{17,3},{19,1},{4,22},{6,... | collective-permute-start | bytes 294920 | tf_op jit(solution)/shard_map/ppermute | solution.py:557
  15.3 0.5 %collective-permute-start.4 = (f32[192,128]{1,0:T(8,128)S(1)}, f32[192,128]{1,0:T(8,128)S(1)}, u32[]{:S(2)}, u32[]{:S(2)}) collective-permute-start(f32[192,128]{1,0:T(8,128)S(1)} %stack.2.refs_0_), channel_id=1, source_target_pairs={{0,16},{2,18},{16,0},{18,2},{1,17},{3,19},{17,1},{19,3},{4,20},{6,... | collective-permute-start | bytes 294920 | tf_op jit(solution)/shard_map/ppermute | solution.py:557
  15.8 0.5 %collective-permute-start.3 = (f32[192,128]{1,0:T(8,128)S(1)}, f32[192,128]{1,0:T(8,128)S(1)}, u32[]{:S(2)}, u32[]{:S(2)}) collective-permute-start(f32[192,128]{1,0:T(8,128)S(1)} %stack.2.refs_0_), channel_id=1, source_target_pairs={{0,2},{2,0},{16,18},{18,16},{1,3},{3,1},{17,19},{19,17},{4,6},{6,4... | collective-permute-start | bytes 294920 | tf_op jit(solution)/shard_map/ppermute | solution.py:557
  16.3 4.6 %target.1 = (f32[320,1536]{1,0:T(8,128)}, f32[320,512]{1,0:T(8,128)}, f32[320,512]{1,0:T(8,128)S(1)}, bf16[384,320]{1,0:T(8,128)(2,1)S(1)}, bf16[640,320]{1,0:T(8,128)(2,1)S(1)}) custom-call(f32[2048,768]{1,0:T(8,128)} %bitcast.11, f32[192,320]{1,0:T(8,128)} %cwgt_hbm.1, f32[320,320]{1,0:T(8,128)} %xwgt_hbm.1, f32[512,768]{1,0:T(8,128)S(1)} %get-tuple-element.29.rows, ...), custom_call_target="tpu_custom_call" | custom-call | flops 3019898880 | bytes 9175040 | tf_op jit(solution)/shard_map/target/pallas_call | solution.py:558
  20.9 0.0 collective-permute-done.5.refs_3_
  20.9 0.0 collective-permute-done.4.refs_2_
  20.9 0.0 collective-permute-done.3.refs_1_
  21.0 0.1 collective-permute-start.6
  21.0 1.6 %prepare.1 = (bf16[320,960]{1,0:T(8,128)(2,1)S(1)}, s32[1,2048]{1,0:T(1,128)S(1)}, bf16[256,128]{1,0:T(8,128)(2,1)S(1)}, f32[128,64]{1,0:T(8,128)S(1)}) custom-call(bf16[640,768]{1,0:T(8,128)(2,1)S(1)} %get-tuple-element.30.pair, s32[4,8]{1,0:T(4,128)S(1)} %get-tuple-element.27.crops_vmem.crops_ref, f32[768,128]{1,0:T(8,128)S(1)} %stack.3.own_ref.before_ref), custom_call_target="tpu_custom_call" | custom-call | flops 629145600 | bytes 2801664 | tf_op jit(solution)/shard_map/prepare/pallas_call | solution.py:587
  22.7 0.1 collective-permute-done.6.other_ref
  22.8 1.9 %context.1 = (bf16[320,256]{1,0:T(8,128)(2,1)S(1)}, f32[128,320]{1,0:T(8,128)S(1)}, f32[320,1024]{1,0:T(8,128)S(1)}, f32[320,512]{1,0:T(8,128)S(1)}) custom-call(s32[4,8]{1,0:T(4,128)S(1)} %get-tuple-element.27.crops_vmem.crops_ref, f32[768,128]{1,0:T(8,128)S(1)} %stack.3.own_ref.before_ref, f32[768,128]{1,0:T(8,128)S(1)} %collective-permute-done.6.other_ref, ...), custom_call_target="tpu_custom_call" | custom-call | flops 78643200 | bytes 4915200 | tf_op jit(solution)/shard_map/context/pallas_call | solution.py:602
  24.7 4.3 %middle.1 = (f32[320,2048]{1,0:T(8,128)}, f32[320,512]{1,0:T(8,128)S(1)}, bf16[960,768]{1,0:T(8,128)(2,1)S(1)}, f32[128,320]{1,0:T(8,128)S(1)}) custom-call(bf16[320,256]{1,0:T(8,128)(2,1)S(1)} %get-tuple-element.35.projected, bf16[320,960]{1,0:T(8,128)(2,1)S(1)} %get-tuple-element.36.grams, s32[1,2048]{1,0:T(1,128)S(1)} %get-tuple-element.37.wanted, ...), custom_call_target="tpu_custom_call" | custom-call | flops 1258291200 | bytes 12779520 | tf_op jit(solution)/shard_map/middle/pallas_call | solution.py:621
  29.0 1.7 %closing.1 = f32[256,256]{1,0:T(8,128)} custom-call(f32[128,320]{1,0:T(8,128)S(1)} %get-tuple-element.43.dslot_ref, f32[128,320]{1,0:T(8,128)S(1)} %get-tuple-element.44.slope_ref, bf16[384,320]{1,0:T(8,128)(2,1)S(1)} %get-tuple-element.33.coarses, bf16[640,320]{1,0:T(8,128)(2,1)S(1)} %get-tuple-element.34.projects, ...), custom_call_target="tpu_custom_call" | custom-call | flops 78643200 | bytes 524288 | tf_op jit(solution)/shard_map/closing/pallas_call | solution.py:647
  30.7 4.5 %all-to-all-start = ((f32[16,16,256]{2,1,0:T(8,128)}), f32[16,16,256]{2,1,0:T(8,128)S(1)}, u32[]{:S(2)}, u32[]{:S(2)}) async-start(f32[16,16,256]{2,1,0:T(8,128)} %bitcast.4), calls=%async_computation | async-start | bytes 524288 | tf_op jit(solution)/shard_map/all_to_all | solution.py:656
  35.3 5.7 %last.1.done_ref = f32[2048,768]{1,0:T(8,128)} custom-call(f32[320,2048]{1,0:T(8,128)} %get-tuple-element.47.de_hbm, f32[320,512]{1,0:T(8,128)S(1)} %get-tuple-element.48.first, bf16[960,768]{1,0:T(8,128)(2,1)S(1)} %get-tuple-element.49.deep), custom_call_target="tpu_custom_call" | custom-call | flops 3019898880 | bytes 12582912 | tf_op jit(solution)/shard_map/last/pallas_call | solution.py:658
  40.9 4.4 %all-to-all-done = f32[16,16,256]{2,1,0:T(8,128)S(1)} async-done(((f32[16,16,256]{2,1,0:T(8,128)}), f32[16,16,256]{2,1,0:T(8,128)S(1)}, u32[]{:S(2)}, u32[]{:S(2)}) %all-to-all-start) | async-done | bytes 262176 | tf_op jit(solution)/shard_map/all_to_all | solution.py:656
  45.3 0.3 scatter.1
  45.6 1.5 %collective-permute-start.7 = (f32[1,32,192]{2,1,0:T(8,128)S(1)}, f32[1,32,192]{2,1,0:T(8,128)S(1)}, u32[]{:S(2)}, u32[]{:S(2)}) collective-permute-start(f32[1,32,192]{2,1,0:T(8,128)S(1)} %get-tuple-element.51), channel_id=1, source_target_pairs={{0,16},{16,0},{1,17},{17,1},{2,18},{18,2},{3,19},{19,3},{4,20},{20... | collective-permute-start | bytes 73736 | tf_op jit(solution)/shard_map/ppermute | solution.py:685
  47.1 2.4 %collective-permute-done.7 = f32[1,32,192]{2,1,0:T(8,128)S(1)} collective-permute-done((f32[1,32,192]{2,1,0:T(8,128)S(1)}, f32[1,32,192]{2,1,0:T(8,128)S(1)}, u32[]{:S(2)}, u32[]{:S(2)}) %collective-permute-start.7) | collective-permute-done | bytes 24608 | tf_op jit(solution)/shard_map/ppermute | solution.py:685
  49.6 0.6 %add.3 = f32[1,32,192]{2,1,0:T(8,128)} add(f32[1,32,192]{2,1,0:T(8,128)S(1)} %get-tuple-element.50, f32[1,32,192]{2,1,0:T(8,128)S(1)} %collective-permute-done.7) | non-fusion elementwise | flops 6144 | bytes 73728 | tf_op jit(solution)/shard_map/add | solution.py:685
  (1 shorter events, 0.0 us)
Async XLA Ops:
  0.6 12.0 %collective-permute-start.1 = (f32[1,32,192]{2,1,0:T(8,128)}, f32[1,32,192]{2,1,0:T(8,128)S(1)}, u32[]{:S(2)}, u32[]{:S(2)}) collective-permute-start(f32[1,32,192]{2,1,0:T(8,128)} %refs_0_.1), channel_id=1, source_target_pairs={{0,4},{4,8},{8,12},{12,0},{1,5},{5,9},{9,13},{13,1},{2,6},{6,10},{... | collective-permute-start | bytes 73736 | tf_op jit(solution)/shard_map/ppermute | solution.py:521
  3.7 9.0 %collective-permute-start = (f32[1,32,192]{2,1,0:T(8,128)}, f32[1,32,192]{2,1,0:T(8,128)S(1)}, u32[]{:S(2)}, u32[]{:S(2)}) collective-permute-start(f32[1,32,192]{2,1,0:T(8,128)} %refs_0_.1), channel_id=1, source_target_pairs={{0,12},{4,0},{8,4},{12,8},{1,13},{5,1},{9,5},{13,9},{2,14},{6,2},{... | collective-permute-start | bytes 73736 | tf_op jit(solution)/shard_map/ppermute | solution.py:521
  5.8 6.9 %collective-permute-start.2 = (f32[1,32,192]{2,1,0:T(8,128)}, f32[1,32,192]{2,1,0:T(8,128)S(1)}, u32[]{:S(2)}, u32[]{:S(2)}) collective-permute-start(f32[1,32,192]{2,1,0:T(8,128)} %refs_0_.1), channel_id=1, source_target_pairs={{0,8},{4,12},{8,0},{12,4},{1,9},{5,13},{9,1},{13,5},{2,10},{6,14},... | collective-permute-start | bytes 73736 | tf_op jit(solution)/shard_map/ppermute | solution.py:521
  6.7 5.9 %copy-start = (f32[1,32,192]{2,1,0:T(8,128)S(1)}, f32[1,32,192]{2,1,0:T(8,128)}, u32[]{:S(2)}) copy-start(f32[1,32,192]{2,1,0:T(8,128)} %refs_0_.1) | copy-start | bytes 73732
  12.8 8.1 %collective-permute-start.5 = (f32[192,128]{1,0:T(8,128)S(1)}, f32[192,128]{1,0:T(8,128)S(1)}, u32[]{:S(2)}, u32[]{:S(2)}) collective-permute-start(f32[192,128]{1,0:T(8,128)S(1)} %stack.2.refs_0_), channel_id=1, source_target_pairs={{0,18},{2,16},{16,2},{18,0},{1,19},{3,17},{17,3},{19,1},{4,22},{6,... | collective-permute-start | bytes 294920 | tf_op jit(solution)/shard_map/ppermute | solution.py:557
  15.3 5.6 %collective-permute-start.4 = (f32[192,128]{1,0:T(8,128)S(1)}, f32[192,128]{1,0:T(8,128)S(1)}, u32[]{:S(2)}, u32[]{:S(2)}) collective-permute-start(f32[192,128]{1,0:T(8,128)S(1)} %stack.2.refs_0_), channel_id=1, source_target_pairs={{0,16},{2,18},{16,0},{18,2},{1,17},{3,19},{17,1},{19,3},{4,20},{6,... | collective-permute-start | bytes 294920 | tf_op jit(solution)/shard_map/ppermute | solution.py:557
  15.8 5.1 %collective-permute-start.3 = (f32[192,128]{1,0:T(8,128)S(1)}, f32[192,128]{1,0:T(8,128)S(1)}, u32[]{:S(2)}, u32[]{:S(2)}) collective-permute-start(f32[192,128]{1,0:T(8,128)S(1)} %stack.2.refs_0_), channel_id=1, source_target_pairs={{0,2},{2,0},{16,18},{18,16},{1,3},{3,1},{17,19},{19,17},{4,6},{6,4... | collective-permute-start | bytes 294920 | tf_op jit(solution)/shard_map/ppermute | solution.py:557
  21.0 1.8 %collective-permute-start.6 = (f32[768,128]{1,0:T(8,128)S(1)}, f32[768,128]{1,0:T(8,128)S(1)}, u32[]{:S(2)}, u32[]{:S(2)}) collective-permute-start(f32[768,128]{1,0:T(8,128)S(1)} %stack.3.own_ref.before_ref), channel_id=1, source_target_pairs={{0,1},{1,0},{2,3},{3,2},{4,5},{5,4},{6,7},{7,6},{8,9},{9,8},{10,11... | collective-permute-start | bytes 1179656 | tf_op jit(solution)/shard_map/ppermute | solution.py:585
  30.7 14.6 %all-to-all-start = ((f32[16,16,256]{2,1,0:T(8,128)}), f32[16,16,256]{2,1,0:T(8,128)S(1)}, u32[]{:S(2)}, u32[]{:S(2)}) async-start(f32[16,16,256]{2,1,0:T(8,128)} %bitcast.4), calls=%async_computation | async-start | bytes 524288 | tf_op jit(solution)/shard_map/all_to_all | solution.py:656
  45.6 4.0 %collective-permute-start.7 = (f32[1,32,192]{2,1,0:T(8,128)S(1)}, f32[1,32,192]{2,1,0:T(8,128)S(1)}, u32[]{:S(2)}, u32[]{:S(2)}) collective-permute-start(f32[1,32,192]{2,1,0:T(8,128)S(1)} %get-tuple-element.51), channel_id=1, source_target_pairs={{0,16},{16,0},{1,17},{17,1},{2,18},{18,2},{3,19},{19,3},{4,20},{20... | collective-permute-start | bytes 73736 | tf_op jit(solution)/shard_map/ppermute | solution.py:685

commit v22 on v21

--- a/solution.py
+++ b/solution.py
@@ -68,11 +68,11 @@
     return slice(here.start + by, here.stop + by)
 
 
-def pair_product(pair, value, dims):
+def pair_product(pair, value):
     rows = pair.shape[0] // 2
     high, low = split(value)
-    both = dot(pair[...], high, dims)
-    return both[:rows] + (both[rows:] + dot(pair[:rows], low, dims))
+    both = dot(pair[...], high)
+    return both[:rows] + (both[rows:] + dot(pair[:rows], low))
 
 
 def chunk(i):
@@ -222,9 +222,9 @@
     slot = lax.broadcasted_iota(jnp.int32, (1, patches * 16), 1) % 16
     line = lax.broadcasted_iota(jnp.int32, lay.shape, 0)
     lay[...] = jnp.where(line == frame * 16 + slot, 1.0, 0.0).astype(BF16)
-    slot = lax.broadcasted_iota(jnp.int32, number.shape, 0) % 16
-    top = row_value(crops_ref, 1, patches, number.shape, 0, 16)
-    left = row_value(crops_ref, 2, patches, number.shape, 0, 16)
+    slot = lax.broadcasted_iota(jnp.int32, number.shape, 1) % 16
+    top = row_value(crops_ref, 1, patches, number.shape, 1, 16)
+    left = row_value(crops_ref, 2, patches, number.shape, 1, 16)
     number[...] = ((top + slot // 4) * SIDE + left + slot % 4).astype(F32)
 
 
@@ -316,7 +316,7 @@
             rows[into, 128:] = jnp.where(row >= 2, line[:, 64:], line[:, :64])
     pre = through(rows[...], coarses, NN)
     gate = sigmoid(pre)
-    slope_ref[...] = gate * (1.0 + pre * (1.0 - gate))
+    slope_ref[...] = (gate * (1.0 + pre * (1.0 - gate))).T
     projected = through(pre * gate, projects, NN).T
     projected_ref[...] = jnp.concatenate(split(projected), axis=1)
     for copy in fetches:
@@ -350,7 +350,7 @@
     sems,
 ):
     width, count = xw.shape
-    slots = dslot_ref.shape[0]
+    slots = dslot_ref.shape[1]
     chunks = chunk_rows(count)
     each = slots // len(chunks)
     tw_loads = [
@@ -406,8 +406,8 @@
             target[here] = de
             parts[here], parts[shift(here, width)] = split(de)
         mine = slice(i * each, (i + 1) * each)
-        both = dot(taking(wanted[:, tokens], each, i * each), parts[...], NT)
-        dslot_ref[mine] = both[:, :width] + both[:, width:]
+        both = dot(parts[...], taking(wanted[:, tokens], each, i * each), NT)
+        dslot_ref[:, mine] = both[:width] + both[width:]
         if i < len(stores):
             stores[i].start()
     for copy in stores + fetches:
@@ -421,16 +421,10 @@
     return both[:count] + (both[count:] + dot(high, pair[rows:], dims))
 
 
-def back_through(value, pair):
-    count, rows = value.shape[0], pair.shape[0] // 2
-    both = dot(jnp.concatenate(split(value), axis=0), pair[...], NT)
-    return both[:count, :rows] + (both[count:, :rows] + both[:count, rows:])
-
-
 def closing_kernel(dslot_ref, slope_ref, coarses, projects, lay, number, send_ref):
-    grad = back_through(back_through(dslot_ref[...], projects) * slope_ref[...], coarses)
-    parts = jnp.concatenate(split(jnp.concatenate([grad, number[...]], axis=1)), axis=1)
-    both = dot(lay[...], parts)
+    grad = pair_product(coarses, pair_product(projects, dslot_ref[...]) * slope_ref[...])
+    parts = jnp.concatenate(split(jnp.concatenate([grad, number[...]], axis=0)), axis=0)
+    both = dot(lay[...], parts, NT)
     send_ref[...] = both[:, :LANES] + both[:, LANES:]
 
 
@@ -592,7 +586,7 @@
             pltpu.VMEM((width, 3 * width), BF16),
             pltpu.VMEM((1, count), jnp.int32),
             pltpu.VMEM((peers * 16, patches * 16), BF16),
-            pltpu.VMEM((patches * 16, LANES - pixels), F32),
+            pltpu.VMEM((LANES - pixels, patches * 16), F32),
         ),
         limit=ROOM,
         in_specs=[VMEM, SMEM, HBM],
@@ -605,7 +599,7 @@
         6 * patches * 16 * width * width,
         (
             pltpu.VMEM((width, 2 * patches * 16), BF16),
-            pltpu.VMEM((patches * 16, width), F32),
+            pltpu.VMEM((width, patches * 16), F32),
             pltpu.VMEM((width, 2 * ROWS), F32),
             pltpu.VMEM((width, ROWS), F32),
         ),
@@ -626,7 +620,7 @@
             pltpu.HBM((width, count), F32),
             pltpu.VMEM((width, ROWS), F32),
             pltpu.VMEM((3 * width, values), BF16),
-            pltpu.VMEM((patches * 16, width), F32),
+            pltpu.VMEM((width, patches * 16), F32),
         ),
         limit=ROOM,
         in_specs=[VMEM] * 6 + [HBM] * 4,

time: 50.5 us -> 50.6 us (level)
  no operation moved by 1% of the time
where the time goes in v22:
time: 50.6 us; the launch traced here: 50.3 us
  Pallas kernels  26.2 us (52%)
  starting transfers between devices  15.8 us (31%)
  waiting for transfers between devices  6.91 us (14%)
  between operations  0.77 us (2%)
  other arithmetic  0.62 us (1%)
    ppermute x3, starting transfers between devices, body(): lax.ppermute(coarse_input, 'far', [(p, (p + k) % far) for p in range(far)])  6.11 us
    pallas_call x1, Pallas kernels, body(): call(input_kernel, 'input', 6 * count * values * width, (pltpu.HBM((width...  5.9 us
    pallas_call x1, Pallas kernels, body(): call(last_kernel, 'last', 6 * count * values * width, pltpu.HBM((count, v...  5.66 us
    pallas_call x1, Pallas kernels, body(): call(target_kernel, 'target', 6 * count * values * width, (pltpu.HBM((wid...  4.55 us
    all_to_all x1, starting transfers between devices, body(): returned = lax.all_to_all(back, patch, 0, 0, tiled=True)  4.51 us
    pallas_call x1, Pallas kernels, body(): call(middle_kernel, 'middle', 6 * count * width * width, (pltpu.HBM((widt...  4.47 us
    all_to_all x1, waiting for transfers between devices, body(): returned = lax.all_to_all(back, patch, 0, 0, tiled=True)  4.37 us
    ppermute x3, starting transfers between devices, body(): lax.ppermute(column, ('lvl', 'y'), [(p, p ^ flip) for p in range(4)])  3.55 us
  transfers between devices with their start and end apart: 9, of which 3 were waited for; matrix products, arithmetic and copies ran while one was open for 0% of the time, Pallas kernels for 35%

profile of v22, /device:TPU:0, one launch (start us, length us, event | category | flops | bytes accessed | tf_op | source)
XLA Modules:
  0.0 50.3 jit_solution(2711626670423551720)
XLA Ops:
  0.6 3.1 %collective-permute-start.1 = (f32[1,32,192]{2,1,0:T(8,128)}, f32[1,32,192]{2,1,0:T(8,128)S(1)}, u32[]{:S(2)}, u32[]{:S(2)}) collective-permute-start(f32[1,32,192]{2,1,0:T(8,128)} %refs_0_.1), channel_id=1, source_target_pairs={{0,4},{4,8},{8,12},{12,0},{1,5},{5,9},{9,13},{13,1},{2,6},{6,10},{... | collective-permute-start | bytes 73736 | tf_op jit(solution)/shard_map/ppermute | solution.py:515
  3.7 2.1 %collective-permute-start = (f32[1,32,192]{2,1,0:T(8,128)}, f32[1,32,192]{2,1,0:T(8,128)S(1)}, u32[]{:S(2)}, u32[]{:S(2)}) collective-permute-start(f32[1,32,192]{2,1,0:T(8,128)} %refs_0_.1), channel_id=1, source_target_pairs={{0,12},{4,0},{8,4},{12,8},{1,13},{5,1},{9,5},{13,9},{2,14},{6,2},{... | collective-permute-start | bytes 73736 | tf_op jit(solution)/shard_map/ppermute | solution.py:515
  5.8 0.9 %collective-permute-start.2 = (f32[1,32,192]{2,1,0:T(8,128)}, f32[1,32,192]{2,1,0:T(8,128)S(1)}, u32[]{:S(2)}, u32[]{:S(2)}) collective-permute-start(f32[1,32,192]{2,1,0:T(8,128)} %refs_0_.1), channel_id=1, source_target_pairs={{0,8},{4,12},{8,0},{12,4},{1,9},{5,13},{9,1},{13,5},{2,10},{6,14},... | collective-permute-start | bytes 73736 | tf_op jit(solution)/shard_map/ppermute | solution.py:515
  6.7 0.0 copy-start
  6.7 5.9 %input.1 = (f32[320,1536]{1,0:T(8,128)}, f32[320,512]{1,0:T(8,128)S(1)}, bf16[640,768]{1,0:T(8,128)(2,1)}, f32[512,768]{1,0:T(8,128)S(1)}, bf16[640,768]{1,0:T(8,128)(2,1)S(1)}, /*index=5*/s32[4,8]{1,0:T(4,128)S(1)}) custom-call(f32[2048,768]{1,0:T(8,128)} %bitcast.9, f32[320,768]{1,0:T(8,128)} %bitcast.12, f32[2048,768]{1,0:T(8,128)} %bitcast.10, ...), custom_call_target="tpu_custom_call" | custom-call | flops 3019898880 | bytes 16253184 | tf_op jit(solution)/shard_map/input/pallas_call | solution.py:521
  12.7 0.0 collective-permute-done.1.refs_2_
  12.7 0.0 collective-permute-done.refs_1_
  12.7 0.0 collective-permute-done.2.refs_3_
  12.7 0.0 copy-done
  12.7 0.1 stack.2.refs_0_
  12.8 2.5 %collective-permute-start.5 = (f32[192,128]{1,0:T(8,128)S(1)}, f32[192,128]{1,0:T(8,128)S(1)}, u32[]{:S(2)}, u32[]{:S(2)}) collective-permute-start(f32[192,128]{1,0:T(8,128)S(1)} %stack.2.refs_0_), channel_id=1, source_target_pairs={{0,18},{2,16},{16,2},{18,0},{1,19},{3,17},{17,3},{19,1},{4,22},{6,... | collective-permute-start | bytes 294920 | tf_op jit(solution)/shard_map/ppermute | solution.py:551
  15.3 0.5 %collective-permute-start.4 = (f32[192,128]{1,0:T(8,128)S(1)}, f32[192,128]{1,0:T(8,128)S(1)}, u32[]{:S(2)}, u32[]{:S(2)}) collective-permute-start(f32[192,128]{1,0:T(8,128)S(1)} %stack.2.refs_0_), channel_id=1, source_target_pairs={{0,16},{2,18},{16,0},{18,2},{1,17},{3,19},{17,1},{19,3},{4,20},{6,... | collective-permute-start | bytes 294920 | tf_op jit(solution)/shard_map/ppermute | solution.py:551
  15.8 0.5 %collective-permute-start.3 = (f32[192,128]{1,0:T(8,128)S(1)}, f32[192,128]{1,0:T(8,128)S(1)}, u32[]{:S(2)}, u32[]{:S(2)}) collective-permute-start(f32[192,128]{1,0:T(8,128)S(1)} %stack.2.refs_0_), channel_id=1, source_target_pairs={{0,2},{2,0},{16,18},{18,16},{1,3},{3,1},{17,19},{19,17},{4,6},{6,4... | collective-permute-start | bytes 294920 | tf_op jit(solution)/shard_map/ppermute | solution.py:551
  16.3 4.6 %target.1 = (f32[320,1536]{1,0:T(8,128)}, f32[320,512]{1,0:T(8,128)}, f32[320,512]{1,0:T(8,128)S(1)}, bf16[384,320]{1,0:T(8,128)(2,1)S(1)}, bf16[640,320]{1,0:T(8,128)(2,1)S(1)}) custom-call(f32[2048,768]{1,0:T(8,128)} %bitcast.11, f32[192,320]{1,0:T(8,128)} %cwgt_hbm.1, f32[320,320]{1,0:T(8,128)} %xwgt_hbm.1, f32[512,768]{1,0:T(8,128)S(1)} %get-tuple-element.29.rows, ...), custom_call_target="tpu_custom_call" | custom-call | flops 3019898880 | bytes 9175040 | tf_op jit(solution)/shard_map/target/pallas_call | solution.py:552
  20.9 0.0 collective-permute-done.5.refs_3_
  20.9 0.0 collective-permute-done.4.refs_2_
  20.9 0.0 collective-permute-done.3.refs_1_
  21.0 0.1 collective-permute-start.6
  21.0 1.6 %prepare.1 = (bf16[320,960]{1,0:T(8,128)(2,1)S(1)}, s32[1,2048]{1,0:T(1,128)S(1)}, bf16[256,128]{1,0:T(8,128)(2,1)S(1)}, f32[64,128]{1,0:T(8,128)S(1)}) custom-call(bf16[640,768]{1,0:T(8,128)(2,1)S(1)} %get-tuple-element.30.pair, s32[4,8]{1,0:T(4,128)S(1)} %get-tuple-element.27.crops_vmem.crops_ref, f32[768,128]{1,0:T(8,128)S(1)} %stack.3.own_ref.before_ref), custom_call_target="tpu_custom_call" | custom-call | flops 629145600 | bytes 2801664 | tf_op jit(solution)/shard_map/prepare/pallas_call | solution.py:581
  22.7 0.1 collective-permute-done.6.other_ref
  22.8 1.9 %context.1 = (bf16[320,256]{1,0:T(8,128)(2,1)S(1)}, f32[320,128]{1,0:T(8,128)S(1)}, f32[320,1024]{1,0:T(8,128)S(1)}, f32[320,512]{1,0:T(8,128)S(1)}) custom-call(s32[4,8]{1,0:T(4,128)S(1)} %get-tuple-element.27.crops_vmem.crops_ref, f32[768,128]{1,0:T(8,128)S(1)} %stack.3.own_ref.before_ref, f32[768,128]{1,0:T(8,128)S(1)} %collective-permute-done.6.other_ref, ...), custom_call_target="tpu_custom_call" | custom-call | flops 78643200 | bytes 4915200 | tf_op jit(solution)/shard_map/context/pallas_call | solution.py:596
  24.7 4.5 %middle.1 = (f32[320,2048]{1,0:T(8,128)}, f32[320,512]{1,0:T(8,128)S(1)}, bf16[960,768]{1,0:T(8,128)(2,1)S(1)}, f32[320,128]{1,0:T(8,128)S(1)}) custom-call(bf16[320,256]{1,0:T(8,128)(2,1)S(1)} %get-tuple-element.35.projected, bf16[320,960]{1,0:T(8,128)(2,1)S(1)} %get-tuple-element.36.grams, s32[1,2048]{1,0:T(1,128)S(1)} %get-tuple-element.37.wanted, ...), custom_call_target="tpu_custom_call" | custom-call | flops 1258291200 | bytes 12779520 | tf_op jit(solution)/shard_map/middle/pallas_call | solution.py:615
  29.2 1.7 %closing.1 = f32[256,256]{1,0:T(8,128)} custom-call(f32[320,128]{1,0:T(8,128)S(1)} %get-tuple-element.43.dslot_ref, f32[320,128]{1,0:T(8,128)S(1)} %get-tuple-element.44.slope_ref, bf16[384,320]{1,0:T(8,128)(2,1)S(1)} %get-tuple-element.33.coarses, bf16[640,320]{1,0:T(8,128)(2,1)S(1)} %get-tuple-element.34.projects, ...), custom_call_target="tpu_custom_call" | custom-call | flops 78643200 | bytes 524288 | tf_op jit(solution)/shard_map/closing/pallas_call | solution.py:641
  30.8 4.5 %all-to-all-start = ((f32[16,16,256]{2,1,0:T(8,128)}), f32[16,16,256]{2,1,0:T(8,128)S(1)}, u32[]{:S(2)}, u32[]{:S(2)}) async-start(f32[16,16,256]{2,1,0:T(8,128)} %bitcast.4), calls=%async_computation | async-start | bytes 524288 | tf_op jit(solution)/shard_map/all_to_all | solution.py:650
  35.4 5.7 %last.1.done_ref = f32[2048,768]{1,0:T(8,128)} custom-call(f32[320,2048]{1,0:T(8,128)} %get-tuple-element.47.de_hbm, f32[320,512]{1,0:T(8,128)S(1)} %get-tuple-element.48.first, bf16[960,768]{1,0:T(8,128)(2,1)S(1)} %get-tuple-element.49.deep), custom_call_target="tpu_custom_call" | custom-call | flops 3019898880 | bytes 12582912 | tf_op jit(solution)/shard_map/last/pallas_call | solution.py:652
  41.0 4.4 %all-to-all-done = f32[16,16,256]{2,1,0:T(8,128)S(1)} async-done(((f32[16,16,256]{2,1,0:T(8,128)}), f32[16,16,256]{2,1,0:T(8,128)S(1)}, u32[]{:S(2)}, u32[]{:S(2)}) %all-to-all-start) | async-done | bytes 262176 | tf_op jit(solution)/shard_map/all_to_all | solution.py:650
  45.4 0.3 scatter.1
  45.7 1.6 %collective-permute-start.7 = (f32[1,32,192]{2,1,0:T(8,128)S(1)}, f32[1,32,192]{2,1,0:T(8,128)S(1)}, u32[]{:S(2)}, u32[]{:S(2)}) collective-permute-start(f32[1,32,192]{2,1,0:T(8,128)S(1)} %get-tuple-element.51), channel_id=1, source_target_pairs={{0,16},{16,0},{1,17},{17,1},{2,18},{18,2},{3,19},{19,3},{4,20},{20... | collective-permute-start | bytes 73736 | tf_op jit(solution)/shard_map/ppermute | solution.py:679
  47.2 2.4 %collective-permute-done.7 = f32[1,32,192]{2,1,0:T(8,128)S(1)} collective-permute-done((f32[1,32,192]{2,1,0:T(8,128)S(1)}, f32[1,32,192]{2,1,0:T(8,128)S(1)}, u32[]{:S(2)}, u32[]{:S(2)}) %collective-permute-start.7) | collective-permute-done | bytes 24608 | tf_op jit(solution)/shard_map/ppermute | solution.py:679
  49.7 0.6 %add.3 = f32[1,32,192]{2,1,0:T(8,128)} add(f32[1,32,192]{2,1,0:T(8,128)S(1)} %get-tuple-element.50, f32[1,32,192]{2,1,0:T(8,128)S(1)} %collective-permute-done.7) | non-fusion elementwise | flops 6144 | bytes 73728 | tf_op jit(solution)/shard_map/add | solution.py:679
  (1 shorter events, 0.0 us)
Async XLA Ops:
  0.6 12.0 %collective-permute-start.1 = (f32[1,32,192]{2,1,0:T(8,128)}, f32[1,32,192]{2,1,0:T(8,128)S(1)}, u32[]{:S(2)}, u32[]{:S(2)}) collective-permute-start(f32[1,32,192]{2,1,0:T(8,128)} %refs_0_.1), channel_id=1, source_target_pairs={{0,4},{4,8},{8,12},{12,0},{1,5},{5,9},{9,13},{13,1},{2,6},{6,10},{... | collective-permute-start | bytes 73736 | tf_op jit(solution)/shard_map/ppermute | solution.py:515
  3.7 9.0 %collective-permute-start = (f32[1,32,192]{2,1,0:T(8,128)}, f32[1,32,192]{2,1,0:T(8,128)S(1)}, u32[]{:S(2)}, u32[]{:S(2)}) collective-permute-start(f32[1,32,192]{2,1,0:T(8,128)} %refs_0_.1), channel_id=1, source_target_pairs={{0,12},{4,0},{8,4},{12,8},{1,13},{5,1},{9,5},{13,9},{2,14},{6,2},{... | collective-permute-start | bytes 73736 | tf_op jit(solution)/shard_map/ppermute | solution.py:515
  5.8 6.9 %collective-permute-start.2 = (f32[1,32,192]{2,1,0:T(8,128)}, f32[1,32,192]{2,1,0:T(8,128)S(1)}, u32[]{:S(2)}, u32[]{:S(2)}) collective-permute-start(f32[1,32,192]{2,1,0:T(8,128)} %refs_0_.1), channel_id=1, source_target_pairs={{0,8},{4,12},{8,0},{12,4},{1,9},{5,13},{9,1},{13,5},{2,10},{6,14},... | collective-permute-start | bytes 73736 | tf_op jit(solution)/shard_map/ppermute | solution.py:515
  6.7 5.9 %copy-start = (f32[1,32,192]{2,1,0:T(8,128)S(1)}, f32[1,32,192]{2,1,0:T(8,128)}, u32[]{:S(2)}) copy-start(f32[1,32,192]{2,1,0:T(8,128)} %refs_0_.1) | copy-start | bytes 73732
  12.8 8.1 %collective-permute-start.5 = (f32[192,128]{1,0:T(8,128)S(1)}, f32[192,128]{1,0:T(8,128)S(1)}, u32[]{:S(2)}, u32[]{:S(2)}) collective-permute-start(f32[192,128]{1,0:T(8,128)S(1)} %stack.2.refs_0_), channel_id=1, source_target_pairs={{0,18},{2,16},{16,2},{18,0},{1,19},{3,17},{17,3},{19,1},{4,22},{6,... | collective-permute-start | bytes 294920 | tf_op jit(solution)/shard_map/ppermute | solution.py:551
  15.3 5.6 %collective-permute-start.4 = (f32[192,128]{1,0:T(8,128)S(1)}, f32[192,128]{1,0:T(8,128)S(1)}, u32[]{:S(2)}, u32[]{:S(2)}) collective-permute-start(f32[192,128]{1,0:T(8,128)S(1)} %stack.2.refs_0_), channel_id=1, source_target_pairs={{0,16},{2,18},{16,0},{18,2},{1,17},{3,19},{17,1},{19,3},{4,20},{6,... | collective-permute-start | bytes 294920 | tf_op jit(solution)/shard_map/ppermute | solution.py:551
  15.8 5.1 %collective-permute-start.3 = (f32[192,128]{1,0:T(8,128)S(1)}, f32[192,128]{1,0:T(8,128)S(1)}, u32[]{:S(2)}, u32[]{:S(2)}) collective-permute-start(f32[192,128]{1,0:T(8,128)S(1)} %stack.2.refs_0_), channel_id=1, source_target_pairs={{0,2},{2,0},{16,18},{18,16},{1,3},{3,1},{17,19},{19,17},{4,6},{6,4... | collective-permute-start | bytes 294920 | tf_op jit(solution)/shard_map/ppermute | solution.py:551
  21.0 1.8 %collective-permute-start.6 = (f32[768,128]{1,0:T(8,128)S(1)}, f32[768,128]{1,0:T(8,128)S(1)}, u32[]{:S(2)}, u32[]{:S(2)}) collective-permute-start(f32[768,128]{1,0:T(8,128)S(1)} %stack.3.own_ref.before_ref), channel_id=1, source_target_pairs={{0,1},{1,0},{2,3},{3,2},{4,5},{5,4},{6,7},{7,6},{8,9},{9,8},{10,11... | collective-permute-start | bytes 1179656 | tf_op jit(solution)/shard_map/ppermute | solution.py:579
  30.8 14.6 %all-to-all-start = ((f32[16,16,256]{2,1,0:T(8,128)}), f32[16,16,256]{2,1,0:T(8,128)S(1)}, u32[]{:S(2)}, u32[]{:S(2)}) async-start(f32[16,16,256]{2,1,0:T(8,128)} %bitcast.4), calls=%async_computation | async-start | bytes 524288 | tf_op jit(solution)/shard_map/all_to_all | solution.py:650
  45.7 4.0 %collective-permute-start.7 = (f32[1,32,192]{2,1,0:T(8,128)S(1)}, f32[1,32,192]{2,1,0:T(8,128)S(1)}, u32[]{:S(2)}, u32[]{:S(2)}) collective-permute-start(f32[1,32,192]{2,1,0:T(8,128)S(1)} %get-tuple-element.51), channel_id=1, source_target_pairs={{0,16},{16,0},{1,17},{17,1},{2,18},{18,2},{3,19},{19,3},{4,20},{20... | collective-permute-start | bytes 73736 | tf_op jit(solution)/shard_map/ppermute | solution.py:679

commit v23 on v21

--- a/solution.py
+++ b/solution.py
@@ -126,16 +126,17 @@
         pltpu.make_async_copy(out.at[:, here], out_hbm.at[:, here], out_sems.at[i])
         for i, here in enumerate(chunks[:-1])
     ]
-    for copy in [fetch] + loads[:2]:
+    for copy in (fetch, loads[0]):
         copy.start()
+    fetch.wait()
+    loads[1].start()
+    pair[:width], pair[width:] = split(weight[...])
+    keep.start()
     for i, here in enumerate(chunks):
         loads[i].wait()
         if i + 2 < len(chunks):
             loads[i + 2].start()
         if i == 0:
-            fetch.wait()
-            pair[:width], pair[width:] = split(weight[...])
-            keep.start()
             fetch_next.start()
         if i == 1:
             fetch_rows.start()
@@ -300,7 +301,7 @@
         frame, top, left = crops_ref[0, j], crops_ref[1, j], crops_ref[2, j]
         near_by = lax.bitwise_xor(frame % 4, me % 4)
         k = (me // 4 - frame // 4 + far) % far
-        k = jnp.where(k == 1, 2, jnp.where(k == 2, 3, jnp.where(k == 3, 1, k)))
+        k = jnp.where(k == 2, 3, jnp.where(k == 3, 2, k))
         here = near_by % 2 == 0
         for a in range(4):
             row = jnp.minimum(top + a, SIDE - 1)
@@ -519,7 +520,7 @@
     column = {0: coarse_input}
     for k in range(1, far):
         column[k] = lax.ppermute(coarse_input, "far", [(p, (p + k) % far) for p in range(far)])
-    column = [column[k] for k in [0, 3, 1, 2] + list(range(4, far))]
+    column = [column[k] for k in [0, 1, 3, 2] + list(range(4, far))]
 
     steps = count // ROWS
     pair_shape = (2 * width, values)

time: 50.5 us -> 52.2 us (1.034)
  starting transfers between devices: 15.8 us -> 17 us
    all_to_all x1, starting transfers between devices: 4.52 us -> 5.75 us  [body(): returned = lax.all_to_all(back, patch, 0, 0, tiled=True)]
where the time goes in v23:
time: 52.2 us; the launch traced here: 51.9 us
  Pallas kernels  26.6 us (51%)
  starting transfers between devices  17 us (33%)
  waiting for transfers between devices  6.89 us (13%)
  between operations  0.77 us (1%)
  other arithmetic  0.62 us (1%)
    pallas_call x1, Pallas kernels, body(): call(input_kernel, 'input', 6 * count * values * width, (pltpu.HBM((width...  6.36 us
    ppermute x3, starting transfers between devices, body(): lax.ppermute(coarse_input, 'far', [(p, (p + k) % far) for p in range(far)])  6.11 us
    all_to_all x1, starting transfers between devices, body(): returned = lax.all_to_all(back, patch, 0, 0, tiled=True)  5.75 us
    pallas_call x1, Pallas kernels, body(): call(last_kernel, 'last', 6 * count * values * width, pltpu.HBM((count, v...  5.66 us
    pallas_call x1, Pallas kernels, body(): call(target_kernel, 'target', 6 * count * values * width, (pltpu.HBM((wid...  4.55 us
    all_to_all x1, waiting for transfers between devices, body(): returned = lax.all_to_all(back, patch, 0, 0, tiled=True)  4.38 us
    pallas_call x1, Pallas kernels, body(): call(middle_kernel, 'middle', 6 * count * width * width, (pltpu.HBM((widt...  4.29 us
    ppermute x3, starting transfers between devices, body(): lax.ppermute(column, ('lvl', 'y'), [(p, p ^ flip) for p in range(4)])  3.55 us
  transfers between devices with their start and end apart: 9, of which 3 were waited for; matrix products, arithmetic and copies ran while one was open for 0% of the time, Pallas kernels for 35%

profile of v23, /device:TPU:0, one launch (start us, length us, event | category | flops | bytes accessed | tf_op | source)
XLA Modules:
  0.0 51.9 jit_solution(5873685019467678248)
XLA Ops:
  0.6 5.1 %collective-permute-start.1 = (f32[1,32,192]{2,1,0:T(8,128)}, f32[1,32,192]{2,1,0:T(8,128)S(1)}, u32[]{:S(2)}, u32[]{:S(2)}) collective-permute-start(f32[1,32,192]{2,1,0:T(8,128)} %refs_0_.1), channel_id=1, source_target_pairs={{0,12},{4,0},{8,4},{12,8},{1,13},{5,1},{9,5},{13,9},{2,14},{6,2},{... | collective-permute-start | bytes 73736 | tf_op jit(solution)/shard_map/ppermute | solution.py:522
  5.7 0.0 collective-permute-start
  5.7 1.0 %collective-permute-start.2 = (f32[1,32,192]{2,1,0:T(8,128)}, f32[1,32,192]{2,1,0:T(8,128)S(1)}, u32[]{:S(2)}, u32[]{:S(2)}) collective-permute-start(f32[1,32,192]{2,1,0:T(8,128)} %refs_0_.1), channel_id=1, source_target_pairs={{0,8},{4,12},{8,0},{12,4},{1,9},{5,13},{9,1},{13,5},{2,10},{6,14},... | collective-permute-start | bytes 73736 | tf_op jit(solution)/shard_map/ppermute | solution.py:522
  6.7 0.0 copy-start
  6.7 6.4 %input.1 = (f32[320,1536]{1,0:T(8,128)}, f32[320,512]{1,0:T(8,128)S(1)}, bf16[640,768]{1,0:T(8,128)(2,1)}, f32[512,768]{1,0:T(8,128)S(1)}, bf16[640,768]{1,0:T(8,128)(2,1)S(1)}, /*index=5*/s32[4,8]{1,0:T(4,128)S(1)}) custom-call(f32[2048,768]{1,0:T(8,128)} %bitcast.9, f32[320,768]{1,0:T(8,128)} %bitcast.12, f32[2048,768]{1,0:T(8,128)} %bitcast.10, ...), custom_call_target="tpu_custom_call" | custom-call | flops 3019898880 | bytes 16253184 | tf_op jit(solution)/shard_map/input/pallas_call | solution.py:528
  13.1 0.0 collective-permute-done.1.refs_2_
  13.1 0.0 collective-permute-done.refs_1_
  13.1 0.0 collective-permute-done.2.refs_3_
  13.1 0.0 copy-done
  13.2 0.1 stack.2.refs_0_
  13.2 2.5 %collective-permute-start.5 = (f32[192,128]{1,0:T(8,128)S(1)}, f32[192,128]{1,0:T(8,128)S(1)}, u32[]{:S(2)}, u32[]{:S(2)}) collective-permute-start(f32[192,128]{1,0:T(8,128)S(1)} %stack.2.refs_0_), channel_id=1, source_target_pairs={{0,18},{2,16},{16,2},{18,0},{1,19},{3,17},{17,3},{19,1},{4,22},{6,... | collective-permute-start | bytes 294920 | tf_op jit(solution)/shard_map/ppermute | solution.py:558
  15.7 0.5 %collective-permute-start.4 = (f32[192,128]{1,0:T(8,128)S(1)}, f32[192,128]{1,0:T(8,128)S(1)}, u32[]{:S(2)}, u32[]{:S(2)}) collective-permute-start(f32[192,128]{1,0:T(8,128)S(1)} %stack.2.refs_0_), channel_id=1, source_target_pairs={{0,16},{2,18},{16,0},{18,2},{1,17},{3,19},{17,1},{19,3},{4,20},{6,... | collective-permute-start | bytes 294920 | tf_op jit(solution)/shard_map/ppermute | solution.py:558
  16.3 0.5 collective-permute-start.3
  16.8 4.6 %target.1 = (f32[320,1536]{1,0:T(8,128)}, f32[320,512]{1,0:T(8,128)}, f32[320,512]{1,0:T(8,128)S(1)}, bf16[384,320]{1,0:T(8,128)(2,1)S(1)}, bf16[640,320]{1,0:T(8,128)(2,1)S(1)}) custom-call(f32[2048,768]{1,0:T(8,128)} %bitcast.11, f32[192,320]{1,0:T(8,128)} %cwgt_hbm.1, f32[320,320]{1,0:T(8,128)} %xwgt_hbm.1, f32[512,768]{1,0:T(8,128)S(1)} %get-tuple-element.29.rows, ...), custom_call_target="tpu_custom_call" | custom-call | flops 3019898880 | bytes 9175040 | tf_op jit(solution)/shard_map/target/pallas_call | solution.py:559
  21.3 0.0 collective-permute-done.5.refs_3_
  21.4 0.0 collective-permute-done.4.refs_2_
  21.4 0.0 collective-permute-done.3.refs_1_
  21.4 0.1 collective-permute-start.6
  21.5 1.6 %prepare.1 = (bf16[320,960]{1,0:T(8,128)(2,1)S(1)}, s32[1,2048]{1,0:T(1,128)S(1)}, bf16[256,128]{1,0:T(8,128)(2,1)S(1)}, f32[128,64]{1,0:T(8,128)S(1)}) custom-call(bf16[640,768]{1,0:T(8,128)(2,1)S(1)} %get-tuple-element.30.pair, s32[4,8]{1,0:T(4,128)S(1)} %get-tuple-element.27.crops_vmem.crops_ref, f32[768,128]{1,0:T(8,128)S(1)} %stack.3.own_ref.before_ref), custom_call_target="tpu_custom_call" | custom-call | flops 629145600 | bytes 2801664 | tf_op jit(solution)/shard_map/prepare/pallas_call | solution.py:588
  23.1 0.1 collective-permute-done.6.other_ref
  23.2 1.9 %context.1 = (bf16[320,256]{1,0:T(8,128)(2,1)S(1)}, f32[128,320]{1,0:T(8,128)S(1)}, f32[320,1024]{1,0:T(8,128)S(1)}, f32[320,512]{1,0:T(8,128)S(1)}) custom-call(s32[4,8]{1,0:T(4,128)S(1)} %get-tuple-element.27.crops_vmem.crops_ref, f32[768,128]{1,0:T(8,128)S(1)} %stack.3.own_ref.before_ref, f32[768,128]{1,0:T(8,128)S(1)} %collective-permute-done.6.other_ref, ...), custom_call_target="tpu_custom_call" | custom-call | flops 78643200 | bytes 4915200 | tf_op jit(solution)/shard_map/context/pallas_call | solution.py:603
  25.1 4.3 %middle.1 = (f32[320,2048]{1,0:T(8,128)}, f32[320,512]{1,0:T(8,128)S(1)}, bf16[960,768]{1,0:T(8,128)(2,1)S(1)}, f32[128,320]{1,0:T(8,128)S(1)}) custom-call(bf16[320,256]{1,0:T(8,128)(2,1)S(1)} %get-tuple-element.35.projected, bf16[320,960]{1,0:T(8,128)(2,1)S(1)} %get-tuple-element.36.grams, s32[1,2048]{1,0:T(1,128)S(1)} %get-tuple-element.37.wanted, ...), custom_call_target="tpu_custom_call" | custom-call | flops 1258291200 | bytes 12779520 | tf_op jit(solution)/shard_map/middle/pallas_call | solution.py:622
  29.4 1.7 %closing.1 = f32[256,256]{1,0:T(8,128)} custom-call(f32[128,320]{1,0:T(8,128)S(1)} %get-tuple-element.43.dslot_ref, f32[128,320]{1,0:T(8,128)S(1)} %get-tuple-element.44.slope_ref, bf16[384,320]{1,0:T(8,128)(2,1)S(1)} %get-tuple-element.33.coarses, bf16[640,320]{1,0:T(8,128)(2,1)S(1)} %get-tuple-element.34.projects, ...), custom_call_target="tpu_custom_call" | custom-call | flops 78643200 | bytes 524288 | tf_op jit(solution)/shard_map/closing/pallas_call | solution.py:648
  31.2 5.8 %all-to-all-start = ((f32[16,16,256]{2,1,0:T(8,128)}), f32[16,16,256]{2,1,0:T(8,128)S(1)}, u32[]{:S(2)}, u32[]{:S(2)}) async-start(f32[16,16,256]{2,1,0:T(8,128)} %bitcast.4), calls=%async_computation | async-start | bytes 524288 | tf_op jit(solution)/shard_map/all_to_all | solution.py:657
  36.9 5.7 %last.1.done_ref = f32[2048,768]{1,0:T(8,128)} custom-call(f32[320,2048]{1,0:T(8,128)} %get-tuple-element.47.de_hbm, f32[320,512]{1,0:T(8,128)S(1)} %get-tuple-element.48.first, bf16[960,768]{1,0:T(8,128)(2,1)S(1)} %get-tuple-element.49.deep), custom_call_target="tpu_custom_call" | custom-call | flops 3019898880 | bytes 12582912 | tf_op jit(solution)/shard_map/last/pallas_call | solution.py:659
  42.6 4.4 %all-to-all-done = f32[16,16,256]{2,1,0:T(8,128)S(1)} async-done(((f32[16,16,256]{2,1,0:T(8,128)}), f32[16,16,256]{2,1,0:T(8,128)S(1)}, u32[]{:S(2)}, u32[]{:S(2)}) %all-to-all-start) | async-done | bytes 262176 | tf_op jit(solution)/shard_map/all_to_all | solution.py:657
  47.0 0.3 scatter.1
  47.3 1.6 %collective-permute-start.7 = (f32[1,32,192]{2,1,0:T(8,128)S(1)}, f32[1,32,192]{2,1,0:T(8,128)S(1)}, u32[]{:S(2)}, u32[]{:S(2)}) collective-permute-start(f32[1,32,192]{2,1,0:T(8,128)S(1)} %get-tuple-element.51), channel_id=1, source_target_pairs={{0,16},{16,0},{1,17},{17,1},{2,18},{18,2},{3,19},{19,3},{4,20},{20... | collective-permute-start | bytes 73736 | tf_op jit(solution)/shard_map/ppermute | solution.py:686
  48.8 2.4 %collective-permute-done.7 = f32[1,32,192]{2,1,0:T(8,128)S(1)} collective-permute-done((f32[1,32,192]{2,1,0:T(8,128)S(1)}, f32[1,32,192]{2,1,0:T(8,128)S(1)}, u32[]{:S(2)}, u32[]{:S(2)}) %collective-permute-start.7) | collective-permute-done | bytes 24608 | tf_op jit(solution)/shard_map/ppermute | solution.py:686
  51.3 0.6 %add.3 = f32[1,32,192]{2,1,0:T(8,128)} add(f32[1,32,192]{2,1,0:T(8,128)S(1)} %get-tuple-element.50, f32[1,32,192]{2,1,0:T(8,128)S(1)} %collective-permute-done.7) | non-fusion elementwise | flops 6144 | bytes 73728 | tf_op jit(solution)/shard_map/add | solution.py:686
  (1 shorter events, 0.0 us)
Async XLA Ops:
  0.6 12.5 %collective-permute-start.1 = (f32[1,32,192]{2,1,0:T(8,128)}, f32[1,32,192]{2,1,0:T(8,128)S(1)}, u32[]{:S(2)}, u32[]{:S(2)}) collective-permute-start(f32[1,32,192]{2,1,0:T(8,128)} %refs_0_.1), channel_id=1, source_target_pairs={{0,12},{4,0},{8,4},{12,8},{1,13},{5,1},{9,5},{13,9},{2,14},{6,2},{... | collective-permute-start | bytes 73736 | tf_op jit(solution)/shard_map/ppermute | solution.py:522
  5.7 7.4 %collective-permute-start = (f32[1,32,192]{2,1,0:T(8,128)}, f32[1,32,192]{2,1,0:T(8,128)S(1)}, u32[]{:S(2)}, u32[]{:S(2)}) collective-permute-start(f32[1,32,192]{2,1,0:T(8,128)} %refs_0_.1), channel_id=1, source_target_pairs={{0,4},{4,8},{8,12},{12,0},{1,5},{5,9},{9,13},{13,1},{2,6},{6,10},{... | collective-permute-start | bytes 73736 | tf_op jit(solution)/shard_map/ppermute | solution.py:522
  5.7 7.4 %collective-permute-start.2 = (f32[1,32,192]{2,1,0:T(8,128)}, f32[1,32,192]{2,1,0:T(8,128)S(1)}, u32[]{:S(2)}, u32[]{:S(2)}) collective-permute-start(f32[1,32,192]{2,1,0:T(8,128)} %refs_0_.1), channel_id=1, source_target_pairs={{0,8},{4,12},{8,0},{12,4},{1,9},{5,13},{9,1},{13,5},{2,10},{6,14},... | collective-permute-start | bytes 73736 | tf_op jit(solution)/shard_map/ppermute | solution.py:522
  6.7 6.4 %copy-start = (f32[1,32,192]{2,1,0:T(8,128)S(1)}, f32[1,32,192]{2,1,0:T(8,128)}, u32[]{:S(2)}) copy-start(f32[1,32,192]{2,1,0:T(8,128)} %refs_0_.1) | copy-start | bytes 73732
  13.2 8.1 %collective-permute-start.5 = (f32[192,128]{1,0:T(8,128)S(1)}, f32[192,128]{1,0:T(8,128)S(1)}, u32[]{:S(2)}, u32[]{:S(2)}) collective-permute-start(f32[192,128]{1,0:T(8,128)S(1)} %stack.2.refs_0_), channel_id=1, source_target_pairs={{0,18},{2,16},{16,2},{18,0},{1,19},{3,17},{17,3},{19,1},{4,22},{6,... | collective-permute-start | bytes 294920 | tf_op jit(solution)/shard_map/ppermute | solution.py:558
  15.7 5.6 %collective-permute-start.4 = (f32[192,128]{1,0:T(8,128)S(1)}, f32[192,128]{1,0:T(8,128)S(1)}, u32[]{:S(2)}, u32[]{:S(2)}) collective-permute-start(f32[192,128]{1,0:T(8,128)S(1)} %stack.2.refs_0_), channel_id=1, source_target_pairs={{0,16},{2,18},{16,0},{18,2},{1,17},{3,19},{17,1},{19,3},{4,20},{6,... | collective-permute-start | bytes 294920 | tf_op jit(solution)/shard_map/ppermute | solution.py:558
  16.3 5.1 %collective-permute-start.3 = (f32[192,128]{1,0:T(8,128)S(1)}, f32[192,128]{1,0:T(8,128)S(1)}, u32[]{:S(2)}, u32[]{:S(2)}) collective-permute-start(f32[192,128]{1,0:T(8,128)S(1)} %stack.2.refs_0_), channel_id=1, source_target_pairs={{0,2},{2,0},{16,18},{18,16},{1,3},{3,1},{17,19},{19,17},{4,6},{6,4... | collective-permute-start | bytes 294920 | tf_op jit(solution)/shard_map/ppermute | solution.py:558
  21.4 1.8 %collective-permute-start.6 = (f32[768,128]{1,0:T(8,128)S(1)}, f32[768,128]{1,0:T(8,128)S(1)}, u32[]{:S(2)}, u32[]{:S(2)}) collective-permute-start(f32[768,128]{1,0:T(8,128)S(1)} %stack.3.own_ref.before_ref), channel_id=1, source_target_pairs={{0,1},{1,0},{2,3},{3,2},{4,5},{5,4},{6,7},{7,6},{8,9},{9,8},{10,11... | collective-permute-start | bytes 1179656 | tf_op jit(solution)/shard_map/ppermute | solution.py:586
  31.2 15.8 %all-to-all-start = ((f32[16,16,256]{2,1,0:T(8,128)}), f32[16,16,256]{2,1,0:T(8,128)S(1)}, u32[]{:S(2)}, u32[]{:S(2)}) async-start(f32[16,16,256]{2,1,0:T(8,128)} %bitcast.4), calls=%async_computation | async-start | bytes 524288 | tf_op jit(solution)/shard_map/all_to_all | solution.py:657
  47.3 4.0 %collective-permute-start.7 = (f32[1,32,192]{2,1,0:T(8,128)S(1)}, f32[1,32,192]{2,1,0:T(8,128)S(1)}, u32[]{:S(2)}, u32[]{:S(2)}) collective-permute-start(f32[1,32,192]{2,1,0:T(8,128)S(1)} %get-tuple-element.51), channel_id=1, source_target_pairs={{0,16},{16,0},{1,17},{17,1},{2,18},{18,2},{3,19},{19,3},{4,20},{20... | collective-permute-start | bytes 73736 | tf_op jit(solution)/shard_map/ppermute | solution.py:686

commit v24 on v21

--- a/solution.py
+++ b/solution.py
@@ -126,12 +126,10 @@
         pltpu.make_async_copy(out.at[:, here], out_hbm.at[:, here], out_sems.at[i])
         for i, here in enumerate(chunks[:-1])
     ]
-    for copy in [fetch] + loads[:2]:
+    for copy in [fetch] + loads:
         copy.start()
     for i, here in enumerate(chunks):
         loads[i].wait()
-        if i + 2 < len(chunks):
-            loads[i + 2].start()
         if i == 0:
             fetch.wait()
             pair[:width], pair[width:] = split(weight[...])

time: 50.5 us -> 51.4 us (1.018)
  Pallas kernels: 26.1 us -> 27 us
    pallas_call x1, Pallas kernels: 5.9 us -> 6.85 us  [body(): call(input_kernel, 'input', 6 * count * values * width, (pltpu.HBM((width...]
  transfers between devices with their start and end apart: 9 -> 9, of which waited for: 3 -> 3; matrix products, arithmetic and copies ran while one was open for 0% -> 0% of each run, Pallas kernels for 35% -> 37%
where the time goes in v24:
time: 51.4 us; the launch traced here: 51.1 us
  Pallas kernels  27 us (53%)
  starting transfers between devices  15.8 us (31%)
  waiting for transfers between devices  6.89 us (13%)
  between operations  0.77 us (1%)
  other arithmetic  0.62 us (1%)
    pallas_call x1, Pallas kernels, body(): call(input_kernel, 'input', 6 * count * values * width, (pltpu.HBM((width...  6.85 us
    ppermute x3, starting transfers between devices, body(): lax.ppermute(coarse_input, 'far', [(p, (p + k) % far) for p in range(far)])  6.11 us
    pallas_call x1, Pallas kernels, body(): call(last_kernel, 'last', 6 * count * values * width, pltpu.HBM((count, v...  5.66 us
    pallas_call x1, Pallas kernels, body(): call(target_kernel, 'target', 6 * count * values * width, (pltpu.HBM((wid...  4.55 us
    all_to_all x1, starting transfers between devices, body(): returned = lax.all_to_all(back, patch, 0, 0, tiled=True)  4.52 us
    all_to_all x1, waiting for transfers between devices, body(): returned = lax.all_to_all(back, patch, 0, 0, tiled=True)  4.38 us
    pallas_call x1, Pallas kernels, body(): call(middle_kernel, 'middle', 6 * count * width * width, (pltpu.HBM((widt...  4.29 us
    ppermute x3, starting transfers between devices, body(): lax.ppermute(column, ('lvl', 'y'), [(p, p ^ flip) for p in range(4)])  3.55 us
  transfers between devices with their start and end apart: 9, of which 3 were waited for; matrix products, arithmetic and copies ran while one was open for 0% of the time, Pallas kernels for 37%

profile of v24, /device:TPU:0, one launch (start us, length us, event | category | flops | bytes accessed | tf_op | source)
XLA Modules:
  0.0 51.1 jit_solution(59985738756573416)
XLA Ops:
  0.6 3.1 %collective-permute-start.1 = (f32[1,32,192]{2,1,0:T(8,128)}, f32[1,32,192]{2,1,0:T(8,128)S(1)}, u32[]{:S(2)}, u32[]{:S(2)}) collective-permute-start(f32[1,32,192]{2,1,0:T(8,128)} %refs_0_.1), channel_id=1, source_target_pairs={{0,4},{4,8},{8,12},{12,0},{1,5},{5,9},{9,13},{13,1},{2,6},{6,10},{... | collective-permute-start | bytes 73736 | tf_op jit(solution)/shard_map/ppermute | solution.py:519
  3.7 2.1 %collective-permute-start = (f32[1,32,192]{2,1,0:T(8,128)}, f32[1,32,192]{2,1,0:T(8,128)S(1)}, u32[]{:S(2)}, u32[]{:S(2)}) collective-permute-start(f32[1,32,192]{2,1,0:T(8,128)} %refs_0_.1), channel_id=1, source_target_pairs={{0,12},{4,0},{8,4},{12,8},{1,13},{5,1},{9,5},{13,9},{2,14},{6,2},{... | collective-permute-start | bytes 73736 | tf_op jit(solution)/shard_map/ppermute | solution.py:519
  5.8 0.9 %collective-permute-start.2 = (f32[1,32,192]{2,1,0:T(8,128)}, f32[1,32,192]{2,1,0:T(8,128)S(1)}, u32[]{:S(2)}, u32[]{:S(2)}) collective-permute-start(f32[1,32,192]{2,1,0:T(8,128)} %refs_0_.1), channel_id=1, source_target_pairs={{0,8},{4,12},{8,0},{12,4},{1,9},{5,13},{9,1},{13,5},{2,10},{6,14},... | collective-permute-start | bytes 73736 | tf_op jit(solution)/shard_map/ppermute | solution.py:519
  6.7 0.0 copy-start
  6.7 6.8 %input.1 = (f32[320,1536]{1,0:T(8,128)}, f32[320,512]{1,0:T(8,128)S(1)}, bf16[640,768]{1,0:T(8,128)(2,1)}, f32[512,768]{1,0:T(8,128)S(1)}, bf16[640,768]{1,0:T(8,128)(2,1)S(1)}, /*index=5*/s32[4,8]{1,0:T(4,128)S(1)}) custom-call(f32[2048,768]{1,0:T(8,128)} %bitcast.9, f32[320,768]{1,0:T(8,128)} %bitcast.12, f32[2048,768]{1,0:T(8,128)} %bitcast.10, ...), custom_call_target="tpu_custom_call" | custom-call | flops 3019898880 | bytes 16253184 | tf_op jit(solution)/shard_map/input/pallas_call | solution.py:525
  13.6 0.0 collective-permute-done.1.refs_2_
  13.6 0.0 collective-permute-done.refs_1_
  13.6 0.0 collective-permute-done.2.refs_3_
  13.6 0.0 copy-done
  13.6 0.1 stack.2.refs_0_
  13.7 2.5 %collective-permute-start.5 = (f32[192,128]{1,0:T(8,128)S(1)}, f32[192,128]{1,0:T(8,128)S(1)}, u32[]{:S(2)}, u32[]{:S(2)}) collective-permute-start(f32[192,128]{1,0:T(8,128)S(1)} %stack.2.refs_0_), channel_id=1, source_target_pairs={{0,18},{2,16},{16,2},{18,0},{1,19},{3,17},{17,3},{19,1},{4,22},{6,... | collective-permute-start | bytes 294920 | tf_op jit(solution)/shard_map/ppermute | solution.py:555
  16.2 0.5 %collective-permute-start.4 = (f32[192,128]{1,0:T(8,128)S(1)}, f32[192,128]{1,0:T(8,128)S(1)}, u32[]{:S(2)}, u32[]{:S(2)}) collective-permute-start(f32[192,128]{1,0:T(8,128)S(1)} %stack.2.refs_0_), channel_id=1, source_target_pairs={{0,16},{2,18},{16,0},{18,2},{1,17},{3,19},{17,1},{19,3},{4,20},{6,... | collective-permute-start | bytes 294920 | tf_op jit(solution)/shard_map/ppermute | solution.py:555
  16.8 0.5 collective-permute-start.3
  17.3 4.5 %target.1 = (f32[320,1536]{1,0:T(8,128)}, f32[320,512]{1,0:T(8,128)}, f32[320,512]{1,0:T(8,128)S(1)}, bf16[384,320]{1,0:T(8,128)(2,1)S(1)}, bf16[640,320]{1,0:T(8,128)(2,1)S(1)}) custom-call(f32[2048,768]{1,0:T(8,128)} %bitcast.11, f32[192,320]{1,0:T(8,128)} %cwgt_hbm.1, f32[320,320]{1,0:T(8,128)} %xwgt_hbm.1, f32[512,768]{1,0:T(8,128)S(1)} %get-tuple-element.29.rows, ...), custom_call_target="tpu_custom_call" | custom-call | flops 3019898880 | bytes 9175040 | tf_op jit(solution)/shard_map/target/pallas_call | solution.py:556
  21.8 0.0 collective-permute-done.5.refs_3_
  21.8 0.0 collective-permute-done.4.refs_2_
  21.9 0.0 collective-permute-done.3.refs_1_
  21.9 0.1 collective-permute-start.6
  22.0 1.6 %prepare.1 = (bf16[320,960]{1,0:T(8,128)(2,1)S(1)}, s32[1,2048]{1,0:T(1,128)S(1)}, bf16[256,128]{1,0:T(8,128)(2,1)S(1)}, f32[128,64]{1,0:T(8,128)S(1)}) custom-call(bf16[640,768]{1,0:T(8,128)(2,1)S(1)} %get-tuple-element.30.pair, s32[4,8]{1,0:T(4,128)S(1)} %get-tuple-element.27.crops_vmem.crops_ref, f32[768,128]{1,0:T(8,128)S(1)} %stack.3.own_ref.before_ref), custom_call_target="tpu_custom_call" | custom-call | flops 629145600 | bytes 2801664 | tf_op jit(solution)/shard_map/prepare/pallas_call | solution.py:585
  23.6 0.1 collective-permute-done.6.other_ref
  23.7 1.9 %context.1 = (bf16[320,256]{1,0:T(8,128)(2,1)S(1)}, f32[128,320]{1,0:T(8,128)S(1)}, f32[320,1024]{1,0:T(8,128)S(1)}, f32[320,512]{1,0:T(8,128)S(1)}) custom-call(s32[4,8]{1,0:T(4,128)S(1)} %get-tuple-element.27.crops_vmem.crops_ref, f32[768,128]{1,0:T(8,128)S(1)} %stack.3.own_ref.before_ref, f32[768,128]{1,0:T(8,128)S(1)} %collective-permute-done.6.other_ref, ...), custom_call_target="tpu_custom_call" | custom-call | flops 78643200 | bytes 4915200 | tf_op jit(solution)/shard_map/context/pallas_call | solution.py:600
  25.6 4.3 %middle.1 = (f32[320,2048]{1,0:T(8,128)}, f32[320,512]{1,0:T(8,128)S(1)}, bf16[960,768]{1,0:T(8,128)(2,1)S(1)}, f32[128,320]{1,0:T(8,128)S(1)}) custom-call(bf16[320,256]{1,0:T(8,128)(2,1)S(1)} %get-tuple-element.35.projected, bf16[320,960]{1,0:T(8,128)(2,1)S(1)} %get-tuple-element.36.grams, s32[1,2048]{1,0:T(1,128)S(1)} %get-tuple-element.37.wanted, ...), custom_call_target="tpu_custom_call" | custom-call | flops 1258291200 | bytes 12779520 | tf_op jit(solution)/shard_map/middle/pallas_call | solution.py:619
  29.9 1.7 %closing.1 = f32[256,256]{1,0:T(8,128)} custom-call(f32[128,320]{1,0:T(8,128)S(1)} %get-tuple-element.43.dslot_ref, f32[128,320]{1,0:T(8,128)S(1)} %get-tuple-element.44.slope_ref, bf16[384,320]{1,0:T(8,128)(2,1)S(1)} %get-tuple-element.33.coarses, bf16[640,320]{1,0:T(8,128)(2,1)S(1)} %get-tuple-element.34.projects, ...), custom_call_target="tpu_custom_call" | custom-call | flops 78643200 | bytes 524288 | tf_op jit(solution)/shard_map/closing/pallas_call | solution.py:645
  31.7 4.5 %all-to-all-start = ((f32[16,16,256]{2,1,0:T(8,128)}), f32[16,16,256]{2,1,0:T(8,128)S(1)}, u32[]{:S(2)}, u32[]{:S(2)}) async-start(f32[16,16,256]{2,1,0:T(8,128)} %bitcast.4), calls=%async_computation | async-start | bytes 524288 | tf_op jit(solution)/shard_map/all_to_all | solution.py:654
  36.2 5.7 %last.1.done_ref = f32[2048,768]{1,0:T(8,128)} custom-call(f32[320,2048]{1,0:T(8,128)} %get-tuple-element.47.de_hbm, f32[320,512]{1,0:T(8,128)S(1)} %get-tuple-element.48.first, bf16[960,768]{1,0:T(8,128)(2,1)S(1)} %get-tuple-element.49.deep), custom_call_target="tpu_custom_call" | custom-call | flops 3019898880 | bytes 12582912 | tf_op jit(solution)/shard_map/last/pallas_call | solution.py:656
  41.9 4.4 %all-to-all-done = f32[16,16,256]{2,1,0:T(8,128)S(1)} async-done(((f32[16,16,256]{2,1,0:T(8,128)}), f32[16,16,256]{2,1,0:T(8,128)S(1)}, u32[]{:S(2)}, u32[]{:S(2)}) %all-to-all-start) | async-done | bytes 262176 | tf_op jit(solution)/shard_map/all_to_all | solution.py:654
  46.3 0.3 scatter.1
  46.5 1.6 %collective-permute-start.7 = (f32[1,32,192]{2,1,0:T(8,128)S(1)}, f32[1,32,192]{2,1,0:T(8,128)S(1)}, u32[]{:S(2)}, u32[]{:S(2)}) collective-permute-start(f32[1,32,192]{2,1,0:T(8,128)S(1)} %get-tuple-element.51), channel_id=1, source_target_pairs={{0,16},{16,0},{1,17},{17,1},{2,18},{18,2},{3,19},{19,3},{4,20},{20... | collective-permute-start | bytes 73736 | tf_op jit(solution)/shard_map/ppermute | solution.py:683
  48.1 2.4 %collective-permute-done.7 = f32[1,32,192]{2,1,0:T(8,128)S(1)} collective-permute-done((f32[1,32,192]{2,1,0:T(8,128)S(1)}, f32[1,32,192]{2,1,0:T(8,128)S(1)}, u32[]{:S(2)}, u32[]{:S(2)}) %collective-permute-start.7) | collective-permute-done | bytes 24608 | tf_op jit(solution)/shard_map/ppermute | solution.py:683
  50.5 0.6 %add.3 = f32[1,32,192]{2,1,0:T(8,128)} add(f32[1,32,192]{2,1,0:T(8,128)S(1)} %get-tuple-element.50, f32[1,32,192]{2,1,0:T(8,128)S(1)} %collective-permute-done.7) | non-fusion elementwise | flops 6144 | bytes 73728 | tf_op jit(solution)/shard_map/add | solution.py:683
  (1 shorter events, 0.0 us)
Async XLA Ops:
  0.6 13.0 %collective-permute-start.1 = (f32[1,32,192]{2,1,0:T(8,128)}, f32[1,32,192]{2,1,0:T(8,128)S(1)}, u32[]{:S(2)}, u32[]{:S(2)}) collective-permute-start(f32[1,32,192]{2,1,0:T(8,128)} %refs_0_.1), channel_id=1, source_target_pairs={{0,4},{4,8},{8,12},{12,0},{1,5},{5,9},{9,13},{13,1},{2,6},{6,10},{... | collective-permute-start | bytes 73736 | tf_op jit(solution)/shard_map/ppermute | solution.py:519
  3.7 9.9 %collective-permute-start = (f32[1,32,192]{2,1,0:T(8,128)}, f32[1,32,192]{2,1,0:T(8,128)S(1)}, u32[]{:S(2)}, u32[]{:S(2)}) collective-permute-start(f32[1,32,192]{2,1,0:T(8,128)} %refs_0_.1), channel_id=1, source_target_pairs={{0,12},{4,0},{8,4},{12,8},{1,13},{5,1},{9,5},{13,9},{2,14},{6,2},{... | collective-permute-start | bytes 73736 | tf_op jit(solution)/shard_map/ppermute | solution.py:519
  5.8 7.8 %collective-permute-start.2 = (f32[1,32,192]{2,1,0:T(8,128)}, f32[1,32,192]{2,1,0:T(8,128)S(1)}, u32[]{:S(2)}, u32[]{:S(2)}) collective-permute-start(f32[1,32,192]{2,1,0:T(8,128)} %refs_0_.1), channel_id=1, source_target_pairs={{0,8},{4,12},{8,0},{12,4},{1,9},{5,13},{9,1},{13,5},{2,10},{6,14},... | collective-permute-start | bytes 73736 | tf_op jit(solution)/shard_map/ppermute | solution.py:519
  6.7 6.9 %copy-start = (f32[1,32,192]{2,1,0:T(8,128)S(1)}, f32[1,32,192]{2,1,0:T(8,128)}, u32[]{:S(2)}) copy-start(f32[1,32,192]{2,1,0:T(8,128)} %refs_0_.1) | copy-start | bytes 73732
  13.7 8.1 %collective-permute-start.5 = (f32[192,128]{1,0:T(8,128)S(1)}, f32[192,128]{1,0:T(8,128)S(1)}, u32[]{:S(2)}, u32[]{:S(2)}) collective-permute-start(f32[192,128]{1,0:T(8,128)S(1)} %stack.2.refs_0_), channel_id=1, source_target_pairs={{0,18},{2,16},{16,2},{18,0},{1,19},{3,17},{17,3},{19,1},{4,22},{6,... | collective-permute-start | bytes 294920 | tf_op jit(solution)/shard_map/ppermute | solution.py:555
  16.2 5.6 %collective-permute-start.4 = (f32[192,128]{1,0:T(8,128)S(1)}, f32[192,128]{1,0:T(8,128)S(1)}, u32[]{:S(2)}, u32[]{:S(2)}) collective-permute-start(f32[192,128]{1,0:T(8,128)S(1)} %stack.2.refs_0_), channel_id=1, source_target_pairs={{0,16},{2,18},{16,0},{18,2},{1,17},{3,19},{17,1},{19,3},{4,20},{6,... | collective-permute-start | bytes 294920 | tf_op jit(solution)/shard_map/ppermute | solution.py:555
  16.8 5.1 %collective-permute-start.3 = (f32[192,128]{1,0:T(8,128)S(1)}, f32[192,128]{1,0:T(8,128)S(1)}, u32[]{:S(2)}, u32[]{:S(2)}) collective-permute-start(f32[192,128]{1,0:T(8,128)S(1)} %stack.2.refs_0_), channel_id=1, source_target_pairs={{0,2},{2,0},{16,18},{18,16},{1,3},{3,1},{17,19},{19,17},{4,6},{6,4... | collective-permute-start | bytes 294920 | tf_op jit(solution)/shard_map/ppermute | solution.py:555
  21.9 1.8 %collective-permute-start.6 = (f32[768,128]{1,0:T(8,128)S(1)}, f32[768,128]{1,0:T(8,128)S(1)}, u32[]{:S(2)}, u32[]{:S(2)}) collective-permute-start(f32[768,128]{1,0:T(8,128)S(1)} %stack.3.own_ref.before_ref), channel_id=1, source_target_pairs={{0,1},{1,0},{2,3},{3,2},{4,5},{5,4},{6,7},{7,6},{8,9},{9,8},{10,11... | collective-permute-start | bytes 1179656 | tf_op jit(solution)/shard_map/ppermute | solution.py:583
  31.7 14.6 %all-to-all-start = ((f32[16,16,256]{2,1,0:T(8,128)}), f32[16,16,256]{2,1,0:T(8,128)S(1)}, u32[]{:S(2)}, u32[]{:S(2)}) async-start(f32[16,16,256]{2,1,0:T(8,128)} %bitcast.4), calls=%async_computation | async-start | bytes 524288 | tf_op jit(solution)/shard_map/all_to_all | solution.py:654
  46.5 4.0 %collective-permute-start.7 = (f32[1,32,192]{2,1,0:T(8,128)S(1)}, f32[1,32,192]{2,1,0:T(8,128)S(1)}, u32[]{:S(2)}, u32[]{:S(2)}) collective-permute-start(f32[1,32,192]{2,1,0:T(8,128)S(1)} %get-tuple-element.51), channel_id=1, source_target_pairs={{0,16},{16,0},{1,17},{17,1},{2,18},{18,2},{3,19},{19,3},{4,20},{20... | collective-permute-start | bytes 73736 | tf_op jit(solution)/shard_map/ppermute | solution.py:683

commit v25 on v21

--- a/solution.py
+++ b/solution.py
@@ -187,11 +187,14 @@
         for i, here in enumerate(chunks[:-1])
     ]
     keep = pltpu.make_async_copy(before_last, before_hbm, sems.at[2])
-    for copy in loads + fetches:
+    for copy in loads[:2]:
         copy.start()
     for i, here in enumerate(chunks):
         if i > 0:
             loads[i - 1].wait()
+        if i == 1:
+            for copy in loads[2:] + fetches:
+                copy.start()
         if i == 2:
             keep.start()
         source = rows if i == 0 else t.at[here]
@@ -304,7 +307,8 @@
         here = near_by % 2 == 0
         for a in range(4):
             row = jnp.minimum(top + a, SIDE - 1)
-            shard = (lax.bitwise_xor(row // 4, side) * 2 + near_by // 2) * far + k
+            code = lax.bitwise_xor(row // 4, side) * 2 + near_by // 2
+            shard = jnp.where(code == 0, 0, 4 - code) * far + k
             row = row % 4
             start = shard * (6 * SIDE)
             wide = pl.ds(pl.multiple_of(start + row * SIDE, SIDE), SIDE)
@@ -553,7 +557,7 @@
     )(*fixed(x, in_weight.T, t, out_weight, crops.T))
     column = stack(pack_kernel, column, xw, half * 3 // 2)
     own = [column]
-    for flip in range(1, 4):
+    for flip in (3, 2, 1):
         own.append(lax.ppermute(column, ("lvl", "y"), [(p, p ^ flip) for p in range(4)]))
     tw, xw_last, tw_last, coarses, projects = call(
         target_kernel,

time: 50.5 us -> 50.5 us (level)
  transfers between devices with their start and end apart: 9 -> 9, of which waited for: 3 -> 4; matrix products, arithmetic and copies ran while one was open for 0% -> 0% of each run, Pallas kernels for 35% -> 35%
where the time goes in v25:
time: 50.5 us; the launch traced here: 50.2 us
  Pallas kernels  26.1 us (52%)
  starting transfers between devices  15.4 us (30%)
  waiting for transfers between devices  7.35 us (15%)
  between operations  0.76 us (2%)
  other arithmetic  0.62 us (1%)
    ppermute x3, starting transfers between devices, body(): lax.ppermute(coarse_input, 'far', [(p, (p + k) % far) for p in range(far)])  6.11 us
    pallas_call x1, Pallas kernels, body(): call(input_kernel, 'input', 6 * count * values * width, (pltpu.HBM((width...  5.9 us
    pallas_call x1, Pallas kernels, body(): call(last_kernel, 'last', 6 * count * values * width, pltpu.HBM((count, v...  5.66 us
    pallas_call x1, Pallas kernels, body(): call(target_kernel, 'target', 6 * count * values * width, (pltpu.HBM((wid...  4.55 us
    all_to_all x1, waiting for transfers between devices, body(): returned = lax.all_to_all(back, patch, 0, 0, tiled=True)  4.38 us
    pallas_call x1, Pallas kernels, body(): call(middle_kernel, 'middle', 6 * count * width * width, (pltpu.HBM((widt...  4.29 us
    all_to_all x1, starting transfers between devices, body(): returned = lax.all_to_all(back, patch, 0, 0, tiled=True)  4.08 us
    ppermute x3, starting transfers between devices, body(): lax.ppermute(column, ('lvl', 'y'), [(p, p ^ flip) for p in range(4)])  3.55 us
  transfers between devices with their start and end apart: 9, of which 4 were waited for; matrix products, arithmetic and copies ran while one was open for 0% of the time, Pallas kernels for 35%

profile of v25, /device:TPU:0, one launch (start us, length us, event | category | flops | bytes accessed | tf_op | source)
XLA Modules:
  0.0 50.2 jit_solution(7937423664033240111)
XLA Ops:
  0.6 3.1 %collective-permute-start.1 = (f32[1,32,192]{2,1,0:T(8,128)}, f32[1,32,192]{2,1,0:T(8,128)S(1)}, u32[]{:S(2)}, u32[]{:S(2)}) collective-permute-start(f32[1,32,192]{2,1,0:T(8,128)} %refs_0_.1), channel_id=1, source_target_pairs={{0,4},{4,8},{8,12},{12,0},{1,5},{5,9},{9,13},{13,1},{2,6},{6,10},{... | collective-permute-start | bytes 73736 | tf_op jit(solution)/shard_map/ppermute | solution.py:525
  3.7 2.1 %collective-permute-start = (f32[1,32,192]{2,1,0:T(8,128)}, f32[1,32,192]{2,1,0:T(8,128)S(1)}, u32[]{:S(2)}, u32[]{:S(2)}) collective-permute-start(f32[1,32,192]{2,1,0:T(8,128)} %refs_0_.1), channel_id=1, source_target_pairs={{0,12},{4,0},{8,4},{12,8},{1,13},{5,1},{9,5},{13,9},{2,14},{6,2},{... | collective-permute-start | bytes 73736 | tf_op jit(solution)/shard_map/ppermute | solution.py:525
  5.8 0.9 %collective-permute-start.2 = (f32[1,32,192]{2,1,0:T(8,128)}, f32[1,32,192]{2,1,0:T(8,128)S(1)}, u32[]{:S(2)}, u32[]{:S(2)}) collective-permute-start(f32[1,32,192]{2,1,0:T(8,128)} %refs_0_.1), channel_id=1, source_target_pairs={{0,8},{4,12},{8,0},{12,4},{1,9},{5,13},{9,1},{13,5},{2,10},{6,14},... | collective-permute-start | bytes 73736 | tf_op jit(solution)/shard_map/ppermute | solution.py:525
  6.7 0.0 copy-start
  6.7 5.9 %input.1 = (f32[320,1536]{1,0:T(8,128)}, f32[320,512]{1,0:T(8,128)S(1)}, bf16[640,768]{1,0:T(8,128)(2,1)}, f32[512,768]{1,0:T(8,128)S(1)}, bf16[640,768]{1,0:T(8,128)(2,1)S(1)}, /*index=5*/s32[4,8]{1,0:T(4,128)S(1)}) custom-call(f32[2048,768]{1,0:T(8,128)} %bitcast.9, f32[320,768]{1,0:T(8,128)} %bitcast.12, f32[2048,768]{1,0:T(8,128)} %bitcast.10, ...), custom_call_target="tpu_custom_call" | custom-call | flops 3019898880 | bytes 16253184 | tf_op jit(solution)/shard_map/input/pallas_call | solution.py:531
  12.7 0.0 collective-permute-done.1.refs_2_
  12.7 0.0 collective-permute-done.refs_1_
  12.7 0.0 collective-permute-done.2.refs_3_
  12.7 0.0 copy-done
  12.7 0.1 stack.2.refs_0_
  12.8 1.6 %collective-permute-start.5 = (f32[192,128]{1,0:T(8,128)S(1)}, f32[192,128]{1,0:T(8,128)S(1)}, u32[]{:S(2)}, u32[]{:S(2)}) collective-permute-start(f32[192,128]{1,0:T(8,128)S(1)} %stack.2.refs_0_), channel_id=1, source_target_pairs={{0,2},{2,0},{16,18},{18,16},{1,3},{3,1},{17,19},{19,17},{4,6},{6,4... | collective-permute-start | bytes 294920 | tf_op jit(solution)/shard_map/ppermute | solution.py:561
  14.4 1.5 %collective-permute-start.4 = (f32[192,128]{1,0:T(8,128)S(1)}, f32[192,128]{1,0:T(8,128)S(1)}, u32[]{:S(2)}, u32[]{:S(2)}) collective-permute-start(f32[192,128]{1,0:T(8,128)S(1)} %stack.2.refs_0_), channel_id=1, source_target_pairs={{0,16},{2,18},{16,0},{18,2},{1,17},{3,19},{17,1},{19,3},{4,20},{6,... | collective-permute-start | bytes 294920 | tf_op jit(solution)/shard_map/ppermute | solution.py:561
  15.9 0.5 collective-permute-start.3
  16.3 4.6 %target.1 = (f32[320,1536]{1,0:T(8,128)}, f32[320,512]{1,0:T(8,128)}, f32[320,512]{1,0:T(8,128)S(1)}, bf16[384,320]{1,0:T(8,128)(2,1)S(1)}, bf16[640,320]{1,0:T(8,128)(2,1)S(1)}) custom-call(f32[2048,768]{1,0:T(8,128)} %bitcast.11, f32[192,320]{1,0:T(8,128)} %cwgt_hbm.1, f32[320,320]{1,0:T(8,128)} %xwgt_hbm.1, f32[512,768]{1,0:T(8,128)S(1)} %get-tuple-element.29.rows, ...), custom_call_target="tpu_custom_call" | custom-call | flops 3019898880 | bytes 9175040 | tf_op jit(solution)/shard_map/target/pallas_call | solution.py:562
  20.9 0.0 collective-permute-done.5.refs_3_
  20.9 0.0 collective-permute-done.4.refs_2_
  20.9 0.5 collective-permute-done.3.refs_1_
  21.4 0.1 collective-permute-start.6
  21.5 1.6 %prepare.1 = (bf16[320,960]{1,0:T(8,128)(2,1)S(1)}, s32[1,2048]{1,0:T(1,128)S(1)}, bf16[256,128]{1,0:T(8,128)(2,1)S(1)}, f32[128,64]{1,0:T(8,128)S(1)}) custom-call(bf16[640,768]{1,0:T(8,128)(2,1)S(1)} %get-tuple-element.30.pair, s32[4,8]{1,0:T(4,128)S(1)} %get-tuple-element.27.crops_vmem.crops_ref, f32[768,128]{1,0:T(8,128)S(1)} %stack.3.own_ref.before_ref), custom_call_target="tpu_custom_call" | custom-call | flops 629145600 | bytes 2801664 | tf_op jit(solution)/shard_map/prepare/pallas_call | solution.py:591
  23.1 0.1 collective-permute-done.6.other_ref
  23.2 2.0 %context.1 = (bf16[320,256]{1,0:T(8,128)(2,1)S(1)}, f32[128,320]{1,0:T(8,128)S(1)}, f32[320,1024]{1,0:T(8,128)S(1)}, f32[320,512]{1,0:T(8,128)S(1)}) custom-call(s32[4,8]{1,0:T(4,128)S(1)} %get-tuple-element.27.crops_vmem.crops_ref, f32[768,128]{1,0:T(8,128)S(1)} %stack.3.own_ref.before_ref, f32[768,128]{1,0:T(8,128)S(1)} %collective-permute-done.6.other_ref, ...), custom_call_target="tpu_custom_call" | custom-call | flops 78643200 | bytes 4915200 | tf_op jit(solution)/shard_map/context/pallas_call | solution.py:606
  25.2 4.3 %middle.1 = (f32[320,2048]{1,0:T(8,128)}, f32[320,512]{1,0:T(8,128)S(1)}, bf16[960,768]{1,0:T(8,128)(2,1)S(1)}, f32[128,320]{1,0:T(8,128)S(1)}) custom-call(bf16[320,256]{1,0:T(8,128)(2,1)S(1)} %get-tuple-element.35.projected, bf16[320,960]{1,0:T(8,128)(2,1)S(1)} %get-tuple-element.36.grams, s32[1,2048]{1,0:T(1,128)S(1)} %get-tuple-element.37.wanted, ...), custom_call_target="tpu_custom_call" | custom-call | flops 1258291200 | bytes 12779520 | tf_op jit(solution)/shard_map/middle/pallas_call | solution.py:625
  29.5 1.7 %closing.1 = f32[256,256]{1,0:T(8,128)} custom-call(f32[128,320]{1,0:T(8,128)S(1)} %get-tuple-element.43.dslot_ref, f32[128,320]{1,0:T(8,128)S(1)} %get-tuple-element.44.slope_ref, bf16[384,320]{1,0:T(8,128)(2,1)S(1)} %get-tuple-element.33.coarses, bf16[640,320]{1,0:T(8,128)(2,1)S(1)} %get-tuple-element.34.projects, ...), custom_call_target="tpu_custom_call" | custom-call | flops 78643200 | bytes 524288 | tf_op jit(solution)/shard_map/closing/pallas_call | solution.py:651
  31.2 4.1 %all-to-all-start = ((f32[16,16,256]{2,1,0:T(8,128)}), f32[16,16,256]{2,1,0:T(8,128)S(1)}, u32[]{:S(2)}, u32[]{:S(2)}) async-start(f32[16,16,256]{2,1,0:T(8,128)} %bitcast.4), calls=%async_computation | async-start | bytes 524288 | tf_op jit(solution)/shard_map/all_to_all | solution.py:660
  35.3 5.7 %last.1.done_ref = f32[2048,768]{1,0:T(8,128)} custom-call(f32[320,2048]{1,0:T(8,128)} %get-tuple-element.47.de_hbm, f32[320,512]{1,0:T(8,128)S(1)} %get-tuple-element.48.first, bf16[960,768]{1,0:T(8,128)(2,1)S(1)} %get-tuple-element.49.deep), custom_call_target="tpu_custom_call" | custom-call | flops 3019898880 | bytes 12582912 | tf_op jit(solution)/shard_map/last/pallas_call | solution.py:662
  41.0 4.4 %all-to-all-done = f32[16,16,256]{2,1,0:T(8,128)S(1)} async-done(((f32[16,16,256]{2,1,0:T(8,128)}), f32[16,16,256]{2,1,0:T(8,128)S(1)}, u32[]{:S(2)}, u32[]{:S(2)}) %all-to-all-start) | async-done | bytes 262176 | tf_op jit(solution)/shard_map/all_to_all | solution.py:660
  45.3 0.3 scatter.1
  45.6 1.6 %collective-permute-start.7 = (f32[1,32,192]{2,1,0:T(8,128)S(1)}, f32[1,32,192]{2,1,0:T(8,128)S(1)}, u32[]{:S(2)}, u32[]{:S(2)}) collective-permute-start(f32[1,32,192]{2,1,0:T(8,128)S(1)} %get-tuple-element.51), channel_id=1, source_target_pairs={{0,16},{16,0},{1,17},{17,1},{2,18},{18,2},{3,19},{19,3},{4,20},{20... | collective-permute-start | bytes 73736 | tf_op jit(solution)/shard_map/ppermute | solution.py:689
  47.2 2.4 %collective-permute-done.7 = f32[1,32,192]{2,1,0:T(8,128)S(1)} collective-permute-done((f32[1,32,192]{2,1,0:T(8,128)S(1)}, f32[1,32,192]{2,1,0:T(8,128)S(1)}, u32[]{:S(2)}, u32[]{:S(2)}) %collective-permute-start.7) | collective-permute-done | bytes 24608 | tf_op jit(solution)/shard_map/ppermute | solution.py:689
  49.6 0.6 %add.3 = f32[1,32,192]{2,1,0:T(8,128)} add(f32[1,32,192]{2,1,0:T(8,128)S(1)} %get-tuple-element.50, f32[1,32,192]{2,1,0:T(8,128)S(1)} %collective-permute-done.7) | non-fusion elementwise | flops 6144 | bytes 73728 | tf_op jit(solution)/shard_map/add | solution.py:689
  (1 shorter events, 0.0 us)
Async XLA Ops:
  0.6 12.0 %collective-permute-start.1 = (f32[1,32,192]{2,1,0:T(8,128)}, f32[1,32,192]{2,1,0:T(8,128)S(1)}, u32[]{:S(2)}, u32[]{:S(2)}) collective-permute-start(f32[1,32,192]{2,1,0:T(8,128)} %refs_0_.1), channel_id=1, source_target_pairs={{0,4},{4,8},{8,12},{12,0},{1,5},{5,9},{9,13},{13,1},{2,6},{6,10},{... | collective-permute-start | bytes 73736 | tf_op jit(solution)/shard_map/ppermute | solution.py:525
  3.7 9.0 %collective-permute-start = (f32[1,32,192]{2,1,0:T(8,128)}, f32[1,32,192]{2,1,0:T(8,128)S(1)}, u32[]{:S(2)}, u32[]{:S(2)}) collective-permute-start(f32[1,32,192]{2,1,0:T(8,128)} %refs_0_.1), channel_id=1, source_target_pairs={{0,12},{4,0},{8,4},{12,8},{1,13},{5,1},{9,5},{13,9},{2,14},{6,2},{... | collective-permute-start | bytes 73736 | tf_op jit(solution)/shard_map/ppermute | solution.py:525
  5.8 6.9 %collective-permute-start.2 = (f32[1,32,192]{2,1,0:T(8,128)}, f32[1,32,192]{2,1,0:T(8,128)S(1)}, u32[]{:S(2)}, u32[]{:S(2)}) collective-permute-start(f32[1,32,192]{2,1,0:T(8,128)} %refs_0_.1), channel_id=1, source_target_pairs={{0,8},{4,12},{8,0},{12,4},{1,9},{5,13},{9,1},{13,5},{2,10},{6,14},... | collective-permute-start | bytes 73736 | tf_op jit(solution)/shard_map/ppermute | solution.py:525
  6.7 5.9 %copy-start = (f32[1,32,192]{2,1,0:T(8,128)S(1)}, f32[1,32,192]{2,1,0:T(8,128)}, u32[]{:S(2)}) copy-start(f32[1,32,192]{2,1,0:T(8,128)} %refs_0_.1) | copy-start | bytes 73732
  12.8 8.1 %collective-permute-start.5 = (f32[192,128]{1,0:T(8,128)S(1)}, f32[192,128]{1,0:T(8,128)S(1)}, u32[]{:S(2)}, u32[]{:S(2)}) collective-permute-start(f32[192,128]{1,0:T(8,128)S(1)} %stack.2.refs_0_), channel_id=1, source_target_pairs={{0,2},{2,0},{16,18},{18,16},{1,3},{3,1},{17,19},{19,17},{4,6},{6,4... | collective-permute-start | bytes 294920 | tf_op jit(solution)/shard_map/ppermute | solution.py:561
  14.4 6.5 %collective-permute-start.4 = (f32[192,128]{1,0:T(8,128)S(1)}, f32[192,128]{1,0:T(8,128)S(1)}, u32[]{:S(2)}, u32[]{:S(2)}) collective-permute-start(f32[192,128]{1,0:T(8,128)S(1)} %stack.2.refs_0_), channel_id=1, source_target_pairs={{0,16},{2,18},{16,0},{18,2},{1,17},{3,19},{17,1},{19,3},{4,20},{6,... | collective-permute-start | bytes 294920 | tf_op jit(solution)/shard_map/ppermute | solution.py:561
  15.9 5.5 %collective-permute-start.3 = (f32[192,128]{1,0:T(8,128)S(1)}, f32[192,128]{1,0:T(8,128)S(1)}, u32[]{:S(2)}, u32[]{:S(2)}) collective-permute-start(f32[192,128]{1,0:T(8,128)S(1)} %stack.2.refs_0_), channel_id=1, source_target_pairs={{0,18},{2,16},{16,2},{18,0},{1,19},{3,17},{17,3},{19,1},{4,22},{6,... | collective-permute-start | bytes 294920 | tf_op jit(solution)/shard_map/ppermute | solution.py:561
  21.4 1.8 %collective-permute-start.6 = (f32[768,128]{1,0:T(8,128)S(1)}, f32[768,128]{1,0:T(8,128)S(1)}, u32[]{:S(2)}, u32[]{:S(2)}) collective-permute-start(f32[768,128]{1,0:T(8,128)S(1)} %stack.3.own_ref.before_ref), channel_id=1, source_target_pairs={{0,1},{1,0},{2,3},{3,2},{4,5},{5,4},{6,7},{7,6},{8,9},{9,8},{10,11... | collective-permute-start | bytes 1179656 | tf_op jit(solution)/shard_map/ppermute | solution.py:589
  31.2 14.1 %all-to-all-start = ((f32[16,16,256]{2,1,0:T(8,128)}), f32[16,16,256]{2,1,0:T(8,128)S(1)}, u32[]{:S(2)}, u32[]{:S(2)}) async-start(f32[16,16,256]{2,1,0:T(8,128)} %bitcast.4), calls=%async_computation | async-start | bytes 524288 | tf_op jit(solution)/shard_map/all_to_all | solution.py:660
  45.6 4.0 %collective-permute-start.7 = (f32[1,32,192]{2,1,0:T(8,128)S(1)}, f32[1,32,192]{2,1,0:T(8,128)S(1)}, u32[]{:S(2)}, u32[]{:S(2)}) collective-permute-start(f32[1,32,192]{2,1,0:T(8,128)S(1)} %get-tuple-element.51), channel_id=1, source_target_pairs={{0,16},{16,0},{1,17},{17,1},{2,18},{18,2},{3,19},{19,3},{4,20},{20... | collective-permute-start | bytes 73736 | tf_op jit(solution)/shard_map/ppermute | solution.py:689
